TPU v7x, 32 devices: a whole 2x2x4 slice. The times are simulated.
32 devices in a mesh: wide: 16 (over z, y, x), chain: 2 (over core).
Axes of the slice: x: 2, y: 2, z: 4, core: 2. Of those that a mesh axis runs over, the one named last changes fastest.
Arguments:
- queries: bfloat16 [8192, 1024], P(('chain', 'wide')), may hold values from -4 to 4
- keys: bfloat16 [8192, 1024], P(('chain', 'wide')), may hold values from -4 to 4
- values: bfloat16 [8192, 1024], P(('chain', 'wide')), may hold values from -6 to 6
Outputs:
- attended: bfloat16 [8192, 1024], P(('chain', 'wide'))
All inputs are finite; a program needn't handle non-finite values.
Results may differ from a plain program's by a relative error of at most 0.005.
Values may be sent and summed in bfloat16 or wider, within the bound.
No kernel may reach another device: no remote copies, remote signals or barrier semaphores. Data moves between devices by JAX's collectives and lax.ppermute only.
A program may use at most 64 MiB of HBM per device.

v0:
```python
import jax
import jax.numpy as jnp
from jax import lax
from jax.sharding import PartitionSpec as P

HEADS = 16
HEAD_DIM = 64


def carried_in(x, axis, combine, identity):
    peers, index = (lax.axis_size(axis), lax.axis_index(axis))
    everything = lax.all_gather(x, axis)
    start = jnp.broadcast_to(jnp.asarray(identity, x.dtype), x.shape)

    def step(k, before):
        reached = k < index
        new = combine(before, everything[k])
        return jnp.where(reached, new, before)

    return lax.fori_loop(0, peers, step, start)


def spread(block, axis, source):
    block = jnp.where(lax.axis_index(axis) == source, block, jnp.zeros_like(block))
    return lax.psum(block, axis)


def add_states(earlier, later):
    return earlier + later


def per_device(queries, keys, values):
    rows = queries.shape[0]
    q_blk = queries.reshape(rows, HEADS, HEAD_DIM)
    k_blk = keys.reshape(rows, HEADS, HEAD_DIM)
    v_blk = values.reshape(rows, HEADS, HEAD_DIM)
    states = jnp.einsum("the,thf->hef", k_blk, v_blk, preferred_element_type=jnp.float32)
    flat_states = states.reshape(HEADS, HEAD_DIM * HEAD_DIM)
    zeros = jnp.zeros_like(flat_states)
    inner = carried_in(flat_states, "wide", add_states, zeros)
    group = spread(inner + flat_states, "wide", lax.axis_size("wide") - 1)
    outer = carried_in(group, "chain", add_states, zeros)
    prefix = (outer + inner).astype(jnp.bfloat16).reshape(HEADS, HEAD_DIM, HEAD_DIM)
    inter = jnp.einsum("the,hef->thf", q_blk, prefix, preferred_element_type=jnp.float32)
    causal = jnp.arange(rows)[:, None] >= jnp.arange(rows)[None, :]
    scores = jnp.einsum("the,she->hts", q_blk, k_blk, preferred_element_type=jnp.float32)
    scores = jnp.where(causal[None], scores, 0.0).astype(jnp.bfloat16)
    intra = jnp.einsum("hts,shf->thf", scores, v_blk, preferred_element_type=jnp.float32)
    total = intra + inter
    normed = total / jnp.sqrt(jnp.mean(total * total, axis=-1, keepdims=True) + 1e-06)
    return normed.astype(jnp.bfloat16).reshape(rows, HEADS * HEAD_DIM)


def solution(mesh):
    placed = (P(("chain", "wide"), None), P(("chain", "wide"), None), P(("chain", "wide"), None))
    return jax.shard_map(
        per_device,
        mesh=mesh,
        in_specs=placed,
        out_specs=P(("chain", "wide"), None),
        check_vma=False,
    )
```

profile of v0, /device:TPU:0, one launch (start us, length us, event | category | flops | bytes accessed | tf_op | source)
XLA Modules:
  0.0 223.6 jit_solution(18276056888529031786)
XLA Ops:
  6.5 0.0 copy-start
  6.5 0.0 all-gather.2.cloned.1.call-start
  6.5 1.3 copy.16
  7.8 1.2 copy.17
  9.1 0.3 fusion.4
  9.4 0.9 all_gather_reshape.3
  10.3 0.0 all-gather.2.cloned.1.call-update
  10.3 0.0 all-reduce.2.cloned.1.call-start
  10.4 0.2 reshape.41
  10.5 0.0 copy-done
  10.6 0.2 copy.15
  10.8 78.4 %all-gather.2.cloned.1.call-done = f32[16,16,4096]{2,1,0:T(8,128)} async-done(((f32[1,16,4096]{2,1,0:T(8,128)}), f32[16,16,4096]{2,1,0:T(8,128)}) %all-gather.2.cloned.1.call-update) | async-done | bytes 4194320 | tf_op jit(solution)/shard_map/all_gather | solution.py:12
  89.2 16.9 %while.28 = (s32[]{:T(128)}, f32[16,4096]{1,0:T(8,128)S(1)}, s32[]{:T(128)}, f32[16,16,4096]{2,1,0:T(8,128)}, s32[]{:T(128)}, /*index=5*/s32[]{:T(128)}) while((s32[]{:T(128)}, f32[16,4096]{1,0:T(8,128)S(1)}, s32[]{:T(128)}, f32[16,16,4096]{2,1,0:T(8,128)}, s32[]{:T(128)}, /*index=5*/s32[]{:T(128)}) %tuple.60), condition=%wide.region_1.2_spmd.clone, body=%wide.region_0.1_spmd.clone.sunk | while | flops 196612 | bytes 786525 | solution.py:20
  89.2 1.0 add_select_fusion.4
  90.3 1.0 add_select_fusion.4
  91.3 1.0 add_select_fusion.4
  92.4 1.0 add_select_fusion.4
  93.5 1.0 add_select_fusion.4
  94.5 1.0 add_select_fusion.4
  95.6 1.0 add_select_fusion.4
  96.6 1.0 add_select_fusion.4
  97.7 1.0 add_select_fusion.4
  98.7 1.0 add_select_fusion.4
  99.8 1.0 add_select_fusion.4
  100.9 1.0 add_select_fusion.4
  101.9 1.0 add_select_fusion.4
  103.0 1.0 add_select_fusion.4
  104.0 1.0 add_select_fusion.4
  105.1 1.0 add_select_fusion.4
  106.1 0.7 select_bitcast_fusion
  106.9 0.0 all-reduce.2.cloned.1.call-update
  106.9 1.3 fusion.2
  108.2 104.1 %all-reduce.2.cloned.1.call-done = f32[1,16,4096]{2,1,0:T(8,128)} async-done(((f32[1,16,4096]{2,1,0:T(8,128)}), f32[1,16,4096]{2,1,0:T(8,128)}) %all-reduce.2.cloned.1.call-update) | async-done | bytes 262160 | tf_op jit(solution)/shard_map/psum | solution.py:25
  212.4 2.4 %all_gather.11 = f32[2,16,4096]{2,1,0:T(8,128)S(1)} all-gather(f32[1,16,4096]{2,1,0:T(8,128)} %all-reduce.2.cloned.1.call-done), channel_id=1, replica_groups=mesh['wide'=16,'chain'=2] {'chain'}, dimensions={0}, use_global_device_ids=true | all-gather | bytes 786432 | tf_op jit(solution)/shard_map/all_gather | solution.py:12
  214.7 0.2 while.29
  214.7 0.1 add_select_fusion.5
  214.8 0.1 add_select_fusion.5
  215.0 0.2 reshape.42
  215.2 0.4 multiply_reduce_fusion
  215.6 0.1 divide_convert_fusion
  215.7 1.0 copy.19
  (5 shorter events, 0.1 us)
Async XLA Ops:
  6.5 4.0 %copy-start = (bf16[256,1024]{1,0:T(8,128)(2,1)S(1)}, bf16[256,1024]{1,0:T(8,128)(2,1)}, u32[]{:S(2)}) copy-start(bf16[256,1024]{1,0:T(8,128)(2,1)} %param.7) | copy-start | bytes 1572868
  6.5 82.7 %all-gather.2.cloned.1.call-start = ((), (), s32[]{:S(2)}) async-start(), calls=%async_computation | async-start | bytes 4456448 | tf_op jit(solution)/shard_map/all_gather | solution.py:12
  10.3 202.1 %all-reduce.2.cloned.1.call-start = ((), (), s32[]{:S(2)}) async-start(), calls=%async_computation.1 | async-start | bytes 524288 | tf_op jit(solution)/shard_map/psum | solution.py:25
Sparse Core Ops, SparseCore 0:
  10.4 78.7 all-gather.1
  107.0 105.3 all-reduce.1
where the time goes:
time: 224 us
  waiting for transfers between devices  183 us (82%)
  other arithmetic  17.6 us (8%)
  between operations  13.5 us (6%)
  local copies, waits for them, and re-layouts  5.07 us (2%)
  blocking collectives  2.38 us (1%)
    psum x1, waiting for transfers between devices, spread(): return lax.psum(block, axis)  104 us
    all_gather x1, waiting for transfers between devices, carried_in(): everything = lax.all_gather(x, axis)  78.4 us
    select_n x18, other arithmetic, step(): return jnp.where(reached, new, before)  16.7 us
  transfers between devices with their start and end apart: 2, of which 2 were waited for; matrix products, arithmetic and copies ran while one was open for 1% of the time, Pallas kernels for 0%

commit v1 on v0

v1 whole, which is shorter than its diff:
```python
import functools

import jax
import jax.numpy as jnp
from jax import lax
from jax.experimental import pallas as pl
from jax.experimental.pallas import tpu as pltpu
from jax.sharding import PartitionSpec as P

HEADS = 16
HEAD_DIM = 64
PAIRS = HEADS // 2
LANES = 2 * HEAD_DIM
AXES = ("chain", "wide")
VMEM = pl.BlockSpec(memory_space=pltpu.VMEM)


def first_head(shape):
    return lax.broadcasted_iota(jnp.int32, shape, len(shape) - 1) < HEAD_DIM


def lanes_of(p):
    return slice(p * LANES, (p + 1) * LANES)


def rows_of(p):
    return slice(p * HEAD_DIM, (p + 1) * HEAD_DIM)


def states_kernel(k_ref, v_ref, out_ref):
    first = first_head((HEAD_DIM, LANES))
    for p in range(PAIRS):
        both = lax.dot_general(
            k_ref[:, lanes_of(p)], v_ref[:, lanes_of(p)], (((0,), (0,)), ((), ())),
            preferred_element_type=jnp.float32)
        packed = jnp.where(first, both[:HEAD_DIM], both[HEAD_DIM:])
        out_ref[rows_of(p), :] = packed.astype(out_ref.dtype)


def scan_kernel(x_ref, out_ref):
    parts = x_ref.shape[0]
    total = jnp.zeros(x_ref.shape[1:], jnp.float32)
    for i in range(parts):
        out_ref[i] = total.astype(out_ref.dtype)
        if i < parts - 1:
            total = total + x_ref[i].astype(jnp.float32)


def scan_rows_kernel(x_ref, out_ref):
    parts = x_ref.shape[0]
    row = lax.broadcasted_iota(jnp.int32, (parts, parts), 0)
    col = lax.broadcasted_iota(jnp.int32, (parts, parts), 1)
    below = jnp.where(col < row, 1.0, 0.0).astype(jnp.bfloat16)
    out_ref[...] = jnp.dot(below, x_ref[...], preferred_element_type=jnp.float32).astype(out_ref.dtype)


def attend_kernel(q_ref, k_ref, v_ref, prefix_ref, out_ref):
    rows = q_ref.shape[0]
    causal = (lax.broadcasted_iota(jnp.int32, (rows, rows), 0)
              >= lax.broadcasted_iota(jnp.int32, (rows, rows), 1))
    first = first_head((rows, LANES))
    first_state = first_head((HEAD_DIM, LANES))
    same = (first_head((LANES, LANES))
            == (lax.broadcasted_iota(jnp.int32, (LANES, LANES), 0) < HEAD_DIM))
    ones = jnp.where(same, 1.0, 0.0).astype(jnp.bfloat16)
    zero = jnp.zeros((), jnp.bfloat16)
    for p in range(PAIRS):
        q, k, v = q_ref[:, lanes_of(p)], k_ref[:, lanes_of(p)], v_ref[:, lanes_of(p)]
        intra = []
        for mine in (first, ~first):
            scores = lax.dot_general(
                jnp.where(mine, q, zero), k, (((1,), (1,)), ((), ())),
                preferred_element_type=jnp.float32)
            scores = jnp.where(causal, scores, 0.0).astype(jnp.bfloat16)
            intra.append(jnp.dot(scores, v, preferred_element_type=jnp.float32))
        packed = prefix_ref[rows_of(p), :]
        prefix = jnp.concatenate(
            [jnp.where(first_state, packed, zero), jnp.where(first_state, zero, packed)], axis=0)
        inter = jnp.dot(q, prefix, preferred_element_type=jnp.float32)
        total = jnp.where(first, intra[0], intra[1]) + inter
        square = total * total
        high = square.astype(jnp.bfloat16)
        low = (square - high.astype(jnp.float32)).astype(jnp.bfloat16)
        sums = (jnp.dot(high, ones, preferred_element_type=jnp.float32)
                + jnp.dot(low, ones, preferred_element_type=jnp.float32))
        out_ref[:, lanes_of(p)] = (total * lax.rsqrt(sums * (1.0 / HEAD_DIM) + 1e-6)).astype(out_ref.dtype)


def call(kernel, shape, dtype, *args, flops=0):
    moved = sum(a.size * a.dtype.itemsize for a in args)
    return pl.pallas_call(
        kernel,
        out_shape=jax.ShapeDtypeStruct(shape, dtype),
        in_specs=[VMEM] * len(args),
        out_specs=VMEM,
        cost_estimate=pl.CostEstimate(flops=flops, bytes_accessed=moved, transcendentals=0),
        compiler_params=pltpu.CompilerParams(vmem_limit_bytes=32 * 1024 * 1024),
    )(*args)


def per_device(parts, queries, keys, values):
    rows = queries.shape[0]
    state_rows = PAIRS * HEAD_DIM
    share = state_rows // parts
    states = call(states_kernel, (state_rows, LANES), jnp.bfloat16, keys, values,
                  flops=2 * rows * LANES * LANES * PAIRS)
    view = (parts, share, LANES) if share > 1 else (parts, LANES)
    mine = lax.all_to_all(states.reshape(view), AXES, 0, 0, tiled=True)
    before = call(scan_kernel if share > 1 else scan_rows_kernel, view, jnp.bfloat16, mine)
    prefix = lax.all_to_all(before, AXES, 0, 0, tiled=True).reshape(state_rows, LANES)
    return call(attend_kernel, queries.shape, jnp.bfloat16, queries, keys, values, prefix,
                flops=4 * rows * rows * HEADS * HEAD_DIM)


def solution(mesh):
    spec = P(AXES, None)
    parts = mesh.shape["chain"] * mesh.shape["wide"]
    return jax.shard_map(
        functools.partial(per_device, parts),
        mesh=mesh,
        in_specs=(spec, spec, spec),
        out_specs=spec,
        check_vma=False,
    )
```

time: 224 us -> 31.2 us (0.14)
  waiting for transfers between devices: 183 us -> 0 us
  blocking collectives: 2.38 us -> 24.9 us
  other arithmetic: 17.6 us -> 0 us
  between operations: 13.5 us -> 0.02 us
  Pallas kernels: 0 us -> 3.93 us
  local copies, waits for them, and re-layouts: 5.07 us -> 2.09 us
    psum x1 -> x0, waiting for transfers between devices: 104 us -> none  [spread(): return lax.psum(block, axis)]
    all_gather x1 -> x0, waiting for transfers between devices: 78.4 us -> none  [carried_in(): everything = lax.all_gather(x, axis)]
    all_to_all x0 -> x2, blocking collectives: none -> 24.9 us  [the longest x1 15 us: per_device(): mine = lax.all_to_all(states.reshape(view), AXES, 0, 0, tiled=True)]
    select_n x18 -> x0, other arithmetic: 16.7 us -> none  [step(): return jnp.where(reached, new, before)]
    pallas_call x0 -> x3, Pallas kernels: none -> 3.93 us  [call(): pl.pallas_call(kernel, out_shape=jax.ShapeDtypeStruct(shape, dtype), in_s...]
    all_gather x1 -> x0, blocking collectives: 2.38 us -> none  [carried_in(): everything = lax.all_gather(x, axis)]
  transfers between devices with their start and end apart: 2 -> 0, of which waited for: 2 -> 0; matrix products, arithmetic and copies ran while one was open for 1% -> 0% of each run, Pallas kernels for 0% -> 0%
where the time goes in v1:
time: 31.2 us; the launch traced here: 31 us
  blocking collectives  24.9 us (80%)
  Pallas kernels  3.93 us (13%)
  local copies, waits for them, and re-layouts  2.09 us (7%)
    all_to_all x1, blocking collectives, per_device(): mine = lax.all_to_all(states.reshape(view), AXES, 0, 0, tiled=True)  15 us
    all_to_all x1, blocking collectives, per_device(): lax.all_to_all(before, AXES, 0, 0, tiled=True).reshape(state_rows, LANES)  9.92 us
    pallas_call x3, Pallas kernels, call(): pl.pallas_call(kernel, out_shape=jax.ShapeDtypeStruct(shape, dtype), in_s...  3.93 us
    unnamed x8, local copies, waits for them, and re-layouts  2.09 us

profile of v1, /device:TPU:0, one launch (start us, length us, event | category | flops | bytes accessed | tf_op | source)
XLA Modules:
  0.0 31.0 jit_solution(6509802302895342232)
XLA Ops:
  0.0 0.0 copy-start
  0.0 1.0 %copy-done = bf16[256,1024]{1,0:T(8,128)(2,1)S(1)} copy-done((bf16[256,1024]{1,0:T(8,128)(2,1)S(1)}, bf16[256,1024]{1,0:T(8,128)(2,1)}, u32[]{:S(2)}) %copy-start) | copy-done | bytes 524312
  1.0 0.0 copy-start.2
  1.0 1.0 %copy-done.2 = bf16[256,1024]{1,0:T(8,128)(2,1)S(1)} copy-done((bf16[256,1024]{1,0:T(8,128)(2,1)S(1)}, bf16[256,1024]{1,0:T(8,128)(2,1)}, u32[]{:S(2)}) %copy-start.2) | copy-done | bytes 524312
  2.1 0.0 copy-start.3
  2.1 0.4 %shard_map.37 = bf16[512,128]{1,0:T(8,128)(2,1)S(1)} custom-call(bf16[256,1024]{1,0:T(8,128)(2,1)S(1)} %copy-done, bf16[256,1024]{1,0:T(8,128)(2,1)S(1)} %copy-done.2), custom_call_target="tpu_custom_call" | custom-call | flops 67108864 | bytes 1048576 | tf_op jit(solution)/shard_map/pallas_call | solution.py:91
  2.4 0.0 copy-start.1
  2.5 15.0 %all_to_all.10.x_ref = bf16[32,16,128]{2,1,0:T(8,128)(2,1)S(1)} all-to-all(bf16[32,16,128]{2,1,0:T(8,128)(2,1)S(1)} %bitcast.3), channel_id=1, replica_groups=mesh['wide'=16,'chain'=2] {'chain','wide'}, dimensions={0} | all-to-all | bytes 262144 | tf_op jit(solution)/shard_map/all_to_all | solution.py:108
  17.5 9.9 %all_to_all.11 = bf16[32,16,128]{2,1,0:T(8,128)(2,1)S(1)} all-to-all(bf16[32,16,128]{2,1,0:T(8,128)(2,1)S(1)} %shard_map.38), channel_id=1, replica_groups=mesh['wide'=16,'chain'=2] {'chain','wide'}, dimensions={0} | all-to-all | bytes 262144 | tf_op jit(solution)/shard_map/all_to_all | solution.py:110
  27.4 0.0 copy-done.3
  27.4 0.0 copy-done.1
  27.4 3.5 %shard_map.39 = bf16[256,1024]{1,0:T(8,128)(2,1)} custom-call(bf16[256,1024]{1,0:T(8,128)(2,1)S(1)} %copy-done.3, bf16[256,1024]{1,0:T(8,128)(2,1)S(1)} %copy-done.1, bf16[256,1024]{1,0:T(8,128)(2,1)S(1)} %copy-done.2, bf16[512,128]{1,0:T(8,128)(2,1)S(1)} %bitcast.2), custom_call_target="tpu_custom_call" | custom-call | flops 268435456 | bytes 1703936 | tf_op jit(solution)/shard_map/pallas_call | solution.py:91
  (1 shorter events, 0.0 us)
Async XLA Ops:
  0.0 1.0 %copy-start = (bf16[256,1024]{1,0:T(8,128)(2,1)S(1)}, bf16[256,1024]{1,0:T(8,128)(2,1)}, u32[]{:S(2)}) copy-start(bf16[256,1024]{1,0:T(8,128)(2,1)} %k_ref.3) | copy-start | bytes 1572868
  1.0 1.0 %copy-start.2 = (bf16[256,1024]{1,0:T(8,128)(2,1)S(1)}, bf16[256,1024]{1,0:T(8,128)(2,1)}, u32[]{:S(2)}) copy-start(bf16[256,1024]{1,0:T(8,128)(2,1)} %v_ref.3) | copy-start | bytes 1572868
  2.1 25.3 %copy-start.3 = (bf16[256,1024]{1,0:T(8,128)(2,1)S(1)}, bf16[256,1024]{1,0:T(8,128)(2,1)}, u32[]{:S(2)}) copy-start(bf16[256,1024]{1,0:T(8,128)(2,1)} %q_ref.1) | copy-start | bytes 1572868
  2.4 25.0 %copy-start.1 = (bf16[256,1024]{1,0:T(8,128)(2,1)S(1)}, bf16[256,1024]{1,0:T(8,128)(2,1)}, u32[]{:S(2)}) copy-start(bf16[256,1024]{1,0:T(8,128)(2,1)} %k_ref.3) | copy-start | bytes 1572868

commit v2 on v1

--- a/solution.py
+++ b/solution.py
@@ -11,7 +11,10 @@
 HEAD_DIM = 64
 PAIRS = HEADS // 2
 LANES = 2 * HEAD_DIM
+SLABS = 4
+SLAB = HEADS * HEAD_DIM // SLABS
 AXES = ("chain", "wide")
+HBM = pl.BlockSpec(memory_space=pltpu.HBM)
 VMEM = pl.BlockSpec(memory_space=pltpu.VMEM)
 
 
@@ -27,9 +30,20 @@
     return slice(p * HEAD_DIM, (p + 1) * HEAD_DIM)
 
 
-def states_kernel(k_ref, v_ref, out_ref):
+def states_kernel(k_hbm, v_hbm, out_ref, k_ref, v_ref, arrived):
+    copies = []
+    for s in range(SLABS):
+        lanes = slice(s * SLAB, (s + 1) * SLAB)
+        copies.append([
+            pltpu.make_async_copy(k_hbm.at[:, lanes], k_ref.at[:, lanes], arrived.at[0, s]),
+            pltpu.make_async_copy(v_hbm.at[:, lanes], v_ref.at[:, lanes], arrived.at[1, s])])
+        for copy in copies[-1]:
+            copy.start()
     first = first_head((HEAD_DIM, LANES))
     for p in range(PAIRS):
+        if p * LANES % SLAB == 0:
+            for copy in copies[p * LANES // SLAB]:
+                copy.wait()
         both = lax.dot_general(
             k_ref[:, lanes_of(p)], v_ref[:, lanes_of(p)], (((0,), (0,)), ((), ())),
             preferred_element_type=jnp.float32)
@@ -54,15 +68,11 @@
     out_ref[...] = jnp.dot(below, x_ref[...], preferred_element_type=jnp.float32).astype(out_ref.dtype)
 
 
-def attend_kernel(q_ref, k_ref, v_ref, prefix_ref, out_ref):
+def intra_kernel(q_ref, k_ref, v_ref, out_ref):
     rows = q_ref.shape[0]
     causal = (lax.broadcasted_iota(jnp.int32, (rows, rows), 0)
               >= lax.broadcasted_iota(jnp.int32, (rows, rows), 1))
     first = first_head((rows, LANES))
-    first_state = first_head((HEAD_DIM, LANES))
-    same = (first_head((LANES, LANES))
-            == (lax.broadcasted_iota(jnp.int32, (LANES, LANES), 0) < HEAD_DIM))
-    ones = jnp.where(same, 1.0, 0.0).astype(jnp.bfloat16)
     zero = jnp.zeros((), jnp.bfloat16)
     for p in range(PAIRS):
         q, k, v = q_ref[:, lanes_of(p)], k_ref[:, lanes_of(p)], v_ref[:, lanes_of(p)]
@@ -73,11 +83,21 @@
                 preferred_element_type=jnp.float32)
             scores = jnp.where(causal, scores, 0.0).astype(jnp.bfloat16)
             intra.append(jnp.dot(scores, v, preferred_element_type=jnp.float32))
+        out_ref[:, lanes_of(p)] = jnp.where(first, intra[0], intra[1])
+
+
+def attend_kernel(q_ref, intra_ref, prefix_ref, out_ref):
+    first_state = first_head((HEAD_DIM, LANES))
+    same = (first_head((LANES, LANES))
+            == (lax.broadcasted_iota(jnp.int32, (LANES, LANES), 0) < HEAD_DIM))
+    ones = jnp.where(same, 1.0, 0.0).astype(jnp.bfloat16)
+    zero = jnp.zeros((), jnp.bfloat16)
+    for p in range(PAIRS):
         packed = prefix_ref[rows_of(p), :]
         prefix = jnp.concatenate(
             [jnp.where(first_state, packed, zero), jnp.where(first_state, zero, packed)], axis=0)
-        inter = jnp.dot(q, prefix, preferred_element_type=jnp.float32)
-        total = jnp.where(first, intra[0], intra[1]) + inter
+        inter = jnp.dot(q_ref[:, lanes_of(p)], prefix, preferred_element_type=jnp.float32)
+        total = intra_ref[:, lanes_of(p)] + inter
         square = total * total
         high = square.astype(jnp.bfloat16)
         low = (square - high.astype(jnp.float32)).astype(jnp.bfloat16)
@@ -86,15 +106,16 @@
         out_ref[:, lanes_of(p)] = (total * lax.rsqrt(sums * (1.0 / HEAD_DIM) + 1e-6)).astype(out_ref.dtype)
 
 
-def call(kernel, shape, dtype, *args, flops=0):
+def call(kernel, shape, dtype, *args, flops=0, memory=VMEM, scratch=(), limit=16):
     moved = sum(a.size * a.dtype.itemsize for a in args)
     return pl.pallas_call(
         kernel,
         out_shape=jax.ShapeDtypeStruct(shape, dtype),
-        in_specs=[VMEM] * len(args),
+        in_specs=[memory] * len(args),
         out_specs=VMEM,
+        scratch_shapes=scratch,
         cost_estimate=pl.CostEstimate(flops=flops, bytes_accessed=moved, transcendentals=0),
-        compiler_params=pltpu.CompilerParams(vmem_limit_bytes=32 * 1024 * 1024),
+        compiler_params=pltpu.CompilerParams(vmem_limit_bytes=limit * 1024 * 1024),
     )(*args)
 
 
@@ -103,13 +124,17 @@
     state_rows = PAIRS * HEAD_DIM
     share = state_rows // parts
     states = call(states_kernel, (state_rows, LANES), jnp.bfloat16, keys, values,
-                  flops=2 * rows * LANES * LANES * PAIRS)
+                  flops=2 * rows * LANES * LANES * PAIRS, memory=HBM, limit=60,
+                  scratch=[pltpu.VMEM(keys.shape, keys.dtype), pltpu.VMEM(values.shape, values.dtype),
+                           pltpu.SemaphoreType.DMA((2, SLABS))])
+    intra = call(intra_kernel, queries.shape, jnp.float32, queries, keys, values,
+                 flops=4 * rows * rows * HEADS * HEAD_DIM)
     view = (parts, share, LANES) if share > 1 else (parts, LANES)
     mine = lax.all_to_all(states.reshape(view), AXES, 0, 0, tiled=True)
     before = call(scan_kernel if share > 1 else scan_rows_kernel, view, jnp.bfloat16, mine)
     prefix = lax.all_to_all(before, AXES, 0, 0, tiled=True).reshape(state_rows, LANES)
-    return call(attend_kernel, queries.shape, jnp.bfloat16, queries, keys, values, prefix,
-                flops=4 * rows * rows * HEADS * HEAD_DIM)
+    return call(attend_kernel, queries.shape, jnp.bfloat16, queries, intra, prefix,
+                flops=2 * rows * HEAD_DIM * HEAD_DIM * HEADS)
 
 
 def solution(mesh):

time: 31.2 us -> 31.3 us (level)
  blocking collectives: 24.9 us -> 15.2 us
  waiting for transfers between devices: 0 us -> 6.4 us
  Pallas kernels: 3.93 us -> 6.74 us
  starting transfers between devices: 0 us -> 2.58 us
  local copies, waits for them, and re-layouts: 2.09 us -> 0.01 us
    all_to_all x1 -> x0, blocking collectives: 9.92 us -> none  [per_device(): lax.all_to_all(before, AXES, 0, 0, tiled=True).reshape(state_rows, LANES)]
    all_to_all x0 -> x1, waiting for transfers between devices: none -> 6.4 us  [per_device(): lax.all_to_all(before, AXES, 0, 0, tiled=True).reshape(state_rows, LANES)]
    pallas_call x3 -> x4, Pallas kernels: 3.93 us -> 6.74 us  [call(): pl.pallas_call(kernel, out_shape=jax.ShapeDtypeStruct(shape, dtype), in_s...]
    all_to_all x0 -> x1, starting transfers between devices: none -> 2.58 us  [per_device(): lax.all_to_all(before, AXES, 0, 0, tiled=True).reshape(state_rows, LANES)]
    unnamed x8 -> x6, local copies, waits for them, and re-layouts: 2.09 us -> 0.01 us
  transfers between devices with their start and end apart: 0 -> 1, of which waited for: 0 -> 1; matrix products, arithmetic and copies ran while one was open for 0% -> 0% of each run, Pallas kernels for 0% -> 5%
where the time goes in v2:
time: 31.3 us; the launch traced here: 31 us
  blocking collectives  15.2 us (49%)
  Pallas kernels  6.74 us (22%)
  waiting for transfers between devices  6.4 us (20%)
  starting transfers between devices  2.58 us (8%)
    all_to_all x1, blocking collectives, per_device(): mine = lax.all_to_all(states.reshape(view), AXES, 0, 0, tiled=True)  15.2 us
    pallas_call x4, Pallas kernels, call(): pl.pallas_call(kernel, out_shape=jax.ShapeDtypeStruct(shape, dtype), in_s...  6.74 us
    all_to_all x1, waiting for transfers between devices, per_device(): lax.all_to_all(before, AXES, 0, 0, tiled=True).reshape(state_rows, LANES)  6.4 us
    all_to_all x1, starting transfers between devices, per_device(): lax.all_to_all(before, AXES, 0, 0, tiled=True).reshape(state_rows, LANES)  2.58 us
  transfers between devices with their start and end apart: 1, of which 1 were waited for; matrix products, arithmetic and copies ran while one was open for 0% of the time, Pallas kernels for 5%

profile of v2, /device:TPU:0, one launch (start us, length us, event | category | flops | bytes accessed | tf_op | source)
XLA Modules:
  0.0 31.0 jit_solution(8269422332414721407)
XLA Ops:
  0.0 0.0 copy-start.1
  0.0 0.0 copy-start.2
  0.0 2.7 %shard_map.38 = bf16[512,128]{1,0:T(8,128)(2,1)} custom-call(bf16[256,1024]{1,0:T(8,128)(2,1)} %k_hbm.1, bf16[256,1024]{1,0:T(8,128)(2,1)} %v_hbm.1), custom_call_target="tpu_custom_call" | custom-call | flops 67108864 | bytes 1048576 | tf_op jit(solution)/shard_map/pallas_call | solution.py:111
  2.7 0.0 copy-start
  2.8 15.2 %all_to_all.10.x_ref = bf16[32,16,128]{2,1,0:T(8,128)(2,1)S(1)} all-to-all(bf16[32,16,128]{2,1,0:T(8,128)(2,1)} %bitcast.3), channel_id=1, replica_groups=mesh['wide'=16,'chain'=2] {'chain','wide'}, dimensions={0} | all-to-all | bytes 262144 | tf_op jit(solution)/shard_map/all_to_all | solution.py:133
  18.0 0.7 %shard_map.39 = bf16[32,16,128]{2,1,0:T(8,128)(2,1)} custom-call(bf16[32,16,128]{2,1,0:T(8,128)(2,1)S(1)} %all_to_all.10.x_ref), custom_call_target="tpu_custom_call" | custom-call | bytes 131072 | tf_op jit(solution)/shard_map/pallas_call | solution.py:111
  18.7 2.6 %all-to-all-start.1 = ((bf16[32,16,128]{2,1,0:T(8,128)(2,1)}), bf16[32,16,128]{2,1,0:T(8,128)(2,1)S(1)}, u32[]{:S(2)}, u32[]{:S(2)}) async-start(bf16[32,16,128]{2,1,0:T(8,128)(2,1)} %shard_map.39), calls=%async_computation.1 | async-start | bytes 262144 | tf_op jit(solution)/shard_map/all_to_all | solution.py:135
  21.3 0.0 copy-done.1
  21.3 0.0 copy-done.2
  21.3 0.0 copy-done
  21.3 1.5 %shard_map.37.intra_ref = f32[256,1024]{1,0:T(8,128)S(1)} custom-call(bf16[256,1024]{1,0:T(8,128)(2,1)S(1)} %copy-done, bf16[256,1024]{1,0:T(8,128)(2,1)S(1)} %copy-done.1, bf16[256,1024]{1,0:T(8,128)(2,1)S(1)} %copy-done.2), custom_call_target="tpu_custom_call" | custom-call | flops 268435456 | bytes 1572864 | tf_op jit(solution)/shard_map/pallas_call | solution.py:111
  22.8 6.4 %all-to-all-done.1 = bf16[32,16,128]{2,1,0:T(8,128)(2,1)S(1)} async-done(((bf16[32,16,128]{2,1,0:T(8,128)(2,1)}), bf16[32,16,128]{2,1,0:T(8,128)(2,1)S(1)}, u32[]{:S(2)}, u32[]{:S(2)}) %all-to-all-start.1) | async-done | bytes 131104 | tf_op jit(solution)/shard_map/all_to_all | solution.py:135
  29.2 1.8 %shard_map.40 = bf16[256,1024]{1,0:T(8,128)(2,1)} custom-call(bf16[256,1024]{1,0:T(8,128)(2,1)S(1)} %copy-done, f32[256,1024]{1,0:T(8,128)S(1)} %shard_map.37.intra_ref, bf16[512,128]{1,0:T(8,128)(2,1)S(1)} %bitcast.2), custom_call_target="tpu_custom_call" | custom-call | flops 33554432 | bytes 1703936 | tf_op jit(solution)/shard_map/pallas_call | solution.py:111
Async XLA Ops:
  0.0 21.3 %copy-start.1 = (bf16[256,1024]{1,0:T(8,128)(2,1)S(1)}, bf16[256,1024]{1,0:T(8,128)(2,1)}, u32[]{:S(2)}) copy-start(bf16[256,1024]{1,0:T(8,128)(2,1)} %k_hbm.1) | copy-start | bytes 1572868
  0.0 21.3 %copy-start.2 = (bf16[256,1024]{1,0:T(8,128)(2,1)S(1)}, bf16[256,1024]{1,0:T(8,128)(2,1)}, u32[]{:S(2)}) copy-start(bf16[256,1024]{1,0:T(8,128)(2,1)} %v_hbm.1) | copy-start | bytes 1572868
  2.7 18.5 %copy-start = (bf16[256,1024]{1,0:T(8,128)(2,1)S(1)}, bf16[256,1024]{1,0:T(8,128)(2,1)}, u32[]{:S(2)}) copy-start(bf16[256,1024]{1,0:T(8,128)(2,1)} %q_ref.3) | copy-start | bytes 1572868
  18.7 10.5 %all-to-all-start.1 = ((bf16[32,16,128]{2,1,0:T(8,128)(2,1)}), bf16[32,16,128]{2,1,0:T(8,128)(2,1)S(1)}, u32[]{:S(2)}, u32[]{:S(2)}) async-start(bf16[32,16,128]{2,1,0:T(8,128)(2,1)} %shard_map.39), calls=%async_computation.1 | async-start | bytes 262144 | tf_op jit(solution)/shard_map/all_to_all | solution.py:135

commit v3 on v2

--- a/solution.py
+++ b/solution.py
@@ -13,8 +13,6 @@
 LANES = 2 * HEAD_DIM
 SLABS = 4
 SLAB = HEADS * HEAD_DIM // SLABS
-AXES = ("chain", "wide")
-HBM = pl.BlockSpec(memory_space=pltpu.HBM)
 VMEM = pl.BlockSpec(memory_space=pltpu.VMEM)
 
 
@@ -51,21 +49,32 @@
         out_ref[rows_of(p), :] = packed.astype(out_ref.dtype)
 
 
-def scan_kernel(x_ref, out_ref):
-    parts = x_ref.shape[0]
-    total = jnp.zeros(x_ref.shape[1:], jnp.float32)
-    for i in range(parts):
-        out_ref[i] = total.astype(out_ref.dtype)
-        if i < parts - 1:
-            total = total + x_ref[i].astype(jnp.float32)
+def totals_kernel(x_ref, out_ref):
+    planes, chains = out_ref.shape[:2]
+    inner = x_ref.shape[0] // chains
+    for c in range(chains):
+        total = x_ref[c * inner]
+        for i in range(1, inner):
+            total = total + x_ref[c * inner + i]
+        for z in range(planes):
+            out_ref[z, c] = total.astype(out_ref.dtype)
 
 
-def scan_rows_kernel(x_ref, out_ref):
-    parts = x_ref.shape[0]
-    row = lax.broadcasted_iota(jnp.int32, (parts, parts), 0)
-    col = lax.broadcasted_iota(jnp.int32, (parts, parts), 1)
-    below = jnp.where(col < row, 1.0, 0.0).astype(jnp.bfloat16)
-    out_ref[...] = jnp.dot(below, x_ref[...], preferred_element_type=jnp.float32).astype(out_ref.dtype)
+def prefix_kernel(x_ref, all_ref, out_ref):
+    planes, chains = all_ref.shape[:2]
+    inner = x_ref.shape[0] // chains
+    plane = lax.axis_index("outer")
+    groups = jnp.zeros(all_ref.shape[2:], jnp.float32)
+    for c in range(chains):
+        total = groups
+        for z in range(planes):
+            there = all_ref[z, c].astype(jnp.float32)
+            total = total + jnp.where(z < plane, there, 0.0)
+            groups = groups + there
+        for i in range(inner):
+            out_ref[c * inner + i] = total.astype(out_ref.dtype)
+            if i < inner - 1:
+                total = total + x_ref[c * inner + i]
 
 
 def intra_kernel(q_ref, k_ref, v_ref, out_ref):
@@ -106,43 +115,58 @@
         out_ref[:, lanes_of(p)] = (total * lax.rsqrt(sums * (1.0 / HEAD_DIM) + 1e-6)).astype(out_ref.dtype)
 
 
-def call(kernel, shape, dtype, *args, flops=0, memory=VMEM, scratch=(), limit=16):
+def call(kernel, outs, *args, flops=0, scratch=(), memory=pltpu.VMEM):
     moved = sum(a.size * a.dtype.itemsize for a in args)
-    return pl.pallas_call(
+    single = not isinstance(outs, list)
+    outs = [pltpu.VMEM(shape, dtype) for shape, dtype in ([outs] if single else outs)]
+    args = [pltpu.with_memory_space_constraint(a, memory) for a in args]
+    got = pl.pallas_call(
         kernel,
-        out_shape=jax.ShapeDtypeStruct(shape, dtype),
-        in_specs=[memory] * len(args),
-        out_specs=VMEM,
+        out_shape=outs,
+        in_specs=[pl.BlockSpec(memory_space=memory)] * len(args),
+        out_specs=[VMEM] * len(outs),
         scratch_shapes=scratch,
         cost_estimate=pl.CostEstimate(flops=flops, bytes_accessed=moved, transcendentals=0),
-        compiler_params=pltpu.CompilerParams(vmem_limit_bytes=limit * 1024 * 1024),
+        compiler_params=pltpu.CompilerParams(vmem_limit_bytes=16 * 1024 * 1024),
     )(*args)
+    return got[0] if single else got
 
 
-def per_device(parts, queries, keys, values):
+def per_device(chains, planes, inner, queries, keys, values):
     rows = queries.shape[0]
-    state_rows = PAIRS * HEAD_DIM
-    share = state_rows // parts
-    states = call(states_kernel, (state_rows, LANES), jnp.bfloat16, keys, values,
-                  flops=2 * rows * LANES * LANES * PAIRS, memory=HBM, limit=60,
-                  scratch=[pltpu.VMEM(keys.shape, keys.dtype), pltpu.VMEM(values.shape, values.dtype),
-                           pltpu.SemaphoreType.DMA((2, SLABS))])
-    intra = call(intra_kernel, queries.shape, jnp.float32, queries, keys, values,
+    members = chains * inner
+    share = PAIRS * HEAD_DIM // members
+    states, keys, values = call(
+        states_kernel,
+        [((PAIRS * HEAD_DIM, LANES), jnp.float32), (keys.shape, keys.dtype), (values.shape, values.dtype)],
+        keys, values, flops=2 * rows * LANES * LANES * PAIRS, memory=pltpu.HBM,
+        scratch=[pltpu.SemaphoreType.DMA((2, SLABS))])
+    mine = lax.all_to_all(states.reshape(members, share, LANES), ("chain", "inner"), 0, 0, tiled=True)
+    totals = call(totals_kernel, ((planes, chains, share, LANES), jnp.bfloat16), mine)
+    totals = lax.all_to_all(totals, "outer", 0, 0, tiled=True)
+    before = call(prefix_kernel, ((members, share, LANES), jnp.bfloat16), mine, totals)
+    prefix = lax.all_to_all(before, ("chain", "inner"), 0, 0, tiled=True)
+    intra = call(intra_kernel, (queries.shape, jnp.float32), queries, keys, values,
                  flops=4 * rows * rows * HEADS * HEAD_DIM)
-    view = (parts, share, LANES) if share > 1 else (parts, LANES)
-    mine = lax.all_to_all(states.reshape(view), AXES, 0, 0, tiled=True)
-    before = call(scan_kernel if share > 1 else scan_rows_kernel, view, jnp.bfloat16, mine)
-    prefix = lax.all_to_all(before, AXES, 0, 0, tiled=True).reshape(state_rows, LANES)
-    return call(attend_kernel, queries.shape, jnp.bfloat16, queries, intra, prefix,
-                flops=2 * rows * HEAD_DIM * HEAD_DIM * HEADS)
+    out = pl.pallas_call(
+        attend_kernel,
+        out_shape=jax.ShapeDtypeStruct(queries.shape, jnp.bfloat16),
+        in_specs=[VMEM] * 3,
+        out_specs=VMEM,
+        compiler_params=pltpu.CompilerParams(vmem_limit_bytes=16 * 1024 * 1024),
+    )(queries, intra, prefix.reshape(PAIRS * HEAD_DIM, LANES))
+    return out
 
 
 def solution(mesh):
-    spec = P(AXES, None)
-    parts = mesh.shape["chain"] * mesh.shape["wide"]
+    wide, chains = mesh.devices.shape
+    inner = 4
+    planes = wide // inner
+    finer = jax.sharding.Mesh(mesh.devices.reshape(planes, inner, chains), ("outer", "inner", "chain"))
+    spec = P(("chain", "outer", "inner"), None)
     return jax.shard_map(
-        functools.partial(per_device, parts),
-        mesh=mesh,
+        functools.partial(per_device, chains, planes, inner),
+        mesh=finer,
         in_specs=(spec, spec, spec),
         out_specs=spec,
         check_vma=False,

time: 31.3 us -> 36.1 us (1.15)
  blocking collectives: 15.2 us -> 22.6 us
  waiting for transfers between devices: 6.4 us -> 3.78 us
  starting transfers between devices: 2.58 us -> 3.37 us
  Pallas kernels: 6.74 us -> 6.01 us
    all_to_all x1 -> x2, blocking collectives: 15.2 us -> 22.6 us  [the longest x1 11.6 us: per_device(): lax.all_to_all(states.reshape(members, share, LANES), ('chain', 'inner'),...]
    all_to_all x1, waiting for transfers between devices: 6.4 us -> 3.78 us  [per_device(): prefix = lax.all_to_all(before, ('chain', 'inner'), 0, 0, tiled=True)]
    all_to_all x1, starting transfers between devices: 2.58 us -> 3.37 us  [per_device(): prefix = lax.all_to_all(before, ('chain', 'inner'), 0, 0, tiled=True)]
    pallas_call x4 -> x5, Pallas kernels: 6.74 us -> 6.01 us  [the longest x4 4.17 us: call(): pl.pallas_call(kernel, out_shape=outs, in_specs=[pl.BlockSpec(memory_spac...]
  transfers between devices with their start and end apart: 1 -> 1, of which waited for: 1 -> 1; matrix products, arithmetic and copies ran while one was open for 0% -> 0% of each run, Pallas kernels for 5% -> 4%
where the time goes in v3:
time: 36.1 us; the launch traced here: 35.8 us
  blocking collectives  22.6 us (63%)
  Pallas kernels  6.01 us (17%)
  waiting for transfers between devices  3.78 us (10%)
  starting transfers between devices  3.37 us (9%)
    all_to_all x1, blocking collectives, per_device(): lax.all_to_all(states.reshape(members, share, LANES), ('chain', 'inner'),...  11.6 us
    all_to_all x1, blocking collectives, per_device(): totals = lax.all_to_all(totals, 'outer', 0, 0, tiled=True)  11 us
    pallas_call x4, Pallas kernels, call(): pl.pallas_call(kernel, out_shape=outs, in_specs=[pl.BlockSpec(memory_spac...  4.17 us
    all_to_all x1, waiting for transfers between devices, per_device(): prefix = lax.all_to_all(before, ('chain', 'inner'), 0, 0, tiled=True)  3.78 us
    all_to_all x1, starting transfers between devices, per_device(): prefix = lax.all_to_all(before, ('chain', 'inner'), 0, 0, tiled=True)  3.37 us
    pallas_call x1, Pallas kernels, per_device(): pl.pallas_call(attend_kernel, out_shape=jax.ShapeDtypeStruct(queries.shap...  1.84 us
  transfers between devices with their start and end apart: 1, of which 1 were waited for; matrix products, arithmetic and copies ran while one was open for 0% of the time, Pallas kernels for 4%

profile of v3, /device:TPU:0, one launch (start us, length us, event | category | flops | bytes accessed | tf_op | source)
XLA Modules:
  0.0 35.8 jit_solution(14211005675115672941)
XLA Ops:
  0.0 2.0 %shard_map.37 = (f32[512,128]{1,0:T(8,128)S(1)}, bf16[256,1024]{1,0:T(8,128)(2,1)S(1)}, bf16[256,1024]{1,0:T(8,128)(2,1)S(1)}) custom-call(bf16[256,1024]{1,0:T(8,128)(2,1)} %k_hbm.1, bf16[256,1024]{1,0:T(8,128)(2,1)} %v_hbm.1), custom_call_target="tpu_custom_call" | custom-call | flops 67108864 | bytes 1048576 | tf_op jit(solution)/shard_map/pallas_call | solution.py:123
  2.0 11.6 %all_to_all.15.x_ref = f32[8,64,128]{2,1,0:T(8,128)S(1)} all-to-all(f32[8,64,128]{2,1,0:T(8,128)S(1)} %bitcast.3), channel_id=1, replica_groups=mesh['outer'=4,'inner'=4,'chain'=2] {'chain','inner'}, dimensions={0} | all-to-all | bytes 524288 | tf_op jit(solution)/shard_map/all_to_all | solution.py:144
  13.6 0.0 copy-start
  13.6 11.0 %all_to_all.16.all_ref = bf16[4,2,64,128]{3,2,1,0:T(8,128)(2,1)S(1)} all-to-all(bf16[4,2,64,128]{3,2,1,0:T(8,128)(2,1)S(1)} %shard_map.39), channel_id=1, replica_groups=mesh['outer'=4,'inner'=4,'chain'=2] {'outer'}, dimensions={0} | all-to-all | bytes 262144 | tf_op jit(solution)/shard_map/all_to_all | solution.py:146
  24.6 0.7 %shard_map.40 = bf16[8,64,128]{2,1,0:T(8,128)(2,1)} custom-call(f32[8,64,128]{2,1,0:T(8,128)S(1)} %all_to_all.15.x_ref, bf16[4,2,64,128]{3,2,1,0:T(8,128)(2,1)S(1)} %all_to_all.16.all_ref), custom_call_target="tpu_custom_call" | custom-call | bytes 393216 | tf_op jit(solution)/shard_map/pallas_call | solution.py:123
  25.3 3.4 %all-to-all-start.2 = ((bf16[8,64,128]{2,1,0:T(8,128)(2,1)}), bf16[8,64,128]{2,1,0:T(8,128)(2,1)S(1)}, u32[]{:S(2)}, u32[]{:S(2)}) async-start(bf16[8,64,128]{2,1,0:T(8,128)(2,1)} %shard_map.40), calls=%async_computation.2 | async-start | bytes 262144 | tf_op jit(solution)/shard_map/all_to_all | solution.py:148
  28.7 0.0 copy-done
  28.7 1.5 %shard_map.38.intra_ref = f32[256,1024]{1,0:T(8,128)S(1)} custom-call(bf16[256,1024]{1,0:T(8,128)(2,1)S(1)} %copy-done, bf16[256,1024]{1,0:T(8,128)(2,1)S(1)} %get-tuple-element.8.k_ref, bf16[256,1024]{1,0:T(8,128)(2,1)S(1)} %get-tuple-element.9.v_ref), custom_call_target="tpu_custom_call" | custom-call | flops 268435456 | bytes 1572864 | tf_op jit(solution)/shard_map/pallas_call | solution.py:123
  30.2 3.8 %all-to-all-done.2 = bf16[8,64,128]{2,1,0:T(8,128)(2,1)S(1)} async-done(((bf16[8,64,128]{2,1,0:T(8,128)(2,1)}), bf16[8,64,128]{2,1,0:T(8,128)(2,1)S(1)}, u32[]{:S(2)}, u32[]{:S(2)}) %all-to-all-start.2) | async-done | bytes 131104 | tf_op jit(solution)/shard_map/all_to_all | solution.py:148
  34.0 1.8 %shard_map.41 = bf16[256,1024]{1,0:T(8,128)(2,1)} custom-call(bf16[256,1024]{1,0:T(8,128)(2,1)S(1)} %copy-done, f32[256,1024]{1,0:T(8,128)S(1)} %shard_map.38.intra_ref, bf16[512,128]{1,0:T(8,128)(2,1)S(1)} %bitcast.2), custom_call_target="tpu_custom_call" | custom-call | tf_op jit(solution)/shard_map/pallas_call | solution.py:151
  (1 shorter events, 0.0 us)
Async XLA Ops:
  13.6 15.1 %copy-start = (bf16[256,1024]{1,0:T(8,128)(2,1)S(1)}, bf16[256,1024]{1,0:T(8,128)(2,1)}, u32[]{:S(2)}) copy-start(bf16[256,1024]{1,0:T(8,128)(2,1)} %q_ref.3) | copy-start | bytes 1572868
  25.3 8.7 %all-to-all-start.2 = ((bf16[8,64,128]{2,1,0:T(8,128)(2,1)}), bf16[8,64,128]{2,1,0:T(8,128)(2,1)S(1)}, u32[]{:S(2)}, u32[]{:S(2)}) async-start(bf16[8,64,128]{2,1,0:T(8,128)(2,1)} %shard_map.40), calls=%async_computation.2 | async-start | bytes 262144 | tf_op jit(solution)/shard_map/all_to_all | solution.py:148

commit v4 on v3

--- a/solution.py
+++ b/solution.py
@@ -28,7 +28,8 @@
     return slice(p * HEAD_DIM, (p + 1) * HEAD_DIM)
 
 
-def states_kernel(k_hbm, v_hbm, out_ref, k_ref, v_ref, arrived):
+def states_kernel(k_hbm, v_hbm, *refs):
+    *outs, k_ref, v_ref, states, arrived = refs
     copies = []
     for s in range(SLABS):
         lanes = slice(s * SLAB, (s + 1) * SLAB)
@@ -38,6 +39,7 @@
         for copy in copies[-1]:
             copy.start()
     first = first_head((HEAD_DIM, LANES))
+    share = states.shape[1]
     for p in range(PAIRS):
         if p * LANES % SLAB == 0:
             for copy in copies[p * LANES // SLAB]:
@@ -46,35 +48,53 @@
             k_ref[:, lanes_of(p)], v_ref[:, lanes_of(p)], (((0,), (0,)), ((), ())),
             preferred_element_type=jnp.float32)
         packed = jnp.where(first, both[:HEAD_DIM], both[HEAD_DIM:])
-        out_ref[rows_of(p), :] = packed.astype(out_ref.dtype)
-
-
-def totals_kernel(x_ref, out_ref):
-    planes, chains = out_ref.shape[:2]
-    inner = x_ref.shape[0] // chains
+        for j in range(HEAD_DIM // share):
+            states[p * HEAD_DIM // share + j] = packed[j * share:(j + 1) * share]
+    me = member()
+    for d, out in enumerate(outs):
+        out[...] = states[me ^ d]
+
+
+def member():
+    return lax.axis_index("chain") * lax.axis_size("inner") + lax.axis_index("inner")
+
+
+def totals_kernel(inner, *refs):
+    *parts, out_ref = refs
+    for c in range(out_ref.shape[0]):
+        total = parts[c * inner][...]
+        for i in range(1, inner):
+            total = total + parts[c * inner + i][...]
+        out_ref[c] = total.astype(out_ref.dtype)
+
+
+def prefix_kernel(inner, members, planes, *refs):
+    parts, totals = refs[:members], refs[members:members + planes]
+    outs, (order, sums, done) = refs[members + planes:-3], refs[-3:]
+    me, chain, plane = member(), lax.axis_index("chain"), lax.axis_index("outer")
+    chains = members // inner
+    for d in range(members):
+        order[me ^ d] = parts[d][...]
+    shape = order.shape[1:]
     for c in range(chains):
-        total = x_ref[c * inner]
-        for i in range(1, inner):
-            total = total + x_ref[c * inner + i]
-        for z in range(planes):
-            out_ref[z, c] = total.astype(out_ref.dtype)
-
-
-def prefix_kernel(x_ref, all_ref, out_ref):
-    planes, chains = all_ref.shape[:2]
-    inner = x_ref.shape[0] // chains
-    plane = lax.axis_index("outer")
-    groups = jnp.zeros(all_ref.shape[2:], jnp.float32)
+        below = jnp.zeros(shape, jnp.float32)
+        whole = jnp.zeros(shape, jnp.float32)
+        for e in range(planes):
+            there = totals[e][c].astype(jnp.float32)
+            below = below + jnp.where((plane ^ e) < plane, there, 0.0)
+            whole = whole + there
+        sums[0, chain ^ c] = below
+        sums[1, chain ^ c] = whole
+    groups = jnp.zeros(shape, jnp.float32)
     for c in range(chains):
-        total = groups
-        for z in range(planes):
-            there = all_ref[z, c].astype(jnp.float32)
-            total = total + jnp.where(z < plane, there, 0.0)
-            groups = groups + there
+        total = groups + sums[0, c]
+        groups = groups + sums[1, c]
         for i in range(inner):
-            out_ref[c * inner + i] = total.astype(out_ref.dtype)
+            done[c * inner + i] = total
             if i < inner - 1:
-                total = total + x_ref[c * inner + i]
+                total = total + order[c * inner + i]
+    for d, out in enumerate(outs):
+        out[...] = done[me ^ d].astype(out.dtype)
 
 
 def intra_kernel(q_ref, k_ref, v_ref, out_ref):
@@ -95,14 +115,20 @@
         out_ref[:, lanes_of(p)] = jnp.where(first, intra[0], intra[1])
 
 
-def attend_kernel(q_ref, intra_ref, prefix_ref, out_ref):
+def attend_kernel(q_ref, intra_ref, *refs):
+    *parts, out_ref, order = refs
+    me = member()
+    for d, part in enumerate(parts):
+        order[me ^ d] = part[...]
+    share = order.shape[1]
     first_state = first_head((HEAD_DIM, LANES))
     same = (first_head((LANES, LANES))
             == (lax.broadcasted_iota(jnp.int32, (LANES, LANES), 0) < HEAD_DIM))
     ones = jnp.where(same, 1.0, 0.0).astype(jnp.bfloat16)
     zero = jnp.zeros((), jnp.bfloat16)
     for p in range(PAIRS):
-        packed = prefix_ref[rows_of(p), :]
+        packed = jnp.concatenate(
+            [order[j] for j in range(p * HEAD_DIM // share, (p + 1) * HEAD_DIM // share)], axis=0)
         prefix = jnp.concatenate(
             [jnp.where(first_state, packed, zero), jnp.where(first_state, zero, packed)], axis=0)
         inter = jnp.dot(q_ref[:, lanes_of(p)], prefix, preferred_element_type=jnp.float32)
@@ -132,30 +158,44 @@
     return got[0] if single else got
 
 
+def swapped_outer(x, planes, e):
+    return lax.ppermute(x, "outer", [(z, z ^ e) for z in range(planes)])
+
+
+def swapped_plane(x, chains, inner, d):
+    across, along = divmod(d, inner)
+    return lax.ppermute(x, ("inner", "chain"), [
+        (i * chains + c, (i ^ along) * chains + (c ^ across)) for i in range(inner) for c in range(chains)])
+
+
 def per_device(chains, planes, inner, queries, keys, values):
     rows = queries.shape[0]
     members = chains * inner
-    share = PAIRS * HEAD_DIM // members
-    states, keys, values = call(
+    share = (PAIRS * HEAD_DIM // members, LANES)
+    *states, keys, values = call(
         states_kernel,
-        [((PAIRS * HEAD_DIM, LANES), jnp.float32), (keys.shape, keys.dtype), (values.shape, values.dtype)],
+        [(share, jnp.float32)] * members + [(keys.shape, keys.dtype), (values.shape, values.dtype)],
         keys, values, flops=2 * rows * LANES * LANES * PAIRS, memory=pltpu.HBM,
-        scratch=[pltpu.SemaphoreType.DMA((2, SLABS))])
-    mine = lax.all_to_all(states.reshape(members, share, LANES), ("chain", "inner"), 0, 0, tiled=True)
-    totals = call(totals_kernel, ((planes, chains, share, LANES), jnp.bfloat16), mine)
-    totals = lax.all_to_all(totals, "outer", 0, 0, tiled=True)
-    before = call(prefix_kernel, ((members, share, LANES), jnp.bfloat16), mine, totals)
-    prefix = lax.all_to_all(before, ("chain", "inner"), 0, 0, tiled=True)
+        scratch=[pltpu.VMEM((members,) + share, jnp.float32), pltpu.SemaphoreType.DMA((2, SLABS))])
+    mine = [states[0]] + [swapped_plane(states[d], chains, inner, d) for d in range(1, members)]
+    total = call(functools.partial(totals_kernel, inner), ((chains,) + share, jnp.bfloat16), *mine)
+    totals = [total] + [swapped_outer(total, planes, e) for e in range(1, planes)]
+    before = call(
+        functools.partial(prefix_kernel, inner, members, planes), [(share, jnp.bfloat16)] * members,
+        *mine, *totals,
+        scratch=[pltpu.VMEM((members,) + share, jnp.float32), pltpu.VMEM((2, chains) + share, jnp.float32),
+                 pltpu.VMEM((members,) + share, jnp.float32)])
+    prefix = [before[0]] + [swapped_plane(before[d], chains, inner, d) for d in range(1, members)]
     intra = call(intra_kernel, (queries.shape, jnp.float32), queries, keys, values,
                  flops=4 * rows * rows * HEADS * HEAD_DIM)
-    out = pl.pallas_call(
+    return pl.pallas_call(
         attend_kernel,
         out_shape=jax.ShapeDtypeStruct(queries.shape, jnp.bfloat16),
-        in_specs=[VMEM] * 3,
+        in_specs=[VMEM] * (2 + members),
         out_specs=VMEM,
+        scratch_shapes=[pltpu.VMEM((members,) + share, jnp.bfloat16)],
         compiler_params=pltpu.CompilerParams(vmem_limit_bytes=16 * 1024 * 1024),
-    )(queries, intra, prefix.reshape(PAIRS * HEAD_DIM, LANES))
-    return out
+    )(queries, intra, *prefix)
 
 
 def solution(mesh):

time: 36.1 us -> 34.8 us (0.964)
  blocking collectives: 22.6 us -> 0 us
  starting transfers between devices: 3.37 us -> 19.6 us
  waiting for transfers between devices: 3.78 us -> 9.44 us
  Pallas kernels: 6.01 us -> 5.42 us
    all_to_all x2 -> x0, blocking collectives: 22.6 us -> none  [the longest x1 11.6 us: per_device(): lax.all_to_all(states.reshape(members, share, LANES), ('chain', 'inner'),...]
    ppermute x0 -> x17, starting transfers between devices: none -> 19.6 us  [the longest x14 15.2 us: swapped_plane(): lax.ppermute(x, ('inner', 'chain'), [(i * chains + c, (i ^ along) * chain...]
    ppermute x0 -> x17, waiting for transfers between devices: none -> 9.44 us  [the longest x3 5.49 us: swapped_outer(): return lax.ppermute(x, 'outer', [(z, z ^ e) for z in range(planes)])]
    all_to_all x1 -> x0, waiting for transfers between devices: 3.78 us -> none  [per_device(): prefix = lax.all_to_all(before, ('chain', 'inner'), 0, 0, tiled=True)]
    all_to_all x1 -> x0, starting transfers between devices: 3.37 us -> none  [per_device(): prefix = lax.all_to_all(before, ('chain', 'inner'), 0, 0, tiled=True)]
    pallas_call x4, Pallas kernels: 4.17 us -> 3.57 us  [call(): pl.pallas_call(kernel, out_shape=outs, in_specs=[pl.BlockSpec(memory_spac...]
  transfers between devices with their start and end apart: 1 -> 17, of which waited for: 1 -> 6; matrix products, arithmetic and copies ran while one was open for 0% -> 0% of each run, Pallas kernels for 4% -> 4%
where the time goes in v4:
time: 34.8 us; the launch traced here: 34.6 us
  starting transfers between devices  19.6 us (56%)
  waiting for transfers between devices  9.44 us (27%)
  Pallas kernels  5.42 us (16%)
    ppermute x14, starting transfers between devices, swapped_plane(): lax.ppermute(x, ('inner', 'chain'), [(i * chains + c, (i ^ along) * chain...  15.2 us
    ppermute x3, waiting for transfers between devices, swapped_outer(): return lax.ppermute(x, 'outer', [(z, z ^ e) for z in range(planes)])  5.49 us
    ppermute x3, starting transfers between devices, swapped_outer(): return lax.ppermute(x, 'outer', [(z, z ^ e) for z in range(planes)])  4.45 us
    ppermute x14, waiting for transfers between devices, swapped_plane(): lax.ppermute(x, ('inner', 'chain'), [(i * chains + c, (i ^ along) * chain...  3.95 us
    pallas_call x4, Pallas kernels, call(): pl.pallas_call(kernel, out_shape=outs, in_specs=[pl.BlockSpec(memory_spac...  3.57 us
    pallas_call x1, Pallas kernels, per_device(): pl.pallas_call(attend_kernel, out_shape=jax.ShapeDtypeStruct(queries.shap...  1.85 us
  transfers between devices with their start and end apart: 17, of which 6 were waited for; matrix products, arithmetic and copies ran while one was open for 0% of the time, Pallas kernels for 4%

profile of v4, /device:TPU:0, one launch (start us, length us, event | category | flops | bytes accessed | tf_op | source)
XLA Modules:
  0.0 34.6 jit_solution(2104640057968728325)
XLA Ops:
  0.0 2.0 %shard_map.37 = (f32[64,128]{1,0:T(8,128)S(1)}, f32[64,128]{1,0:T(8,128)S(1)}, f32[64,128]{1,0:T(8,128)S(1)}, f32[64,128]{1,0:T(8,128)S(1)}, f32[64,128]{1,0:T(8...) custom-call(bf16[256,1024]{1,0:T(8,128)(2,1)} %k_hbm.1, ...), custom_call_target="tpu_custom_call" | custom-call | flops 67108864 | bytes 1048576 | tf_op jit(solution)/shard_map/pallas_call | solution.py:149
  2.0 0.0 copy-start
  2.0 3.0 %collective-permute-start = (f32[64,128]{1,0:T(8,128)S(1)}, f32[64,128]{1,0:T(8,128)S(1)}, u32[]{:S(2)}, u32[]{:S(2)}) collective-permute-start(f32[64,128]{1,0:T(8,128)S(1)} %get-tuple-element.26), channel_id=1, source_target_pairs={{0,2},{1,3},{2,0},{3,1},{4,6},{5,7},{6,4},{7,5},{8,10},{9,11},{10,... | collective-permute-start | bytes 98312 | tf_op jit(solution)/shard_map/ppermute | solution.py:167
  5.0 1.5 %collective-permute-start.1 = (f32[64,128]{1,0:T(8,128)S(1)}, f32[64,128]{1,0:T(8,128)S(1)}, u32[]{:S(2)}, u32[]{:S(2)}) collective-permute-start(f32[64,128]{1,0:T(8,128)S(1)} %get-tuple-element.27), channel_id=1, source_target_pairs={{0,4},{1,5},{2,6},{3,7},{4,0},{5,1},{6,2},{7,3},{8,12},{9,13},{10,... | collective-permute-start | bytes 98312 | tf_op jit(solution)/shard_map/ppermute | solution.py:167
  6.5 0.0 collective-permute-start.2
  6.6 0.0 collective-permute-start.3
  6.6 2.1 %collective-permute-start.4 = (f32[64,128]{1,0:T(8,128)S(1)}, f32[64,128]{1,0:T(8,128)S(1)}, u32[]{:S(2)}, u32[]{:S(2)}) collective-permute-start(f32[64,128]{1,0:T(8,128)S(1)} %get-tuple-element.30), channel_id=1, source_target_pairs={{0,3},{1,2},{2,1},{3,0},{4,7},{5,6},{6,5},{7,4},{8,11},{9,10},{10,... | collective-permute-start | bytes 98312 | tf_op jit(solution)/shard_map/ppermute | solution.py:167
  8.6 0.0 collective-permute-done.refs_1_
  8.6 1.1 %collective-permute-start.5 = (f32[64,128]{1,0:T(8,128)S(1)}, f32[64,128]{1,0:T(8,128)S(1)}, u32[]{:S(2)}, u32[]{:S(2)}) collective-permute-start(f32[64,128]{1,0:T(8,128)S(1)} %get-tuple-element.31), channel_id=1, source_target_pairs={{0,5},{1,4},{2,7},{3,6},{4,1},{5,0},{6,3},{7,2},{8,13},{9,12},{10,... | collective-permute-start | bytes 98312 | tf_op jit(solution)/shard_map/ppermute | solution.py:167
  9.8 0.0 collective-permute-done.1.refs_2_
  9.8 0.6 %collective-permute-start.6 = (f32[64,128]{1,0:T(8,128)S(1)}, f32[64,128]{1,0:T(8,128)S(1)}, u32[]{:S(2)}, u32[]{:S(2)}) collective-permute-start(f32[64,128]{1,0:T(8,128)S(1)} %get-tuple-element.32), channel_id=1, source_target_pairs={{0,7},{1,6},{2,5},{3,4},{4,3},{5,2},{6,1},{7,0},{8,15},{9,14},{10,... | collective-permute-start | bytes 98312 | tf_op jit(solution)/shard_map/ppermute | solution.py:167
  10.3 1.4 %collective-permute-done.2.refs_3_ = f32[64,128]{1,0:T(8,128)S(1)} collective-permute-done((f32[64,128]{1,0:T(8,128)S(1)}, f32[64,128]{1,0:T(8,128)S(1)}, u32[]{:S(2)}, u32[]{:S(2)}) %collective-permute-start.2) | collective-permute-done | bytes 32800 | tf_op jit(solution)/shard_map/ppermute | solution.py:167
  11.8 0.0 collective-permute-done.3.refs_4_
  11.8 0.0 collective-permute-done.4.refs_5_
  11.8 0.4 %collective-permute-done.5.refs_6_ = f32[64,128]{1,0:T(8,128)S(1)} collective-permute-done((f32[64,128]{1,0:T(8,128)S(1)}, f32[64,128]{1,0:T(8,128)S(1)}, u32[]{:S(2)}, u32[]{:S(2)}) %collective-permute-start.5) | collective-permute-done | bytes 32800 | tf_op jit(solution)/shard_map/ppermute | solution.py:167
  12.2 1.8 %collective-permute-done.6.refs_7_ = f32[64,128]{1,0:T(8,128)S(1)} collective-permute-done((f32[64,128]{1,0:T(8,128)S(1)}, f32[64,128]{1,0:T(8,128)S(1)}, u32[]{:S(2)}, u32[]{:S(2)}) %collective-permute-start.6) | collective-permute-done | bytes 32800 | tf_op jit(solution)/shard_map/ppermute | solution.py:167
  14.0 1.6 %collective-permute-start.7 = (bf16[2,64,128]{2,1,0:T(8,128)(2,1)S(1)}, bf16[2,64,128]{2,1,0:T(8,128)(2,1)S(1)}, u32[]{:S(2)}, u32[]{:S(2)}) collective-permute-start(bf16[2,64,128]{2,1,0:T(8,128)(2,1)S(1)} %shard_map.39.refs_8_), channel_id=1, source_target_pairs={{0,8},{8,0},{16,24},{24,16},{1,9},{9,1},{17,25},{25,17},{2,10},{10... | collective-permute-start | bytes 98312 | tf_op jit(solution)/shard_map/ppermute | solution.py:162
  15.7 2.6 %collective-permute-start.8 = (bf16[2,64,128]{2,1,0:T(8,128)(2,1)S(1)}, bf16[2,64,128]{2,1,0:T(8,128)(2,1)S(1)}, u32[]{:S(2)}, u32[]{:S(2)}) collective-permute-start(bf16[2,64,128]{2,1,0:T(8,128)(2,1)S(1)} %shard_map.39.refs_8_), channel_id=1, source_target_pairs={{0,16},{8,24},{16,0},{24,8},{1,17},{9,25},{17,1},{25,9},{2,18},{10... | collective-permute-start | bytes 98312 | tf_op jit(solution)/shard_map/ppermute | solution.py:162
  18.3 0.2 collective-permute-start.9
  18.5 0.0 collective-permute-done.7.refs_9_
  18.5 2.6 %collective-permute-done.8.refs_10_ = bf16[2,64,128]{2,1,0:T(8,128)(2,1)S(1)} collective-permute-done((bf16[2,64,128]{2,1,0:T(8,128)(2,1)S(1)}, bf16[2,64,128]{2,1,0:T(8,128)(2,1)S(1)}, u32[]{:S(2)}, u32[]{:S(2)}) %collective-permute-start.8) | collective-permute-done | bytes 32800 | tf_op jit(solution)/shard_map/ppermute | solution.py:162
  21.1 2.9 %collective-permute-done.9.refs_11_ = bf16[2,64,128]{2,1,0:T(8,128)(2,1)S(1)} collective-permute-done((bf16[2,64,128]{2,1,0:T(8,128)(2,1)S(1)}, bf16[2,64,128]{2,1,0:T(8,128)(2,1)S(1)}, u32[]{:S(2)}, u32[]{:S(2)}) %collective-permute-start.9) | collective-permute-done | bytes 32800 | tf_op jit(solution)/shard_map/ppermute | solution.py:162
  24.0 0.1 shard_map.40
  24.0 0.6 %collective-permute-start.10 = (bf16[64,128]{1,0:T(8,128)(2,1)S(1)}, bf16[64,128]{1,0:T(8,128)(2,1)S(1)}, u32[]{:S(2)}, u32[]{:S(2)}) collective-permute-start(bf16[64,128]{1,0:T(8,128)(2,1)S(1)} %get-tuple-element.34), channel_id=1, source_target_pairs={{0,2},{1,3},{2,0},{3,1},{4,6},{5,7},{6,4},{7,5},{8,10},{9,11},{10,... | collective-permute-start | bytes 49160 | tf_op jit(solution)/shard_map/ppermute | solution.py:167
  24.6 0.8 %collective-permute-start.11 = (bf16[64,128]{1,0:T(8,128)(2,1)S(1)}, bf16[64,128]{1,0:T(8,128)(2,1)S(1)}, u32[]{:S(2)}, u32[]{:S(2)}) collective-permute-start(bf16[64,128]{1,0:T(8,128)(2,1)S(1)} %get-tuple-element.35), channel_id=1, source_target_pairs={{0,4},{1,5},{2,6},{3,7},{4,0},{5,1},{6,2},{7,3},{8,12},{9,13},{10,... | collective-permute-start | bytes 49160 | tf_op jit(solution)/shard_map/ppermute | solution.py:167
  25.4 2.2 %collective-permute-start.12 = (bf16[64,128]{1,0:T(8,128)(2,1)S(1)}, bf16[64,128]{1,0:T(8,128)(2,1)S(1)}, u32[]{:S(2)}, u32[]{:S(2)}) collective-permute-start(bf16[64,128]{1,0:T(8,128)(2,1)S(1)} %get-tuple-element.36), channel_id=1, source_target_pairs={{0,6},{1,7},{2,4},{3,5},{4,2},{5,3},{6,0},{7,1},{8,14},{9,15},{10,... | collective-permute-start | bytes 49160 | tf_op jit(solution)/shard_map/ppermute | solution.py:167
  27.6 0.0 collective-permute-start.13
  27.6 0.6 %collective-permute-start.14 = (bf16[64,128]{1,0:T(8,128)(2,1)S(1)}, bf16[64,128]{1,0:T(8,128)(2,1)S(1)}, u32[]{:S(2)}, u32[]{:S(2)}) collective-permute-start(bf16[64,128]{1,0:T(8,128)(2,1)S(1)} %get-tuple-element.38), channel_id=1, source_target_pairs={{0,3},{1,2},{2,1},{3,0},{4,7},{5,6},{6,5},{7,4},{8,11},{9,10},{10,... | collective-permute-start | bytes 49160 | tf_op jit(solution)/shard_map/ppermute | solution.py:167
  28.3 0.0 collective-permute-done.10.refs_1_
  28.3 0.4 %collective-permute-start.15 = (bf16[64,128]{1,0:T(8,128)(2,1)S(1)}, bf16[64,128]{1,0:T(8,128)(2,1)S(1)}, u32[]{:S(2)}, u32[]{:S(2)}) collective-permute-start(bf16[64,128]{1,0:T(8,128)(2,1)S(1)} %get-tuple-element.39), channel_id=1, source_target_pairs={{0,5},{1,4},{2,7},{3,6},{4,1},{5,0},{6,3},{7,2},{8,13},{9,12},{10,... | collective-permute-start | bytes 49160 | tf_op jit(solution)/shard_map/ppermute | solution.py:167
  28.7 0.0 collective-permute-done.11.refs_2_
  28.7 2.3 %collective-permute-start.16 = (bf16[64,128]{1,0:T(8,128)(2,1)S(1)}, bf16[64,128]{1,0:T(8,128)(2,1)S(1)}, u32[]{:S(2)}, u32[]{:S(2)}) collective-permute-start(bf16[64,128]{1,0:T(8,128)(2,1)S(1)} %get-tuple-element.40), channel_id=1, source_target_pairs={{0,7},{1,6},{2,5},{3,4},{4,3},{5,2},{6,1},{7,0},{8,15},{9,14},{10,... | collective-permute-start | bytes 49160 | tf_op jit(solution)/shard_map/ppermute | solution.py:167
  30.9 0.0 copy-done
  30.9 1.5 %shard_map.38.intra_ref = f32[256,1024]{1,0:T(8,128)S(1)} custom-call(bf16[256,1024]{1,0:T(8,128)(2,1)S(1)} %copy-done, bf16[256,1024]{1,0:T(8,128)(2,1)S(1)} %get-tuple-element.23.k_ref, bf16[256,1024]{1,0:T(8,128)(2,1)S(1)} %get-tuple-element.24.v_ref), custom_call_target="tpu_custom_call" | custom-call | flops 268435456 | bytes 1572864 | tf_op jit(solution)/shard_map/pallas_call | solution.py:149
  32.4 0.0 collective-permute-done.12.refs_3_
  32.4 0.0 collective-permute-done.13.refs_4_
  32.4 0.0 collective-permute-done.14.refs_5_
  32.5 0.0 collective-permute-done.15.refs_6_
  32.5 0.3 collective-permute-done.16.refs_7_
  32.7 1.9 %shard_map.41 = bf16[256,1024]{1,0:T(8,128)(2,1)} custom-call(bf16[256,1024]{1,0:T(8,128)(2,1)S(1)} %copy-done, f32[256,1024]{1,0:T(8,128)S(1)} %shard_map.38.intra_ref, bf16[64,128]{1,0:T(8,128)(2,1)S(1)} %get-tuple-element.33.refs_0_, bf16[64,128]{1,0:T(8,128)(2,1)S(1)} %collective-permute-done.10.refs_1_, ...), custom_call_target="tpu_custom_call" | custom-call | tf_op jit(solution)/shard_map/pallas_call | solution.py:191
  (1 shorter events, 0.0 us)
Async XLA Ops:
  2.0 28.9 %copy-start = (bf16[256,1024]{1,0:T(8,128)(2,1)S(1)}, bf16[256,1024]{1,0:T(8,128)(2,1)}, u32[]{:S(2)}) copy-start(bf16[256,1024]{1,0:T(8,128)(2,1)} %q_ref.3) | copy-start | bytes 1572868
  2.0 6.6 %collective-permute-start = (f32[64,128]{1,0:T(8,128)S(1)}, f32[64,128]{1,0:T(8,128)S(1)}, u32[]{:S(2)}, u32[]{:S(2)}) collective-permute-start(f32[64,128]{1,0:T(8,128)S(1)} %get-tuple-element.26), channel_id=1, source_target_pairs={{0,2},{1,3},{2,0},{3,1},{4,6},{5,7},{6,4},{7,5},{8,10},{9,11},{10,... | collective-permute-start | bytes 98312 | tf_op jit(solution)/shard_map/ppermute | solution.py:167
  5.0 4.7 %collective-permute-start.1 = (f32[64,128]{1,0:T(8,128)S(1)}, f32[64,128]{1,0:T(8,128)S(1)}, u32[]{:S(2)}, u32[]{:S(2)}) collective-permute-start(f32[64,128]{1,0:T(8,128)S(1)} %get-tuple-element.27), channel_id=1, source_target_pairs={{0,4},{1,5},{2,6},{3,7},{4,0},{5,1},{6,2},{7,3},{8,12},{9,13},{10,... | collective-permute-start | bytes 98312 | tf_op jit(solution)/shard_map/ppermute | solution.py:167
  6.5 5.2 %collective-permute-start.2 = (f32[64,128]{1,0:T(8,128)S(1)}, f32[64,128]{1,0:T(8,128)S(1)}, u32[]{:S(2)}, u32[]{:S(2)}) collective-permute-start(f32[64,128]{1,0:T(8,128)S(1)} %get-tuple-element.28), channel_id=1, source_target_pairs={{0,6},{1,7},{2,4},{3,5},{4,2},{5,3},{6,0},{7,1},{8,14},{9,15},{10,... | collective-permute-start | bytes 98312 | tf_op jit(solution)/shard_map/ppermute | solution.py:167
  6.6 5.2 %collective-permute-start.3 = (f32[64,128]{1,0:T(8,128)S(1)}, f32[64,128]{1,0:T(8,128)S(1)}, u32[]{:S(2)}, u32[]{:S(2)}) collective-permute-start(f32[64,128]{1,0:T(8,128)S(1)} %get-tuple-element.29), channel_id=1, source_target_pairs={{0,1},{1,0},{2,3},{3,2},{4,5},{5,4},{6,7},{7,6},{8,9},{9,8},{10,11... | collective-permute-start | bytes 98312 | tf_op jit(solution)/shard_map/ppermute | solution.py:167
  6.6 5.2 %collective-permute-start.4 = (f32[64,128]{1,0:T(8,128)S(1)}, f32[64,128]{1,0:T(8,128)S(1)}, u32[]{:S(2)}, u32[]{:S(2)}) collective-permute-start(f32[64,128]{1,0:T(8,128)S(1)} %get-tuple-element.30), channel_id=1, source_target_pairs={{0,3},{1,2},{2,1},{3,0},{4,7},{5,6},{6,5},{7,4},{8,11},{9,10},{10,... | collective-permute-start | bytes 98312 | tf_op jit(solution)/shard_map/ppermute | solution.py:167
  8.6 3.6 %collective-permute-start.5 = (f32[64,128]{1,0:T(8,128)S(1)}, f32[64,128]{1,0:T(8,128)S(1)}, u32[]{:S(2)}, u32[]{:S(2)}) collective-permute-start(f32[64,128]{1,0:T(8,128)S(1)} %get-tuple-element.31), channel_id=1, source_target_pairs={{0,5},{1,4},{2,7},{3,6},{4,1},{5,0},{6,3},{7,2},{8,13},{9,12},{10,... | collective-permute-start | bytes 98312 | tf_op jit(solution)/shard_map/ppermute | solution.py:167
  9.8 4.2 %collective-permute-start.6 = (f32[64,128]{1,0:T(8,128)S(1)}, f32[64,128]{1,0:T(8,128)S(1)}, u32[]{:S(2)}, u32[]{:S(2)}) collective-permute-start(f32[64,128]{1,0:T(8,128)S(1)} %get-tuple-element.32), channel_id=1, source_target_pairs={{0,7},{1,6},{2,5},{3,4},{4,3},{5,2},{6,1},{7,0},{8,15},{9,14},{10,... | collective-permute-start | bytes 98312 | tf_op jit(solution)/shard_map/ppermute | solution.py:167
  14.0 4.5 %collective-permute-start.7 = (bf16[2,64,128]{2,1,0:T(8,128)(2,1)S(1)}, bf16[2,64,128]{2,1,0:T(8,128)(2,1)S(1)}, u32[]{:S(2)}, u32[]{:S(2)}) collective-permute-start(bf16[2,64,128]{2,1,0:T(8,128)(2,1)S(1)} %shard_map.39.refs_8_), channel_id=1, source_target_pairs={{0,8},{8,0},{16,24},{24,16},{1,9},{9,1},{17,25},{25,17},{2,10},{10... | collective-permute-start | bytes 98312 | tf_op jit(solution)/shard_map/ppermute | solution.py:162
  15.7 5.4 %collective-permute-start.8 = (bf16[2,64,128]{2,1,0:T(8,128)(2,1)S(1)}, bf16[2,64,128]{2,1,0:T(8,128)(2,1)S(1)}, u32[]{:S(2)}, u32[]{:S(2)}) collective-permute-start(bf16[2,64,128]{2,1,0:T(8,128)(2,1)S(1)} %shard_map.39.refs_8_), channel_id=1, source_target_pairs={{0,16},{8,24},{16,0},{24,8},{1,17},{9,25},{17,1},{25,9},{2,18},{10... | collective-permute-start | bytes 98312 | tf_op jit(solution)/shard_map/ppermute | solution.py:162
  18.3 5.7 %collective-permute-start.9 = (bf16[2,64,128]{2,1,0:T(8,128)(2,1)S(1)}, bf16[2,64,128]{2,1,0:T(8,128)(2,1)S(1)}, u32[]{:S(2)}, u32[]{:S(2)}) collective-permute-start(bf16[2,64,128]{2,1,0:T(8,128)(2,1)S(1)} %shard_map.39.refs_8_), channel_id=1, source_target_pairs={{0,24},{8,16},{16,8},{24,0},{1,25},{9,17},{17,9},{25,1},{2,26},{10... | collective-permute-start | bytes 98312 | tf_op jit(solution)/shard_map/ppermute | solution.py:162
  24.0 4.2 %collective-permute-start.10 = (bf16[64,128]{1,0:T(8,128)(2,1)S(1)}, bf16[64,128]{1,0:T(8,128)(2,1)S(1)}, u32[]{:S(2)}, u32[]{:S(2)}) collective-permute-start(bf16[64,128]{1,0:T(8,128)(2,1)S(1)} %get-tuple-element.34), channel_id=1, source_target_pairs={{0,2},{1,3},{2,0},{3,1},{4,6},{5,7},{6,4},{7,5},{8,10},{9,11},{10,... | collective-permute-start | bytes 49160 | tf_op jit(solution)/shard_map/ppermute | solution.py:167
  24.6 4.0 %collective-permute-start.11 = (bf16[64,128]{1,0:T(8,128)(2,1)S(1)}, bf16[64,128]{1,0:T(8,128)(2,1)S(1)}, u32[]{:S(2)}, u32[]{:S(2)}) collective-permute-start(bf16[64,128]{1,0:T(8,128)(2,1)S(1)} %get-tuple-element.35), channel_id=1, source_target_pairs={{0,4},{1,5},{2,6},{3,7},{4,0},{5,1},{6,2},{7,3},{8,12},{9,13},{10,... | collective-permute-start | bytes 49160 | tf_op jit(solution)/shard_map/ppermute | solution.py:167
  25.4 7.0 %collective-permute-start.12 = (bf16[64,128]{1,0:T(8,128)(2,1)S(1)}, bf16[64,128]{1,0:T(8,128)(2,1)S(1)}, u32[]{:S(2)}, u32[]{:S(2)}) collective-permute-start(bf16[64,128]{1,0:T(8,128)(2,1)S(1)} %get-tuple-element.36), channel_id=1, source_target_pairs={{0,6},{1,7},{2,4},{3,5},{4,2},{5,3},{6,0},{7,1},{8,14},{9,15},{10,... | collective-permute-start | bytes 49160 | tf_op jit(solution)/shard_map/ppermute | solution.py:167
  27.6 4.8 %collective-permute-start.13 = (bf16[64,128]{1,0:T(8,128)(2,1)S(1)}, bf16[64,128]{1,0:T(8,128)(2,1)S(1)}, u32[]{:S(2)}, u32[]{:S(2)}) collective-permute-start(bf16[64,128]{1,0:T(8,128)(2,1)S(1)} %get-tuple-element.37), channel_id=1, source_target_pairs={{0,1},{1,0},{2,3},{3,2},{4,5},{5,4},{6,7},{7,6},{8,9},{9,8},{10,11... | collective-permute-start | bytes 49160 | tf_op jit(solution)/shard_map/ppermute | solution.py:167
  27.6 4.8 %collective-permute-start.14 = (bf16[64,128]{1,0:T(8,128)(2,1)S(1)}, bf16[64,128]{1,0:T(8,128)(2,1)S(1)}, u32[]{:S(2)}, u32[]{:S(2)}) collective-permute-start(bf16[64,128]{1,0:T(8,128)(2,1)S(1)} %get-tuple-element.38), channel_id=1, source_target_pairs={{0,3},{1,2},{2,1},{3,0},{4,7},{5,6},{6,5},{7,4},{8,11},{9,10},{10,... | collective-permute-start | bytes 49160 | tf_op jit(solution)/shard_map/ppermute | solution.py:167
  28.3 4.2 %collective-permute-start.15 = (bf16[64,128]{1,0:T(8,128)(2,1)S(1)}, bf16[64,128]{1,0:T(8,128)(2,1)S(1)}, u32[]{:S(2)}, u32[]{:S(2)}) collective-permute-start(bf16[64,128]{1,0:T(8,128)(2,1)S(1)} %get-tuple-element.39), channel_id=1, source_target_pairs={{0,5},{1,4},{2,7},{3,6},{4,1},{5,0},{6,3},{7,2},{8,13},{9,12},{10,... | collective-permute-start | bytes 49160 | tf_op jit(solution)/shard_map/ppermute | solution.py:167
  28.7 4.1 %collective-permute-start.16 = (bf16[64,128]{1,0:T(8,128)(2,1)S(1)}, bf16[64,128]{1,0:T(8,128)(2,1)S(1)}, u32[]{:S(2)}, u32[]{:S(2)}) collective-permute-start(bf16[64,128]{1,0:T(8,128)(2,1)S(1)} %get-tuple-element.40), channel_id=1, source_target_pairs={{0,7},{1,6},{2,5},{3,4},{4,3},{5,2},{6,1},{7,0},{8,15},{9,14},{10,... | collective-permute-start | bytes 49160 | tf_op jit(solution)/shard_map/ppermute | solution.py:167

commit v5 on v3

--- a/solution.py
+++ b/solution.py
@@ -28,7 +28,8 @@
     return slice(p * HEAD_DIM, (p + 1) * HEAD_DIM)
 
 
-def states_kernel(k_hbm, v_hbm, out_ref, k_ref, v_ref, arrived):
+def states_kernel(k_hbm, v_hbm, *refs):
+    *outs, k_ref, v_ref, states, arrived = refs
     copies = []
     for s in range(SLABS):
         lanes = slice(s * SLAB, (s + 1) * SLAB)
@@ -38,6 +39,7 @@
         for copy in copies[-1]:
             copy.start()
     first = first_head((HEAD_DIM, LANES))
+    share = states.shape[1]
     for p in range(PAIRS):
         if p * LANES % SLAB == 0:
             for copy in copies[p * LANES // SLAB]:
@@ -46,35 +48,50 @@
             k_ref[:, lanes_of(p)], v_ref[:, lanes_of(p)], (((0,), (0,)), ((), ())),
             preferred_element_type=jnp.float32)
         packed = jnp.where(first, both[:HEAD_DIM], both[HEAD_DIM:])
-        out_ref[rows_of(p), :] = packed.astype(out_ref.dtype)
-
-
-def totals_kernel(x_ref, out_ref):
-    planes, chains = out_ref.shape[:2]
-    inner = x_ref.shape[0] // chains
-    for c in range(chains):
-        total = x_ref[c * inner]
-        for i in range(1, inner):
-            total = total + x_ref[c * inner + i]
-        for z in range(planes):
-            out_ref[z, c] = total.astype(out_ref.dtype)
-
-
-def prefix_kernel(x_ref, all_ref, out_ref):
-    planes, chains = all_ref.shape[:2]
-    inner = x_ref.shape[0] // chains
+        row = p * HEAD_DIM
+        states[row // share, row % share:row % share + HEAD_DIM, :] = packed
+    me = lax.axis_index("inner")
+    for d, out in enumerate(outs):
+        out[...] = states[me ^ d].astype(out.dtype)
+
+
+def totals_kernel(*refs):
+    *parts, out_ref, sent_ref = refs
+    total = parts[0][...]
+    for part in parts[1:]:
+        total = total + part[...].astype(jnp.float32)
+    out_ref[...] = total
+    sent_ref[...] = total.astype(sent_ref.dtype)
+
+
+def planes_kernel(*refs):
+    *totals, below_ref, whole_ref = refs
     plane = lax.axis_index("outer")
-    groups = jnp.zeros(all_ref.shape[2:], jnp.float32)
-    for c in range(chains):
-        total = groups
-        for z in range(planes):
-            there = all_ref[z, c].astype(jnp.float32)
-            total = total + jnp.where(z < plane, there, 0.0)
-            groups = groups + there
-        for i in range(inner):
-            out_ref[c * inner + i] = total.astype(out_ref.dtype)
-            if i < inner - 1:
-                total = total + x_ref[c * inner + i]
+    whole = totals[0][...]
+    below = jnp.zeros_like(whole)
+    for e, there in enumerate(totals[1:], 1):
+        there = there[...].astype(jnp.float32)
+        below = below + jnp.where((plane ^ e) < plane, there, 0.0)
+        whole = whole + there
+    below_ref[...] = below
+    whole_ref[...] = whole
+
+
+def prefix_kernel(*refs):
+    inner = refs[-1].shape[0]
+    parts, bases, outs, order = refs[:inner], refs[inner:-1 - inner], refs[-1 - inner:-1], refs[-1]
+    me = lax.axis_index("inner")
+    for d, part in enumerate(parts):
+        order[me ^ d] = part[...].astype(jnp.float32)
+    total = bases[0][...]
+    for base in bases[1:]:
+        total = total + base[...]
+    for i in range(inner):
+        here = order[i]
+        order[i] = total
+        total = total + here
+    for d, out in enumerate(outs):
+        out[...] = order[me ^ d].astype(out.dtype)
 
 
 def intra_kernel(q_ref, k_ref, v_ref, out_ref):
@@ -95,14 +112,20 @@
         out_ref[:, lanes_of(p)] = jnp.where(first, intra[0], intra[1])
 
 
-def attend_kernel(q_ref, intra_ref, prefix_ref, out_ref):
+def attend_kernel(q_ref, intra_ref, *refs):
+    *parts, out_ref, order = refs
+    me = lax.axis_index("inner")
+    for d, part in enumerate(parts):
+        order[me ^ d] = part[...]
+    share = order.shape[1]
     first_state = first_head((HEAD_DIM, LANES))
     same = (first_head((LANES, LANES))
             == (lax.broadcasted_iota(jnp.int32, (LANES, LANES), 0) < HEAD_DIM))
     ones = jnp.where(same, 1.0, 0.0).astype(jnp.bfloat16)
     zero = jnp.zeros((), jnp.bfloat16)
     for p in range(PAIRS):
-        packed = prefix_ref[rows_of(p), :]
+        row = p * HEAD_DIM
+        packed = order[row // share, row % share:row % share + HEAD_DIM, :]
         prefix = jnp.concatenate(
             [jnp.where(first_state, packed, zero), jnp.where(first_state, zero, packed)], axis=0)
         inter = jnp.dot(q_ref[:, lanes_of(p)], prefix, preferred_element_type=jnp.float32)
@@ -132,30 +155,39 @@
     return got[0] if single else got
 
 
+def swapped(arrays, axis, own):
+    size = len(arrays)
+    got = {d: lax.ppermute(arrays[d], axis, [(i, i ^ d) for i in range(size)]) for d in reversed(range(1, size))}
+    return [own] + [got[d] for d in range(1, size)]
+
+
 def per_device(chains, planes, inner, queries, keys, values):
     rows = queries.shape[0]
-    members = chains * inner
-    share = PAIRS * HEAD_DIM // members
-    states, keys, values = call(
+    share = (PAIRS * HEAD_DIM // inner, LANES)
+    own, *states, keys, values = call(
         states_kernel,
-        [((PAIRS * HEAD_DIM, LANES), jnp.float32), (keys.shape, keys.dtype), (values.shape, values.dtype)],
+        [(share, jnp.float32)] + [(share, jnp.bfloat16)] * (inner - 1)
+        + [(keys.shape, keys.dtype), (values.shape, values.dtype)],
         keys, values, flops=2 * rows * LANES * LANES * PAIRS, memory=pltpu.HBM,
-        scratch=[pltpu.SemaphoreType.DMA((2, SLABS))])
-    mine = lax.all_to_all(states.reshape(members, share, LANES), ("chain", "inner"), 0, 0, tiled=True)
-    totals = call(totals_kernel, ((planes, chains, share, LANES), jnp.bfloat16), mine)
-    totals = lax.all_to_all(totals, "outer", 0, 0, tiled=True)
-    before = call(prefix_kernel, ((members, share, LANES), jnp.bfloat16), mine, totals)
-    prefix = lax.all_to_all(before, ("chain", "inner"), 0, 0, tiled=True)
+        scratch=[pltpu.VMEM((inner,) + share, jnp.float32), pltpu.SemaphoreType.DMA((2, SLABS))])
+    mine = swapped([own] + states, "inner", own)
+    total, sent = call(totals_kernel, [(share, jnp.float32), (share, jnp.bfloat16)], *mine)
+    totals = swapped([sent] * planes, "outer", total)
+    below, whole = call(planes_kernel, [(share, jnp.float32)] * 2, *totals)
+    groups = [lax.ppermute(whole, "chain", [(c, c + s) for c in range(chains - s)]) for s in range(1, chains)]
+    before = call(prefix_kernel, [(share, jnp.bfloat16)] * inner, *mine, below, *groups,
+                  scratch=[pltpu.VMEM((inner,) + share, jnp.float32)])
+    prefix = swapped(before, "inner", before[0])
     intra = call(intra_kernel, (queries.shape, jnp.float32), queries, keys, values,
                  flops=4 * rows * rows * HEADS * HEAD_DIM)
-    out = pl.pallas_call(
+    return pl.pallas_call(
         attend_kernel,
         out_shape=jax.ShapeDtypeStruct(queries.shape, jnp.bfloat16),
-        in_specs=[VMEM] * 3,
+        in_specs=[VMEM] * (2 + inner),
         out_specs=VMEM,
+        scratch_shapes=[pltpu.VMEM((inner,) + share, jnp.bfloat16)],
         compiler_params=pltpu.CompilerParams(vmem_limit_bytes=16 * 1024 * 1024),
-    )(queries, intra, prefix.reshape(PAIRS * HEAD_DIM, LANES))
-    return out
+    )(queries, intra, *prefix)
 
 
 def solution(mesh):

time: 36.1 us -> 31.6 us (0.88)
  blocking collectives: 22.6 us -> 0 us
  starting transfers between devices: 3.37 us -> 13.8 us
  waiting for transfers between devices: 3.78 us -> 12 us
  Pallas kernels: 6.01 us -> 5.44 us
    all_to_all x2 -> x0, blocking collectives: 22.6 us -> none  [the longest x1 11.6 us: per_device(): lax.all_to_all(states.reshape(members, share, LANES), ('chain', 'inner'),...]
    ppermute x0 -> x10, starting transfers between devices: none -> 13.8 us  [the longest x9 12.5 us: swapped(): lax.ppermute(arrays[d], axis, [(i, i ^ d) for i in range(size)])]
    ppermute x0 -> x10, waiting for transfers between devices: none -> 12 us  [the longest x9 11.1 us: swapped(): lax.ppermute(arrays[d], axis, [(i, i ^ d) for i in range(size)])]
    all_to_all x1 -> x0, waiting for transfers between devices: 3.78 us -> none  [per_device(): prefix = lax.all_to_all(before, ('chain', 'inner'), 0, 0, tiled=True)]
    all_to_all x1 -> x0, starting transfers between devices: 3.37 us -> none  [per_device(): prefix = lax.all_to_all(before, ('chain', 'inner'), 0, 0, tiled=True)]
    pallas_call x4 -> x5, Pallas kernels: 4.17 us -> 3.59 us  [call(): pl.pallas_call(kernel, out_shape=outs, in_specs=[pl.BlockSpec(memory_spac...]
  transfers between devices with their start and end apart: 1 -> 10, of which waited for: 1 -> 7; matrix products, arithmetic and copies ran while one was open for 0% -> 0% of each run, Pallas kernels for 4% -> 5%
where the time goes in v5:
time: 31.6 us; the launch traced here: 31.4 us
  starting transfers between devices  13.8 us (44%)
  waiting for transfers between devices  12 us (38%)
  Pallas kernels  5.44 us (17%)
    ppermute x9, starting transfers between devices, swapped(): lax.ppermute(arrays[d], axis, [(i, i ^ d) for i in range(size)])  12.5 us
    ppermute x9, waiting for transfers between devices, swapped(): lax.ppermute(arrays[d], axis, [(i, i ^ d) for i in range(size)])  11.1 us
    pallas_call x5, Pallas kernels, call(): pl.pallas_call(kernel, out_shape=outs, in_specs=[pl.BlockSpec(memory_spac...  3.59 us
    pallas_call x1, Pallas kernels, per_device(): pl.pallas_call(attend_kernel, out_shape=jax.ShapeDtypeStruct(queries.shap...  1.85 us
    ppermute x1, starting transfers between devices, per_device(): lax.ppermute(whole, 'chain', [(c, c + s) for c in range(chains - s)])  1.29 us
    ppermute x1, waiting for transfers between devices, per_device(): lax.ppermute(whole, 'chain', [(c, c + s) for c in range(chains - s)])  0.88 us
  transfers between devices with their start and end apart: 10, of which 7 were waited for; matrix products, arithmetic and copies ran while one was open for 0% of the time, Pallas kernels for 5%

profile of v5, /device:TPU:0, one launch (start us, length us, event | category | flops | bytes accessed | tf_op | source)
XLA Modules:
  0.0 31.4 jit_solution(839338437541451921)
XLA Ops:
  0.0 2.0 %shard_map.37 = (f32[128,128]{1,0:T(8,128)S(1)}, bf16[128,128]{1,0:T(8,128)(2,1)S(1)}, bf16[128,128]{1,0:T(8,128)(2,1)S(1)}, bf16[128,128]{1,0:T(8,128)(2,1)S(1)...) custom-call(bf16[256,1024]{1,0:T(8,128)(2,1)} %k_hbm.1, bf16[256,1024]{1,0:T(8,128)(2,1)} %v_hbm.1), custom_call_target="tpu_custom_call" | custom-call | flops 67108864 | bytes 1048576 | tf_op jit(solution)/shard_map/pallas_call | solution.py:146
  2.0 0.0 copy-start
  2.0 3.0 %collective-permute-start = (bf16[128,128]{1,0:T(8,128)(2,1)S(1)}, bf16[128,128]{1,0:T(8,128)(2,1)S(1)}, u32[]{:S(2)}, u32[]{:S(2)}) collective-permute-start(bf16[128,128]{1,0:T(8,128)(2,1)S(1)} %get-tuple-element.22), channel_id=1, source_target_pairs={{0,2},{2,0},{4,6},{6,4},{1,3},{3,1},{5,7},{7,5},{8,10},{10,8},{12,... | collective-permute-start | bytes 98312 | tf_op jit(solution)/shard_map/ppermute | solution.py:160
  5.0 1.5 %collective-permute-start.1 = (bf16[128,128]{1,0:T(8,128)(2,1)S(1)}, bf16[128,128]{1,0:T(8,128)(2,1)S(1)}, u32[]{:S(2)}, u32[]{:S(2)}) collective-permute-start(bf16[128,128]{1,0:T(8,128)(2,1)S(1)} %get-tuple-element.23), channel_id=1, source_target_pairs={{0,4},{2,6},{4,0},{6,2},{1,5},{3,7},{5,1},{7,3},{8,12},{10,14},{12... | collective-permute-start | bytes 98312 | tf_op jit(solution)/shard_map/ppermute | solution.py:160
  6.6 0.0 collective-permute-start.2
  6.6 0.4 %collective-permute-done.refs_1_ = bf16[128,128]{1,0:T(8,128)(2,1)S(1)} collective-permute-done((bf16[128,128]{1,0:T(8,128)(2,1)S(1)}, bf16[128,128]{1,0:T(8,128)(2,1)S(1)}, u32[]{:S(2)}, u32[]{:S(2)}) %collective-permute-start) | collective-permute-done | bytes 32800 | tf_op jit(solution)/shard_map/ppermute | solution.py:160
  6.9 2.0 %collective-permute-done.1.refs_2_ = bf16[128,128]{1,0:T(8,128)(2,1)S(1)} collective-permute-done((bf16[128,128]{1,0:T(8,128)(2,1)S(1)}, bf16[128,128]{1,0:T(8,128)(2,1)S(1)}, u32[]{:S(2)}, u32[]{:S(2)}) %collective-permute-start.1) | collective-permute-done | bytes 32800 | tf_op jit(solution)/shard_map/ppermute | solution.py:160
  8.9 2.4 %collective-permute-done.2.refs_3_ = bf16[128,128]{1,0:T(8,128)(2,1)S(1)} collective-permute-done((bf16[128,128]{1,0:T(8,128)(2,1)S(1)}, bf16[128,128]{1,0:T(8,128)(2,1)S(1)}, u32[]{:S(2)}, u32[]{:S(2)}) %collective-permute-start.2) | collective-permute-done | bytes 32800 | tf_op jit(solution)/shard_map/ppermute | solution.py:160
  11.4 1.6 %collective-permute-start.3 = (bf16[128,128]{1,0:T(8,128)(2,1)S(1)}, bf16[128,128]{1,0:T(8,128)(2,1)S(1)}, u32[]{:S(2)}, u32[]{:S(2)}) collective-permute-start(bf16[128,128]{1,0:T(8,128)(2,1)S(1)} %get-tuple-element.26), channel_id=1, source_target_pairs={{0,8},{8,0},{16,24},{24,16},{1,9},{9,1},{17,25},{25,17},{2,10},{10... | collective-permute-start | bytes 98312 | tf_op jit(solution)/shard_map/ppermute | solution.py:160
  13.0 2.6 %collective-permute-start.4 = (bf16[128,128]{1,0:T(8,128)(2,1)S(1)}, bf16[128,128]{1,0:T(8,128)(2,1)S(1)}, u32[]{:S(2)}, u32[]{:S(2)}) collective-permute-start(bf16[128,128]{1,0:T(8,128)(2,1)S(1)} %get-tuple-element.26), channel_id=1, source_target_pairs={{0,16},{8,24},{16,0},{24,8},{1,17},{9,25},{17,1},{25,9},{2,18},{10... | collective-permute-start | bytes 98312 | tf_op jit(solution)/shard_map/ppermute | solution.py:160
  15.6 0.2 collective-permute-start.5
  15.8 0.0 collective-permute-done.3.refs_1_
  15.8 2.6 %collective-permute-done.4.refs_2_ = bf16[128,128]{1,0:T(8,128)(2,1)S(1)} collective-permute-done((bf16[128,128]{1,0:T(8,128)(2,1)S(1)}, bf16[128,128]{1,0:T(8,128)(2,1)S(1)}, u32[]{:S(2)}, u32[]{:S(2)}) %collective-permute-start.4) | collective-permute-done | bytes 32800 | tf_op jit(solution)/shard_map/ppermute | solution.py:160
  18.5 2.9 %collective-permute-done.5.refs_3_ = bf16[128,128]{1,0:T(8,128)(2,1)S(1)} collective-permute-done((bf16[128,128]{1,0:T(8,128)(2,1)S(1)}, bf16[128,128]{1,0:T(8,128)(2,1)S(1)}, u32[]{:S(2)}, u32[]{:S(2)}) %collective-permute-start.5) | collective-permute-done | bytes 32800 | tf_op jit(solution)/shard_map/ppermute | solution.py:160
  21.4 1.3 %collective-permute-start.6 = (f32[128,128]{1,0:T(8,128)S(1)}, f32[128,128]{1,0:T(8,128)S(1)}, u32[]{:S(2)}, u32[]{:S(2)}) collective-permute-start(f32[128,128]{1,0:T(8,128)S(1)} %get-tuple-element.28), channel_id=1, source_target_pairs={{0,1},{2,3},{4,5},{6,7},{8,9},{10,11},{12,13},{14,15},{16,17},{18,... | collective-permute-start | bytes 196616 | tf_op jit(solution)/shard_map/ppermute | solution.py:177
  22.7 0.9 %collective-permute-done.6.refs_5_ = f32[128,128]{1,0:T(8,128)S(1)} collective-permute-done((f32[128,128]{1,0:T(8,128)S(1)}, f32[128,128]{1,0:T(8,128)S(1)}, u32[]{:S(2)}, u32[]{:S(2)}) %collective-permute-start.6) | collective-permute-done | bytes 65568 | tf_op jit(solution)/shard_map/ppermute | solution.py:177
  23.6 0.1 shard_map.41
  23.6 0.6 %collective-permute-start.7 = (bf16[128,128]{1,0:T(8,128)(2,1)S(1)}, bf16[128,128]{1,0:T(8,128)(2,1)S(1)}, u32[]{:S(2)}, u32[]{:S(2)}) collective-permute-start(bf16[128,128]{1,0:T(8,128)(2,1)S(1)} %get-tuple-element.30), channel_id=1, source_target_pairs={{0,2},{2,0},{4,6},{6,4},{1,3},{3,1},{5,7},{7,5},{8,10},{10,8},{12,... | collective-permute-start | bytes 98312 | tf_op jit(solution)/shard_map/ppermute | solution.py:160
  24.2 0.5 %collective-permute-start.8 = (bf16[128,128]{1,0:T(8,128)(2,1)S(1)}, bf16[128,128]{1,0:T(8,128)(2,1)S(1)}, u32[]{:S(2)}, u32[]{:S(2)}) collective-permute-start(bf16[128,128]{1,0:T(8,128)(2,1)S(1)} %get-tuple-element.31), channel_id=1, source_target_pairs={{0,4},{2,6},{4,0},{6,2},{1,5},{3,7},{5,1},{7,3},{8,12},{10,14},{12... | collective-permute-start | bytes 98312 | tf_op jit(solution)/shard_map/ppermute | solution.py:160
  24.7 2.5 %collective-permute-start.9 = (bf16[128,128]{1,0:T(8,128)(2,1)S(1)}, bf16[128,128]{1,0:T(8,128)(2,1)S(1)}, u32[]{:S(2)}, u32[]{:S(2)}) collective-permute-start(bf16[128,128]{1,0:T(8,128)(2,1)S(1)} %get-tuple-element.32), channel_id=1, source_target_pairs={{0,6},{2,4},{4,2},{6,0},{1,7},{3,5},{5,3},{7,1},{8,14},{10,12},{12... | collective-permute-start | bytes 98312 | tf_op jit(solution)/shard_map/ppermute | solution.py:160
  27.2 0.0 copy-done
  27.2 1.5 %shard_map.38.intra_ref = f32[256,1024]{1,0:T(8,128)S(1)} custom-call(bf16[256,1024]{1,0:T(8,128)(2,1)S(1)} %copy-done, bf16[256,1024]{1,0:T(8,128)(2,1)S(1)} %get-tuple-element.19.k_ref, bf16[256,1024]{1,0:T(8,128)(2,1)S(1)} %get-tuple-element.20.v_ref), custom_call_target="tpu_custom_call" | custom-call | flops 268435456 | bytes 1572864 | tf_op jit(solution)/shard_map/pallas_call | solution.py:146
  28.7 0.0 collective-permute-done.7.refs_1_
  28.7 0.0 collective-permute-done.8.refs_2_
  28.7 0.9 %collective-permute-done.9.refs_3_ = bf16[128,128]{1,0:T(8,128)(2,1)S(1)} collective-permute-done((bf16[128,128]{1,0:T(8,128)(2,1)S(1)}, bf16[128,128]{1,0:T(8,128)(2,1)S(1)}, u32[]{:S(2)}, u32[]{:S(2)}) %collective-permute-start.9) | collective-permute-done | bytes 32800 | tf_op jit(solution)/shard_map/ppermute | solution.py:160
  29.5 1.9 %shard_map.42 = bf16[256,1024]{1,0:T(8,128)(2,1)} custom-call(bf16[256,1024]{1,0:T(8,128)(2,1)S(1)} %copy-done, f32[256,1024]{1,0:T(8,128)S(1)} %shard_map.38.intra_ref, bf16[128,128]{1,0:T(8,128)(2,1)S(1)} %get-tuple-element.29.refs_0_, bf16[128,128]{1,0:T(8,128)(2,1)S(1)} %collective-permute-done.7.refs_1_, ...), custom_call_target="tpu_custom_call" | custom-call | tf_op jit(solution)/shard_map/pallas_call | solution.py:183
  (2 shorter events, 0.1 us)
Async XLA Ops:
  2.0 25.2 %copy-start = (bf16[256,1024]{1,0:T(8,128)(2,1)S(1)}, bf16[256,1024]{1,0:T(8,128)(2,1)}, u32[]{:S(2)}) copy-start(bf16[256,1024]{1,0:T(8,128)(2,1)} %q_ref.3) | copy-start | bytes 1572868
  2.0 4.9 %collective-permute-start = (bf16[128,128]{1,0:T(8,128)(2,1)S(1)}, bf16[128,128]{1,0:T(8,128)(2,1)S(1)}, u32[]{:S(2)}, u32[]{:S(2)}) collective-permute-start(bf16[128,128]{1,0:T(8,128)(2,1)S(1)} %get-tuple-element.22), channel_id=1, source_target_pairs={{0,2},{2,0},{4,6},{6,4},{1,3},{3,1},{5,7},{7,5},{8,10},{10,8},{12,... | collective-permute-start | bytes 98312 | tf_op jit(solution)/shard_map/ppermute | solution.py:160
  5.0 3.9 %collective-permute-start.1 = (bf16[128,128]{1,0:T(8,128)(2,1)S(1)}, bf16[128,128]{1,0:T(8,128)(2,1)S(1)}, u32[]{:S(2)}, u32[]{:S(2)}) collective-permute-start(bf16[128,128]{1,0:T(8,128)(2,1)S(1)} %get-tuple-element.23), channel_id=1, source_target_pairs={{0,4},{2,6},{4,0},{6,2},{1,5},{3,7},{5,1},{7,3},{8,12},{10,14},{12... | collective-permute-start | bytes 98312 | tf_op jit(solution)/shard_map/ppermute | solution.py:160
  6.6 4.8 %collective-permute-start.2 = (bf16[128,128]{1,0:T(8,128)(2,1)S(1)}, bf16[128,128]{1,0:T(8,128)(2,1)S(1)}, u32[]{:S(2)}, u32[]{:S(2)}) collective-permute-start(bf16[128,128]{1,0:T(8,128)(2,1)S(1)} %get-tuple-element.24), channel_id=1, source_target_pairs={{0,6},{2,4},{4,2},{6,0},{1,7},{3,5},{5,3},{7,1},{8,14},{10,12},{12... | collective-permute-start | bytes 98312 | tf_op jit(solution)/shard_map/ppermute | solution.py:160
  11.4 4.5 %collective-permute-start.3 = (bf16[128,128]{1,0:T(8,128)(2,1)S(1)}, bf16[128,128]{1,0:T(8,128)(2,1)S(1)}, u32[]{:S(2)}, u32[]{:S(2)}) collective-permute-start(bf16[128,128]{1,0:T(8,128)(2,1)S(1)} %get-tuple-element.26), channel_id=1, source_target_pairs={{0,8},{8,0},{16,24},{24,16},{1,9},{9,1},{17,25},{25,17},{2,10},{10... | collective-permute-start | bytes 98312 | tf_op jit(solution)/shard_map/ppermute | solution.py:160
  13.0 5.4 %collective-permute-start.4 = (bf16[128,128]{1,0:T(8,128)(2,1)S(1)}, bf16[128,128]{1,0:T(8,128)(2,1)S(1)}, u32[]{:S(2)}, u32[]{:S(2)}) collective-permute-start(bf16[128,128]{1,0:T(8,128)(2,1)S(1)} %get-tuple-element.26), channel_id=1, source_target_pairs={{0,16},{8,24},{16,0},{24,8},{1,17},{9,25},{17,1},{25,9},{2,18},{10... | collective-permute-start | bytes 98312 | tf_op jit(solution)/shard_map/ppermute | solution.py:160
  15.6 5.7 %collective-permute-start.5 = (bf16[128,128]{1,0:T(8,128)(2,1)S(1)}, bf16[128,128]{1,0:T(8,128)(2,1)S(1)}, u32[]{:S(2)}, u32[]{:S(2)}) collective-permute-start(bf16[128,128]{1,0:T(8,128)(2,1)S(1)} %get-tuple-element.26), channel_id=1, source_target_pairs={{0,24},{8,16},{16,8},{24,0},{1,25},{9,17},{17,9},{25,1},{2,26},{10... | collective-permute-start | bytes 98312 | tf_op jit(solution)/shard_map/ppermute | solution.py:160
  21.4 2.2 %collective-permute-start.6 = (f32[128,128]{1,0:T(8,128)S(1)}, f32[128,128]{1,0:T(8,128)S(1)}, u32[]{:S(2)}, u32[]{:S(2)}) collective-permute-start(f32[128,128]{1,0:T(8,128)S(1)} %get-tuple-element.28), channel_id=1, source_target_pairs={{0,1},{2,3},{4,5},{6,7},{8,9},{10,11},{12,13},{14,15},{16,17},{18,... | collective-permute-start | bytes 196616 | tf_op jit(solution)/shard_map/ppermute | solution.py:177
  23.6 5.0 %collective-permute-start.7 = (bf16[128,128]{1,0:T(8,128)(2,1)S(1)}, bf16[128,128]{1,0:T(8,128)(2,1)S(1)}, u32[]{:S(2)}, u32[]{:S(2)}) collective-permute-start(bf16[128,128]{1,0:T(8,128)(2,1)S(1)} %get-tuple-element.30), channel_id=1, source_target_pairs={{0,2},{2,0},{4,6},{6,4},{1,3},{3,1},{5,7},{7,5},{8,10},{10,8},{12,... | collective-permute-start | bytes 98312 | tf_op jit(solution)/shard_map/ppermute | solution.py:160
  24.2 4.5 %collective-permute-start.8 = (bf16[128,128]{1,0:T(8,128)(2,1)S(1)}, bf16[128,128]{1,0:T(8,128)(2,1)S(1)}, u32[]{:S(2)}, u32[]{:S(2)}) collective-permute-start(bf16[128,128]{1,0:T(8,128)(2,1)S(1)} %get-tuple-element.31), channel_id=1, source_target_pairs={{0,4},{2,6},{4,0},{6,2},{1,5},{3,7},{5,1},{7,3},{8,12},{10,14},{12... | collective-permute-start | bytes 98312 | tf_op jit(solution)/shard_map/ppermute | solution.py:160
  24.7 4.8 %collective-permute-start.9 = (bf16[128,128]{1,0:T(8,128)(2,1)S(1)}, bf16[128,128]{1,0:T(8,128)(2,1)S(1)}, u32[]{:S(2)}, u32[]{:S(2)}) collective-permute-start(bf16[128,128]{1,0:T(8,128)(2,1)S(1)} %get-tuple-element.32), channel_id=1, source_target_pairs={{0,6},{2,4},{4,2},{6,0},{1,7},{3,5},{5,3},{7,1},{8,14},{10,12},{12... | collective-permute-start | bytes 98312 | tf_op jit(solution)/shard_map/ppermute | solution.py:160

commit v6 on v1

v6 whole, which is shorter than its diff:
```python
import functools

import jax
import jax.numpy as jnp
from jax import lax
from jax.experimental import pallas as pl
from jax.experimental.pallas import tpu as pltpu
from jax.sharding import PartitionSpec as P

HEADS = 16
HEAD_DIM = 64
PAIRS = HEADS // 2
LANES = 2 * HEAD_DIM
AXES = ("chain", "wide")
CHUNKS = 4
SLAB = 256
VMEM = pl.BlockSpec(memory_space=pltpu.VMEM)
BF16 = jnp.bfloat16
F32 = jnp.float32


def first_head(shape):
    return lax.broadcasted_iota(jnp.int32, shape, len(shape) - 1) < HEAD_DIM


def lanes_of(p):
    return slice(p * LANES, (p + 1) * LANES)


def rows_of(p):
    return slice(p * HEAD_DIM, (p + 1) * HEAD_DIM)


def states_kernel(k_hbm, v_hbm, out_ref, k_ref, v_ref, sums, arrived):
    rows = k_ref.shape[0] // CHUNKS
    copies = []
    for s in range(CHUNKS):
        chunk = pl.ds(s * rows, rows)
        copies.append([
            pltpu.make_async_copy(k_hbm.at[chunk], k_ref.at[chunk], arrived.at[0, s]),
            pltpu.make_async_copy(v_hbm.at[chunk], v_ref.at[chunk], arrived.at[1, s])])
        for copy in copies[-1]:
            copy.start()
    first = first_head((HEAD_DIM, LANES))
    for s in range(CHUNKS):
        for copy in copies[s]:
            copy.wait()
        chunk = slice(s * rows, (s + 1) * rows)
        for p in range(PAIRS):
            both = lax.dot_general(
                k_ref[chunk, lanes_of(p)], v_ref[chunk, lanes_of(p)], (((0,), (0,)), ((), ())),
                preferred_element_type=F32)
            packed = jnp.where(first, both[:HEAD_DIM], both[HEAD_DIM:])
            if s > 0:
                packed = sums[rows_of(p), :] + packed
            if s < CHUNKS - 1:
                sums[rows_of(p), :] = packed
            else:
                out_ref[rows_of(p), :] = packed.astype(out_ref.dtype)


def scan_kernel(x_ref, out_ref):
    parts = x_ref.shape[0]
    total = jnp.zeros(x_ref.shape[1:], F32)
    for i in range(parts):
        out_ref[i] = total.astype(out_ref.dtype)
        if i < parts - 1:
            total = total + x_ref[i].astype(F32)


def scan_rows_kernel(x_ref, out_ref):
    parts = x_ref.shape[0]
    row = lax.broadcasted_iota(jnp.int32, (parts, parts), 0)
    col = lax.broadcasted_iota(jnp.int32, (parts, parts), 1)
    below = jnp.where(col < row, 1.0, 0.0).astype(BF16)
    out_ref[...] = jnp.dot(below, x_ref[...], preferred_element_type=F32).astype(out_ref.dtype)


def intra_kernel(q_ref, k_ref, v_ref, out_ref):
    rows = q_ref.shape[0]
    causal = (lax.broadcasted_iota(jnp.int32, (rows, rows), 0)
              >= lax.broadcasted_iota(jnp.int32, (rows, rows), 1))
    first = first_head((rows, LANES))
    zero = jnp.zeros((), BF16)
    for p in range(PAIRS):
        q, k, v = q_ref[:, lanes_of(p)], k_ref[:, lanes_of(p)], v_ref[:, lanes_of(p)]
        intra = []
        for mine in (first, ~first):
            scores = lax.dot_general(
                jnp.where(mine, q, zero), k, (((1,), (1,)), ((), ())),
                preferred_element_type=F32)
            scores = jnp.where(causal, scores, 0.0).astype(BF16)
            intra.append(jnp.dot(scores, v, preferred_element_type=F32))
        out_ref[:, lanes_of(p)] = jnp.where(first, intra[0], intra[1])


def attend_kernel(q_ref, intra_ref, prefix_ref, out_hbm, out_ref, sent):
    heads = SLAB // HEAD_DIM
    blocks = ([lax.broadcasted_iota(jnp.int32, (SLAB, SLAB), d) // HEAD_DIM for d in range(2)])
    same = blocks[0] == blocks[1]
    ones = jnp.where(same, 1.0, 0.0).astype(BF16)
    zero = jnp.zeros((), BF16)
    copies = []
    for s in range(HEADS // heads):
        lanes = slice(s * SLAB, (s + 1) * SLAB)
        rows = []
        for p in range(s * heads // 2, (s + 1) * heads // 2):
            rows += [jnp.concatenate([prefix_ref[rows_of(p), :]] * (SLAB // LANES), axis=1)] * 2
        prefix = jnp.where(same, jnp.concatenate(rows, axis=0), zero)
        inter = jnp.dot(q_ref[:, lanes], prefix, preferred_element_type=F32)
        total = intra_ref[:, lanes] + inter
        square = total * total
        high = square.astype(BF16)
        low = (square - high.astype(F32)).astype(BF16)
        sums = (jnp.dot(high, ones, preferred_element_type=F32)
                + jnp.dot(low, ones, preferred_element_type=F32))
        out_ref[:, lanes] = (total * lax.rsqrt(sums * (1.0 / HEAD_DIM) + 1e-6)).astype(out_ref.dtype)
        copies.append(pltpu.make_async_copy(out_ref.at[:, lanes], out_hbm.at[:, lanes], sent.at[s]))
        copies[-1].start()
    for copy in copies:
        copy.wait()


def call(kernel, outs, *args, flops=0, scratch=(), source=pltpu.VMEM, result=pltpu.VMEM):
    moved = sum(a.size * a.dtype.itemsize for a in args)
    single = not isinstance(outs, list)
    outs = [outs] if single else outs
    got = pl.pallas_call(
        kernel,
        out_shape=[result(shape, dtype) for shape, dtype in outs],
        in_specs=[pl.BlockSpec(memory_space=source)] * len(args),
        out_specs=[pl.BlockSpec(memory_space=result)] * len(outs),
        scratch_shapes=scratch,
        cost_estimate=pl.CostEstimate(flops=flops, bytes_accessed=moved, transcendentals=0),
        compiler_params=pltpu.CompilerParams(vmem_limit_bytes=16 * 1024 * 1024),
    )(*[pltpu.with_memory_space_constraint(a, source) for a in args])
    return got[0] if single else got


def per_device(parts, queries, keys, values):
    rows = queries.shape[0]
    state = (PAIRS * HEAD_DIM, LANES)
    share = state[0] // parts
    states, keys, values = call(
        states_kernel, [(state, BF16), (keys.shape, keys.dtype), (values.shape, values.dtype)],
        keys, values, flops=2 * rows * LANES * LANES * PAIRS, source=pltpu.HBM,
        scratch=[pltpu.VMEM(state, F32), pltpu.SemaphoreType.DMA((2, CHUNKS))])
    view = (parts, share, LANES) if share > 1 else (parts, LANES)
    mine = lax.all_to_all(states.reshape(view), AXES, 0, 0, tiled=True)
    mine, queries = lax.optimization_barrier((mine, queries))
    before = call(scan_kernel if share > 1 else scan_rows_kernel, (view, BF16), mine)
    prefix = lax.all_to_all(before, AXES, 0, 0, tiled=True).reshape(state)
    intra = call(intra_kernel, (queries.shape, F32), queries, keys, values,
                 flops=4 * rows * rows * HEADS * HEAD_DIM)
    return call(attend_kernel, (queries.shape, BF16), queries, intra, prefix, result=pltpu.HBM,
                flops=2 * rows * SLAB * HEADS * HEAD_DIM,
                scratch=[pltpu.VMEM(queries.shape, BF16), pltpu.SemaphoreType.DMA((HEADS * HEAD_DIM // SLAB,))])


def solution(mesh):
    spec = P(AXES, None)
    parts = mesh.shape["chain"] * mesh.shape["wide"]
    return jax.shard_map(
        functools.partial(per_device, parts),
        mesh=mesh,
        in_specs=(spec, spec, spec),
        out_specs=spec,
        check_vma=False,
    )
```

time: 31.2 us -> 30.1 us (0.965)
  blocking collectives: 24.9 us -> 15 us
  waiting for transfers between devices: 0 us -> 6.41 us
  starting transfers between devices: 0 us -> 2.58 us
  local copies, waits for them, and re-layouts: 2.09 us -> 0.01 us
  Pallas kernels: 3.93 us -> 5.79 us
    all_to_all x1 -> x0, blocking collectives: 9.92 us -> none  [per_device(): lax.all_to_all(before, AXES, 0, 0, tiled=True).reshape(state_rows, LANES)]
    all_to_all x0 -> x1, waiting for transfers between devices: none -> 6.41 us  [per_device(): prefix = lax.all_to_all(before, AXES, 0, 0, tiled=True).reshape(state)]
    all_to_all x0 -> x1, starting transfers between devices: none -> 2.58 us  [per_device(): prefix = lax.all_to_all(before, AXES, 0, 0, tiled=True).reshape(state)]
    unnamed x8 -> x2, local copies, waits for them, and re-layouts: 2.09 us -> 0.01 us
    pallas_call x3 -> x4, Pallas kernels: 3.93 us -> 5.79 us  [call(): pl.pallas_call(kernel, out_shape=[result(shape, dtype) for shape, dtype i...]
  transfers between devices with their start and end apart: 0 -> 1, of which waited for: 0 -> 1; matrix products, arithmetic and copies ran while one was open for 0% -> 0% of each run, Pallas kernels for 0% -> 5%
where the time goes in v6:
time: 30.1 us; the launch traced here: 29.8 us
  blocking collectives  15 us (50%)
  waiting for transfers between devices  6.41 us (21%)
  Pallas kernels  5.79 us (19%)
  starting transfers between devices  2.58 us (9%)
    all_to_all x1, blocking collectives, per_device(): mine = lax.all_to_all(states.reshape(view), AXES, 0, 0, tiled=True)  15 us
    all_to_all x1, waiting for transfers between devices, per_device(): prefix = lax.all_to_all(before, AXES, 0, 0, tiled=True).reshape(state)  6.41 us
    pallas_call x4, Pallas kernels, call(): pl.pallas_call(kernel, out_shape=[result(shape, dtype) for shape, dtype i...  5.79 us
    all_to_all x1, starting transfers between devices, per_device(): prefix = lax.all_to_all(before, AXES, 0, 0, tiled=True).reshape(state)  2.58 us
  transfers between devices with their start and end apart: 1, of which 1 were waited for; matrix products, arithmetic and copies ran while one was open for 0% of the time, Pallas kernels for 5%

profile of v6, /device:TPU:0, one launch (start us, length us, event | category | flops | bytes accessed | tf_op | source)
XLA Modules:
  0.0 29.8 jit_solution(18290558711342187457)
XLA Ops:
  0.0 2.1 %shard_map.37 = (bf16[512,128]{1,0:T(8,128)(2,1)S(1)}, bf16[256,1024]{1,0:T(8,128)(2,1)S(1)}, bf16[256,1024]{1,0:T(8,128)(2,1)S(1)}) custom-call(bf16[256,1024]{1,0:T(8,128)(2,1)} %k_hbm.1, bf16[256,1024]{1,0:T(8,128)(2,1)} %v_hbm.1), custom_call_target="tpu_custom_call" | custom-call | flops 67108864 | bytes 1048576 | tf_op jit(solution)/shard_map/pallas_call | solution.py:128
  2.1 0.0 copy-start
  2.1 15.0 %all_to_all.10.x_ref = bf16[32,16,128]{2,1,0:T(8,128)(2,1)S(1)} all-to-all(bf16[32,16,128]{2,1,0:T(8,128)(2,1)S(1)} %bitcast.3), channel_id=1, replica_groups=mesh['wide'=16,'chain'=2] {'chain','wide'}, dimensions={0} | all-to-all | bytes 262144 | tf_op jit(solution)/shard_map/all_to_all | solution.py:149
  17.1 0.7 %shard_map.39 = bf16[32,16,128]{2,1,0:T(8,128)(2,1)} custom-call(bf16[32,16,128]{2,1,0:T(8,128)(2,1)S(1)} %all_to_all.10.x_ref), custom_call_target="tpu_custom_call" | custom-call | bytes 131072 | tf_op jit(solution)/shard_map/pallas_call | solution.py:128
  17.8 2.6 %all-to-all-start.1 = ((bf16[32,16,128]{2,1,0:T(8,128)(2,1)}), bf16[32,16,128]{2,1,0:T(8,128)(2,1)S(1)}, u32[]{:S(2)}, u32[]{:S(2)}) async-start(bf16[32,16,128]{2,1,0:T(8,128)(2,1)} %shard_map.39), calls=%async_computation.1 | async-start | bytes 262144 | tf_op jit(solution)/shard_map/all_to_all | solution.py:152
  20.4 0.0 copy-done
  20.4 1.5 %shard_map.38.intra_ref = f32[256,1024]{1,0:T(8,128)S(1)} custom-call(bf16[256,1024]{1,0:T(8,128)(2,1)S(1)} %copy-done, bf16[256,1024]{1,0:T(8,128)(2,1)S(1)} %get-tuple-element.12.k_ref, bf16[256,1024]{1,0:T(8,128)(2,1)S(1)} %get-tuple-element.13.v_ref), custom_call_target="tpu_custom_call" | custom-call | flops 268435456 | bytes 1572864 | tf_op jit(solution)/shard_map/pallas_call | solution.py:128
  21.9 6.4 %all-to-all-done.1 = bf16[32,16,128]{2,1,0:T(8,128)(2,1)S(1)} async-done(((bf16[32,16,128]{2,1,0:T(8,128)(2,1)}), bf16[32,16,128]{2,1,0:T(8,128)(2,1)S(1)}, u32[]{:S(2)}, u32[]{:S(2)}) %all-to-all-start.1) | async-done | bytes 131104 | tf_op jit(solution)/shard_map/all_to_all | solution.py:152
  28.3 1.5 %shard_map.40 = bf16[256,1024]{1,0:T(8,128)(2,1)} custom-call(bf16[256,1024]{1,0:T(8,128)(2,1)S(1)} %copy-done, f32[256,1024]{1,0:T(8,128)S(1)} %shard_map.38.intra_ref, bf16[512,128]{1,0:T(8,128)(2,1)S(1)} %bitcast.2), custom_call_target="tpu_custom_call" | custom-call | flops 134217728 | bytes 1703936 | tf_op jit(solution)/shard_map/pallas_call | solution.py:128
Async XLA Ops:
  2.1 18.3 %copy-start = (bf16[256,1024]{1,0:T(8,128)(2,1)S(1)}, bf16[256,1024]{1,0:T(8,128)(2,1)}, u32[]{:S(2)}) copy-start(bf16[256,1024]{1,0:T(8,128)(2,1)} %q_ref.1) | copy-start | bytes 1572868
  17.8 10.5 %all-to-all-start.1 = ((bf16[32,16,128]{2,1,0:T(8,128)(2,1)}), bf16[32,16,128]{2,1,0:T(8,128)(2,1)S(1)}, u32[]{:S(2)}, u32[]{:S(2)}) async-start(bf16[32,16,128]{2,1,0:T(8,128)(2,1)} %shard_map.39), calls=%async_computation.1 | async-start | bytes 262144 | tf_op jit(solution)/shard_map/all_to_all | solution.py:152

commit v7 on v6

--- a/solution.py
+++ b/solution.py
@@ -59,21 +59,22 @@
                 out_ref[rows_of(p), :] = packed.astype(out_ref.dtype)
 
 
-def scan_kernel(x_ref, out_ref):
-    parts = x_ref.shape[0]
-    total = jnp.zeros(x_ref.shape[1:], F32)
-    for i in range(parts):
-        out_ref[i] = total.astype(out_ref.dtype)
-        if i < parts - 1:
-            total = total + x_ref[i].astype(F32)
+def totals_kernel(x_ref, out_ref):
+    total = x_ref[0].astype(F32)
+    for i in range(1, x_ref.shape[0]):
+        total = total + x_ref[i].astype(F32)
+    out_ref[...] = total
 
 
-def scan_rows_kernel(x_ref, out_ref):
-    parts = x_ref.shape[0]
-    row = lax.broadcasted_iota(jnp.int32, (parts, parts), 0)
-    col = lax.broadcasted_iota(jnp.int32, (parts, parts), 1)
-    below = jnp.where(col < row, 1.0, 0.0).astype(BF16)
-    out_ref[...] = jnp.dot(below, x_ref[...], preferred_element_type=F32).astype(out_ref.dtype)
+def scan_kernel(x_ref, *refs):
+    *groups, out_ref = refs
+    chain = lax.axis_index("chain")
+    total = jnp.zeros(x_ref.shape[1:], F32)
+    for d, group in enumerate(groups, 1):
+        total = total + jnp.where((chain ^ d) < chain, group[...], 0.0)
+    for i in reversed(range(x_ref.shape[0])):
+        out_ref[i] = total.astype(out_ref.dtype)
+        total = total + x_ref[i].astype(F32)
 
 
 def intra_kernel(q_ref, k_ref, v_ref, out_ref):
@@ -137,19 +138,22 @@
     return got[0] if single else got
 
 
-def per_device(parts, queries, keys, values):
+def per_device(chains, wide, queries, keys, values):
     rows = queries.shape[0]
     state = (PAIRS * HEAD_DIM, LANES)
-    share = state[0] // parts
+    share = state[0] // wide
     states, keys, values = call(
         states_kernel, [(state, BF16), (keys.shape, keys.dtype), (values.shape, values.dtype)],
         keys, values, flops=2 * rows * LANES * LANES * PAIRS, source=pltpu.HBM,
         scratch=[pltpu.VMEM(state, F32), pltpu.SemaphoreType.DMA((2, CHUNKS))])
-    view = (parts, share, LANES) if share > 1 else (parts, LANES)
-    mine = lax.all_to_all(states.reshape(view), AXES, 0, 0, tiled=True)
+    view = (wide, share, LANES)
+    order = [list(reversed(range(wide)))]
+    mine = lax.all_to_all(states.reshape(view), "wide", 0, 0, axis_index_groups=order, tiled=True)
     mine, queries = lax.optimization_barrier((mine, queries))
-    before = call(scan_kernel if share > 1 else scan_rows_kernel, (view, BF16), mine)
-    prefix = lax.all_to_all(before, AXES, 0, 0, tiled=True).reshape(state)
+    total = call(totals_kernel, (view[1:], F32), mine)
+    groups = [lax.ppermute(total, "chain", [(c, c ^ d) for c in range(chains)]) for d in range(1, chains)]
+    before = call(scan_kernel, (view, BF16), mine, *groups)
+    prefix = lax.all_to_all(before, "wide", 0, 0, axis_index_groups=order, tiled=True).reshape(state)
     intra = call(intra_kernel, (queries.shape, F32), queries, keys, values,
                  flops=4 * rows * rows * HEADS * HEAD_DIM)
     return call(attend_kernel, (queries.shape, BF16), queries, intra, prefix, result=pltpu.HBM,
@@ -159,9 +163,8 @@
 
 def solution(mesh):
     spec = P(AXES, None)
-    parts = mesh.shape["chain"] * mesh.shape["wide"]
     return jax.shard_map(
-        functools.partial(per_device, parts),
+        functools.partial(per_device, mesh.shape["chain"], mesh.shape["wide"]),
         mesh=mesh,
         in_specs=(spec, spec, spec),
         out_specs=spec,

time: 30.1 us -> 30.9 us (1.027)
  starting transfers between devices: 2.58 us -> 7.47 us
  waiting for transfers between devices: 6.41 us -> 3.89 us
  blocking collectives: 15 us -> 13.5 us
    all_to_all x1, starting transfers between devices: 2.58 us -> 7.4 us  [per_device(): lax.all_to_all(before, 'wide', 0, 0, axis_index_groups=order, tiled=True)]
    all_to_all x1, waiting for transfers between devices: 6.41 us -> 2.72 us  [per_device(): lax.all_to_all(before, 'wide', 0, 0, axis_index_groups=order, tiled=True)]
    all_to_all x1, blocking collectives: 15 us -> 13.5 us  [per_device(): lax.all_to_all(states.reshape(view), 'wide', 0, 0, axis_index_groups=orde...]
    ppermute x0 -> x1, waiting for transfers between devices: none -> 1.17 us  [per_device(): lax.ppermute(total, 'chain', [(c, c ^ d) for c in range(chains)])]
    pallas_call x4 -> x5, Pallas kernels: 5.79 us -> 5.8 us  [call(): pl.pallas_call(kernel, out_shape=[result(shape, dtype) for shape, dtype i...]
  transfers between devices with their start and end apart: 1 -> 2, of which waited for: 1 -> 2; matrix products, arithmetic and copies ran while one was open for 0% -> 0% of each run, Pallas kernels for 5% -> 5%
where the time goes in v7:
time: 30.9 us; the launch traced here: 30.7 us
  blocking collectives  13.5 us (44%)
  starting transfers between devices  7.47 us (24%)
  Pallas kernels  5.8 us (19%)
  waiting for transfers between devices  3.89 us (13%)
    all_to_all x1, blocking collectives, per_device(): lax.all_to_all(states.reshape(view), 'wide', 0, 0, axis_index_groups=orde...  13.5 us
    all_to_all x1, starting transfers between devices, per_device(): lax.all_to_all(before, 'wide', 0, 0, axis_index_groups=order, tiled=True)  7.4 us
    pallas_call x5, Pallas kernels, call(): pl.pallas_call(kernel, out_shape=[result(shape, dtype) for shape, dtype i...  5.8 us
    all_to_all x1, waiting for transfers between devices, per_device(): lax.all_to_all(before, 'wide', 0, 0, axis_index_groups=order, tiled=True)  2.72 us
    ppermute x1, waiting for transfers between devices, per_device(): lax.ppermute(total, 'chain', [(c, c ^ d) for c in range(chains)])  1.17 us
  transfers between devices with their start and end apart: 2, of which 2 were waited for; matrix products, arithmetic and copies ran while one was open for 0% of the time, Pallas kernels for 5%

profile of v7, /device:TPU:0, one launch (start us, length us, event | category | flops | bytes accessed | tf_op | source)
XLA Modules:
  0.0 30.7 jit_solution(3129176623246752146)
XLA Ops:
  0.0 2.1 %shard_map.37 = (bf16[512,128]{1,0:T(8,128)(2,1)S(1)}, bf16[256,1024]{1,0:T(8,128)(2,1)S(1)}, bf16[256,1024]{1,0:T(8,128)(2,1)S(1)}) custom-call(bf16[256,1024]{1,0:T(8,128)(2,1)} %k_hbm.1, bf16[256,1024]{1,0:T(8,128)(2,1)} %v_hbm.1), custom_call_target="tpu_custom_call" | custom-call | flops 67108864 | bytes 1048576 | tf_op jit(solution)/shard_map/pallas_call | solution.py:129
  2.1 0.0 copy-start
  2.1 13.5 %all_to_all.10.x_ref = bf16[16,32,128]{2,1,0:T(8,128)(2,1)S(1)} all-to-all(bf16[16,32,128]{2,1,0:T(8,128)(2,1)S(1)} %bitcast.3), channel_id=1, replica_groups={{30,28,26,24,22,20,18,16,14,12,10,8,6,4,2,0},{31,29,27,25,23,21,19,17,1..., dimensions={0} | all-to-all | bytes 262144 | tf_op jit(solution)/shard_map/all_to_all | solution.py:151
  15.6 0.1 collective-permute-start
  15.7 1.2 %collective-permute-done.refs_0_ = f32[32,128]{1,0:T(8,128)S(1)} collective-permute-done((f32[32,128]{1,0:T(8,128)S(1)}, f32[32,128]{1,0:T(8,128)S(1)}, u32[]{:S(2)}, u32[]{:S(2)}) %collective-permute-start) | collective-permute-done | bytes 16416 | tf_op jit(solution)/shard_map/ppermute | solution.py:154
  16.9 0.7 %shard_map.40 = bf16[16,32,128]{2,1,0:T(8,128)(2,1)} custom-call(bf16[16,32,128]{2,1,0:T(8,128)(2,1)S(1)} %all_to_all.10.x_ref, f32[32,128]{1,0:T(8,128)S(1)} %collective-permute-done.refs_0_), custom_call_target="tpu_custom_call" | custom-call | bytes 147456 | tf_op jit(solution)/shard_map/pallas_call | solution.py:129
  17.5 7.4 %all-to-all-start.1 = ((bf16[16,32,128]{2,1,0:T(8,128)(2,1)}), bf16[16,32,128]{2,1,0:T(8,128)(2,1)S(1)}, u32[]{:S(2)}, u32[]{:S(2)}) async-start(bf16[16,32,128]{2,1,0:T(8,128)(2,1)} %shard_map.40), calls=%async_computation.1 | async-start | bytes 262144 | tf_op jit(solution)/shard_map/all_to_all | solution.py:156
  24.9 0.0 copy-done
  24.9 1.5 %shard_map.38.intra_ref = f32[256,1024]{1,0:T(8,128)S(1)} custom-call(bf16[256,1024]{1,0:T(8,128)(2,1)S(1)} %copy-done, bf16[256,1024]{1,0:T(8,128)(2,1)S(1)} %get-tuple-element.12.k_ref, bf16[256,1024]{1,0:T(8,128)(2,1)S(1)} %get-tuple-element.13.v_ref), custom_call_target="tpu_custom_call" | custom-call | flops 268435456 | bytes 1572864 | tf_op jit(solution)/shard_map/pallas_call | solution.py:129
  26.4 2.7 %all-to-all-done.1 = bf16[16,32,128]{2,1,0:T(8,128)(2,1)S(1)} async-done(((bf16[16,32,128]{2,1,0:T(8,128)(2,1)}), bf16[16,32,128]{2,1,0:T(8,128)(2,1)S(1)}, u32[]{:S(2)}, u32[]{:S(2)}) %all-to-all-start.1) | async-done | bytes 131104 | tf_op jit(solution)/shard_map/all_to_all | solution.py:156
  29.1 1.5 %shard_map.41 = bf16[256,1024]{1,0:T(8,128)(2,1)} custom-call(bf16[256,1024]{1,0:T(8,128)(2,1)S(1)} %copy-done, f32[256,1024]{1,0:T(8,128)S(1)} %shard_map.38.intra_ref, bf16[512,128]{1,0:T(8,128)(2,1)S(1)} %bitcast.2), custom_call_target="tpu_custom_call" | custom-call | flops 134217728 | bytes 1703936 | tf_op jit(solution)/shard_map/pallas_call | solution.py:129
  (1 shorter events, 0.0 us)
Async XLA Ops:
  2.1 22.8 %copy-start = (bf16[256,1024]{1,0:T(8,128)(2,1)S(1)}, bf16[256,1024]{1,0:T(8,128)(2,1)}, u32[]{:S(2)}) copy-start(bf16[256,1024]{1,0:T(8,128)(2,1)} %q_ref.1) | copy-start | bytes 1572868
  15.6 1.2 %collective-permute-start = (f32[32,128]{1,0:T(8,128)S(1)}, f32[32,128]{1,0:T(8,128)S(1)}, u32[]{:S(2)}, u32[]{:S(2)}) collective-permute-start(f32[32,128]{1,0:T(8,128)S(1)} %shard_map.39), channel_id=1, source_target_pairs={{0,1},{1,0},{2,3},{3,2},{4,5},{5,4},{6,7},{7,6},{8,9},{9,8},{10,11... | collective-permute-start | bytes 49160 | tf_op jit(solution)/shard_map/ppermute | solution.py:154
  17.5 11.6 %all-to-all-start.1 = ((bf16[16,32,128]{2,1,0:T(8,128)(2,1)}), bf16[16,32,128]{2,1,0:T(8,128)(2,1)S(1)}, u32[]{:S(2)}, u32[]{:S(2)}) async-start(bf16[16,32,128]{2,1,0:T(8,128)(2,1)} %shard_map.40), calls=%async_computation.1 | async-start | bytes 262144 | tf_op jit(solution)/shard_map/all_to_all | solution.py:156

commit v8 on v6

--- a/solution.py
+++ b/solution.py
@@ -31,7 +31,9 @@
     return slice(p * HEAD_DIM, (p + 1) * HEAD_DIM)
 
 
-def states_kernel(k_hbm, v_hbm, out_ref, k_ref, v_ref, sums, arrived):
+def states_kernel(places, k_hbm, v_hbm, out_ref, k_ref, v_ref, sums, arrived):
+    share = out_ref.shape[0] // len(places)
+    moved = places != list(range(len(places)))
     rows = k_ref.shape[0] // CHUNKS
     copies = []
     for s in range(CHUNKS):
@@ -55,25 +57,21 @@
                 packed = sums[rows_of(p), :] + packed
             if s < CHUNKS - 1:
                 sums[rows_of(p), :] = packed
+            elif not moved:
+                out_ref[rows_of(p), :] = packed.astype(out_ref.dtype)
             else:
-                out_ref[rows_of(p), :] = packed.astype(out_ref.dtype)
+                for j in range(HEAD_DIM // share):
+                    place = places[p * HEAD_DIM // share + j] * share
+                    out_ref[place:place + share, :] = packed[j * share:(j + 1) * share].astype(out_ref.dtype)
 
 
-def scan_kernel(x_ref, out_ref):
+def scan_kernel(order, leads, x_ref, out_ref):
     parts = x_ref.shape[0]
     total = jnp.zeros(x_ref.shape[1:], F32)
     for i in range(parts):
-        out_ref[i] = total.astype(out_ref.dtype)
+        out_ref[leads[i]] = total.astype(out_ref.dtype)
         if i < parts - 1:
-            total = total + x_ref[i].astype(F32)
-
-
-def scan_rows_kernel(x_ref, out_ref):
-    parts = x_ref.shape[0]
-    row = lax.broadcasted_iota(jnp.int32, (parts, parts), 0)
-    col = lax.broadcasted_iota(jnp.int32, (parts, parts), 1)
-    below = jnp.where(col < row, 1.0, 0.0).astype(BF16)
-    out_ref[...] = jnp.dot(below, x_ref[...], preferred_element_type=F32).astype(out_ref.dtype)
+            total = total + x_ref[order[i]].astype(F32)
 
 
 def intra_kernel(q_ref, k_ref, v_ref, out_ref):
@@ -137,19 +135,28 @@
     return got[0] if single else got
 
 
-def per_device(parts, queries, keys, values):
+def led_by(parts, first):
+    order = list(range(parts))
+    order[0], order[first] = first, 0
+    return order
+
+
+def per_device(wide, parts, queries, keys, values):
     rows = queries.shape[0]
     state = (PAIRS * HEAD_DIM, LANES)
     share = state[0] // parts
+    first = led_by(parts, parts - 1)
+    second = led_by(parts, 3 * wide // 4 - 1) if share % 16 == 0 else first
+    places = [first[second[s]] for s in range(parts)]
     states, keys, values = call(
-        states_kernel, [(state, BF16), (keys.shape, keys.dtype), (values.shape, values.dtype)],
+        functools.partial(states_kernel, places), [(state, BF16), (keys.shape, keys.dtype), (values.shape, values.dtype)],
         keys, values, flops=2 * rows * LANES * LANES * PAIRS, source=pltpu.HBM,
         scratch=[pltpu.VMEM(state, F32), pltpu.SemaphoreType.DMA((2, CHUNKS))])
-    view = (parts, share, LANES) if share > 1 else (parts, LANES)
-    mine = lax.all_to_all(states.reshape(view), AXES, 0, 0, tiled=True)
+    view = (parts, share, LANES)
+    mine = lax.all_to_all(states.reshape(view), AXES, 0, 0, axis_index_groups=[first], tiled=True)
     mine, queries = lax.optimization_barrier((mine, queries))
-    before = call(scan_kernel if share > 1 else scan_rows_kernel, (view, BF16), mine)
-    prefix = lax.all_to_all(before, AXES, 0, 0, tiled=True).reshape(state)
+    before = call(functools.partial(scan_kernel, first, second), (view, BF16), mine)
+    prefix = lax.all_to_all(before, AXES, 0, 0, axis_index_groups=[second], tiled=True).reshape(state)
     intra = call(intra_kernel, (queries.shape, F32), queries, keys, values,
                  flops=4 * rows * rows * HEADS * HEAD_DIM)
     return call(attend_kernel, (queries.shape, BF16), queries, intra, prefix, result=pltpu.HBM,
@@ -161,7 +168,7 @@
     spec = P(AXES, None)
     parts = mesh.shape["chain"] * mesh.shape["wide"]
     return jax.shard_map(
-        functools.partial(per_device, parts),
+        functools.partial(per_device, mesh.shape["wide"], parts),
         mesh=mesh,
         in_specs=(spec, spec, spec),
         out_specs=spec,

time: 30.1 us -> 31.2 us (1.037)
  blocking collectives: 15 us -> 15.8 us
  waiting for transfers between devices: 6.41 us -> 6.82 us
    all_to_all x1, blocking collectives: 15 us -> 15.8 us  [per_device(): lax.all_to_all(states.reshape(view), AXES, 0, 0, axis_index_groups=[first...]
    all_to_all x1, waiting for transfers between devices: 6.41 us -> 6.82 us  [per_device(): lax.all_to_all(before, AXES, 0, 0, axis_index_groups=[second], tiled=True)]
where the time goes in v8:
time: 31.2 us; the launch traced here: 31 us
  blocking collectives  15.8 us (51%)
  waiting for transfers between devices  6.82 us (22%)
  Pallas kernels  5.79 us (19%)
  starting transfers between devices  2.58 us (8%)
    all_to_all x1, blocking collectives, per_device(): lax.all_to_all(states.reshape(view), AXES, 0, 0, axis_index_groups=[first...  15.8 us
    all_to_all x1, waiting for transfers between devices, per_device(): lax.all_to_all(before, AXES, 0, 0, axis_index_groups=[second], tiled=True)  6.82 us
    pallas_call x4, Pallas kernels, call(): pl.pallas_call(kernel, out_shape=[result(shape, dtype) for shape, dtype i...  5.79 us
    all_to_all x1, starting transfers between devices, per_device(): lax.all_to_all(before, AXES, 0, 0, axis_index_groups=[second], tiled=True)  2.58 us
  transfers between devices with their start and end apart: 1, of which 1 were waited for; matrix products, arithmetic and copies ran while one was open for 0% of the time, Pallas kernels for 5%

profile of v8, /device:TPU:0, one launch (start us, length us, event | category | flops | bytes accessed | tf_op | source)
XLA Modules:
  0.0 31.0 jit_solution(6192773640355028191)
XLA Ops:
  0.0 2.1 %shard_map.37 = (bf16[512,128]{1,0:T(8,128)(2,1)S(1)}, bf16[256,1024]{1,0:T(8,128)(2,1)S(1)}, bf16[256,1024]{1,0:T(8,128)(2,1)S(1)}) custom-call(bf16[256,1024]{1,0:T(8,128)(2,1)} %k_hbm.1, bf16[256,1024]{1,0:T(8,128)(2,1)} %v_hbm.1), custom_call_target="tpu_custom_call" | custom-call | flops 67108864 | bytes 1048576 | tf_op jit(solution)/shard_map/pallas_call | solution.py:126
  2.1 0.0 copy-start
  2.1 15.8 %all_to_all.10.x_ref = bf16[32,16,128]{2,1,0:T(8,128)(2,1)S(1)} all-to-all(bf16[32,16,128]{2,1,0:T(8,128)(2,1)S(1)} %bitcast.3), channel_id=1, replica_groups={{31,2,4,6,8,10,12,14,16,18,20,22,24,26,28,30,1,3,5,7,9,11,13,15,17,19,2..., dimensions={0} | all-to-all | bytes 262144 | tf_op jit(solution)/shard_map/all_to_all | solution.py:156
  17.9 0.7 %shard_map.39 = bf16[32,16,128]{2,1,0:T(8,128)(2,1)} custom-call(bf16[32,16,128]{2,1,0:T(8,128)(2,1)S(1)} %all_to_all.10.x_ref), custom_call_target="tpu_custom_call" | custom-call | bytes 131072 | tf_op jit(solution)/shard_map/pallas_call | solution.py:126
  18.6 2.6 %all-to-all-start.1 = ((bf16[32,16,128]{2,1,0:T(8,128)(2,1)}), bf16[32,16,128]{2,1,0:T(8,128)(2,1)S(1)}, u32[]{:S(2)}, u32[]{:S(2)}) async-start(bf16[32,16,128]{2,1,0:T(8,128)(2,1)} %shard_map.39), calls=%async_computation.1 | async-start | bytes 262144 | tf_op jit(solution)/shard_map/all_to_all | solution.py:159
  21.2 0.0 copy-done
  21.2 1.5 %shard_map.38.intra_ref = f32[256,1024]{1,0:T(8,128)S(1)} custom-call(bf16[256,1024]{1,0:T(8,128)(2,1)S(1)} %copy-done, bf16[256,1024]{1,0:T(8,128)(2,1)S(1)} %get-tuple-element.12.k_ref, bf16[256,1024]{1,0:T(8,128)(2,1)S(1)} %get-tuple-element.13.v_ref), custom_call_target="tpu_custom_call" | custom-call | flops 268435456 | bytes 1572864 | tf_op jit(solution)/shard_map/pallas_call | solution.py:126
  22.7 6.8 %all-to-all-done.1 = bf16[32,16,128]{2,1,0:T(8,128)(2,1)S(1)} async-done(((bf16[32,16,128]{2,1,0:T(8,128)(2,1)}), bf16[32,16,128]{2,1,0:T(8,128)(2,1)S(1)}, u32[]{:S(2)}, u32[]{:S(2)}) %all-to-all-start.1) | async-done | bytes 131104 | tf_op jit(solution)/shard_map/all_to_all | solution.py:159
  29.5 1.5 %shard_map.40 = bf16[256,1024]{1,0:T(8,128)(2,1)} custom-call(bf16[256,1024]{1,0:T(8,128)(2,1)S(1)} %copy-done, f32[256,1024]{1,0:T(8,128)S(1)} %shard_map.38.intra_ref, bf16[512,128]{1,0:T(8,128)(2,1)S(1)} %bitcast.2), custom_call_target="tpu_custom_call" | custom-call | flops 134217728 | bytes 1703936 | tf_op jit(solution)/shard_map/pallas_call | solution.py:126
Async XLA Ops:
  2.1 19.1 %copy-start = (bf16[256,1024]{1,0:T(8,128)(2,1)S(1)}, bf16[256,1024]{1,0:T(8,128)(2,1)}, u32[]{:S(2)}) copy-start(bf16[256,1024]{1,0:T(8,128)(2,1)} %q_ref.1) | copy-start | bytes 1572868
  18.6 10.9 %all-to-all-start.1 = ((bf16[32,16,128]{2,1,0:T(8,128)(2,1)}), bf16[32,16,128]{2,1,0:T(8,128)(2,1)S(1)}, u32[]{:S(2)}, u32[]{:S(2)}) async-start(bf16[32,16,128]{2,1,0:T(8,128)(2,1)} %shard_map.39), calls=%async_computation.1 | async-start | bytes 262144 | tf_op jit(solution)/shard_map/all_to_all | solution.py:159

commit v9 on v7

v9 whole, which is shorter than its diff:
```python
import functools

import jax
import jax.numpy as jnp
from jax import lax
from jax.experimental import pallas as pl
from jax.experimental.pallas import tpu as pltpu
from jax.sharding import PartitionSpec as P

HEADS = 16
HEAD_DIM = 64
PAIRS = HEADS // 2
LANES = 2 * HEAD_DIM
SLABS = 4
SLAB = 256
VMEM = pl.BlockSpec(memory_space=pltpu.VMEM)
BF16 = jnp.bfloat16
F32 = jnp.float32


def first_head(shape):
    return lax.broadcasted_iota(jnp.int32, shape, len(shape) - 1) < HEAD_DIM


def lanes_of(p):
    return slice(p * LANES, (p + 1) * LANES)


def rows_of(p):
    return slice(p * HEAD_DIM, (p + 1) * HEAD_DIM)


def states_kernel(k_hbm, v_hbm, *refs):
    *outs, k_ref, v_ref, states, arrived = refs
    copies = []
    for s in range(SLABS):
        lanes = slice(s * SLAB, (s + 1) * SLAB)
        copies.append([
            pltpu.make_async_copy(k_hbm.at[:, lanes], k_ref.at[:, lanes], arrived.at[0, s]),
            pltpu.make_async_copy(v_hbm.at[:, lanes], v_ref.at[:, lanes], arrived.at[1, s])])
        for copy in copies[-1]:
            copy.start()
    first = first_head((HEAD_DIM, LANES))
    share = states.shape[1]
    for p in range(PAIRS):
        if p * LANES % SLAB == 0:
            for copy in copies[p * LANES // SLAB]:
                copy.wait()
        both = lax.dot_general(
            k_ref[:, lanes_of(p)], v_ref[:, lanes_of(p)], (((0,), (0,)), ((), ())),
            preferred_element_type=jnp.float32)
        packed = jnp.where(first, both[:HEAD_DIM], both[HEAD_DIM:])
        row = p * HEAD_DIM
        states[row // share, row % share:row % share + HEAD_DIM, :] = packed
    me = lax.axis_index("inner")
    for d, out in enumerate(outs):
        out[...] = states[me ^ d].astype(out.dtype)


def totals_kernel(*refs):
    *parts, own, out_ref, sent_ref = refs
    total = own[...]
    for part in parts:
        total = total + part[...].astype(F32)
    out_ref[...] = total
    sent_ref[...] = total.astype(sent_ref.dtype)


def planes_kernel(*refs):
    *totals, own, below_ref, whole_ref = refs
    plane = lax.axis_index("outer")
    whole = own[...]
    below = jnp.zeros_like(whole)
    for e, there in zip(reversed(range(1, len(totals) + 1)), totals):
        there = there[...].astype(F32)
        below = below + jnp.where((plane ^ e) < plane, there, 0.0)
        whole = whole + there
    below_ref[...] = below
    whole_ref[...] = whole


def prefix_kernel(inner, *refs):
    *ins, order = refs
    parts, below, groups, outs = ins[:inner], ins[inner], ins[inner + 1:-inner], ins[-inner:]
    me, chain = lax.axis_index("inner"), lax.axis_index("chain")
    for d, part in zip(reversed(range(inner)), parts):
        order[me ^ d] = part[...].astype(F32)
    total = below[...]
    for d, group in enumerate(groups, 1):
        total = total + jnp.where((chain ^ d) < chain, group[...], 0.0)
    for i in range(inner):
        here = order[i]
        order[i] = total
        total = total + here
    for d, out in enumerate(outs):
        out[...] = order[me ^ d].astype(out.dtype)


def intra_kernel(q_ref, k_ref, v_ref, out_ref):
    rows = q_ref.shape[0]
    causal = (lax.broadcasted_iota(jnp.int32, (rows, rows), 0)
              >= lax.broadcasted_iota(jnp.int32, (rows, rows), 1))
    first = first_head((rows, LANES))
    zero = jnp.zeros((), BF16)
    for p in range(PAIRS):
        q, k, v = q_ref[:, lanes_of(p)], k_ref[:, lanes_of(p)], v_ref[:, lanes_of(p)]
        intra = []
        for mine in (first, ~first):
            scores = lax.dot_general(
                jnp.where(mine, q, zero), k, (((1,), (1,)), ((), ())),
                preferred_element_type=F32)
            scores = jnp.where(causal, scores, 0.0).astype(BF16)
            intra.append(jnp.dot(scores, v, preferred_element_type=F32))
        out_ref[:, lanes_of(p)] = jnp.where(first, intra[0], intra[1])


def attend_kernel(inner, q_ref, intra_ref, *refs):
    *parts, out_hbm, out_ref, prefix_ref, sent = refs
    me = lax.axis_index("inner")
    for d, part in zip(reversed(range(inner)), parts):
        prefix_ref[me ^ d] = part[...]
    share = prefix_ref.shape[1]
    heads = SLAB // HEAD_DIM
    blocks = ([lax.broadcasted_iota(jnp.int32, (SLAB, SLAB), d) // HEAD_DIM for d in range(2)])
    same = blocks[0] == blocks[1]
    ones = jnp.where(same, 1.0, 0.0).astype(BF16)
    zero = jnp.zeros((), BF16)
    copies = []
    for s in range(HEADS // heads):
        lanes = slice(s * SLAB, (s + 1) * SLAB)
        rows = []
        for p in range(s * heads // 2, (s + 1) * heads // 2):
            row = p * HEAD_DIM
            pair = prefix_ref[row // share, row % share:row % share + HEAD_DIM, :]
            rows += [jnp.concatenate([pair] * (SLAB // LANES), axis=1)] * 2
        prefix = jnp.where(same, jnp.concatenate(rows, axis=0), zero)
        inter = jnp.dot(q_ref[:, lanes], prefix, preferred_element_type=F32)
        total = intra_ref[:, lanes] + inter
        square = total * total
        high = square.astype(BF16)
        low = (square - high.astype(F32)).astype(BF16)
        sums = (jnp.dot(high, ones, preferred_element_type=F32)
                + jnp.dot(low, ones, preferred_element_type=F32))
        out_ref[:, lanes] = (total * lax.rsqrt(sums * (1.0 / HEAD_DIM) + 1e-6)).astype(out_ref.dtype)
        copies.append(pltpu.make_async_copy(out_ref.at[:, lanes], out_hbm.at[:, lanes], sent.at[s]))
        copies[-1].start()
    for copy in copies:
        copy.wait()


def call(kernel, outs, *args, flops=0, scratch=(), source=pltpu.VMEM, result=pltpu.VMEM):
    moved = sum(a.size * a.dtype.itemsize for a in args)
    single = not isinstance(outs, list)
    outs = [outs] if single else outs
    got = pl.pallas_call(
        kernel,
        out_shape=[result(shape, dtype) for shape, dtype in outs],
        in_specs=[pl.BlockSpec(memory_space=source)] * len(args),
        out_specs=[pl.BlockSpec(memory_space=result)] * len(outs),
        scratch_shapes=scratch,
        cost_estimate=pl.CostEstimate(flops=flops, bytes_accessed=moved, transcendentals=0),
        compiler_params=pltpu.CompilerParams(vmem_limit_bytes=16 * 1024 * 1024),
    )(*[pltpu.with_memory_space_constraint(a, source) for a in args])
    return got[0] if single else got


def swapped(arrays, axis, own):
    size = len(arrays)
    return [lax.ppermute(arrays[d], axis, [(i, i ^ d) for i in range(size)]) for d in reversed(range(1, size))] + [own]


def per_device(chains, planes, inner, queries, keys, values):
    rows = queries.shape[0]
    share = (PAIRS * HEAD_DIM // inner, LANES)
    own, *states, keys, values = call(
        states_kernel,
        [(share, F32)] + [(share, BF16)] * (inner - 1) + [(keys.shape, keys.dtype), (values.shape, values.dtype)],
        keys, values, flops=2 * rows * LANES * LANES * PAIRS, source=pltpu.HBM,
        scratch=[pltpu.VMEM((inner,) + share, F32), pltpu.SemaphoreType.DMA((2, SLABS))])
    mine = swapped([own] + states, "inner", own)
    total, sent = call(totals_kernel, [(share, F32), (share, BF16)], *mine)
    totals = swapped([sent] * planes, "outer", total)
    below, whole = call(planes_kernel, [(share, F32)] * 2, *totals)
    groups = [lax.ppermute(whole, "chain", [(c, c ^ d) for c in range(chains)]) for d in range(1, chains)]
    before = call(functools.partial(prefix_kernel, inner), [(share, BF16)] * inner, *mine, below, *groups,
                  scratch=[pltpu.VMEM((inner,) + share, F32)])
    prefix = swapped(before, "inner", before[0])
    intra = call(intra_kernel, (queries.shape, F32), queries, keys, values,
                 flops=4 * rows * rows * HEADS * HEAD_DIM)
    return call(functools.partial(attend_kernel, inner), (queries.shape, BF16), queries, intra, *prefix,
                result=pltpu.HBM, flops=2 * rows * SLAB * HEADS * HEAD_DIM,
                scratch=[pltpu.VMEM(queries.shape, BF16), pltpu.VMEM((inner,) + share, BF16),
                         pltpu.SemaphoreType.DMA((HEADS * HEAD_DIM // SLAB,))])


def solution(mesh):
    wide, chains = mesh.devices.shape
    inner = 4
    planes = wide // inner
    finer = jax.sharding.Mesh(mesh.devices.reshape(planes, inner, chains), ("outer", "inner", "chain"))
    spec = P(("chain", "outer", "inner"), None)
    return jax.shard_map(
        functools.partial(per_device, chains, planes, inner),
        mesh=finer,
        in_specs=(spec, spec, spec),
        out_specs=spec,
        check_vma=False,
    )
```

time: 30.9 us -> 28 us (0.906)
  blocking collectives: 13.5 us -> 0 us
  waiting for transfers between devices: 3.89 us -> 9.96 us
  starting transfers between devices: 7.47 us -> 12.7 us
  Pallas kernels: 5.8 us -> 5.13 us
    all_to_all x1 -> x0, blocking collectives: 13.5 us -> none  [per_device(): lax.all_to_all(states.reshape(view), 'wide', 0, 0, axis_index_groups=orde...]
    ppermute x1 -> x10, starting transfers between devices: 0.07 us -> 12.7 us  [the longest x9 12.6 us: swapped(): lax.ppermute(arrays[d], axis, [(i, i ^ d) for i in range(size)])]
    ppermute x1 -> x10, waiting for transfers between devices: 1.17 us -> 9.96 us  [the longest x9 8.72 us: swapped(): lax.ppermute(arrays[d], axis, [(i, i ^ d) for i in range(size)])]
    all_to_all x1 -> x0, starting transfers between devices: 7.4 us -> none  [per_device(): lax.all_to_all(before, 'wide', 0, 0, axis_index_groups=order, tiled=True)]
    all_to_all x1 -> x0, waiting for transfers between devices: 2.72 us -> none  [per_device(): lax.all_to_all(before, 'wide', 0, 0, axis_index_groups=order, tiled=True)]
    pallas_call x5 -> x6, Pallas kernels: 5.8 us -> 5.13 us  [call(): pl.pallas_call(kernel, out_shape=[result(shape, dtype) for shape, dtype i...]
  transfers between devices with their start and end apart: 2 -> 10, of which waited for: 2 -> 8; matrix products, arithmetic and copies ran while one was open for 0% -> 0% of each run, Pallas kernels for 5% -> 5%
where the time goes in v9:
time: 28 us; the launch traced here: 27.9 us
  starting transfers between devices  12.7 us (45%)
  waiting for transfers between devices  9.96 us (36%)
  Pallas kernels  5.13 us (18%)
    ppermute x9, starting transfers between devices, swapped(): lax.ppermute(arrays[d], axis, [(i, i ^ d) for i in range(size)])  12.6 us
    ppermute x9, waiting for transfers between devices, swapped(): lax.ppermute(arrays[d], axis, [(i, i ^ d) for i in range(size)])  8.72 us
    pallas_call x6, Pallas kernels, call(): pl.pallas_call(kernel, out_shape=[result(shape, dtype) for shape, dtype i...  5.13 us
    ppermute x1, waiting for transfers between devices, per_device(): lax.ppermute(whole, 'chain', [(c, c ^ d) for c in range(chains)])  1.24 us
  transfers between devices with their start and end apart: 10, of which 8 were waited for; matrix products, arithmetic and copies ran while one was open for 0% of the time, Pallas kernels for 5%

profile of v9, /device:TPU:0, one launch (start us, length us, event | category | flops | bytes accessed | tf_op | source)
XLA Modules:
  0.0 27.9 jit_solution(4713957303854516676)
XLA Ops:
  0.0 2.0 %shard_map.37 = (f32[128,128]{1,0:T(8,128)S(1)}, bf16[128,128]{1,0:T(8,128)(2,1)S(1)}, bf16[128,128]{1,0:T(8,128)(2,1)S(1)}, bf16[128,128]{1,0:T(8,128)(2,1)S(1)...) custom-call(bf16[256,1024]{1,0:T(8,128)(2,1)} %k_hbm.1, bf16[256,1024]{1,0:T(8,128)(2,1)} %v_hbm.1), custom_call_target="tpu_custom_call" | custom-call | flops 67108864 | bytes 1048576 | tf_op jit(solution)/shard_map/pallas_call | solution.py:155
  2.0 0.0 copy-start
  2.0 4.0 %collective-permute-start = (bf16[128,128]{1,0:T(8,128)(2,1)S(1)}, bf16[128,128]{1,0:T(8,128)(2,1)S(1)}, u32[]{:S(2)}, u32[]{:S(2)}) collective-permute-start(bf16[128,128]{1,0:T(8,128)(2,1)S(1)} %get-tuple-element.21), channel_id=1, source_target_pairs={{0,6},{2,4},{4,2},{6,0},{1,7},{3,5},{5,3},{7,1},{8,14},{10,12},{12... | collective-permute-start | bytes 98312 | tf_op jit(solution)/shard_map/ppermute | solution.py:169
  6.0 0.5 %collective-permute-start.1 = (bf16[128,128]{1,0:T(8,128)(2,1)S(1)}, bf16[128,128]{1,0:T(8,128)(2,1)S(1)}, u32[]{:S(2)}, u32[]{:S(2)}) collective-permute-start(bf16[128,128]{1,0:T(8,128)(2,1)S(1)} %get-tuple-element.22), channel_id=1, source_target_pairs={{0,4},{2,6},{4,0},{6,2},{1,5},{3,7},{5,1},{7,3},{8,12},{10,14},{12... | collective-permute-start | bytes 98312 | tf_op jit(solution)/shard_map/ppermute | solution.py:169
  6.5 0.1 collective-permute-start.2
  6.6 1.3 %collective-permute-done.refs_0_ = bf16[128,128]{1,0:T(8,128)(2,1)S(1)} collective-permute-done((bf16[128,128]{1,0:T(8,128)(2,1)S(1)}, bf16[128,128]{1,0:T(8,128)(2,1)S(1)}, u32[]{:S(2)}, u32[]{:S(2)}) %collective-permute-start) | collective-permute-done | bytes 32800 | tf_op jit(solution)/shard_map/ppermute | solution.py:169
  7.9 2.0 %collective-permute-done.1.refs_1_ = bf16[128,128]{1,0:T(8,128)(2,1)S(1)} collective-permute-done((bf16[128,128]{1,0:T(8,128)(2,1)S(1)}, bf16[128,128]{1,0:T(8,128)(2,1)S(1)}, u32[]{:S(2)}, u32[]{:S(2)}) %collective-permute-start.1) | collective-permute-done | bytes 32800 | tf_op jit(solution)/shard_map/ppermute | solution.py:169
  9.9 0.5 %collective-permute-done.2.refs_2_ = bf16[128,128]{1,0:T(8,128)(2,1)S(1)} collective-permute-done((bf16[128,128]{1,0:T(8,128)(2,1)S(1)}, bf16[128,128]{1,0:T(8,128)(2,1)S(1)}, u32[]{:S(2)}, u32[]{:S(2)}) %collective-permute-start.2) | collective-permute-done | bytes 32800 | tf_op jit(solution)/shard_map/ppermute | solution.py:169
  10.4 3.7 %collective-permute-start.3 = (bf16[128,128]{1,0:T(8,128)(2,1)S(1)}, bf16[128,128]{1,0:T(8,128)(2,1)S(1)}, u32[]{:S(2)}, u32[]{:S(2)}) collective-permute-start(bf16[128,128]{1,0:T(8,128)(2,1)S(1)} %get-tuple-element.25), channel_id=1, source_target_pairs={{0,24},{8,16},{16,8},{24,0},{1,25},{9,17},{17,9},{25,1},{2,26},{10... | collective-permute-start | bytes 98312 | tf_op jit(solution)/shard_map/ppermute | solution.py:169
  14.1 0.0 collective-permute-start.4
  14.1 0.8 %collective-permute-start.5 = (bf16[128,128]{1,0:T(8,128)(2,1)S(1)}, bf16[128,128]{1,0:T(8,128)(2,1)S(1)}, u32[]{:S(2)}, u32[]{:S(2)}) collective-permute-start(bf16[128,128]{1,0:T(8,128)(2,1)S(1)} %get-tuple-element.25), channel_id=1, source_target_pairs={{0,8},{8,0},{16,24},{24,16},{1,9},{9,1},{17,25},{25,17},{2,10},{10... | collective-permute-start | bytes 98312 | tf_op jit(solution)/shard_map/ppermute | solution.py:169
  14.9 1.3 %collective-permute-done.3.refs_0_ = bf16[128,128]{1,0:T(8,128)(2,1)S(1)} collective-permute-done((bf16[128,128]{1,0:T(8,128)(2,1)S(1)}, bf16[128,128]{1,0:T(8,128)(2,1)S(1)}, u32[]{:S(2)}, u32[]{:S(2)}) %collective-permute-start.3) | collective-permute-done | bytes 32800 | tf_op jit(solution)/shard_map/ppermute | solution.py:169
  16.2 2.7 %collective-permute-done.4.refs_1_ = bf16[128,128]{1,0:T(8,128)(2,1)S(1)} collective-permute-done((bf16[128,128]{1,0:T(8,128)(2,1)S(1)}, bf16[128,128]{1,0:T(8,128)(2,1)S(1)}, u32[]{:S(2)}, u32[]{:S(2)}) %collective-permute-start.4) | collective-permute-done | bytes 32800 | tf_op jit(solution)/shard_map/ppermute | solution.py:169
  18.9 0.0 collective-permute-done.5.refs_2_
  18.9 0.1 collective-permute-start.6
  19.0 1.2 %collective-permute-done.6.refs_5_ = f32[128,128]{1,0:T(8,128)S(1)} collective-permute-done((f32[128,128]{1,0:T(8,128)S(1)}, f32[128,128]{1,0:T(8,128)S(1)}, u32[]{:S(2)}, u32[]{:S(2)}) %collective-permute-start.6) | collective-permute-done | bytes 65568 | tf_op jit(solution)/shard_map/ppermute | solution.py:184
  20.3 0.1 shard_map.41
  20.3 1.6 %collective-permute-start.7 = (bf16[128,128]{1,0:T(8,128)(2,1)S(1)}, bf16[128,128]{1,0:T(8,128)(2,1)S(1)}, u32[]{:S(2)}, u32[]{:S(2)}) collective-permute-start(bf16[128,128]{1,0:T(8,128)(2,1)S(1)} %get-tuple-element.29), channel_id=1, source_target_pairs={{0,6},{2,4},{4,2},{6,0},{1,7},{3,5},{5,3},{7,1},{8,14},{10,12},{12... | collective-permute-start | bytes 98312 | tf_op jit(solution)/shard_map/ppermute | solution.py:169
  21.9 0.5 %collective-permute-start.8 = (bf16[128,128]{1,0:T(8,128)(2,1)S(1)}, bf16[128,128]{1,0:T(8,128)(2,1)S(1)}, u32[]{:S(2)}, u32[]{:S(2)}) collective-permute-start(bf16[128,128]{1,0:T(8,128)(2,1)S(1)} %get-tuple-element.30), channel_id=1, source_target_pairs={{0,4},{2,6},{4,0},{6,2},{1,5},{3,7},{5,1},{7,3},{8,12},{10,14},{12... | collective-permute-start | bytes 98312 | tf_op jit(solution)/shard_map/ppermute | solution.py:169
  22.4 1.5 %collective-permute-start.9 = (bf16[128,128]{1,0:T(8,128)(2,1)S(1)}, bf16[128,128]{1,0:T(8,128)(2,1)S(1)}, u32[]{:S(2)}, u32[]{:S(2)}) collective-permute-start(bf16[128,128]{1,0:T(8,128)(2,1)S(1)} %get-tuple-element.31), channel_id=1, source_target_pairs={{0,2},{2,0},{4,6},{6,4},{1,3},{3,1},{5,7},{7,5},{8,10},{10,8},{12,... | collective-permute-start | bytes 98312 | tf_op jit(solution)/shard_map/ppermute | solution.py:169
  23.9 0.0 copy-done
  23.9 1.5 %shard_map.38.intra_ref = f32[256,1024]{1,0:T(8,128)S(1)} custom-call(bf16[256,1024]{1,0:T(8,128)(2,1)S(1)} %copy-done, bf16[256,1024]{1,0:T(8,128)(2,1)S(1)} %get-tuple-element.19.k_ref, bf16[256,1024]{1,0:T(8,128)(2,1)S(1)} %get-tuple-element.20.v_ref), custom_call_target="tpu_custom_call" | custom-call | flops 268435456 | bytes 1572864 | tf_op jit(solution)/shard_map/pallas_call | solution.py:155
  25.4 0.0 collective-permute-done.7.refs_0_
  25.4 0.4 %collective-permute-done.8.refs_1_ = bf16[128,128]{1,0:T(8,128)(2,1)S(1)} collective-permute-done((bf16[128,128]{1,0:T(8,128)(2,1)S(1)}, bf16[128,128]{1,0:T(8,128)(2,1)S(1)}, u32[]{:S(2)}, u32[]{:S(2)}) %collective-permute-start.8) | collective-permute-done | bytes 32800 | tf_op jit(solution)/shard_map/ppermute | solution.py:169
  25.8 0.5 %collective-permute-done.9.refs_2_ = bf16[128,128]{1,0:T(8,128)(2,1)S(1)} collective-permute-done((bf16[128,128]{1,0:T(8,128)(2,1)S(1)}, bf16[128,128]{1,0:T(8,128)(2,1)S(1)}, u32[]{:S(2)}, u32[]{:S(2)}) %collective-permute-start.9) | collective-permute-done | bytes 32800 | tf_op jit(solution)/shard_map/ppermute | solution.py:169
  26.3 1.5 %shard_map.42 = bf16[256,1024]{1,0:T(8,128)(2,1)} custom-call(bf16[256,1024]{1,0:T(8,128)(2,1)S(1)} %copy-done, f32[256,1024]{1,0:T(8,128)S(1)} %shard_map.38.intra_ref, bf16[128,128]{1,0:T(8,128)(2,1)S(1)} %collective-permute-done.7.refs_0_, bf16[128,128]{1,0:T(8,128)(2,1)S(1)} %collective-permute-done.8.refs_1_, ...), custom_call_target="tpu_custom_call" | custom-call | flops 134217728 | bytes 1703936 | tf_op jit(solution)/shard_map/pallas_call | solution.py:155
  (2 shorter events, 0.1 us)
Async XLA Ops:
  2.0 21.9 %copy-start = (bf16[256,1024]{1,0:T(8,128)(2,1)S(1)}, bf16[256,1024]{1,0:T(8,128)(2,1)}, u32[]{:S(2)}) copy-start(bf16[256,1024]{1,0:T(8,128)(2,1)} %q_ref.3) | copy-start | bytes 1572868
  2.0 5.9 %collective-permute-start = (bf16[128,128]{1,0:T(8,128)(2,1)S(1)}, bf16[128,128]{1,0:T(8,128)(2,1)S(1)}, u32[]{:S(2)}, u32[]{:S(2)}) collective-permute-start(bf16[128,128]{1,0:T(8,128)(2,1)S(1)} %get-tuple-element.21), channel_id=1, source_target_pairs={{0,6},{2,4},{4,2},{6,0},{1,7},{3,5},{5,3},{7,1},{8,14},{10,12},{12... | collective-permute-start | bytes 98312 | tf_op jit(solution)/shard_map/ppermute | solution.py:169
  6.0 3.9 %collective-permute-start.1 = (bf16[128,128]{1,0:T(8,128)(2,1)S(1)}, bf16[128,128]{1,0:T(8,128)(2,1)S(1)}, u32[]{:S(2)}, u32[]{:S(2)}) collective-permute-start(bf16[128,128]{1,0:T(8,128)(2,1)S(1)} %get-tuple-element.22), channel_id=1, source_target_pairs={{0,4},{2,6},{4,0},{6,2},{1,5},{3,7},{5,1},{7,3},{8,12},{10,14},{12... | collective-permute-start | bytes 98312 | tf_op jit(solution)/shard_map/ppermute | solution.py:169
  6.5 3.9 %collective-permute-start.2 = (bf16[128,128]{1,0:T(8,128)(2,1)S(1)}, bf16[128,128]{1,0:T(8,128)(2,1)S(1)}, u32[]{:S(2)}, u32[]{:S(2)}) collective-permute-start(bf16[128,128]{1,0:T(8,128)(2,1)S(1)} %get-tuple-element.23), channel_id=1, source_target_pairs={{0,2},{2,0},{4,6},{6,4},{1,3},{3,1},{5,7},{7,5},{8,10},{10,8},{12,... | collective-permute-start | bytes 98312 | tf_op jit(solution)/shard_map/ppermute | solution.py:169
  10.4 5.8 %collective-permute-start.3 = (bf16[128,128]{1,0:T(8,128)(2,1)S(1)}, bf16[128,128]{1,0:T(8,128)(2,1)S(1)}, u32[]{:S(2)}, u32[]{:S(2)}) collective-permute-start(bf16[128,128]{1,0:T(8,128)(2,1)S(1)} %get-tuple-element.25), channel_id=1, source_target_pairs={{0,24},{8,16},{16,8},{24,0},{1,25},{9,17},{17,9},{25,1},{2,26},{10... | collective-permute-start | bytes 98312 | tf_op jit(solution)/shard_map/ppermute | solution.py:169
  14.1 4.8 %collective-permute-start.4 = (bf16[128,128]{1,0:T(8,128)(2,1)S(1)}, bf16[128,128]{1,0:T(8,128)(2,1)S(1)}, u32[]{:S(2)}, u32[]{:S(2)}) collective-permute-start(bf16[128,128]{1,0:T(8,128)(2,1)S(1)} %get-tuple-element.25), channel_id=1, source_target_pairs={{0,16},{8,24},{16,0},{24,8},{1,17},{9,25},{17,1},{25,9},{2,18},{10... | collective-permute-start | bytes 98312 | tf_op jit(solution)/shard_map/ppermute | solution.py:169
  14.1 4.8 %collective-permute-start.5 = (bf16[128,128]{1,0:T(8,128)(2,1)S(1)}, bf16[128,128]{1,0:T(8,128)(2,1)S(1)}, u32[]{:S(2)}, u32[]{:S(2)}) collective-permute-start(bf16[128,128]{1,0:T(8,128)(2,1)S(1)} %get-tuple-element.25), channel_id=1, source_target_pairs={{0,8},{8,0},{16,24},{24,16},{1,9},{9,1},{17,25},{25,17},{2,10},{10... | collective-permute-start | bytes 98312 | tf_op jit(solution)/shard_map/ppermute | solution.py:169
  18.9 1.3 %collective-permute-start.6 = (f32[128,128]{1,0:T(8,128)S(1)}, f32[128,128]{1,0:T(8,128)S(1)}, u32[]{:S(2)}, u32[]{:S(2)}) collective-permute-start(f32[128,128]{1,0:T(8,128)S(1)} %get-tuple-element.28), channel_id=1, source_target_pairs={{0,1},{1,0},{2,3},{3,2},{4,5},{5,4},{6,7},{7,6},{8,9},{9,8},{10,11... | collective-permute-start | bytes 196616 | tf_op jit(solution)/shard_map/ppermute | solution.py:184
  20.3 5.0 %collective-permute-start.7 = (bf16[128,128]{1,0:T(8,128)(2,1)S(1)}, bf16[128,128]{1,0:T(8,128)(2,1)S(1)}, u32[]{:S(2)}, u32[]{:S(2)}) collective-permute-start(bf16[128,128]{1,0:T(8,128)(2,1)S(1)} %get-tuple-element.29), channel_id=1, source_target_pairs={{0,6},{2,4},{4,2},{6,0},{1,7},{3,5},{5,3},{7,1},{8,14},{10,12},{12... | collective-permute-start | bytes 98312 | tf_op jit(solution)/shard_map/ppermute | solution.py:169
  21.9 3.9 %collective-permute-start.8 = (bf16[128,128]{1,0:T(8,128)(2,1)S(1)}, bf16[128,128]{1,0:T(8,128)(2,1)S(1)}, u32[]{:S(2)}, u32[]{:S(2)}) collective-permute-start(bf16[128,128]{1,0:T(8,128)(2,1)S(1)} %get-tuple-element.30), channel_id=1, source_target_pairs={{0,4},{2,6},{4,0},{6,2},{1,5},{3,7},{5,1},{7,3},{8,12},{10,14},{12... | collective-permute-start | bytes 98312 | tf_op jit(solution)/shard_map/ppermute | solution.py:169
  22.4 3.9 %collective-permute-start.9 = (bf16[128,128]{1,0:T(8,128)(2,1)S(1)}, bf16[128,128]{1,0:T(8,128)(2,1)S(1)}, u32[]{:S(2)}, u32[]{:S(2)}) collective-permute-start(bf16[128,128]{1,0:T(8,128)(2,1)S(1)} %get-tuple-element.31), channel_id=1, source_target_pairs={{0,2},{2,0},{4,6},{6,4},{1,3},{3,1},{5,7},{7,5},{8,10},{10,8},{12,... | collective-permute-start | bytes 98312 | tf_op jit(solution)/shard_map/ppermute | solution.py:169

commit v10 on v9

--- a/solution.py
+++ b/solution.py
@@ -30,8 +30,7 @@
     return slice(p * HEAD_DIM, (p + 1) * HEAD_DIM)
 
 
-def states_kernel(k_hbm, v_hbm, *refs):
-    *outs, k_ref, v_ref, states, arrived = refs
+def states_kernel(k_hbm, v_hbm, out_ref, k_ref, v_ref, arrived):
     copies = []
     for s in range(SLABS):
         lanes = slice(s * SLAB, (s + 1) * SLAB)
@@ -41,59 +40,65 @@
         for copy in copies[-1]:
             copy.start()
     first = first_head((HEAD_DIM, LANES))
-    share = states.shape[1]
+    share = out_ref.shape[1]
     for p in range(PAIRS):
         if p * LANES % SLAB == 0:
             for copy in copies[p * LANES // SLAB]:
                 copy.wait()
         both = lax.dot_general(
             k_ref[:, lanes_of(p)], v_ref[:, lanes_of(p)], (((0,), (0,)), ((), ())),
-            preferred_element_type=jnp.float32)
+            preferred_element_type=F32)
         packed = jnp.where(first, both[:HEAD_DIM], both[HEAD_DIM:])
         row = p * HEAD_DIM
-        states[row // share, row % share:row % share + HEAD_DIM, :] = packed
-    me = lax.axis_index("inner")
+        out_ref[row // share, row % share:row % share + HEAD_DIM, :] = packed.astype(out_ref.dtype)
+
+
+def shares_kernel(chains, *refs):
+    states, outs = refs[:chains], refs[chains:]
+    me, chain = lax.axis_index("inner"), lax.axis_index("chain")
     for d, out in enumerate(outs):
-        out[...] = states[me ^ d].astype(out.dtype)
+        for e, state in enumerate(states):
+            out[chain ^ e] = state[me ^ d]
 
 
 def totals_kernel(*refs):
-    *parts, own, out_ref, sent_ref = refs
-    total = own[...]
-    for part in parts:
-        total = total + part[...].astype(F32)
-    out_ref[...] = total
-    sent_ref[...] = total.astype(sent_ref.dtype)
-
-
-def planes_kernel(*refs):
-    *totals, own, below_ref, whole_ref = refs
-    plane = lax.axis_index("outer")
-    whole = own[...]
-    below = jnp.zeros_like(whole)
-    for e, there in zip(reversed(range(1, len(totals) + 1)), totals):
-        there = there[...].astype(F32)
-        below = below + jnp.where((plane ^ e) < plane, there, 0.0)
-        whole = whole + there
-    below_ref[...] = below
-    whole_ref[...] = whole
-
-
-def prefix_kernel(inner, *refs):
+    *parts, out_ref, sent_ref = refs
+    for c in range(out_ref.shape[0]):
+        total = parts[0][c].astype(F32)
+        for part in parts[1:]:
+            total = total + part[c].astype(F32)
+        out_ref[c] = total
+        sent_ref[c] = total.astype(sent_ref.dtype)
+
+
+def prefix_kernel(inner, planes, *refs):
     *ins, order = refs
-    parts, below, groups, outs = ins[:inner], ins[inner], ins[inner + 1:-inner], ins[-inner:]
+    parts, totals, outs = ins[:inner], ins[inner:inner + planes], ins[inner + planes:]
+    me, plane = lax.axis_index("inner"), lax.axis_index("outer")
+    groups = jnp.zeros(order.shape[1:], F32)
+    for c in range(outs[0].shape[0]):
+        for d, part in zip(reversed(range(inner)), parts):
+            order[me ^ d] = part[c].astype(F32)
+        total = groups
+        for e, there in zip(reversed(range(planes)), totals):
+            there = there[c].astype(F32)
+            groups = groups + there
+            if e > 0:
+                total = total + jnp.where((plane ^ e) < plane, there, 0.0)
+        for i in range(inner):
+            here = order[i]
+            order[i] = total
+            total = total + here
+        for d, out in enumerate(outs):
+            out[c] = order[me ^ d].astype(out.dtype)
+
+
+def deal_kernel(inner, *refs):
+    parts, outs = refs[:inner], refs[inner:]
     me, chain = lax.axis_index("inner"), lax.axis_index("chain")
     for d, part in zip(reversed(range(inner)), parts):
-        order[me ^ d] = part[...].astype(F32)
-    total = below[...]
-    for d, group in enumerate(groups, 1):
-        total = total + jnp.where((chain ^ d) < chain, group[...], 0.0)
-    for i in range(inner):
-        here = order[i]
-        order[i] = total
-        total = total + here
-    for d, out in enumerate(outs):
-        out[...] = order[me ^ d].astype(out.dtype)
+        for e, out in enumerate(outs):
+            out[me ^ d] = part[chain ^ e]
 
 
 def intra_kernel(q_ref, k_ref, v_ref, out_ref):
@@ -114,11 +119,14 @@
         out_ref[:, lanes_of(p)] = jnp.where(first, intra[0], intra[1])
 
 
-def attend_kernel(inner, q_ref, intra_ref, *refs):
-    *parts, out_hbm, out_ref, prefix_ref, sent = refs
-    me = lax.axis_index("inner")
-    for d, part in zip(reversed(range(inner)), parts):
-        prefix_ref[me ^ d] = part[...]
+def attend_kernel(chains, q_ref, intra_ref, *refs):
+    *dealt, out_hbm, out_ref, prefix_ref, sent = refs
+    away = lax.axis_index("chain") ^ (chains - 1)
+    for i in range(prefix_ref.shape[0]):
+        prefix = dealt[0][i]
+        for e in range(1, chains):
+            prefix = jnp.where(away == e, dealt[e][i], prefix)
+        prefix_ref[i] = prefix
     share = prefix_ref.shape[1]
     heads = SLAB // HEAD_DIM
     blocks = ([lax.broadcasted_iota(jnp.int32, (SLAB, SLAB), d) // HEAD_DIM for d in range(2)])
@@ -164,32 +172,44 @@
     return got[0] if single else got
 
 
-def swapped(arrays, axis, own):
+def swapped(arrays, axis, chains):
     size = len(arrays)
-    return [lax.ppermute(arrays[d], axis, [(i, i ^ d) for i in range(size)]) for d in reversed(range(1, size))] + [own]
+    got = []
+    for d in reversed(range(1, size)):
+        pairs = [(i * chains + c, (i ^ d if c == chains - 1 else i) * chains + c) for i in range(size) for c in range(chains)]
+        got.append(lax.ppermute(arrays[d], (axis, "chain"), pairs))
+    return got + [arrays[0]]
+
+
+def across(x, chains, e):
+    return lax.ppermute(x, "chain", [(c, c ^ e) for c in range(chains)])
 
 
 def per_device(chains, planes, inner, queries, keys, values):
     rows = queries.shape[0]
     share = (PAIRS * HEAD_DIM // inner, LANES)
-    own, *states, keys, values = call(
-        states_kernel,
-        [(share, F32)] + [(share, BF16)] * (inner - 1) + [(keys.shape, keys.dtype), (values.shape, values.dtype)],
+    whole = ((inner,) + share, BF16)
+    both = ((chains,) + share, BF16)
+    states, keys, values = call(
+        states_kernel, [whole, (keys.shape, keys.dtype), (values.shape, values.dtype)],
         keys, values, flops=2 * rows * LANES * LANES * PAIRS, source=pltpu.HBM,
-        scratch=[pltpu.VMEM((inner,) + share, F32), pltpu.SemaphoreType.DMA((2, SLABS))])
-    mine = swapped([own] + states, "inner", own)
-    total, sent = call(totals_kernel, [(share, F32), (share, BF16)], *mine)
-    totals = swapped([sent] * planes, "outer", total)
-    below, whole = call(planes_kernel, [(share, F32)] * 2, *totals)
-    groups = [lax.ppermute(whole, "chain", [(c, c ^ d) for c in range(chains)]) for d in range(1, chains)]
-    before = call(functools.partial(prefix_kernel, inner), [(share, BF16)] * inner, *mine, below, *groups,
+        scratch=[pltpu.SemaphoreType.DMA((2, SLABS))])
+    shares = call(functools.partial(shares_kernel, chains), [both] * inner,
+                  states, *[across(states, chains, e) for e in range(1, chains)])
+    mine = swapped(shares, "inner", chains)
+    total, sent = call(totals_kernel, [(both[0], F32), both], *mine)
+    totals = swapped([sent] * planes, "outer", chains)[:-1] + [total]
+    before = call(functools.partial(prefix_kernel, inner, planes), [both] * inner, *mine, *totals,
                   scratch=[pltpu.VMEM((inner,) + share, F32)])
-    prefix = swapped(before, "inner", before[0])
+    *before, queries = lax.optimization_barrier((*before, queries))
+    back = swapped(before, "inner", chains)
+    dealt = call(functools.partial(deal_kernel, inner), [whole] * chains, *back)
+    dealt = [dealt[0]] + [across(dealt[e], chains, e) for e in range(1, chains)]
     intra = call(intra_kernel, (queries.shape, F32), queries, keys, values,
                  flops=4 * rows * rows * HEADS * HEAD_DIM)
-    return call(functools.partial(attend_kernel, inner), (queries.shape, BF16), queries, intra, *prefix,
+    return call(functools.partial(attend_kernel, chains), (queries.shape, BF16), queries, intra, *dealt,
                 result=pltpu.HBM, flops=2 * rows * SLAB * HEADS * HEAD_DIM,
-                scratch=[pltpu.VMEM(queries.shape, BF16), pltpu.VMEM((inner,) + share, BF16),
+                scratch=[pltpu.VMEM(queries.shape, BF16), pltpu.VMEM(*whole),
                          pltpu.SemaphoreType.DMA((HEADS * HEAD_DIM // SLAB,))])
 
 

time: 28 us -> 42.5 us (1.52)
  starting transfers between devices: 12.7 us -> 35.7 us
  waiting for transfers between devices: 9.96 us -> 1.01 us
    ppermute x10 -> x11, starting transfers between devices: 12.7 us -> 35.7 us  [the longest x2 29.6 us: across(): return lax.ppermute(x, 'chain', [(c, c ^ e) for c in range(chains)])]
    ppermute x10 -> x11, waiting for transfers between devices: 9.96 us -> 1.01 us  [the longest x2 0.99 us: across(): return lax.ppermute(x, 'chain', [(c, c ^ e) for c in range(chains)])]
    pallas_call x6 -> x7, Pallas kernels: 5.13 us -> 5.23 us  [call(): pl.pallas_call(kernel, out_shape=[result(shape, dtype) for shape, dtype i...]
  transfers between devices with their start and end apart: 10 -> 11, of which waited for: 8 -> 1; matrix products, arithmetic and copies ran while one was open for 0% -> 0% of each run, Pallas kernels for 5% -> 3%
where the time goes in v10:
time: 42.5 us; the launch traced here: 42.2 us
  starting transfers between devices  35.7 us (84%)
  Pallas kernels  5.23 us (12%)
  waiting for transfers between devices  1.01 us (2%)
    ppermute x2, starting transfers between devices, across(): return lax.ppermute(x, 'chain', [(c, c ^ e) for c in range(chains)])  29.6 us
    ppermute x9, starting transfers between devices, swapped(): got.append(lax.ppermute(arrays[d], (axis, 'chain'), pairs))  6.11 us
    pallas_call x7, Pallas kernels, call(): pl.pallas_call(kernel, out_shape=[result(shape, dtype) for shape, dtype i...  5.23 us
    ppermute x2, waiting for transfers between devices, across(): return lax.ppermute(x, 'chain', [(c, c ^ e) for c in range(chains)])  0.99 us
  transfers between devices with their start and end apart: 11, of which 1 were waited for; matrix products, arithmetic and copies ran while one was open for 0% of the time, Pallas kernels for 3%

profile of v10, /device:TPU:0, one launch (start us, length us, event | category | flops | bytes accessed | tf_op | source)
XLA Modules:
  0.0 42.2 jit_solution(2915585835618671153)
XLA Ops:
  0.0 2.0 %shard_map.37 = (bf16[4,128,128]{2,1,0:T(8,128)(2,1)S(1)}, bf16[256,1024]{1,0:T(8,128)(2,1)S(1)}, bf16[256,1024]{1,0:T(8,128)(2,1)S(1)}) custom-call(bf16[256,1024]{1,0:T(8,128)(2,1)} %k_hbm.1, bf16[256,1024]{1,0:T(8,128)(2,1)} %v_hbm.1), custom_call_target="tpu_custom_call" | custom-call | flops 67108864 | bytes 1048576 | tf_op jit(solution)/shard_map/pallas_call | solution.py:163
  2.0 0.5 %collective-permute-start = (bf16[4,128,128]{2,1,0:T(8,128)(2,1)S(1)}, bf16[4,128,128]{2,1,0:T(8,128)(2,1)S(1)}, u32[]{:S(2)}, u32[]{:S(2)}) collective-permute-start(bf16[4,128,128]{2,1,0:T(8,128)(2,1)S(1)} %get-tuple-element.25.refs_0_), channel_id=1, source_target_pairs={{0,1},{1,0},{2,3},{3,2},{4,5},{5,4},{6,7},{7,6},{8,9},{9,8},{10,11... | collective-permute-start | bytes 393224 | tf_op jit(solution)/shard_map/ppermute | solution.py:185
  2.5 1.0 %collective-permute-done.refs_1_ = bf16[4,128,128]{2,1,0:T(8,128)(2,1)S(1)} collective-permute-done((bf16[4,128,128]{2,1,0:T(8,128)(2,1)S(1)}, bf16[4,128,128]{2,1,0:T(8,128)(2,1)S(1)}, u32[]{:S(2)}, u32[]{:S(2)}) %collective-permute-start) | collective-permute-done | bytes 131104 | tf_op jit(solution)/shard_map/ppermute | solution.py:185
  3.5 0.7 %collective-permute-start.1 = (bf16[2,128,128]{2,1,0:T(8,128)(2,1)S(1)}, bf16[2,128,128]{2,1,0:T(8,128)(2,1)S(1)}, u32[]{:S(2)}, u32[]{:S(2)}) collective-permute-start(bf16[2,128,128]{2,1,0:T(8,128)(2,1)S(1)} %get-tuple-element.26), channel_id=1, source_target_pairs={{0,0},{1,7},{2,2},{3,5},{4,4},{5,3},{6,6},{7,1},{8,8},{9,15},{10,1... | collective-permute-start | bytes 196616 | tf_op jit(solution)/shard_map/ppermute | solution.py:180
  4.2 0.7 %collective-permute-start.2 = (bf16[2,128,128]{2,1,0:T(8,128)(2,1)S(1)}, bf16[2,128,128]{2,1,0:T(8,128)(2,1)S(1)}, u32[]{:S(2)}, u32[]{:S(2)}) collective-permute-start(bf16[2,128,128]{2,1,0:T(8,128)(2,1)S(1)} %get-tuple-element.27), channel_id=1, source_target_pairs={{0,0},{1,5},{2,2},{3,7},{4,4},{5,1},{6,6},{7,3},{8,8},{9,13},{10,1... | collective-permute-start | bytes 196616 | tf_op jit(solution)/shard_map/ppermute | solution.py:180
  4.9 0.7 %collective-permute-start.3 = (bf16[2,128,128]{2,1,0:T(8,128)(2,1)S(1)}, bf16[2,128,128]{2,1,0:T(8,128)(2,1)S(1)}, u32[]{:S(2)}, u32[]{:S(2)}) collective-permute-start(bf16[2,128,128]{2,1,0:T(8,128)(2,1)S(1)} %get-tuple-element.28), channel_id=1, source_target_pairs={{0,0},{1,3},{2,2},{3,1},{4,4},{5,7},{6,6},{7,5},{8,8},{9,11},{10,1... | collective-permute-start | bytes 196616 | tf_op jit(solution)/shard_map/ppermute | solution.py:180
  5.5 0.0 collective-permute-done.1.refs_0_
  5.5 0.0 collective-permute-done.2.refs_1_
  5.6 0.0 collective-permute-done.3.refs_2_
  5.6 0.0 copy-start
  5.6 0.8 %collective-permute-start.4 = (bf16[2,128,128]{2,1,0:T(8,128)(2,1)S(1)}, bf16[2,128,128]{2,1,0:T(8,128)(2,1)S(1)}, u32[]{:S(2)}, u32[]{:S(2)}) collective-permute-start(bf16[2,128,128]{2,1,0:T(8,128)(2,1)S(1)} %get-tuple-element.30), channel_id=1, source_target_pairs={{0,0},{1,25},{8,8},{9,17},{16,16},{17,9},{24,24},{25,1},{2,2},{3,2... | collective-permute-start | bytes 196616 | tf_op jit(solution)/shard_map/ppermute | solution.py:180
  6.4 0.7 %collective-permute-start.5 = (bf16[2,128,128]{2,1,0:T(8,128)(2,1)S(1)}, bf16[2,128,128]{2,1,0:T(8,128)(2,1)S(1)}, u32[]{:S(2)}, u32[]{:S(2)}) collective-permute-start(bf16[2,128,128]{2,1,0:T(8,128)(2,1)S(1)} %get-tuple-element.30), channel_id=1, source_target_pairs={{0,0},{1,17},{8,8},{9,25},{16,16},{17,1},{24,24},{25,9},{2,2},{3,1... | collective-permute-start | bytes 196616 | tf_op jit(solution)/shard_map/ppermute | solution.py:180
  7.1 0.7 %collective-permute-start.6 = (bf16[2,128,128]{2,1,0:T(8,128)(2,1)S(1)}, bf16[2,128,128]{2,1,0:T(8,128)(2,1)S(1)}, u32[]{:S(2)}, u32[]{:S(2)}) collective-permute-start(bf16[2,128,128]{2,1,0:T(8,128)(2,1)S(1)} %get-tuple-element.30), channel_id=1, source_target_pairs={{0,0},{1,9},{8,8},{9,1},{16,16},{17,25},{24,24},{25,17},{2,2},{3,1... | collective-permute-start | bytes 196616 | tf_op jit(solution)/shard_map/ppermute | solution.py:180
  7.8 0.0 collective-permute-done.4.refs_4_
  7.8 0.0 collective-permute-done.5.refs_5_
  7.8 0.0 collective-permute-done.6.refs_6_
  7.8 0.1 shard_map.40
  8.0 0.7 %collective-permute-start.7 = (bf16[2,128,128]{2,1,0:T(8,128)(2,1)S(1)}, bf16[2,128,128]{2,1,0:T(8,128)(2,1)S(1)}, u32[]{:S(2)}, u32[]{:S(2)}) collective-permute-start(bf16[2,128,128]{2,1,0:T(8,128)(2,1)S(1)} %get-tuple-element.39), channel_id=1, source_target_pairs={{0,0},{1,7},{2,2},{3,5},{4,4},{5,3},{6,6},{7,1},{8,8},{9,15},{10,1... | collective-permute-start | bytes 196616 | tf_op jit(solution)/shard_map/ppermute | solution.py:180
  8.6 0.7 %collective-permute-start.8 = (bf16[2,128,128]{2,1,0:T(8,128)(2,1)S(1)}, bf16[2,128,128]{2,1,0:T(8,128)(2,1)S(1)}, u32[]{:S(2)}, u32[]{:S(2)}) collective-permute-start(bf16[2,128,128]{2,1,0:T(8,128)(2,1)S(1)} %get-tuple-element.40), channel_id=1, source_target_pairs={{0,0},{1,5},{2,2},{3,7},{4,4},{5,1},{6,6},{7,3},{8,8},{9,13},{10,1... | collective-permute-start | bytes 196616 | tf_op jit(solution)/shard_map/ppermute | solution.py:180
  9.3 0.7 %collective-permute-start.9 = (bf16[2,128,128]{2,1,0:T(8,128)(2,1)S(1)}, bf16[2,128,128]{2,1,0:T(8,128)(2,1)S(1)}, u32[]{:S(2)}, u32[]{:S(2)}) collective-permute-start(bf16[2,128,128]{2,1,0:T(8,128)(2,1)S(1)} %get-tuple-element.41), channel_id=1, source_target_pairs={{0,0},{1,3},{2,2},{3,1},{4,4},{5,7},{6,6},{7,5},{8,8},{9,11},{10,1... | collective-permute-start | bytes 196616 | tf_op jit(solution)/shard_map/ppermute | solution.py:180
  10.0 0.0 collective-permute-done.7.refs_0_
  10.0 0.0 collective-permute-done.8.refs_1_
  10.0 0.0 collective-permute-done.9.refs_2_
  10.0 29.1 %collective-permute-start.10 = (bf16[4,128,128]{2,1,0:T(8,128)(2,1)S(1)}, bf16[4,128,128]{2,1,0:T(8,128)(2,1)S(1)}, u32[]{:S(2)}, u32[]{:S(2)}) collective-permute-start(bf16[4,128,128]{2,1,0:T(8,128)(2,1)S(1)} %get-tuple-element.44), channel_id=1, source_target_pairs={{0,1},{1,0},{2,3},{3,2},{4,5},{5,4},{6,7},{7,6},{8,9},{9,8},{10,11... | collective-permute-start | bytes 393224 | tf_op jit(solution)/shard_map/ppermute | solution.py:185
  39.1 0.0 copy-done
  39.1 1.5 %shard_map.41.intra_ref = f32[256,1024]{1,0:T(8,128)S(1)} custom-call(bf16[256,1024]{1,0:T(8,128)(2,1)S(1)} %copy-done, bf16[256,1024]{1,0:T(8,128)(2,1)S(1)} %get-tuple-element.37.k_ref, bf16[256,1024]{1,0:T(8,128)(2,1)S(1)} %get-tuple-element.38.v_ref), custom_call_target="tpu_custom_call" | custom-call | flops 268435456 | bytes 1572864 | tf_op jit(solution)/shard_map/pallas_call | solution.py:163
  40.6 0.0 collective-permute-done.10.refs_1_
  40.6 1.5 %shard_map.43 = bf16[256,1024]{1,0:T(8,128)(2,1)} custom-call(bf16[256,1024]{1,0:T(8,128)(2,1)S(1)} %copy-done, f32[256,1024]{1,0:T(8,128)S(1)} %shard_map.41.intra_ref, bf16[4,128,128]{2,1,0:T(8,128)(2,1)S(1)} %get-tuple-element.43.refs_0_, bf16[4,128,128]{2,1,0:T(8,128)(2,1)S(1)} %collective-permute-done.10.refs_1_), custom_call_target="tpu_custom_call" | custom-call | flops 134217728 | bytes 1835008 | tf_op jit(solution)/shard_map/pallas_call | solution.py:163
  (3 shorter events, 0.1 us)
Async XLA Ops:
  2.0 1.5 %collective-permute-start = (bf16[4,128,128]{2,1,0:T(8,128)(2,1)S(1)}, bf16[4,128,128]{2,1,0:T(8,128)(2,1)S(1)}, u32[]{:S(2)}, u32[]{:S(2)}) collective-permute-start(bf16[4,128,128]{2,1,0:T(8,128)(2,1)S(1)} %get-tuple-element.25.refs_0_), channel_id=1, source_target_pairs={{0,1},{1,0},{2,3},{3,2},{4,5},{5,4},{6,7},{7,6},{8,9},{9,8},{10,11... | collective-permute-start | bytes 393224 | tf_op jit(solution)/shard_map/ppermute | solution.py:185
  3.5 2.0 %collective-permute-start.1 = (bf16[2,128,128]{2,1,0:T(8,128)(2,1)S(1)}, bf16[2,128,128]{2,1,0:T(8,128)(2,1)S(1)}, u32[]{:S(2)}, u32[]{:S(2)}) collective-permute-start(bf16[2,128,128]{2,1,0:T(8,128)(2,1)S(1)} %get-tuple-element.26), channel_id=1, source_target_pairs={{0,0},{1,7},{2,2},{3,5},{4,4},{5,3},{6,6},{7,1},{8,8},{9,15},{10,1... | collective-permute-start | bytes 196616 | tf_op jit(solution)/shard_map/ppermute | solution.py:180
  4.2 1.4 %collective-permute-start.2 = (bf16[2,128,128]{2,1,0:T(8,128)(2,1)S(1)}, bf16[2,128,128]{2,1,0:T(8,128)(2,1)S(1)}, u32[]{:S(2)}, u32[]{:S(2)}) collective-permute-start(bf16[2,128,128]{2,1,0:T(8,128)(2,1)S(1)} %get-tuple-element.27), channel_id=1, source_target_pairs={{0,0},{1,5},{2,2},{3,7},{4,4},{5,1},{6,6},{7,3},{8,8},{9,13},{10,1... | collective-permute-start | bytes 196616 | tf_op jit(solution)/shard_map/ppermute | solution.py:180
  4.9 0.7 %collective-permute-start.3 = (bf16[2,128,128]{2,1,0:T(8,128)(2,1)S(1)}, bf16[2,128,128]{2,1,0:T(8,128)(2,1)S(1)}, u32[]{:S(2)}, u32[]{:S(2)}) collective-permute-start(bf16[2,128,128]{2,1,0:T(8,128)(2,1)S(1)} %get-tuple-element.28), channel_id=1, source_target_pairs={{0,0},{1,3},{2,2},{3,1},{4,4},{5,7},{6,6},{7,5},{8,8},{9,11},{10,1... | collective-permute-start | bytes 196616 | tf_op jit(solution)/shard_map/ppermute | solution.py:180
  5.6 33.5 %copy-start = (bf16[256,1024]{1,0:T(8,128)(2,1)S(1)}, bf16[256,1024]{1,0:T(8,128)(2,1)}, u32[]{:S(2)}) copy-start(bf16[256,1024]{1,0:T(8,128)(2,1)} %q_ref.1) | copy-start | bytes 1572868
  5.6 2.2 %collective-permute-start.4 = (bf16[2,128,128]{2,1,0:T(8,128)(2,1)S(1)}, bf16[2,128,128]{2,1,0:T(8,128)(2,1)S(1)}, u32[]{:S(2)}, u32[]{:S(2)}) collective-permute-start(bf16[2,128,128]{2,1,0:T(8,128)(2,1)S(1)} %get-tuple-element.30), channel_id=1, source_target_pairs={{0,0},{1,25},{8,8},{9,17},{16,16},{17,9},{24,24},{25,1},{2,2},{3,2... | collective-permute-start | bytes 196616 | tf_op jit(solution)/shard_map/ppermute | solution.py:180
  6.4 1.4 %collective-permute-start.5 = (bf16[2,128,128]{2,1,0:T(8,128)(2,1)S(1)}, bf16[2,128,128]{2,1,0:T(8,128)(2,1)S(1)}, u32[]{:S(2)}, u32[]{:S(2)}) collective-permute-start(bf16[2,128,128]{2,1,0:T(8,128)(2,1)S(1)} %get-tuple-element.30), channel_id=1, source_target_pairs={{0,0},{1,17},{8,8},{9,25},{16,16},{17,1},{24,24},{25,9},{2,2},{3,1... | collective-permute-start | bytes 196616 | tf_op jit(solution)/shard_map/ppermute | solution.py:180
  7.1 0.7 %collective-permute-start.6 = (bf16[2,128,128]{2,1,0:T(8,128)(2,1)S(1)}, bf16[2,128,128]{2,1,0:T(8,128)(2,1)S(1)}, u32[]{:S(2)}, u32[]{:S(2)}) collective-permute-start(bf16[2,128,128]{2,1,0:T(8,128)(2,1)S(1)} %get-tuple-element.30), channel_id=1, source_target_pairs={{0,0},{1,9},{8,8},{9,1},{16,16},{17,25},{24,24},{25,17},{2,2},{3,1... | collective-permute-start | bytes 196616 | tf_op jit(solution)/shard_map/ppermute | solution.py:180
  8.0 2.0 %collective-permute-start.7 = (bf16[2,128,128]{2,1,0:T(8,128)(2,1)S(1)}, bf16[2,128,128]{2,1,0:T(8,128)(2,1)S(1)}, u32[]{:S(2)}, u32[]{:S(2)}) collective-permute-start(bf16[2,128,128]{2,1,0:T(8,128)(2,1)S(1)} %get-tuple-element.39), channel_id=1, source_target_pairs={{0,0},{1,7},{2,2},{3,5},{4,4},{5,3},{6,6},{7,1},{8,8},{9,15},{10,1... | collective-permute-start | bytes 196616 | tf_op jit(solution)/shard_map/ppermute | solution.py:180
  8.6 1.4 %collective-permute-start.8 = (bf16[2,128,128]{2,1,0:T(8,128)(2,1)S(1)}, bf16[2,128,128]{2,1,0:T(8,128)(2,1)S(1)}, u32[]{:S(2)}, u32[]{:S(2)}) collective-permute-start(bf16[2,128,128]{2,1,0:T(8,128)(2,1)S(1)} %get-tuple-element.40), channel_id=1, source_target_pairs={{0,0},{1,5},{2,2},{3,7},{4,4},{5,1},{6,6},{7,3},{8,8},{9,13},{10,1... | collective-permute-start | bytes 196616 | tf_op jit(solution)/shard_map/ppermute | solution.py:180
  9.3 0.7 %collective-permute-start.9 = (bf16[2,128,128]{2,1,0:T(8,128)(2,1)S(1)}, bf16[2,128,128]{2,1,0:T(8,128)(2,1)S(1)}, u32[]{:S(2)}, u32[]{:S(2)}) collective-permute-start(bf16[2,128,128]{2,1,0:T(8,128)(2,1)S(1)} %get-tuple-element.41), channel_id=1, source_target_pairs={{0,0},{1,3},{2,2},{3,1},{4,4},{5,7},{6,6},{7,5},{8,8},{9,11},{10,1... | collective-permute-start | bytes 196616 | tf_op jit(solution)/shard_map/ppermute | solution.py:180
  10.0 30.6 %collective-permute-start.10 = (bf16[4,128,128]{2,1,0:T(8,128)(2,1)S(1)}, bf16[4,128,128]{2,1,0:T(8,128)(2,1)S(1)}, u32[]{:S(2)}, u32[]{:S(2)}) collective-permute-start(bf16[4,128,128]{2,1,0:T(8,128)(2,1)S(1)} %get-tuple-element.44), channel_id=1, source_target_pairs={{0,1},{1,0},{2,3},{3,2},{4,5},{5,4},{6,7},{7,6},{8,9},{9,8},{10,11... | collective-permute-start | bytes 393224 | tf_op jit(solution)/shard_map/ppermute | solution.py:185

commit v11 on v9

--- a/solution.py
+++ b/solution.py
@@ -66,17 +66,17 @@
     sent_ref[...] = total.astype(sent_ref.dtype)
 
 
-def planes_kernel(*refs):
-    *totals, own, below_ref, whole_ref = refs
-    plane = lax.axis_index("outer")
-    whole = own[...]
-    below = jnp.zeros_like(whole)
-    for e, there in zip(reversed(range(1, len(totals) + 1)), totals):
-        there = there[...].astype(F32)
-        below = below + jnp.where((plane ^ e) < plane, there, 0.0)
-        whole = whole + there
-    below_ref[...] = below
+def planes_kernel(step, *refs):
+    if step > 1:
+        below_in, *refs = refs
+    whole_in, there_ref, below_ref, whole_ref, *sent = refs
+    there = there_ref[...].astype(F32)
+    below = jnp.where((lax.axis_index("outer") & step) != 0, there, 0.0)
+    below_ref[...] = below + below_in[...] if step > 1 else below
+    whole = whole_in[...] + there
     whole_ref[...] = whole
+    for ref in sent:
+        ref[...] = whole.astype(ref.dtype)
 
 
 def prefix_kernel(inner, *refs):
@@ -137,10 +137,7 @@
         inter = jnp.dot(q_ref[:, lanes], prefix, preferred_element_type=F32)
         total = intra_ref[:, lanes] + inter
         square = total * total
-        high = square.astype(BF16)
-        low = (square - high.astype(F32)).astype(BF16)
-        sums = (jnp.dot(high, ones, preferred_element_type=F32)
-                + jnp.dot(low, ones, preferred_element_type=F32))
+        sums = jnp.dot(square.astype(BF16), ones, preferred_element_type=F32)
         out_ref[:, lanes] = (total * lax.rsqrt(sums * (1.0 / HEAD_DIM) + 1e-6)).astype(out_ref.dtype)
         copies.append(pltpu.make_async_copy(out_ref.at[:, lanes], out_hbm.at[:, lanes], sent.at[s]))
         copies[-1].start()
@@ -179,10 +176,16 @@
         scratch=[pltpu.VMEM((inner,) + share, F32), pltpu.SemaphoreType.DMA((2, SLABS))])
     mine = swapped([own] + states, "inner", own)
     total, sent = call(totals_kernel, [(share, F32), (share, BF16)], *mine)
-    totals = swapped([sent] * planes, "outer", total)
-    below, whole = call(planes_kernel, [(share, F32)] * 2, *totals)
+    below, whole, step = [], total, 1
+    while step < planes:
+        there = lax.ppermute(sent, "outer", [(z, z ^ step) for z in range(planes)])
+        last = 2 * step >= planes
+        below, whole, *sent = call(
+            functools.partial(planes_kernel, step), [(share, F32)] * 2 + [(share, BF16)] * (not last),
+            *below, whole, there)
+        below, sent, step = [below], sent[0] if sent else None, 2 * step
     groups = [lax.ppermute(whole, "chain", [(c, c ^ d) for c in range(chains)]) for d in range(1, chains)]
-    before = call(functools.partial(prefix_kernel, inner), [(share, BF16)] * inner, *mine, below, *groups,
+    before = call(functools.partial(prefix_kernel, inner), [(share, BF16)] * inner, *mine, *below, *groups,
                   scratch=[pltpu.VMEM((inner,) + share, F32)])
     prefix = swapped(before, "inner", before[0])
     intra = call(intra_kernel, (queries.shape, F32), queries, keys, values,

time: 28 us -> 28 us (level)
    ppermute x0 -> x2, starting transfers between devices: none -> 4.59 us  [per_device(): there = lax.ppermute(sent, 'outer', [(z, z ^ step) for z in range(planes)])]
    ppermute x9 -> x6, starting transfers between devices: 12.6 us -> 8.17 us  [swapped(): lax.ppermute(arrays[d], axis, [(i, i ^ d) for i in range(size)])]
    ppermute x0 -> x2, waiting for transfers between devices: none -> 4.27 us  [per_device(): there = lax.ppermute(sent, 'outer', [(z, z ^ step) for z in range(planes)])]
    ppermute x9 -> x6, waiting for transfers between devices: 8.72 us -> 4.61 us  [swapped(): lax.ppermute(arrays[d], axis, [(i, i ^ d) for i in range(size)])]
    pallas_call x6 -> x7, Pallas kernels: 5.13 us -> 4.86 us  [call(): pl.pallas_call(kernel, out_shape=[result(shape, dtype) for shape, dtype i...]
  transfers between devices with their start and end apart: 10 -> 9, of which waited for: 8 -> 8; matrix products, arithmetic and copies ran while one was open for 0% -> 0% of each run, Pallas kernels for 5% -> 5%
where the time goes in v11:
time: 28 us; the launch traced here: 27.9 us
  starting transfers between devices  12.8 us (46%)
  waiting for transfers between devices  10.1 us (36%)
  Pallas kernels  4.86 us (17%)
    ppermute x6, starting transfers between devices, swapped(): lax.ppermute(arrays[d], axis, [(i, i ^ d) for i in range(size)])  8.17 us
    pallas_call x7, Pallas kernels, call(): pl.pallas_call(kernel, out_shape=[result(shape, dtype) for shape, dtype i...  4.86 us
    ppermute x6, waiting for transfers between devices, swapped(): lax.ppermute(arrays[d], axis, [(i, i ^ d) for i in range(size)])  4.61 us
    ppermute x2, starting transfers between devices, per_device(): there = lax.ppermute(sent, 'outer', [(z, z ^ step) for z in range(planes)])  4.59 us
    ppermute x2, waiting for transfers between devices, per_device(): there = lax.ppermute(sent, 'outer', [(z, z ^ step) for z in range(planes)])  4.27 us
    ppermute x1, waiting for transfers between devices, per_device(): lax.ppermute(whole, 'chain', [(c, c ^ d) for c in range(chains)])  1.24 us
  transfers between devices with their start and end apart: 9, of which 8 were waited for; matrix products, arithmetic and copies ran while one was open for 0% of the time, Pallas kernels for 5%

profile of v11, /device:TPU:0, one launch (start us, length us, event | category | flops | bytes accessed | tf_op | source)
XLA Modules:
  0.0 27.9 jit_solution(5721609134435767000)
XLA Ops:
  0.0 2.0 %shard_map.37 = (f32[128,128]{1,0:T(8,128)S(1)}, bf16[128,128]{1,0:T(8,128)(2,1)S(1)}, bf16[128,128]{1,0:T(8,128)(2,1)S(1)}, bf16[128,128]{1,0:T(8,128)(2,1)S(1)...) custom-call(bf16[256,1024]{1,0:T(8,128)(2,1)} %k_hbm.1, bf16[256,1024]{1,0:T(8,128)(2,1)} %v_hbm.1), custom_call_target="tpu_custom_call" | custom-call | flops 67108864 | bytes 1048576 | tf_op jit(solution)/shard_map/pallas_call | solution.py:152
  2.0 0.0 copy-start
  2.0 4.0 %collective-permute-start = (bf16[128,128]{1,0:T(8,128)(2,1)S(1)}, bf16[128,128]{1,0:T(8,128)(2,1)S(1)}, u32[]{:S(2)}, u32[]{:S(2)}) collective-permute-start(bf16[128,128]{1,0:T(8,128)(2,1)S(1)} %get-tuple-element.24), channel_id=1, source_target_pairs={{0,6},{2,4},{4,2},{6,0},{1,7},{3,5},{5,3},{7,1},{8,14},{10,12},{12... | collective-permute-start | bytes 98312 | tf_op jit(solution)/shard_map/ppermute | solution.py:166
  6.0 0.5 %collective-permute-start.1 = (bf16[128,128]{1,0:T(8,128)(2,1)S(1)}, bf16[128,128]{1,0:T(8,128)(2,1)S(1)}, u32[]{:S(2)}, u32[]{:S(2)}) collective-permute-start(bf16[128,128]{1,0:T(8,128)(2,1)S(1)} %get-tuple-element.25), channel_id=1, source_target_pairs={{0,4},{2,6},{4,0},{6,2},{1,5},{3,7},{5,1},{7,3},{8,12},{10,14},{12... | collective-permute-start | bytes 98312 | tf_op jit(solution)/shard_map/ppermute | solution.py:166
  6.5 0.1 collective-permute-start.2
  6.6 1.3 %collective-permute-done.refs_0_ = bf16[128,128]{1,0:T(8,128)(2,1)S(1)} collective-permute-done((bf16[128,128]{1,0:T(8,128)(2,1)S(1)}, bf16[128,128]{1,0:T(8,128)(2,1)S(1)}, u32[]{:S(2)}, u32[]{:S(2)}) %collective-permute-start) | collective-permute-done | bytes 32800 | tf_op jit(solution)/shard_map/ppermute | solution.py:166
  7.9 2.0 %collective-permute-done.1.refs_1_ = bf16[128,128]{1,0:T(8,128)(2,1)S(1)} collective-permute-done((bf16[128,128]{1,0:T(8,128)(2,1)S(1)}, bf16[128,128]{1,0:T(8,128)(2,1)S(1)}, u32[]{:S(2)}, u32[]{:S(2)}) %collective-permute-start.1) | collective-permute-done | bytes 32800 | tf_op jit(solution)/shard_map/ppermute | solution.py:166
  9.9 0.5 %collective-permute-done.2.refs_2_ = bf16[128,128]{1,0:T(8,128)(2,1)S(1)} collective-permute-done((bf16[128,128]{1,0:T(8,128)(2,1)S(1)}, bf16[128,128]{1,0:T(8,128)(2,1)S(1)}, u32[]{:S(2)}, u32[]{:S(2)}) %collective-permute-start.2) | collective-permute-done | bytes 32800 | tf_op jit(solution)/shard_map/ppermute | solution.py:166
  10.4 1.6 %collective-permute-start.3 = (bf16[128,128]{1,0:T(8,128)(2,1)S(1)}, bf16[128,128]{1,0:T(8,128)(2,1)S(1)}, u32[]{:S(2)}, u32[]{:S(2)}) collective-permute-start(bf16[128,128]{1,0:T(8,128)(2,1)S(1)} %get-tuple-element.29), channel_id=1, source_target_pairs={{0,8},{8,0},{16,24},{24,16},{1,9},{9,1},{17,25},{25,17},{2,10},{10... | collective-permute-start | bytes 98312 | tf_op jit(solution)/shard_map/ppermute | solution.py:181
  12.1 2.3 %collective-permute-done.3.refs_1_ = bf16[128,128]{1,0:T(8,128)(2,1)S(1)} collective-permute-done((bf16[128,128]{1,0:T(8,128)(2,1)S(1)}, bf16[128,128]{1,0:T(8,128)(2,1)S(1)}, u32[]{:S(2)}, u32[]{:S(2)}) %collective-permute-start.3) | collective-permute-done | bytes 32800 | tf_op jit(solution)/shard_map/ppermute | solution.py:181
  14.4 2.9 %collective-permute-start.4 = (bf16[128,128]{1,0:T(8,128)(2,1)S(1)}, bf16[128,128]{1,0:T(8,128)(2,1)S(1)}, u32[]{:S(2)}, u32[]{:S(2)}) collective-permute-start(bf16[128,128]{1,0:T(8,128)(2,1)S(1)} %get-tuple-element.32), channel_id=1, source_target_pairs={{0,16},{8,24},{16,0},{24,8},{1,17},{9,25},{17,1},{25,9},{2,18},{10... | collective-permute-start | bytes 98312 | tf_op jit(solution)/shard_map/ppermute | solution.py:181
  17.4 1.9 %collective-permute-done.4.refs_2_ = bf16[128,128]{1,0:T(8,128)(2,1)S(1)} collective-permute-done((bf16[128,128]{1,0:T(8,128)(2,1)S(1)}, bf16[128,128]{1,0:T(8,128)(2,1)S(1)}, u32[]{:S(2)}, u32[]{:S(2)}) %collective-permute-start.4) | collective-permute-done | bytes 32800 | tf_op jit(solution)/shard_map/ppermute | solution.py:181
  19.3 0.1 collective-permute-start.5
  19.4 1.2 %collective-permute-done.5.refs_5_ = f32[128,128]{1,0:T(8,128)S(1)} collective-permute-done((f32[128,128]{1,0:T(8,128)S(1)}, f32[128,128]{1,0:T(8,128)S(1)}, u32[]{:S(2)}, u32[]{:S(2)}) %collective-permute-start.5) | collective-permute-done | bytes 65568 | tf_op jit(solution)/shard_map/ppermute | solution.py:187
  20.6 0.1 shard_map.42
  20.7 1.6 %collective-permute-start.6 = (bf16[128,128]{1,0:T(8,128)(2,1)S(1)}, bf16[128,128]{1,0:T(8,128)(2,1)S(1)}, u32[]{:S(2)}, u32[]{:S(2)}) collective-permute-start(bf16[128,128]{1,0:T(8,128)(2,1)S(1)} %get-tuple-element.35), channel_id=1, source_target_pairs={{0,6},{2,4},{4,2},{6,0},{1,7},{3,5},{5,3},{7,1},{8,14},{10,12},{12... | collective-permute-start | bytes 98312 | tf_op jit(solution)/shard_map/ppermute | solution.py:166
  22.3 0.4 %collective-permute-start.7 = (bf16[128,128]{1,0:T(8,128)(2,1)S(1)}, bf16[128,128]{1,0:T(8,128)(2,1)S(1)}, u32[]{:S(2)}, u32[]{:S(2)}) collective-permute-start(bf16[128,128]{1,0:T(8,128)(2,1)S(1)} %get-tuple-element.36), channel_id=1, source_target_pairs={{0,4},{2,6},{4,0},{6,2},{1,5},{3,7},{5,1},{7,3},{8,12},{10,14},{12... | collective-permute-start | bytes 98312 | tf_op jit(solution)/shard_map/ppermute | solution.py:166
  22.7 1.6 %collective-permute-start.8 = (bf16[128,128]{1,0:T(8,128)(2,1)S(1)}, bf16[128,128]{1,0:T(8,128)(2,1)S(1)}, u32[]{:S(2)}, u32[]{:S(2)}) collective-permute-start(bf16[128,128]{1,0:T(8,128)(2,1)S(1)} %get-tuple-element.37), channel_id=1, source_target_pairs={{0,2},{2,0},{4,6},{6,4},{1,3},{3,1},{5,7},{7,5},{8,10},{10,8},{12,... | collective-permute-start | bytes 98312 | tf_op jit(solution)/shard_map/ppermute | solution.py:166
  24.3 0.0 copy-done
  24.3 1.5 %shard_map.38.intra_ref = f32[256,1024]{1,0:T(8,128)S(1)} custom-call(bf16[256,1024]{1,0:T(8,128)(2,1)S(1)} %copy-done, bf16[256,1024]{1,0:T(8,128)(2,1)S(1)} %get-tuple-element.22.k_ref, bf16[256,1024]{1,0:T(8,128)(2,1)S(1)} %get-tuple-element.23.v_ref), custom_call_target="tpu_custom_call" | custom-call | flops 268435456 | bytes 1572864 | tf_op jit(solution)/shard_map/pallas_call | solution.py:152
  25.8 0.0 collective-permute-done.6.refs_0_
  25.8 0.4 %collective-permute-done.7.refs_1_ = bf16[128,128]{1,0:T(8,128)(2,1)S(1)} collective-permute-done((bf16[128,128]{1,0:T(8,128)(2,1)S(1)}, bf16[128,128]{1,0:T(8,128)(2,1)S(1)}, u32[]{:S(2)}, u32[]{:S(2)}) %collective-permute-start.7) | collective-permute-done | bytes 32800 | tf_op jit(solution)/shard_map/ppermute | solution.py:166
  26.2 0.4 %collective-permute-done.8.refs_2_ = bf16[128,128]{1,0:T(8,128)(2,1)S(1)} collective-permute-done((bf16[128,128]{1,0:T(8,128)(2,1)S(1)}, bf16[128,128]{1,0:T(8,128)(2,1)S(1)}, u32[]{:S(2)}, u32[]{:S(2)}) %collective-permute-start.8) | collective-permute-done | bytes 32800 | tf_op jit(solution)/shard_map/ppermute | solution.py:166
  26.6 1.3 %shard_map.43 = bf16[256,1024]{1,0:T(8,128)(2,1)} custom-call(bf16[256,1024]{1,0:T(8,128)(2,1)S(1)} %copy-done, f32[256,1024]{1,0:T(8,128)S(1)} %shard_map.38.intra_ref, bf16[128,128]{1,0:T(8,128)(2,1)S(1)} %collective-permute-done.6.refs_0_, bf16[128,128]{1,0:T(8,128)(2,1)S(1)} %collective-permute-done.7.refs_1_, ...), custom_call_target="tpu_custom_call" | custom-call | flops 134217728 | bytes 1703936 | tf_op jit(solution)/shard_map/pallas_call | solution.py:152
  (3 shorter events, 0.0 us)
Async XLA Ops:
  2.0 22.3 %copy-start = (bf16[256,1024]{1,0:T(8,128)(2,1)S(1)}, bf16[256,1024]{1,0:T(8,128)(2,1)}, u32[]{:S(2)}) copy-start(bf16[256,1024]{1,0:T(8,128)(2,1)} %q_ref.3) | copy-start | bytes 1572868
  2.0 5.9 %collective-permute-start = (bf16[128,128]{1,0:T(8,128)(2,1)S(1)}, bf16[128,128]{1,0:T(8,128)(2,1)S(1)}, u32[]{:S(2)}, u32[]{:S(2)}) collective-permute-start(bf16[128,128]{1,0:T(8,128)(2,1)S(1)} %get-tuple-element.24), channel_id=1, source_target_pairs={{0,6},{2,4},{4,2},{6,0},{1,7},{3,5},{5,3},{7,1},{8,14},{10,12},{12... | collective-permute-start | bytes 98312 | tf_op jit(solution)/shard_map/ppermute | solution.py:166
  6.0 3.9 %collective-permute-start.1 = (bf16[128,128]{1,0:T(8,128)(2,1)S(1)}, bf16[128,128]{1,0:T(8,128)(2,1)S(1)}, u32[]{:S(2)}, u32[]{:S(2)}) collective-permute-start(bf16[128,128]{1,0:T(8,128)(2,1)S(1)} %get-tuple-element.25), channel_id=1, source_target_pairs={{0,4},{2,6},{4,0},{6,2},{1,5},{3,7},{5,1},{7,3},{8,12},{10,14},{12... | collective-permute-start | bytes 98312 | tf_op jit(solution)/shard_map/ppermute | solution.py:166
  6.5 3.9 %collective-permute-start.2 = (bf16[128,128]{1,0:T(8,128)(2,1)S(1)}, bf16[128,128]{1,0:T(8,128)(2,1)S(1)}, u32[]{:S(2)}, u32[]{:S(2)}) collective-permute-start(bf16[128,128]{1,0:T(8,128)(2,1)S(1)} %get-tuple-element.26), channel_id=1, source_target_pairs={{0,2},{2,0},{4,6},{6,4},{1,3},{3,1},{5,7},{7,5},{8,10},{10,8},{12,... | collective-permute-start | bytes 98312 | tf_op jit(solution)/shard_map/ppermute | solution.py:166
  10.4 4.0 %collective-permute-start.3 = (bf16[128,128]{1,0:T(8,128)(2,1)S(1)}, bf16[128,128]{1,0:T(8,128)(2,1)S(1)}, u32[]{:S(2)}, u32[]{:S(2)}) collective-permute-start(bf16[128,128]{1,0:T(8,128)(2,1)S(1)} %get-tuple-element.29), channel_id=1, source_target_pairs={{0,8},{8,0},{16,24},{24,16},{1,9},{9,1},{17,25},{25,17},{2,10},{10... | collective-permute-start | bytes 98312 | tf_op jit(solution)/shard_map/ppermute | solution.py:181
  14.4 4.9 %collective-permute-start.4 = (bf16[128,128]{1,0:T(8,128)(2,1)S(1)}, bf16[128,128]{1,0:T(8,128)(2,1)S(1)}, u32[]{:S(2)}, u32[]{:S(2)}) collective-permute-start(bf16[128,128]{1,0:T(8,128)(2,1)S(1)} %get-tuple-element.32), channel_id=1, source_target_pairs={{0,16},{8,24},{16,0},{24,8},{1,17},{9,25},{17,1},{25,9},{2,18},{10... | collective-permute-start | bytes 98312 | tf_op jit(solution)/shard_map/ppermute | solution.py:181
  19.3 1.3 %collective-permute-start.5 = (f32[128,128]{1,0:T(8,128)S(1)}, f32[128,128]{1,0:T(8,128)S(1)}, u32[]{:S(2)}, u32[]{:S(2)}) collective-permute-start(f32[128,128]{1,0:T(8,128)S(1)} %get-tuple-element.34), channel_id=1, source_target_pairs={{0,1},{1,0},{2,3},{3,2},{4,5},{5,4},{6,7},{7,6},{8,9},{9,8},{10,11... | collective-permute-start | bytes 196616 | tf_op jit(solution)/shard_map/ppermute | solution.py:187
  20.7 5.0 %collective-permute-start.6 = (bf16[128,128]{1,0:T(8,128)(2,1)S(1)}, bf16[128,128]{1,0:T(8,128)(2,1)S(1)}, u32[]{:S(2)}, u32[]{:S(2)}) collective-permute-start(bf16[128,128]{1,0:T(8,128)(2,1)S(1)} %get-tuple-element.35), channel_id=1, source_target_pairs={{0,6},{2,4},{4,2},{6,0},{1,7},{3,5},{5,3},{7,1},{8,14},{10,12},{12... | collective-permute-start | bytes 98312 | tf_op jit(solution)/shard_map/ppermute | solution.py:166
  22.3 3.9 %collective-permute-start.7 = (bf16[128,128]{1,0:T(8,128)(2,1)S(1)}, bf16[128,128]{1,0:T(8,128)(2,1)S(1)}, u32[]{:S(2)}, u32[]{:S(2)}) collective-permute-start(bf16[128,128]{1,0:T(8,128)(2,1)S(1)} %get-tuple-element.36), channel_id=1, source_target_pairs={{0,4},{2,6},{4,0},{6,2},{1,5},{3,7},{5,1},{7,3},{8,12},{10,14},{12... | collective-permute-start | bytes 98312 | tf_op jit(solution)/shard_map/ppermute | solution.py:166
  22.7 3.9 %collective-permute-start.8 = (bf16[128,128]{1,0:T(8,128)(2,1)S(1)}, bf16[128,128]{1,0:T(8,128)(2,1)S(1)}, u32[]{:S(2)}, u32[]{:S(2)}) collective-permute-start(bf16[128,128]{1,0:T(8,128)(2,1)S(1)} %get-tuple-element.37), channel_id=1, source_target_pairs={{0,2},{2,0},{4,6},{6,4},{1,3},{3,1},{5,7},{7,5},{8,10},{10,8},{12,... | collective-permute-start | bytes 98312 | tf_op jit(solution)/shard_map/ppermute | solution.py:166

commit v12 on v9

--- a/solution.py
+++ b/solution.py
@@ -12,6 +12,7 @@
 PAIRS = HEADS // 2
 LANES = 2 * HEAD_DIM
 SLABS = 4
+HALVES = 2
 SLAB = 256
 VMEM = pl.BlockSpec(memory_space=pltpu.VMEM)
 BF16 = jnp.bfloat16
@@ -32,12 +33,16 @@
 
 def states_kernel(k_hbm, v_hbm, *refs):
     *outs, k_ref, v_ref, states, arrived = refs
+    rows = k_ref.shape[0] // HALVES
     copies = []
     for s in range(SLABS):
         lanes = slice(s * SLAB, (s + 1) * SLAB)
-        copies.append([
-            pltpu.make_async_copy(k_hbm.at[:, lanes], k_ref.at[:, lanes], arrived.at[0, s]),
-            pltpu.make_async_copy(v_hbm.at[:, lanes], v_ref.at[:, lanes], arrived.at[1, s])])
+        copies.append([])
+        for r in range(HALVES):
+            part = (pl.ds(r * rows, rows), lanes)
+            copies[-1] += [
+                pltpu.make_async_copy(k_hbm.at[part], k_ref.at[part], arrived.at[0, s, r]),
+                pltpu.make_async_copy(v_hbm.at[part], v_ref.at[part], arrived.at[1, s, r])]
         for copy in copies[-1]:
             copy.start()
     first = first_head((HEAD_DIM, LANES))
@@ -137,10 +142,7 @@
         inter = jnp.dot(q_ref[:, lanes], prefix, preferred_element_type=F32)
         total = intra_ref[:, lanes] + inter
         square = total * total
-        high = square.astype(BF16)
-        low = (square - high.astype(F32)).astype(BF16)
-        sums = (jnp.dot(high, ones, preferred_element_type=F32)
-                + jnp.dot(low, ones, preferred_element_type=F32))
+        sums = jnp.dot(square.astype(BF16), ones, preferred_element_type=F32)
         out_ref[:, lanes] = (total * lax.rsqrt(sums * (1.0 / HEAD_DIM) + 1e-6)).astype(out_ref.dtype)
         copies.append(pltpu.make_async_copy(out_ref.at[:, lanes], out_hbm.at[:, lanes], sent.at[s]))
         copies[-1].start()
@@ -176,7 +178,7 @@
         states_kernel,
         [(share, F32)] + [(share, BF16)] * (inner - 1) + [(keys.shape, keys.dtype), (values.shape, values.dtype)],
         keys, values, flops=2 * rows * LANES * LANES * PAIRS, source=pltpu.HBM,
-        scratch=[pltpu.VMEM((inner,) + share, F32), pltpu.SemaphoreType.DMA((2, SLABS))])
+        scratch=[pltpu.VMEM((inner,) + share, F32), pltpu.SemaphoreType.DMA((2, SLABS, HALVES))])
     mine = swapped([own] + states, "inner", own)
     total, sent = call(totals_kernel, [(share, F32), (share, BF16)], *mine)
     totals = swapped([sent] * planes, "outer", total)

time: 28 us -> 27.8 us (level)
  no operation moved by 1% of the time
where the time goes in v12:
time: 27.8 us; the launch traced here: 27.6 us
  starting transfers between devices  12.7 us (46%)
  waiting for transfers between devices  9.96 us (36%)
  Pallas kernels  4.9 us (18%)
    ppermute x9, starting transfers between devices, swapped(): lax.ppermute(arrays[d], axis, [(i, i ^ d) for i in range(size)])  12.6 us
    ppermute x9, waiting for transfers between devices, swapped(): lax.ppermute(arrays[d], axis, [(i, i ^ d) for i in range(size)])  8.72 us
    pallas_call x6, Pallas kernels, call(): pl.pallas_call(kernel, out_shape=[result(shape, dtype) for shape, dtype i...  4.9 us
    ppermute x1, waiting for transfers between devices, per_device(): lax.ppermute(whole, 'chain', [(c, c ^ d) for c in range(chains)])  1.24 us
  transfers between devices with their start and end apart: 10, of which 8 were waited for; matrix products, arithmetic and copies ran while one was open for 0% of the time, Pallas kernels for 5%

profile of v12, /device:TPU:0, one launch (start us, length us, event | category | flops | bytes accessed | tf_op | source)
XLA Modules:
  0.0 27.6 jit_solution(15686149734845300394)
XLA Ops:
  0.0 2.0 %shard_map.37 = (f32[128,128]{1,0:T(8,128)S(1)}, bf16[128,128]{1,0:T(8,128)(2,1)S(1)}, bf16[128,128]{1,0:T(8,128)(2,1)S(1)}, bf16[128,128]{1,0:T(8,128)(2,1)S(1)...) custom-call(bf16[256,1024]{1,0:T(8,128)(2,1)} %k_hbm.1, bf16[256,1024]{1,0:T(8,128)(2,1)} %v_hbm.1), custom_call_target="tpu_custom_call" | custom-call | flops 67108864 | bytes 1048576 | tf_op jit(solution)/shard_map/pallas_call | solution.py:157
  2.1 0.0 copy-start
  2.1 4.0 %collective-permute-start = (bf16[128,128]{1,0:T(8,128)(2,1)S(1)}, bf16[128,128]{1,0:T(8,128)(2,1)S(1)}, u32[]{:S(2)}, u32[]{:S(2)}) collective-permute-start(bf16[128,128]{1,0:T(8,128)(2,1)S(1)} %get-tuple-element.21), channel_id=1, source_target_pairs={{0,6},{2,4},{4,2},{6,0},{1,7},{3,5},{5,3},{7,1},{8,14},{10,12},{12... | collective-permute-start | bytes 98312 | tf_op jit(solution)/shard_map/ppermute | solution.py:171
  6.0 0.5 %collective-permute-start.1 = (bf16[128,128]{1,0:T(8,128)(2,1)S(1)}, bf16[128,128]{1,0:T(8,128)(2,1)S(1)}, u32[]{:S(2)}, u32[]{:S(2)}) collective-permute-start(bf16[128,128]{1,0:T(8,128)(2,1)S(1)} %get-tuple-element.22), channel_id=1, source_target_pairs={{0,4},{2,6},{4,0},{6,2},{1,5},{3,7},{5,1},{7,3},{8,12},{10,14},{12... | collective-permute-start | bytes 98312 | tf_op jit(solution)/shard_map/ppermute | solution.py:171
  6.5 0.1 collective-permute-start.2
  6.7 1.3 %collective-permute-done.refs_0_ = bf16[128,128]{1,0:T(8,128)(2,1)S(1)} collective-permute-done((bf16[128,128]{1,0:T(8,128)(2,1)S(1)}, bf16[128,128]{1,0:T(8,128)(2,1)S(1)}, u32[]{:S(2)}, u32[]{:S(2)}) %collective-permute-start) | collective-permute-done | bytes 32800 | tf_op jit(solution)/shard_map/ppermute | solution.py:171
  7.9 2.0 %collective-permute-done.1.refs_1_ = bf16[128,128]{1,0:T(8,128)(2,1)S(1)} collective-permute-done((bf16[128,128]{1,0:T(8,128)(2,1)S(1)}, bf16[128,128]{1,0:T(8,128)(2,1)S(1)}, u32[]{:S(2)}, u32[]{:S(2)}) %collective-permute-start.1) | collective-permute-done | bytes 32800 | tf_op jit(solution)/shard_map/ppermute | solution.py:171
  9.9 0.5 %collective-permute-done.2.refs_2_ = bf16[128,128]{1,0:T(8,128)(2,1)S(1)} collective-permute-done((bf16[128,128]{1,0:T(8,128)(2,1)S(1)}, bf16[128,128]{1,0:T(8,128)(2,1)S(1)}, u32[]{:S(2)}, u32[]{:S(2)}) %collective-permute-start.2) | collective-permute-done | bytes 32800 | tf_op jit(solution)/shard_map/ppermute | solution.py:171
  10.5 3.7 %collective-permute-start.3 = (bf16[128,128]{1,0:T(8,128)(2,1)S(1)}, bf16[128,128]{1,0:T(8,128)(2,1)S(1)}, u32[]{:S(2)}, u32[]{:S(2)}) collective-permute-start(bf16[128,128]{1,0:T(8,128)(2,1)S(1)} %get-tuple-element.25), channel_id=1, source_target_pairs={{0,24},{8,16},{16,8},{24,0},{1,25},{9,17},{17,9},{25,1},{2,26},{10... | collective-permute-start | bytes 98312 | tf_op jit(solution)/shard_map/ppermute | solution.py:171
  14.1 0.0 collective-permute-start.4
  14.1 0.8 %collective-permute-start.5 = (bf16[128,128]{1,0:T(8,128)(2,1)S(1)}, bf16[128,128]{1,0:T(8,128)(2,1)S(1)}, u32[]{:S(2)}, u32[]{:S(2)}) collective-permute-start(bf16[128,128]{1,0:T(8,128)(2,1)S(1)} %get-tuple-element.25), channel_id=1, source_target_pairs={{0,8},{8,0},{16,24},{24,16},{1,9},{9,1},{17,25},{25,17},{2,10},{10... | collective-permute-start | bytes 98312 | tf_op jit(solution)/shard_map/ppermute | solution.py:171
  14.9 1.3 %collective-permute-done.3.refs_0_ = bf16[128,128]{1,0:T(8,128)(2,1)S(1)} collective-permute-done((bf16[128,128]{1,0:T(8,128)(2,1)S(1)}, bf16[128,128]{1,0:T(8,128)(2,1)S(1)}, u32[]{:S(2)}, u32[]{:S(2)}) %collective-permute-start.3) | collective-permute-done | bytes 32800 | tf_op jit(solution)/shard_map/ppermute | solution.py:171
  16.2 2.7 %collective-permute-done.4.refs_1_ = bf16[128,128]{1,0:T(8,128)(2,1)S(1)} collective-permute-done((bf16[128,128]{1,0:T(8,128)(2,1)S(1)}, bf16[128,128]{1,0:T(8,128)(2,1)S(1)}, u32[]{:S(2)}, u32[]{:S(2)}) %collective-permute-start.4) | collective-permute-done | bytes 32800 | tf_op jit(solution)/shard_map/ppermute | solution.py:171
  18.9 0.0 collective-permute-done.5.refs_2_
  19.0 0.1 collective-permute-start.6
  19.1 1.2 %collective-permute-done.6.refs_5_ = f32[128,128]{1,0:T(8,128)S(1)} collective-permute-done((f32[128,128]{1,0:T(8,128)S(1)}, f32[128,128]{1,0:T(8,128)S(1)}, u32[]{:S(2)}, u32[]{:S(2)}) %collective-permute-start.6) | collective-permute-done | bytes 65568 | tf_op jit(solution)/shard_map/ppermute | solution.py:186
  20.3 0.1 shard_map.41
  20.4 1.6 %collective-permute-start.7 = (bf16[128,128]{1,0:T(8,128)(2,1)S(1)}, bf16[128,128]{1,0:T(8,128)(2,1)S(1)}, u32[]{:S(2)}, u32[]{:S(2)}) collective-permute-start(bf16[128,128]{1,0:T(8,128)(2,1)S(1)} %get-tuple-element.29), channel_id=1, source_target_pairs={{0,6},{2,4},{4,2},{6,0},{1,7},{3,5},{5,3},{7,1},{8,14},{10,12},{12... | collective-permute-start | bytes 98312 | tf_op jit(solution)/shard_map/ppermute | solution.py:171
  21.9 0.5 %collective-permute-start.8 = (bf16[128,128]{1,0:T(8,128)(2,1)S(1)}, bf16[128,128]{1,0:T(8,128)(2,1)S(1)}, u32[]{:S(2)}, u32[]{:S(2)}) collective-permute-start(bf16[128,128]{1,0:T(8,128)(2,1)S(1)} %get-tuple-element.30), channel_id=1, source_target_pairs={{0,4},{2,6},{4,0},{6,2},{1,5},{3,7},{5,1},{7,3},{8,12},{10,14},{12... | collective-permute-start | bytes 98312 | tf_op jit(solution)/shard_map/ppermute | solution.py:171
  22.4 1.5 %collective-permute-start.9 = (bf16[128,128]{1,0:T(8,128)(2,1)S(1)}, bf16[128,128]{1,0:T(8,128)(2,1)S(1)}, u32[]{:S(2)}, u32[]{:S(2)}) collective-permute-start(bf16[128,128]{1,0:T(8,128)(2,1)S(1)} %get-tuple-element.31), channel_id=1, source_target_pairs={{0,2},{2,0},{4,6},{6,4},{1,3},{3,1},{5,7},{7,5},{8,10},{10,8},{12,... | collective-permute-start | bytes 98312 | tf_op jit(solution)/shard_map/ppermute | solution.py:171
  23.9 0.0 copy-done
  23.9 1.5 %shard_map.38.intra_ref = f32[256,1024]{1,0:T(8,128)S(1)} custom-call(bf16[256,1024]{1,0:T(8,128)(2,1)S(1)} %copy-done, bf16[256,1024]{1,0:T(8,128)(2,1)S(1)} %get-tuple-element.19.k_ref, bf16[256,1024]{1,0:T(8,128)(2,1)S(1)} %get-tuple-element.20.v_ref), custom_call_target="tpu_custom_call" | custom-call | flops 268435456 | bytes 1572864 | tf_op jit(solution)/shard_map/pallas_call | solution.py:157
  25.4 0.0 collective-permute-done.7.refs_0_
  25.4 0.4 %collective-permute-done.8.refs_1_ = bf16[128,128]{1,0:T(8,128)(2,1)S(1)} collective-permute-done((bf16[128,128]{1,0:T(8,128)(2,1)S(1)}, bf16[128,128]{1,0:T(8,128)(2,1)S(1)}, u32[]{:S(2)}, u32[]{:S(2)}) %collective-permute-start.8) | collective-permute-done | bytes 32800 | tf_op jit(solution)/shard_map/ppermute | solution.py:171
  25.8 0.5 %collective-permute-done.9.refs_2_ = bf16[128,128]{1,0:T(8,128)(2,1)S(1)} collective-permute-done((bf16[128,128]{1,0:T(8,128)(2,1)S(1)}, bf16[128,128]{1,0:T(8,128)(2,1)S(1)}, u32[]{:S(2)}, u32[]{:S(2)}) %collective-permute-start.9) | collective-permute-done | bytes 32800 | tf_op jit(solution)/shard_map/ppermute | solution.py:171
  26.4 1.3 %shard_map.42 = bf16[256,1024]{1,0:T(8,128)(2,1)} custom-call(bf16[256,1024]{1,0:T(8,128)(2,1)S(1)} %copy-done, f32[256,1024]{1,0:T(8,128)S(1)} %shard_map.38.intra_ref, bf16[128,128]{1,0:T(8,128)(2,1)S(1)} %collective-permute-done.7.refs_0_, bf16[128,128]{1,0:T(8,128)(2,1)S(1)} %collective-permute-done.8.refs_1_, ...), custom_call_target="tpu_custom_call" | custom-call | flops 134217728 | bytes 1703936 | tf_op jit(solution)/shard_map/pallas_call | solution.py:157
  (2 shorter events, 0.1 us)
Async XLA Ops:
  2.1 21.9 %copy-start = (bf16[256,1024]{1,0:T(8,128)(2,1)S(1)}, bf16[256,1024]{1,0:T(8,128)(2,1)}, u32[]{:S(2)}) copy-start(bf16[256,1024]{1,0:T(8,128)(2,1)} %q_ref.3) | copy-start | bytes 1572868
  2.1 5.9 %collective-permute-start = (bf16[128,128]{1,0:T(8,128)(2,1)S(1)}, bf16[128,128]{1,0:T(8,128)(2,1)S(1)}, u32[]{:S(2)}, u32[]{:S(2)}) collective-permute-start(bf16[128,128]{1,0:T(8,128)(2,1)S(1)} %get-tuple-element.21), channel_id=1, source_target_pairs={{0,6},{2,4},{4,2},{6,0},{1,7},{3,5},{5,3},{7,1},{8,14},{10,12},{12... | collective-permute-start | bytes 98312 | tf_op jit(solution)/shard_map/ppermute | solution.py:171
  6.0 3.9 %collective-permute-start.1 = (bf16[128,128]{1,0:T(8,128)(2,1)S(1)}, bf16[128,128]{1,0:T(8,128)(2,1)S(1)}, u32[]{:S(2)}, u32[]{:S(2)}) collective-permute-start(bf16[128,128]{1,0:T(8,128)(2,1)S(1)} %get-tuple-element.22), channel_id=1, source_target_pairs={{0,4},{2,6},{4,0},{6,2},{1,5},{3,7},{5,1},{7,3},{8,12},{10,14},{12... | collective-permute-start | bytes 98312 | tf_op jit(solution)/shard_map/ppermute | solution.py:171
  6.5 3.9 %collective-permute-start.2 = (bf16[128,128]{1,0:T(8,128)(2,1)S(1)}, bf16[128,128]{1,0:T(8,128)(2,1)S(1)}, u32[]{:S(2)}, u32[]{:S(2)}) collective-permute-start(bf16[128,128]{1,0:T(8,128)(2,1)S(1)} %get-tuple-element.23), channel_id=1, source_target_pairs={{0,2},{2,0},{4,6},{6,4},{1,3},{3,1},{5,7},{7,5},{8,10},{10,8},{12,... | collective-permute-start | bytes 98312 | tf_op jit(solution)/shard_map/ppermute | solution.py:171
  10.5 5.8 %collective-permute-start.3 = (bf16[128,128]{1,0:T(8,128)(2,1)S(1)}, bf16[128,128]{1,0:T(8,128)(2,1)S(1)}, u32[]{:S(2)}, u32[]{:S(2)}) collective-permute-start(bf16[128,128]{1,0:T(8,128)(2,1)S(1)} %get-tuple-element.25), channel_id=1, source_target_pairs={{0,24},{8,16},{16,8},{24,0},{1,25},{9,17},{17,9},{25,1},{2,26},{10... | collective-permute-start | bytes 98312 | tf_op jit(solution)/shard_map/ppermute | solution.py:171
  14.1 4.8 %collective-permute-start.4 = (bf16[128,128]{1,0:T(8,128)(2,1)S(1)}, bf16[128,128]{1,0:T(8,128)(2,1)S(1)}, u32[]{:S(2)}, u32[]{:S(2)}) collective-permute-start(bf16[128,128]{1,0:T(8,128)(2,1)S(1)} %get-tuple-element.25), channel_id=1, source_target_pairs={{0,16},{8,24},{16,0},{24,8},{1,17},{9,25},{17,1},{25,9},{2,18},{10... | collective-permute-start | bytes 98312 | tf_op jit(solution)/shard_map/ppermute | solution.py:171
  14.1 4.8 %collective-permute-start.5 = (bf16[128,128]{1,0:T(8,128)(2,1)S(1)}, bf16[128,128]{1,0:T(8,128)(2,1)S(1)}, u32[]{:S(2)}, u32[]{:S(2)}) collective-permute-start(bf16[128,128]{1,0:T(8,128)(2,1)S(1)} %get-tuple-element.25), channel_id=1, source_target_pairs={{0,8},{8,0},{16,24},{24,16},{1,9},{9,1},{17,25},{25,17},{2,10},{10... | collective-permute-start | bytes 98312 | tf_op jit(solution)/shard_map/ppermute | solution.py:171
  19.0 1.3 %collective-permute-start.6 = (f32[128,128]{1,0:T(8,128)S(1)}, f32[128,128]{1,0:T(8,128)S(1)}, u32[]{:S(2)}, u32[]{:S(2)}) collective-permute-start(f32[128,128]{1,0:T(8,128)S(1)} %get-tuple-element.28), channel_id=1, source_target_pairs={{0,1},{1,0},{2,3},{3,2},{4,5},{5,4},{6,7},{7,6},{8,9},{9,8},{10,11... | collective-permute-start | bytes 196616 | tf_op jit(solution)/shard_map/ppermute | solution.py:186
  20.4 5.0 %collective-permute-start.7 = (bf16[128,128]{1,0:T(8,128)(2,1)S(1)}, bf16[128,128]{1,0:T(8,128)(2,1)S(1)}, u32[]{:S(2)}, u32[]{:S(2)}) collective-permute-start(bf16[128,128]{1,0:T(8,128)(2,1)S(1)} %get-tuple-element.29), channel_id=1, source_target_pairs={{0,6},{2,4},{4,2},{6,0},{1,7},{3,5},{5,3},{7,1},{8,14},{10,12},{12... | collective-permute-start | bytes 98312 | tf_op jit(solution)/shard_map/ppermute | solution.py:171
  21.9 3.9 %collective-permute-start.8 = (bf16[128,128]{1,0:T(8,128)(2,1)S(1)}, bf16[128,128]{1,0:T(8,128)(2,1)S(1)}, u32[]{:S(2)}, u32[]{:S(2)}) collective-permute-start(bf16[128,128]{1,0:T(8,128)(2,1)S(1)} %get-tuple-element.30), channel_id=1, source_target_pairs={{0,4},{2,6},{4,0},{6,2},{1,5},{3,7},{5,1},{7,3},{8,12},{10,14},{12... | collective-permute-start | bytes 98312 | tf_op jit(solution)/shard_map/ppermute | solution.py:171
  22.4 3.9 %collective-permute-start.9 = (bf16[128,128]{1,0:T(8,128)(2,1)S(1)}, bf16[128,128]{1,0:T(8,128)(2,1)S(1)}, u32[]{:S(2)}, u32[]{:S(2)}) collective-permute-start(bf16[128,128]{1,0:T(8,128)(2,1)S(1)} %get-tuple-element.31), channel_id=1, source_target_pairs={{0,2},{2,0},{4,6},{6,4},{1,3},{3,1},{5,7},{7,5},{8,10},{10,8},{12,... | collective-permute-start | bytes 98312 | tf_op jit(solution)/shard_map/ppermute | solution.py:171

commit v13 on v12

--- a/solution.py
+++ b/solution.py
@@ -184,11 +184,23 @@
     totals = swapped([sent] * planes, "outer", total)
     below, whole = call(planes_kernel, [(share, F32)] * 2, *totals)
     groups = [lax.ppermute(whole, "chain", [(c, c ^ d) for c in range(chains)]) for d in range(1, chains)]
-    before = call(functools.partial(prefix_kernel, inner), [(share, BF16)] * inner, *mine, below, *groups,
-                  scratch=[pltpu.VMEM((inner,) + share, F32)])
-    prefix = swapped(before, "inner", before[0])
-    intra = call(intra_kernel, (queries.shape, F32), queries, keys, values,
-                 flops=4 * rows * rows * HEADS * HEAD_DIM)
+    leads = lax.axis_index("chain") == 0
+
+    def inside(queries, keys, values):
+        return call(intra_kernel, (queries.shape, F32), queries, keys, values,
+                    flops=4 * rows * rows * HEADS * HEAD_DIM)
+
+    def way_back(*bases):
+        before = call(functools.partial(prefix_kernel, inner), [(share, BF16)] * inner, *mine, *bases,
+                      scratch=[pltpu.VMEM((inner,) + share, F32)])
+        return swapped(before, "inner", before[0])
+
+    prefix, intra = lax.cond(
+        leads,
+        lambda: (way_back(below), inside(queries, keys, values)),
+        lambda: ([jnp.zeros(share, BF16)] * inner, inside(queries, keys, values)))
+    prefix, groups = lax.optimization_barrier((prefix, groups))
+    prefix = lax.cond(leads, lambda: prefix, lambda: way_back(below, *groups))
     return call(functools.partial(attend_kernel, inner), (queries.shape, BF16), queries, intra, *prefix,
                 result=pltpu.HBM, flops=2 * rows * SLAB * HEADS * HEAD_DIM,
                 scratch=[pltpu.VMEM(queries.shape, BF16), pltpu.VMEM((inner,) + share, BF16),

time: 27.8 us -> 30.6 us (1.10)
  local copies, waits for them, and re-layouts: 0.01 us -> 2.28 us
  waiting for transfers between devices: 9.96 us -> 10.3 us
    cond x0 -> x3, local copies, waits for them, and re-layouts: none -> 2.28 us
    ppermute x9, waiting for transfers between devices: 8.72 us -> 10.3 us  [swapped(): lax.ppermute(arrays[d], axis, [(i, i ^ d) for i in range(size)])]
    ppermute x1, waiting for transfers between devices: 1.24 us -> 0.01 us  [per_device(): lax.ppermute(whole, 'chain', [(c, c ^ d) for c in range(chains)])]
  transfers between devices with their start and end apart: 10 -> 10, of which waited for: 8 -> 7; matrix products, arithmetic and copies ran while one was open for 0% -> 0% of each run, Pallas kernels for 5% -> 5%
where the time goes in v13:
time: 30.6 us; the launch traced here: 30.3 us
  starting transfers between devices  12.7 us (42%)
  waiting for transfers between devices  10.3 us (34%)
  Pallas kernels  4.96 us (16%)
  local copies, waits for them, and re-layouts  2.28 us (7%)
    ppermute x9, starting transfers between devices, swapped(): lax.ppermute(arrays[d], axis, [(i, i ^ d) for i in range(size)])  12.6 us
    ppermute x9, waiting for transfers between devices, swapped(): lax.ppermute(arrays[d], axis, [(i, i ^ d) for i in range(size)])  10.3 us
    pallas_call x6, Pallas kernels, call(): pl.pallas_call(kernel, out_shape=[result(shape, dtype) for shape, dtype i...  4.96 us
    cond x3, local copies, waits for them, and re-layouts  2.28 us
  transfers between devices with their start and end apart: 10, of which 7 were waited for; matrix products, arithmetic and copies ran while one was open for 0% of the time, Pallas kernels for 5%

profile of v13, /device:TPU:0, one launch (start us, length us, event | category | flops | bytes accessed | tf_op | source)
XLA Modules:
  0.0 30.3 jit_solution(3053252772164458969)
XLA Ops:
  0.0 0.0 copy-start
  0.0 2.1 %shard_map.37 = (f32[128,128]{1,0:T(8,128)S(1)}, bf16[128,128]{1,0:T(8,128)(2,1)S(1)}, bf16[128,128]{1,0:T(8,128)(2,1)S(1)}, bf16[128,128]{1,0:T(8,128)(2,1)S(1)...) custom-call(bf16[256,1024]{1,0:T(8,128)(2,1)} %k_hbm.1, bf16[256,1024]{1,0:T(8,128)(2,1)} %v_hbm.1), custom_call_target="tpu_custom_call" | custom-call | flops 67108864 | bytes 1048576 | tf_op jit(solution)/shard_map/pallas_call | solution.py:157
  2.1 4.0 %collective-permute-start.6 = (bf16[128,128]{1,0:T(8,128)(2,1)S(1)}, bf16[128,128]{1,0:T(8,128)(2,1)S(1)}, u32[]{:S(2)}, u32[]{:S(2)}) collective-permute-start(bf16[128,128]{1,0:T(8,128)(2,1)S(1)} %get-tuple-element.98), channel_id=1, source_target_pairs={{0,6},{2,4},{4,2},{6,0},{1,7},{3,5},{5,3},{7,1},{8,14},{10,12},{12... | collective-permute-start | bytes 98312 | tf_op jit(solution)/shard_map/ppermute | solution.py:171
  6.1 0.5 %collective-permute-start.7 = (bf16[128,128]{1,0:T(8,128)(2,1)S(1)}, bf16[128,128]{1,0:T(8,128)(2,1)S(1)}, u32[]{:S(2)}, u32[]{:S(2)}) collective-permute-start(bf16[128,128]{1,0:T(8,128)(2,1)S(1)} %get-tuple-element.99), channel_id=1, source_target_pairs={{0,4},{2,6},{4,0},{6,2},{1,5},{3,7},{5,1},{7,3},{8,12},{10,14},{12... | collective-permute-start | bytes 98312 | tf_op jit(solution)/shard_map/ppermute | solution.py:171
  6.6 0.1 collective-permute-start.8
  6.7 1.3 %collective-permute-done.6.refs_0_ = bf16[128,128]{1,0:T(8,128)(2,1)S(1)} collective-permute-done((bf16[128,128]{1,0:T(8,128)(2,1)S(1)}, bf16[128,128]{1,0:T(8,128)(2,1)S(1)}, u32[]{:S(2)}, u32[]{:S(2)}) %collective-permute-start.6) | collective-permute-done | bytes 32800 | tf_op jit(solution)/shard_map/ppermute | solution.py:171
  8.0 2.0 %collective-permute-done.7.refs_1_ = bf16[128,128]{1,0:T(8,128)(2,1)S(1)} collective-permute-done((bf16[128,128]{1,0:T(8,128)(2,1)S(1)}, bf16[128,128]{1,0:T(8,128)(2,1)S(1)}, u32[]{:S(2)}, u32[]{:S(2)}) %collective-permute-start.7) | collective-permute-done | bytes 32800 | tf_op jit(solution)/shard_map/ppermute | solution.py:171
  10.0 0.5 %collective-permute-done.8.refs_2_ = bf16[128,128]{1,0:T(8,128)(2,1)S(1)} collective-permute-done((bf16[128,128]{1,0:T(8,128)(2,1)S(1)}, bf16[128,128]{1,0:T(8,128)(2,1)S(1)}, u32[]{:S(2)}, u32[]{:S(2)}) %collective-permute-start.8) | collective-permute-done | bytes 32800 | tf_op jit(solution)/shard_map/ppermute | solution.py:171
  10.5 1.6 %collective-permute-start.11 = (bf16[128,128]{1,0:T(8,128)(2,1)S(1)}, bf16[128,128]{1,0:T(8,128)(2,1)S(1)}, u32[]{:S(2)}, u32[]{:S(2)}) collective-permute-start(bf16[128,128]{1,0:T(8,128)(2,1)S(1)} %get-tuple-element.102), channel_id=1, source_target_pairs={{0,8},{8,0},{16,24},{24,16},{1,9},{9,1},{17,25},{25,17},{2,10},{10... | collective-permute-start | bytes 98312 | tf_op jit(solution)/shard_map/ppermute | solution.py:171
  12.2 2.6 %collective-permute-start.10 = (bf16[128,128]{1,0:T(8,128)(2,1)S(1)}, bf16[128,128]{1,0:T(8,128)(2,1)S(1)}, u32[]{:S(2)}, u32[]{:S(2)}) collective-permute-start(bf16[128,128]{1,0:T(8,128)(2,1)S(1)} %get-tuple-element.102), channel_id=1, source_target_pairs={{0,16},{8,24},{16,0},{24,8},{1,17},{9,25},{17,1},{25,9},{2,18},{10... | collective-permute-start | bytes 98312 | tf_op jit(solution)/shard_map/ppermute | solution.py:171
  14.7 0.2 collective-permute-start.9
  15.0 0.0 collective-permute-done.11.refs_2_
  15.0 2.6 %collective-permute-done.10.refs_1_ = bf16[128,128]{1,0:T(8,128)(2,1)S(1)} collective-permute-done((bf16[128,128]{1,0:T(8,128)(2,1)S(1)}, bf16[128,128]{1,0:T(8,128)(2,1)S(1)}, u32[]{:S(2)}, u32[]{:S(2)}) %collective-permute-start.10) | collective-permute-done | bytes 32800 | tf_op jit(solution)/shard_map/ppermute | solution.py:171
  17.6 2.9 %collective-permute-done.9.refs_0_ = bf16[128,128]{1,0:T(8,128)(2,1)S(1)} collective-permute-done((bf16[128,128]{1,0:T(8,128)(2,1)S(1)}, bf16[128,128]{1,0:T(8,128)(2,1)S(1)}, u32[]{:S(2)}, u32[]{:S(2)}) %collective-permute-start.9) | collective-permute-done | bytes 32800 | tf_op jit(solution)/shard_map/ppermute | solution.py:171
  20.5 0.1 collective-permute-start.12
  20.6 0.0 copy-done
  20.6 6.2 %conditional.2 = (bf16[128,128]{1,0:T(8,128)(2,1)}, bf16[128,128]{1,0:T(8,128)(2,1)}, bf16[128,128]{1,0:T(8,128)(2,1)}, bf16[128,128]{1,0:T(8,128)(2,1)S(1)}, f32[256,1024]{1,0:T(8,128)S(1)}) conditional(s32[]{:T(128)} %convert_element_type.4, (bf16[256,1024]{1,0:T(8,128)(2,1)S(1)}, bf16[256,1024]{1,0:T(8,128)(2,1)S(1)}, ...), branch_computations={%region_0.0_spmd, %region_1.0_spmd} | conditional | flops 268435456 | bytes 2195616 | solution.py:198
  20.6 0.1 branch_1_fun.2
  20.7 1.6 %collective-permute-start = (bf16[128,128]{1,0:T(8,128)(2,1)S(1)}, bf16[128,128]{1,0:T(8,128)(2,1)}, u32[]{:S(2)}, u32[]{:S(2)}) collective-permute-start(bf16[128,128]{1,0:T(8,128)(2,1)S(1)} %get-tuple-element.55), channel_id=1, source_target_pairs={{0,6},{2,4},{4,2},{6,0},{1,7},{3,5},{5,3},{7,1},{8,14},{10,12},{12... | collective-permute-start | bytes 98312 | tf_op jit(solution)/shard_map/cond/branch_1_fun/ppermute | solution.py:171
  22.2 0.5 %collective-permute-start.1 = (bf16[128,128]{1,0:T(8,128)(2,1)S(1)}, bf16[128,128]{1,0:T(8,128)(2,1)}, u32[]{:S(2)}, u32[]{:S(2)}) collective-permute-start(bf16[128,128]{1,0:T(8,128)(2,1)S(1)} %get-tuple-element.56), channel_id=1, source_target_pairs={{0,4},{2,6},{4,0},{6,2},{1,5},{3,7},{5,1},{7,3},{8,12},{10,14},{12... | collective-permute-start | bytes 98312 | tf_op jit(solution)/shard_map/cond/branch_1_fun/ppermute | solution.py:171
  22.7 1.5 %collective-permute-start.2 = (bf16[128,128]{1,0:T(8,128)(2,1)S(1)}, bf16[128,128]{1,0:T(8,128)(2,1)}, u32[]{:S(2)}, u32[]{:S(2)}) collective-permute-start(bf16[128,128]{1,0:T(8,128)(2,1)S(1)} %get-tuple-element.57), channel_id=1, source_target_pairs={{0,2},{2,0},{4,6},{6,4},{1,3},{3,1},{5,7},{7,5},{8,10},{10,8},{12,... | collective-permute-start | bytes 98312 | tf_op jit(solution)/shard_map/cond/branch_1_fun/ppermute | solution.py:171
  24.2 1.5 %branch_1_fun.3 = f32[256,1024]{1,0:T(8,128)S(1)} custom-call(bf16[256,1024]{1,0:T(8,128)(2,1)S(1)} %get-tuple-element.59.q_ref, bf16[256,1024]{1,0:T(8,128)(2,1)S(1)} %get-tuple-element.60.k_ref, bf16[256,1024]{1,0:T(8,128)(2,1)S(1)} %get-tuple-element.61.v_ref), custom_call_target="tpu_custom_call" | custom-call | flops 268435456 | bytes 1572864 | tf_op jit(solution)/shard_map/cond/branch_1_fun/pallas_call | solution.py:157
  25.7 0.0 collective-permute-done
  25.7 0.5 %collective-permute-done.1 = bf16[128,128]{1,0:T(8,128)(2,1)} collective-permute-done((bf16[128,128]{1,0:T(8,128)(2,1)S(1)}, bf16[128,128]{1,0:T(8,128)(2,1)}, u32[]{:S(2)}, u32[]{:S(2)}) %collective-permute-start.1) | collective-permute-done | bytes 32800 | tf_op jit(solution)/shard_map/cond/branch_1_fun/ppermute | solution.py:171
  26.3 0.5 %collective-permute-done.2 = bf16[128,128]{1,0:T(8,128)(2,1)} collective-permute-done((bf16[128,128]{1,0:T(8,128)(2,1)S(1)}, bf16[128,128]{1,0:T(8,128)(2,1)}, u32[]{:S(2)}, u32[]{:S(2)}) %collective-permute-start.2) | collective-permute-done | bytes 32800 | tf_op jit(solution)/shard_map/cond/branch_1_fun/ppermute | solution.py:171
  26.8 0.0 collective-permute-done.12
  26.8 2.3 %conditional.3 = (bf16[128,128]{1,0:T(8,128)(2,1)S(1)}, bf16[128,128]{1,0:T(8,128)(2,1)S(1)}, bf16[128,128]{1,0:T(8,128)(2,1)S(1)}, bf16[128,128]{1,0:T(8,128)(2,1)S(1)}) conditional(s32[]{:T(128)} %convert_element_type.4, (bf16[128,128]{1,0:T(8,128)(2,1)S(1)}, bf16[128,128]{1,0:T(8,128)(2,1)S(1)}, bf16[128,128]{1,0:T(8,128)(2,1)S(1)}, ...), branch_computations={%region_2.0_spmd, %region_3.0_spmd} | conditional | bytes 688280 | solution.py:203
  26.8 0.8 %copy.18 = bf16[128,128]{1,0:T(8,128)(2,1)S(1)} copy(bf16[128,128]{1,0:T(8,128)(2,1)} %get-tuple-element.134) | data formatting | bytes 65536 | tf_op jit(solution)/shard_map/cond
  27.5 0.8 %copy.19 = bf16[128,128]{1,0:T(8,128)(2,1)S(1)} copy(bf16[128,128]{1,0:T(8,128)(2,1)} %get-tuple-element.135) | data formatting | bytes 65536 | tf_op jit(solution)/shard_map/cond
  28.3 0.8 %copy.20 = bf16[128,128]{1,0:T(8,128)(2,1)S(1)} copy(bf16[128,128]{1,0:T(8,128)(2,1)} %get-tuple-element.136) | data formatting | bytes 65536 | tf_op jit(solution)/shard_map/cond
  29.0 1.3 %shard_map.40 = bf16[256,1024]{1,0:T(8,128)(2,1)} custom-call(bf16[256,1024]{1,0:T(8,128)(2,1)S(1)} %copy-done, f32[256,1024]{1,0:T(8,128)S(1)} %get-tuple-element.105.intra_ref, bf16[128,128]{1,0:T(8,128)(2,1)S(1)} %get-tuple-element.116.refs_0_, bf16[128,128]{1,0:T(8,128)(2,1)S(1)} %get-tuple-element.117.refs_1_, ...), custom_call_target="tpu_custom_call" | custom-call | flops 134217728 | bytes 1703936 | tf_op jit(solution)/shard_map/pallas_call | solution.py:157
  (2 shorter events, 0.1 us)
Async XLA Ops:
  0.0 20.6 %copy-start = (bf16[256,1024]{1,0:T(8,128)(2,1)S(1)}, bf16[256,1024]{1,0:T(8,128)(2,1)}, u32[]{:S(2)}) copy-start(bf16[256,1024]{1,0:T(8,128)(2,1)} %q_ref.1) | copy-start | bytes 1572868
  2.1 5.9 %collective-permute-start.6 = (bf16[128,128]{1,0:T(8,128)(2,1)S(1)}, bf16[128,128]{1,0:T(8,128)(2,1)S(1)}, u32[]{:S(2)}, u32[]{:S(2)}) collective-permute-start(bf16[128,128]{1,0:T(8,128)(2,1)S(1)} %get-tuple-element.98), channel_id=1, source_target_pairs={{0,6},{2,4},{4,2},{6,0},{1,7},{3,5},{5,3},{7,1},{8,14},{10,12},{12... | collective-permute-start | bytes 98312 | tf_op jit(solution)/shard_map/ppermute | solution.py:171
  6.1 3.9 %collective-permute-start.7 = (bf16[128,128]{1,0:T(8,128)(2,1)S(1)}, bf16[128,128]{1,0:T(8,128)(2,1)S(1)}, u32[]{:S(2)}, u32[]{:S(2)}) collective-permute-start(bf16[128,128]{1,0:T(8,128)(2,1)S(1)} %get-tuple-element.99), channel_id=1, source_target_pairs={{0,4},{2,6},{4,0},{6,2},{1,5},{3,7},{5,1},{7,3},{8,12},{10,14},{12... | collective-permute-start | bytes 98312 | tf_op jit(solution)/shard_map/ppermute | solution.py:171
  6.6 3.9 %collective-permute-start.8 = (bf16[128,128]{1,0:T(8,128)(2,1)S(1)}, bf16[128,128]{1,0:T(8,128)(2,1)S(1)}, u32[]{:S(2)}, u32[]{:S(2)}) collective-permute-start(bf16[128,128]{1,0:T(8,128)(2,1)S(1)} %get-tuple-element.100), channel_id=1, source_target_pairs={{0,2},{2,0},{4,6},{6,4},{1,3},{3,1},{5,7},{7,5},{8,10},{10,8},{12,... | collective-permute-start | bytes 98312 | tf_op jit(solution)/shard_map/ppermute | solution.py:171
  10.5 4.5 %collective-permute-start.11 = (bf16[128,128]{1,0:T(8,128)(2,1)S(1)}, bf16[128,128]{1,0:T(8,128)(2,1)S(1)}, u32[]{:S(2)}, u32[]{:S(2)}) collective-permute-start(bf16[128,128]{1,0:T(8,128)(2,1)S(1)} %get-tuple-element.102), channel_id=1, source_target_pairs={{0,8},{8,0},{16,24},{24,16},{1,9},{9,1},{17,25},{25,17},{2,10},{10... | collective-permute-start | bytes 98312 | tf_op jit(solution)/shard_map/ppermute | solution.py:171
  12.2 5.4 %collective-permute-start.10 = (bf16[128,128]{1,0:T(8,128)(2,1)S(1)}, bf16[128,128]{1,0:T(8,128)(2,1)S(1)}, u32[]{:S(2)}, u32[]{:S(2)}) collective-permute-start(bf16[128,128]{1,0:T(8,128)(2,1)S(1)} %get-tuple-element.102), channel_id=1, source_target_pairs={{0,16},{8,24},{16,0},{24,8},{1,17},{9,25},{17,1},{25,9},{2,18},{10... | collective-permute-start | bytes 98312 | tf_op jit(solution)/shard_map/ppermute | solution.py:171
  14.7 5.7 %collective-permute-start.9 = (bf16[128,128]{1,0:T(8,128)(2,1)S(1)}, bf16[128,128]{1,0:T(8,128)(2,1)S(1)}, u32[]{:S(2)}, u32[]{:S(2)}) collective-permute-start(bf16[128,128]{1,0:T(8,128)(2,1)S(1)} %get-tuple-element.102), channel_id=1, source_target_pairs={{0,24},{8,16},{16,8},{24,0},{1,25},{9,17},{17,9},{25,1},{2,26},{10... | collective-permute-start | bytes 98312 | tf_op jit(solution)/shard_map/ppermute | solution.py:171
  20.5 6.3 %collective-permute-start.12 = (f32[128,128]{1,0:T(8,128)S(1)}, f32[128,128]{1,0:T(8,128)S(1)}, u32[]{:S(2)}, u32[]{:S(2)}) collective-permute-start(f32[128,128]{1,0:T(8,128)S(1)} %get-tuple-element.110), channel_id=1, source_target_pairs={{0,1},{1,0},{2,3},{3,2},{4,5},{5,4},{6,7},{7,6},{8,9},{9,8},{10,11... | collective-permute-start | bytes 196616 | tf_op jit(solution)/shard_map/ppermute | solution.py:186
  20.7 5.0 %collective-permute-start = (bf16[128,128]{1,0:T(8,128)(2,1)S(1)}, bf16[128,128]{1,0:T(8,128)(2,1)}, u32[]{:S(2)}, u32[]{:S(2)}) collective-permute-start(bf16[128,128]{1,0:T(8,128)(2,1)S(1)} %get-tuple-element.55), channel_id=1, source_target_pairs={{0,6},{2,4},{4,2},{6,0},{1,7},{3,5},{5,3},{7,1},{8,14},{10,12},{12... | collective-permute-start | bytes 98312 | tf_op jit(solution)/shard_map/cond/branch_1_fun/ppermute | solution.py:171
  22.2 4.0 %collective-permute-start.1 = (bf16[128,128]{1,0:T(8,128)(2,1)S(1)}, bf16[128,128]{1,0:T(8,128)(2,1)}, u32[]{:S(2)}, u32[]{:S(2)}) collective-permute-start(bf16[128,128]{1,0:T(8,128)(2,1)S(1)} %get-tuple-element.56), channel_id=1, source_target_pairs={{0,4},{2,6},{4,0},{6,2},{1,5},{3,7},{5,1},{7,3},{8,12},{10,14},{12... | collective-permute-start | bytes 98312 | tf_op jit(solution)/shard_map/cond/branch_1_fun/ppermute | solution.py:171
  22.7 4.0 %collective-permute-start.2 = (bf16[128,128]{1,0:T(8,128)(2,1)S(1)}, bf16[128,128]{1,0:T(8,128)(2,1)}, u32[]{:S(2)}, u32[]{:S(2)}) collective-permute-start(bf16[128,128]{1,0:T(8,128)(2,1)S(1)} %get-tuple-element.57), channel_id=1, source_target_pairs={{0,2},{2,0},{4,6},{6,4},{1,3},{3,1},{5,7},{7,5},{8,10},{10,8},{12,... | collective-permute-start | bytes 98312 | tf_op jit(solution)/shard_map/cond/branch_1_fun/ppermute | solution.py:171

commit v14 on v12

--- a/solution.py
+++ b/solution.py
@@ -76,7 +76,7 @@
     plane = lax.axis_index("outer")
     whole = own[...]
     below = jnp.zeros_like(whole)
-    for e, there in zip(reversed(range(1, len(totals) + 1)), totals):
+    for e, there in enumerate(totals, 1):
         there = there[...].astype(F32)
         below = below + jnp.where((plane ^ e) < plane, there, 0.0)
         whole = whole + there
@@ -119,11 +119,30 @@
         out_ref[:, lanes_of(p)] = jnp.where(first, intra[0], intra[1])
 
 
-def attend_kernel(inner, q_ref, intra_ref, *refs):
-    *parts, out_hbm, out_ref, prefix_ref, sent = refs
+def settle_kernel(inner, *refs):
+    *parts, out_ref = refs
     me = lax.axis_index("inner")
     for d, part in zip(reversed(range(inner)), parts):
-        prefix_ref[me ^ d] = part[...]
+        out_ref[me ^ d] = part[...]
+
+
+def unused_kernel(*refs):
+    del refs
+
+
+def attend_kernel(q_ref, first_intra, first_prefix, later_intra, later_prefix, *refs):
+    leads = lax.axis_index("chain") == 0
+
+    @pl.when(leads)
+    def _():
+        attend(q_ref, first_intra, first_prefix, *refs)
+
+    @pl.when(~leads)
+    def _():
+        attend(q_ref, later_intra, later_prefix, *refs)
+
+
+def attend(q_ref, intra_ref, prefix_ref, out_hbm, out_ref, sent):
     share = prefix_ref.shape[1]
     heads = SLAB // HEAD_DIM
     blocks = ([lax.broadcasted_iota(jnp.int32, (SLAB, SLAB), d) // HEAD_DIM for d in range(2)])
@@ -181,18 +200,31 @@
         scratch=[pltpu.VMEM((inner,) + share, F32), pltpu.SemaphoreType.DMA((2, SLABS, HALVES))])
     mine = swapped([own] + states, "inner", own)
     total, sent = call(totals_kernel, [(share, F32), (share, BF16)], *mine)
-    totals = swapped([sent] * planes, "outer", total)
+    total, queries = lax.optimization_barrier((total, queries))
+    *totals, _ = swapped([sent] * planes, "outer", total)
+    totals = totals[::-1] + [total]
     below, whole = call(planes_kernel, [(share, F32)] * 2, *totals)
     groups = [lax.ppermute(whole, "chain", [(c, c ^ d) for c in range(chains)]) for d in range(1, chains)]
-    before = call(functools.partial(prefix_kernel, inner), [(share, BF16)] * inner, *mine, below, *groups,
-                  scratch=[pltpu.VMEM((inner,) + share, F32)])
-    prefix = swapped(before, "inner", before[0])
-    intra = call(intra_kernel, (queries.shape, F32), queries, keys, values,
-                 flops=4 * rows * rows * HEADS * HEAD_DIM)
-    return call(functools.partial(attend_kernel, inner), (queries.shape, BF16), queries, intra, *prefix,
+    leads = lax.axis_index("chain") == 0
+    results = [(queries.shape, F32), ((inner,) + share, BF16)]
+
+    def way_back(*bases):
+        before = call(functools.partial(prefix_kernel, inner), [(share, BF16)] * inner, *mine, *bases,
+                      scratch=[pltpu.VMEM((inner,) + share, F32)])
+        prefix = swapped(before, "inner", before[0])
+        intra = call(intra_kernel, results[0], queries, keys, values,
+                     flops=4 * rows * rows * HEADS * HEAD_DIM)
+        return intra, call(functools.partial(settle_kernel, inner), results[1], *prefix)
+
+    def unused():
+        return tuple(call(unused_kernel, results))
+
+    first = lax.cond(leads, lambda: way_back(below), unused)
+    first, groups = lax.optimization_barrier((first, groups))
+    later = lax.cond(leads, unused, lambda: way_back(below, *groups))
+    return call(attend_kernel, (queries.shape, BF16), queries, *first, *later,
                 result=pltpu.HBM, flops=2 * rows * SLAB * HEADS * HEAD_DIM,
-                scratch=[pltpu.VMEM(queries.shape, BF16), pltpu.VMEM((inner,) + share, BF16),
-                         pltpu.SemaphoreType.DMA((HEADS * HEAD_DIM // SLAB,))])
+                scratch=[pltpu.VMEM(queries.shape, BF16), pltpu.SemaphoreType.DMA((HEADS * HEAD_DIM // SLAB,))])
 
 
 def solution(mesh):

time: 27.8 us -> 29.2 us (1.050)
  local copies, waits for them, and re-layouts: 0.01 us -> 2.24 us
  waiting for transfers between devices: 9.96 us -> 9.03 us
    unnamed x2 -> x6, local copies, waits for them, and re-layouts: 0.01 us -> 2.24 us
    ppermute x1, waiting for transfers between devices: 1.24 us -> 0.01 us  [per_device(): lax.ppermute(whole, 'chain', [(c, c ^ d) for c in range(chains)])]
    ppermute x9, waiting for transfers between devices: 8.72 us -> 9.03 us  [swapped(): lax.ppermute(arrays[d], axis, [(i, i ^ d) for i in range(size)])]
    pallas_call x6 -> x8, Pallas kernels: 4.9 us -> 4.96 us  [call(): pl.pallas_call(kernel, out_shape=[result(shape, dtype) for shape, dtype i...]
  transfers between devices with their start and end apart: 10 -> 10, of which waited for: 8 -> 7; matrix products, arithmetic and copies ran while one was open for 0% -> 0% of each run, Pallas kernels for 5% -> 5%
where the time goes in v14:
time: 29.2 us; the launch traced here: 29 us
  starting transfers between devices  12.7 us (43%)
  waiting for transfers between devices  9.03 us (31%)
  Pallas kernels  4.96 us (17%)
  local copies, waits for them, and re-layouts  2.24 us (8%)
    ppermute x9, starting transfers between devices, swapped(): lax.ppermute(arrays[d], axis, [(i, i ^ d) for i in range(size)])  12.6 us
    ppermute x9, waiting for transfers between devices, swapped(): lax.ppermute(arrays[d], axis, [(i, i ^ d) for i in range(size)])  9.03 us
    pallas_call x8, Pallas kernels, call(): pl.pallas_call(kernel, out_shape=[result(shape, dtype) for shape, dtype i...  4.96 us
    unnamed x6, local copies, waits for them, and re-layouts  2.24 us
  transfers between devices with their start and end apart: 10, of which 7 were waited for; matrix products, arithmetic and copies ran while one was open for 0% of the time, Pallas kernels for 5%

profile of v14, /device:TPU:0, one launch (start us, length us, event | category | flops | bytes accessed | tf_op | source)
XLA Modules:
  0.0 29.0 jit_solution(9924649613691485041)
XLA Ops:
  0.0 0.0 copy-start
  0.0 2.1 %shard_map.37 = (f32[128,128]{1,0:T(8,128)S(1)}, bf16[128,128]{1,0:T(8,128)(2,1)S(1)}, bf16[128,128]{1,0:T(8,128)(2,1)S(1)}, bf16[128,128]{1,0:T(8,128)(2,1)S(1)...) custom-call(bf16[256,1024]{1,0:T(8,128)(2,1)} %k_hbm.1, bf16[256,1024]{1,0:T(8,128)(2,1)} %v_hbm.1), custom_call_target="tpu_custom_call" | custom-call | flops 67108864 | bytes 1048576 | tf_op jit(solution)/shard_map/pallas_call | solution.py:176
  2.1 4.0 %collective-permute-start.6 = (bf16[128,128]{1,0:T(8,128)(2,1)S(1)}, bf16[128,128]{1,0:T(8,128)(2,1)S(1)}, u32[]{:S(2)}, u32[]{:S(2)}) collective-permute-start(bf16[128,128]{1,0:T(8,128)(2,1)S(1)} %get-tuple-element.83), channel_id=1, source_target_pairs={{0,6},{2,4},{4,2},{6,0},{1,7},{3,5},{5,3},{7,1},{8,14},{10,12},{12... | collective-permute-start | bytes 98312 | tf_op jit(solution)/shard_map/ppermute | solution.py:190
  6.1 0.5 %collective-permute-start.7 = (bf16[128,128]{1,0:T(8,128)(2,1)S(1)}, bf16[128,128]{1,0:T(8,128)(2,1)S(1)}, u32[]{:S(2)}, u32[]{:S(2)}) collective-permute-start(bf16[128,128]{1,0:T(8,128)(2,1)S(1)} %get-tuple-element.84), channel_id=1, source_target_pairs={{0,4},{2,6},{4,0},{6,2},{1,5},{3,7},{5,1},{7,3},{8,12},{10,14},{12... | collective-permute-start | bytes 98312 | tf_op jit(solution)/shard_map/ppermute | solution.py:190
  6.6 0.1 collective-permute-start.8
  6.7 1.3 %collective-permute-done.6.refs_0_ = bf16[128,128]{1,0:T(8,128)(2,1)S(1)} collective-permute-done((bf16[128,128]{1,0:T(8,128)(2,1)S(1)}, bf16[128,128]{1,0:T(8,128)(2,1)S(1)}, u32[]{:S(2)}, u32[]{:S(2)}) %collective-permute-start.6) | collective-permute-done | bytes 32800 | tf_op jit(solution)/shard_map/ppermute | solution.py:190
  8.0 2.0 %collective-permute-done.7.refs_1_ = bf16[128,128]{1,0:T(8,128)(2,1)S(1)} collective-permute-done((bf16[128,128]{1,0:T(8,128)(2,1)S(1)}, bf16[128,128]{1,0:T(8,128)(2,1)S(1)}, u32[]{:S(2)}, u32[]{:S(2)}) %collective-permute-start.7) | collective-permute-done | bytes 32800 | tf_op jit(solution)/shard_map/ppermute | solution.py:190
  10.0 0.5 %collective-permute-done.8.refs_2_ = bf16[128,128]{1,0:T(8,128)(2,1)S(1)} collective-permute-done((bf16[128,128]{1,0:T(8,128)(2,1)S(1)}, bf16[128,128]{1,0:T(8,128)(2,1)S(1)}, u32[]{:S(2)}, u32[]{:S(2)}) %collective-permute-start.8) | collective-permute-done | bytes 32800 | tf_op jit(solution)/shard_map/ppermute | solution.py:190
  10.5 3.7 %collective-permute-start.11 = (bf16[128,128]{1,0:T(8,128)(2,1)S(1)}, bf16[128,128]{1,0:T(8,128)(2,1)S(1)}, u32[]{:S(2)}, u32[]{:S(2)}) collective-permute-start(bf16[128,128]{1,0:T(8,128)(2,1)S(1)} %get-tuple-element.91), channel_id=1, source_target_pairs={{0,24},{8,16},{16,8},{24,0},{1,25},{9,17},{17,9},{25,1},{2,26},{10... | collective-permute-start | bytes 98312 | tf_op jit(solution)/shard_map/ppermute | solution.py:190
  14.2 0.0 collective-permute-start.10
  14.2 0.8 %collective-permute-start.9 = (bf16[128,128]{1,0:T(8,128)(2,1)S(1)}, bf16[128,128]{1,0:T(8,128)(2,1)S(1)}, u32[]{:S(2)}, u32[]{:S(2)}) collective-permute-start(bf16[128,128]{1,0:T(8,128)(2,1)S(1)} %get-tuple-element.91), channel_id=1, source_target_pairs={{0,8},{8,0},{16,24},{24,16},{1,9},{9,1},{17,25},{25,17},{2,10},{10... | collective-permute-start | bytes 98312 | tf_op jit(solution)/shard_map/ppermute | solution.py:190
  15.0 1.3 %collective-permute-done.11.refs_2_ = bf16[128,128]{1,0:T(8,128)(2,1)S(1)} collective-permute-done((bf16[128,128]{1,0:T(8,128)(2,1)S(1)}, bf16[128,128]{1,0:T(8,128)(2,1)S(1)}, u32[]{:S(2)}, u32[]{:S(2)}) %collective-permute-start.11) | collective-permute-done | bytes 32800 | tf_op jit(solution)/shard_map/ppermute | solution.py:190
  16.3 2.7 %collective-permute-done.10.refs_1_ = bf16[128,128]{1,0:T(8,128)(2,1)S(1)} collective-permute-done((bf16[128,128]{1,0:T(8,128)(2,1)S(1)}, bf16[128,128]{1,0:T(8,128)(2,1)S(1)}, u32[]{:S(2)}, u32[]{:S(2)}) %collective-permute-start.10) | collective-permute-done | bytes 32800 | tf_op jit(solution)/shard_map/ppermute | solution.py:190
  19.0 0.0 collective-permute-done.9.refs_0_
  19.0 0.1 collective-permute-start.12
  19.1 0.0 copy-done
  19.1 6.4 %conditional.2 = ((f32[256,1024]{1,0:T(8,128)S(1)}, bf16[4,128,128]{2,1,0:T(8,128)(2,1)S(1)})) conditional(s32[]{:T(128)} %convert_element_type.4, () %tuple.22, (bf16[256,1024]{1,0:T(8,128)(2,1)S(1)}, bf16[256,1024]{1,0:T(8,128)(2,1)S(1)}, bf16[256,1024]{1,0:T(8,128)(2,1)S(1)}, bf16[128,128]{1,0:T(8,128)(2,1)S(1)}, bf16[128,128]{1,0:T(8,128)(2,1)S(1)}, ...), branch_computations={%region_0.0_spmd, %region_1.0_spmd} | conditional | flops 268435456 | bytes 2326672 | solution.py:222
  19.2 0.1 branch_1_fun.5
  19.2 1.6 %collective-permute-start = (bf16[128,128]{1,0:T(8,128)(2,1)S(1)}, bf16[128,128]{1,0:T(8,128)(2,1)S(1)}, u32[]{:S(2)}, u32[]{:S(2)}) collective-permute-start(bf16[128,128]{1,0:T(8,128)(2,1)S(1)} %get-tuple-element.47), channel_id=1, source_target_pairs={{0,6},{2,4},{4,2},{6,0},{1,7},{3,5},{5,3},{7,1},{8,14},{10,12},{12... | collective-permute-start | bytes 98312 | tf_op jit(solution)/shard_map/cond/branch_1_fun/ppermute | solution.py:190
  20.8 0.5 %collective-permute-start.1 = (bf16[128,128]{1,0:T(8,128)(2,1)S(1)}, bf16[128,128]{1,0:T(8,128)(2,1)S(1)}, u32[]{:S(2)}, u32[]{:S(2)}) collective-permute-start(bf16[128,128]{1,0:T(8,128)(2,1)S(1)} %get-tuple-element.48), channel_id=1, source_target_pairs={{0,4},{2,6},{4,0},{6,2},{1,5},{3,7},{5,1},{7,3},{8,12},{10,14},{12... | collective-permute-start | bytes 98312 | tf_op jit(solution)/shard_map/cond/branch_1_fun/ppermute | solution.py:190
  21.3 1.5 %collective-permute-start.2 = (bf16[128,128]{1,0:T(8,128)(2,1)S(1)}, bf16[128,128]{1,0:T(8,128)(2,1)S(1)}, u32[]{:S(2)}, u32[]{:S(2)}) collective-permute-start(bf16[128,128]{1,0:T(8,128)(2,1)S(1)} %get-tuple-element.49), channel_id=1, source_target_pairs={{0,2},{2,0},{4,6},{6,4},{1,3},{3,1},{5,7},{7,5},{8,10},{10,8},{12,... | collective-permute-start | bytes 98312 | tf_op jit(solution)/shard_map/cond/branch_1_fun/ppermute | solution.py:190
  22.8 1.5 %branch_1_fun.4 = f32[256,1024]{1,0:T(8,128)S(1)} custom-call(bf16[256,1024]{1,0:T(8,128)(2,1)S(1)} %get-tuple-element.39.q_ref, bf16[256,1024]{1,0:T(8,128)(2,1)S(1)} %get-tuple-element.40.k_ref, bf16[256,1024]{1,0:T(8,128)(2,1)S(1)} %get-tuple-element.41.v_ref), custom_call_target="tpu_custom_call" | custom-call | flops 268435456 | bytes 1572864 | tf_op jit(solution)/shard_map/cond/branch_1_fun/pallas_call | solution.py:176
  24.3 0.0 collective-permute-done.refs_0_
  24.3 1.0 %collective-permute-done.1.refs_1_ = bf16[128,128]{1,0:T(8,128)(2,1)S(1)} collective-permute-done((bf16[128,128]{1,0:T(8,128)(2,1)S(1)}, bf16[128,128]{1,0:T(8,128)(2,1)S(1)}, u32[]{:S(2)}, u32[]{:S(2)}) %collective-permute-start.1) | collective-permute-done | bytes 32800 | tf_op jit(solution)/shard_map/cond/branch_1_fun/ppermute | solution.py:190
  25.3 0.2 collective-permute-done.2.refs_2_
  25.5 0.0 copy-start.1
  25.5 1.0 %copy-done.1 = f32[256,1024]{1,0:T(8,128)} copy-done((f32[256,1024]{1,0:T(8,128)}, f32[256,1024]{1,0:T(8,128)S(1)}, u32[]{:S(2)}) %copy-start.1) | copy-done | bytes 1048600
  26.5 0.0 collective-permute-done.12
  26.5 0.0 copy-start.2
  26.5 1.2 %copy-done.2 = f32[256,1024]{1,0:T(8,128)S(1)} copy-done((f32[256,1024]{1,0:T(8,128)S(1)}, f32[256,1024]{1,0:T(8,128)}, u32[]{:S(2)}) %copy-start.2) | copy-done | bytes 1048600
  27.8 1.3 %shard_map.40 = bf16[256,1024]{1,0:T(8,128)(2,1)} custom-call(bf16[256,1024]{1,0:T(8,128)(2,1)S(1)} %copy-done, f32[256,1024]{1,0:T(8,128)S(1)} %copy-done.2, bf16[4,128,128]{2,1,0:T(8,128)(2,1)S(1)} %get-tuple-element.98.first_prefix, f32[256,1024]{1,0:T(8,128)S(1)} %get-tuple-element.100.later_intra, bf16[4,128,128]{2,1,0:T(8,128)(2,1)S(1)} %get-tuple-element.101.later_prefix), custom_call_target="tpu_custom_call" | custom-call | flops 134217728 | bytes 2883584 | tf_op jit(solution)/shard_map/pallas_call | solution.py:176
  (5 shorter events, 0.1 us)
Async XLA Ops:
  0.0 19.1 %copy-start = (bf16[256,1024]{1,0:T(8,128)(2,1)S(1)}, bf16[256,1024]{1,0:T(8,128)(2,1)}, u32[]{:S(2)}) copy-start(bf16[256,1024]{1,0:T(8,128)(2,1)} %q_ref) | copy-start | bytes 1572868
  2.1 5.9 %collective-permute-start.6 = (bf16[128,128]{1,0:T(8,128)(2,1)S(1)}, bf16[128,128]{1,0:T(8,128)(2,1)S(1)}, u32[]{:S(2)}, u32[]{:S(2)}) collective-permute-start(bf16[128,128]{1,0:T(8,128)(2,1)S(1)} %get-tuple-element.83), channel_id=1, source_target_pairs={{0,6},{2,4},{4,2},{6,0},{1,7},{3,5},{5,3},{7,1},{8,14},{10,12},{12... | collective-permute-start | bytes 98312 | tf_op jit(solution)/shard_map/ppermute | solution.py:190
  6.1 3.9 %collective-permute-start.7 = (bf16[128,128]{1,0:T(8,128)(2,1)S(1)}, bf16[128,128]{1,0:T(8,128)(2,1)S(1)}, u32[]{:S(2)}, u32[]{:S(2)}) collective-permute-start(bf16[128,128]{1,0:T(8,128)(2,1)S(1)} %get-tuple-element.84), channel_id=1, source_target_pairs={{0,4},{2,6},{4,0},{6,2},{1,5},{3,7},{5,1},{7,3},{8,12},{10,14},{12... | collective-permute-start | bytes 98312 | tf_op jit(solution)/shard_map/ppermute | solution.py:190
  6.6 3.9 %collective-permute-start.8 = (bf16[128,128]{1,0:T(8,128)(2,1)S(1)}, bf16[128,128]{1,0:T(8,128)(2,1)S(1)}, u32[]{:S(2)}, u32[]{:S(2)}) collective-permute-start(bf16[128,128]{1,0:T(8,128)(2,1)S(1)} %get-tuple-element.85), channel_id=1, source_target_pairs={{0,2},{2,0},{4,6},{6,4},{1,3},{3,1},{5,7},{7,5},{8,10},{10,8},{12,... | collective-permute-start | bytes 98312 | tf_op jit(solution)/shard_map/ppermute | solution.py:190
  10.5 5.8 %collective-permute-start.11 = (bf16[128,128]{1,0:T(8,128)(2,1)S(1)}, bf16[128,128]{1,0:T(8,128)(2,1)S(1)}, u32[]{:S(2)}, u32[]{:S(2)}) collective-permute-start(bf16[128,128]{1,0:T(8,128)(2,1)S(1)} %get-tuple-element.91), channel_id=1, source_target_pairs={{0,24},{8,16},{16,8},{24,0},{1,25},{9,17},{17,9},{25,1},{2,26},{10... | collective-permute-start | bytes 98312 | tf_op jit(solution)/shard_map/ppermute | solution.py:190
  14.2 4.8 %collective-permute-start.10 = (bf16[128,128]{1,0:T(8,128)(2,1)S(1)}, bf16[128,128]{1,0:T(8,128)(2,1)S(1)}, u32[]{:S(2)}, u32[]{:S(2)}) collective-permute-start(bf16[128,128]{1,0:T(8,128)(2,1)S(1)} %get-tuple-element.91), channel_id=1, source_target_pairs={{0,16},{8,24},{16,0},{24,8},{1,17},{9,25},{17,1},{25,9},{2,18},{10... | collective-permute-start | bytes 98312 | tf_op jit(solution)/shard_map/ppermute | solution.py:190
  14.2 4.8 %collective-permute-start.9 = (bf16[128,128]{1,0:T(8,128)(2,1)S(1)}, bf16[128,128]{1,0:T(8,128)(2,1)S(1)}, u32[]{:S(2)}, u32[]{:S(2)}) collective-permute-start(bf16[128,128]{1,0:T(8,128)(2,1)S(1)} %get-tuple-element.91), channel_id=1, source_target_pairs={{0,8},{8,0},{16,24},{24,16},{1,9},{9,1},{17,25},{25,17},{2,10},{10... | collective-permute-start | bytes 98312 | tf_op jit(solution)/shard_map/ppermute | solution.py:190
  19.0 7.5 %collective-permute-start.12 = (f32[128,128]{1,0:T(8,128)S(1)}, f32[128,128]{1,0:T(8,128)S(1)}, u32[]{:S(2)}, u32[]{:S(2)}) collective-permute-start(f32[128,128]{1,0:T(8,128)S(1)} %get-tuple-element.96), channel_id=1, source_target_pairs={{0,1},{1,0},{2,3},{3,2},{4,5},{5,4},{6,7},{7,6},{8,9},{9,8},{10,11... | collective-permute-start | bytes 196616 | tf_op jit(solution)/shard_map/ppermute | solution.py:207
  19.2 5.0 %collective-permute-start = (bf16[128,128]{1,0:T(8,128)(2,1)S(1)}, bf16[128,128]{1,0:T(8,128)(2,1)S(1)}, u32[]{:S(2)}, u32[]{:S(2)}) collective-permute-start(bf16[128,128]{1,0:T(8,128)(2,1)S(1)} %get-tuple-element.47), channel_id=1, source_target_pairs={{0,6},{2,4},{4,2},{6,0},{1,7},{3,5},{5,3},{7,1},{8,14},{10,12},{12... | collective-permute-start | bytes 98312 | tf_op jit(solution)/shard_map/cond/branch_1_fun/ppermute | solution.py:190
  20.8 4.5 %collective-permute-start.1 = (bf16[128,128]{1,0:T(8,128)(2,1)S(1)}, bf16[128,128]{1,0:T(8,128)(2,1)S(1)}, u32[]{:S(2)}, u32[]{:S(2)}) collective-permute-start(bf16[128,128]{1,0:T(8,128)(2,1)S(1)} %get-tuple-element.48), channel_id=1, source_target_pairs={{0,4},{2,6},{4,0},{6,2},{1,5},{3,7},{5,1},{7,3},{8,12},{10,14},{12... | collective-permute-start | bytes 98312 | tf_op jit(solution)/shard_map/cond/branch_1_fun/ppermute | solution.py:190
  21.3 4.2 %collective-permute-start.2 = (bf16[128,128]{1,0:T(8,128)(2,1)S(1)}, bf16[128,128]{1,0:T(8,128)(2,1)S(1)}, u32[]{:S(2)}, u32[]{:S(2)}) collective-permute-start(bf16[128,128]{1,0:T(8,128)(2,1)S(1)} %get-tuple-element.49), channel_id=1, source_target_pairs={{0,2},{2,0},{4,6},{6,4},{1,3},{3,1},{5,7},{7,5},{8,10},{10,8},{12,... | collective-permute-start | bytes 98312 | tf_op jit(solution)/shard_map/cond/branch_1_fun/ppermute | solution.py:190
  25.5 1.0 %copy-start.1 = (f32[256,1024]{1,0:T(8,128)}, f32[256,1024]{1,0:T(8,128)S(1)}, u32[]{:S(2)}) copy-start(f32[256,1024]{1,0:T(8,128)S(1)} %get-tuple-element.97.first_intra) | copy-start | bytes 3145732
  26.5 1.2 %copy-start.2 = (f32[256,1024]{1,0:T(8,128)S(1)}, f32[256,1024]{1,0:T(8,128)}, u32[]{:S(2)}) copy-start(f32[256,1024]{1,0:T(8,128)} %copy-done.1) | copy-start | bytes 3145732

commit v15 on v14

--- a/solution.py
+++ b/solution.py
@@ -130,19 +130,8 @@
     del refs
 
 
-def attend_kernel(q_ref, first_intra, first_prefix, later_intra, later_prefix, *refs):
-    leads = lax.axis_index("chain") == 0
-
-    @pl.when(leads)
-    def _():
-        attend(q_ref, first_intra, first_prefix, *refs)
-
-    @pl.when(~leads)
-    def _():
-        attend(q_ref, later_intra, later_prefix, *refs)
-
-
-def attend(q_ref, intra_ref, prefix_ref, out_hbm, out_ref, sent):
+def attend_kernel(q_ref, intra_ref, prefix_ref, *refs):
+    *_, out_hbm, out_ref, sent = refs
     share = prefix_ref.shape[1]
     heads = SLAB // HEAD_DIM
     blocks = ([lax.broadcasted_iota(jnp.int32, (SLAB, SLAB), d) // HEAD_DIM for d in range(2)])
@@ -169,19 +158,27 @@
         copy.wait()
 
 
-def call(kernel, outs, *args, flops=0, scratch=(), source=pltpu.VMEM, result=pltpu.VMEM):
+def call(kernel, outs, *args, flops=0, scratch=(), source=pltpu.VMEM, result=pltpu.VMEM, onto=None):
     moved = sum(a.size * a.dtype.itemsize for a in args)
     single = not isinstance(outs, list)
     outs = [outs] if single else outs
+    specs = [pl.BlockSpec(memory_space=source)] * len(args)
+    args = [pltpu.with_memory_space_constraint(a, source) for a in args]
+    aliases = {}
+    if onto is not None:
+        aliases = {len(args): 0}
+        specs.append(pl.BlockSpec(memory_space=result))
+        args.append(pltpu.with_memory_space_constraint(onto, result))
     got = pl.pallas_call(
         kernel,
         out_shape=[result(shape, dtype) for shape, dtype in outs],
-        in_specs=[pl.BlockSpec(memory_space=source)] * len(args),
+        in_specs=specs,
         out_specs=[pl.BlockSpec(memory_space=result)] * len(outs),
         scratch_shapes=scratch,
+        input_output_aliases=aliases,
         cost_estimate=pl.CostEstimate(flops=flops, bytes_accessed=moved, transcendentals=0),
         compiler_params=pltpu.CompilerParams(vmem_limit_bytes=16 * 1024 * 1024),
-    )(*[pltpu.with_memory_space_constraint(a, source) for a in args])
+    )(*args)
     return got[0] if single else got
 
 
@@ -206,25 +203,22 @@
     below, whole = call(planes_kernel, [(share, F32)] * 2, *totals)
     groups = [lax.ppermute(whole, "chain", [(c, c ^ d) for c in range(chains)]) for d in range(1, chains)]
     leads = lax.axis_index("chain") == 0
-    results = [(queries.shape, F32), ((inner,) + share, BF16)]
-
-    def way_back(*bases):
+    output = (queries.shape, BF16)
+
+    def way_back(onto, *bases):
         before = call(functools.partial(prefix_kernel, inner), [(share, BF16)] * inner, *mine, *bases,
                       scratch=[pltpu.VMEM((inner,) + share, F32)])
         prefix = swapped(before, "inner", before[0])
-        intra = call(intra_kernel, results[0], queries, keys, values,
+        intra = call(intra_kernel, (queries.shape, F32), queries, keys, values,
                      flops=4 * rows * rows * HEADS * HEAD_DIM)
-        return intra, call(functools.partial(settle_kernel, inner), results[1], *prefix)
-
-    def unused():
-        return tuple(call(unused_kernel, results))
-
-    first = lax.cond(leads, lambda: way_back(below), unused)
-    first, groups = lax.optimization_barrier((first, groups))
-    later = lax.cond(leads, unused, lambda: way_back(below, *groups))
-    return call(attend_kernel, (queries.shape, BF16), queries, *first, *later,
-                result=pltpu.HBM, flops=2 * rows * SLAB * HEADS * HEAD_DIM,
-                scratch=[pltpu.VMEM(queries.shape, BF16), pltpu.SemaphoreType.DMA((HEADS * HEAD_DIM // SLAB,))])
+        prefix = call(functools.partial(settle_kernel, inner), ((inner,) + share, BF16), *prefix)
+        return call(attend_kernel, output, queries, intra, prefix, result=pltpu.HBM, onto=onto,
+                    flops=2 * rows * SLAB * HEADS * HEAD_DIM,
+                    scratch=[pltpu.VMEM(*output), pltpu.SemaphoreType.DMA((HEADS * HEAD_DIM // SLAB,))])
+
+    out = lax.cond(leads, lambda: way_back(None, below), lambda: call(unused_kernel, output, result=pltpu.HBM))
+    out, groups = lax.optimization_barrier((out, groups))
+    return lax.cond(leads, lambda out: out, lambda out: way_back(out, below, *groups), out)
 
 
 def solution(mesh):

time: 29.2 us -> 26.8 us (0.918)
  local copies, waits for them, and re-layouts: 2.24 us -> 0.01 us
    unnamed x6 -> x2, local copies, waits for them, and re-layouts: 2.24 us -> 0.01 us
    pallas_call x8 -> x7, Pallas kernels: 4.96 us -> 4.96 us  [call(): pl.pallas_call(kernel, out_shape=[result(shape, dtype) for shape, dtype i...]
  transfers between devices with their start and end apart: 10 -> 10, of which waited for: 7 -> 7; matrix products, arithmetic and copies ran while one was open for 0% -> 0% of each run, Pallas kernels for 5% -> 11%
where the time goes in v15:
time: 26.8 us; the launch traced here: 26.7 us
  starting transfers between devices  12.7 us (47%)
  waiting for transfers between devices  8.91 us (33%)
  Pallas kernels  4.96 us (19%)
    ppermute x9, starting transfers between devices, swapped(): lax.ppermute(arrays[d], axis, [(i, i ^ d) for i in range(size)])  12.6 us
    ppermute x9, waiting for transfers between devices, swapped(): lax.ppermute(arrays[d], axis, [(i, i ^ d) for i in range(size)])  8.9 us
    pallas_call x7, Pallas kernels, call(): pl.pallas_call(kernel, out_shape=[result(shape, dtype) for shape, dtype i...  4.96 us
  transfers between devices with their start and end apart: 10, of which 7 were waited for; matrix products, arithmetic and copies ran while one was open for 0% of the time, Pallas kernels for 11%

profile of v15, /device:TPU:0, one launch (start us, length us, event | category | flops | bytes accessed | tf_op | source)
XLA Modules:
  0.0 26.7 jit_solution(14519248286186005552)
XLA Ops:
  0.0 0.0 copy-start
  0.0 2.1 %shard_map.39 = (f32[128,128]{1,0:T(8,128)S(1)}, bf16[128,128]{1,0:T(8,128)(2,1)S(1)}, bf16[128,128]{1,0:T(8,128)(2,1)S(1)}, bf16[128,128]{1,0:T(8,128)(2,1)S(1)...) custom-call(bf16[256,1024]{1,0:T(8,128)(2,1)} %k_hbm.1, bf16[256,1024]{1,0:T(8,128)(2,1)} %v_hbm.1), custom_call_target="tpu_custom_call" | custom-call | flops 67108864 | bytes 1048576 | tf_op jit(solution)/shard_map/pallas_call | solution.py:172
  2.1 4.0 %collective-permute-start.6 = (bf16[128,128]{1,0:T(8,128)(2,1)S(1)}, bf16[128,128]{1,0:T(8,128)(2,1)S(1)}, u32[]{:S(2)}, u32[]{:S(2)}) collective-permute-start(bf16[128,128]{1,0:T(8,128)(2,1)S(1)} %get-tuple-element.88), channel_id=1, source_target_pairs={{0,6},{2,4},{4,2},{6,0},{1,7},{3,5},{5,3},{7,1},{8,14},{10,12},{12... | collective-permute-start | bytes 98312 | tf_op jit(solution)/shard_map/ppermute | solution.py:187
  6.1 0.5 %collective-permute-start.7 = (bf16[128,128]{1,0:T(8,128)(2,1)S(1)}, bf16[128,128]{1,0:T(8,128)(2,1)S(1)}, u32[]{:S(2)}, u32[]{:S(2)}) collective-permute-start(bf16[128,128]{1,0:T(8,128)(2,1)S(1)} %get-tuple-element.89), channel_id=1, source_target_pairs={{0,4},{2,6},{4,0},{6,2},{1,5},{3,7},{5,1},{7,3},{8,12},{10,14},{12... | collective-permute-start | bytes 98312 | tf_op jit(solution)/shard_map/ppermute | solution.py:187
  6.6 0.1 collective-permute-start.8
  6.7 1.3 %collective-permute-done.6.refs_0_ = bf16[128,128]{1,0:T(8,128)(2,1)S(1)} collective-permute-done((bf16[128,128]{1,0:T(8,128)(2,1)S(1)}, bf16[128,128]{1,0:T(8,128)(2,1)S(1)}, u32[]{:S(2)}, u32[]{:S(2)}) %collective-permute-start.6) | collective-permute-done | bytes 32800 | tf_op jit(solution)/shard_map/ppermute | solution.py:187
  8.0 2.0 %collective-permute-done.7.refs_1_ = bf16[128,128]{1,0:T(8,128)(2,1)S(1)} collective-permute-done((bf16[128,128]{1,0:T(8,128)(2,1)S(1)}, bf16[128,128]{1,0:T(8,128)(2,1)S(1)}, u32[]{:S(2)}, u32[]{:S(2)}) %collective-permute-start.7) | collective-permute-done | bytes 32800 | tf_op jit(solution)/shard_map/ppermute | solution.py:187
  10.0 0.5 %collective-permute-done.8.refs_2_ = bf16[128,128]{1,0:T(8,128)(2,1)S(1)} collective-permute-done((bf16[128,128]{1,0:T(8,128)(2,1)S(1)}, bf16[128,128]{1,0:T(8,128)(2,1)S(1)}, u32[]{:S(2)}, u32[]{:S(2)}) %collective-permute-start.8) | collective-permute-done | bytes 32800 | tf_op jit(solution)/shard_map/ppermute | solution.py:187
  10.5 3.7 %collective-permute-start.11 = (bf16[128,128]{1,0:T(8,128)(2,1)S(1)}, bf16[128,128]{1,0:T(8,128)(2,1)S(1)}, u32[]{:S(2)}, u32[]{:S(2)}) collective-permute-start(bf16[128,128]{1,0:T(8,128)(2,1)S(1)} %get-tuple-element.96), channel_id=1, source_target_pairs={{0,24},{8,16},{16,8},{24,0},{1,25},{9,17},{17,9},{25,1},{2,26},{10... | collective-permute-start | bytes 98312 | tf_op jit(solution)/shard_map/ppermute | solution.py:187
  14.2 0.0 collective-permute-start.10
  14.2 0.8 %collective-permute-start.9 = (bf16[128,128]{1,0:T(8,128)(2,1)S(1)}, bf16[128,128]{1,0:T(8,128)(2,1)S(1)}, u32[]{:S(2)}, u32[]{:S(2)}) collective-permute-start(bf16[128,128]{1,0:T(8,128)(2,1)S(1)} %get-tuple-element.96), channel_id=1, source_target_pairs={{0,8},{8,0},{16,24},{24,16},{1,9},{9,1},{17,25},{25,17},{2,10},{10... | collective-permute-start | bytes 98312 | tf_op jit(solution)/shard_map/ppermute | solution.py:187
  15.0 1.3 %collective-permute-done.11.refs_2_ = bf16[128,128]{1,0:T(8,128)(2,1)S(1)} collective-permute-done((bf16[128,128]{1,0:T(8,128)(2,1)S(1)}, bf16[128,128]{1,0:T(8,128)(2,1)S(1)}, u32[]{:S(2)}, u32[]{:S(2)}) %collective-permute-start.11) | collective-permute-done | bytes 32800 | tf_op jit(solution)/shard_map/ppermute | solution.py:187
  16.3 2.7 %collective-permute-done.10.refs_1_ = bf16[128,128]{1,0:T(8,128)(2,1)S(1)} collective-permute-done((bf16[128,128]{1,0:T(8,128)(2,1)S(1)}, bf16[128,128]{1,0:T(8,128)(2,1)S(1)}, u32[]{:S(2)}, u32[]{:S(2)}) %collective-permute-start.10) | collective-permute-done | bytes 32800 | tf_op jit(solution)/shard_map/ppermute | solution.py:187
  19.0 0.0 collective-permute-done.9.refs_0_
  19.0 0.1 collective-permute-start.12
  19.1 0.0 copy-done
  19.1 7.5 %conditional.2 = (bf16[256,1024]{1,0:T(8,128)(2,1)}) conditional(s32[]{:T(128)} %convert_element_type.4, () %tuple.20, (bf16[256,1024]{1,0:T(8,128)(2,1)S(1)}, bf16[256,1024]{1,0:T(8,128)(2,1)S(1)}, bf16[256,1024]{1,0:T(8,128)(2,1)S(1)}, bf16[128,128]{1,0:T(8,128)(2,1)S(1)}, bf16[128,128]{1,0:T(8,128)(2,1)S(1)}, ...), branch_computations={%region_0.0_spmd, %region_1.0_spmd} | conditional | flops 402653184 | bytes 4030592 | solution.py:219
  19.2 0.1 branch_1_fun.5
  19.2 1.6 %collective-permute-start = (bf16[128,128]{1,0:T(8,128)(2,1)S(1)}, bf16[128,128]{1,0:T(8,128)(2,1)S(1)}, u32[]{:S(2)}, u32[]{:S(2)}) collective-permute-start(bf16[128,128]{1,0:T(8,128)(2,1)S(1)} %get-tuple-element.56), channel_id=1, source_target_pairs={{0,6},{2,4},{4,2},{6,0},{1,7},{3,5},{5,3},{7,1},{8,14},{10,12},{12... | collective-permute-start | bytes 98312 | tf_op jit(solution)/shard_map/cond/branch_1_fun/ppermute | solution.py:187
  20.8 0.5 %collective-permute-start.1 = (bf16[128,128]{1,0:T(8,128)(2,1)S(1)}, bf16[128,128]{1,0:T(8,128)(2,1)S(1)}, u32[]{:S(2)}, u32[]{:S(2)}) collective-permute-start(bf16[128,128]{1,0:T(8,128)(2,1)S(1)} %get-tuple-element.57), channel_id=1, source_target_pairs={{0,4},{2,6},{4,0},{6,2},{1,5},{3,7},{5,1},{7,3},{8,12},{10,14},{12... | collective-permute-start | bytes 98312 | tf_op jit(solution)/shard_map/cond/branch_1_fun/ppermute | solution.py:187
  21.3 1.5 %collective-permute-start.2 = (bf16[128,128]{1,0:T(8,128)(2,1)S(1)}, bf16[128,128]{1,0:T(8,128)(2,1)S(1)}, u32[]{:S(2)}, u32[]{:S(2)}) collective-permute-start(bf16[128,128]{1,0:T(8,128)(2,1)S(1)} %get-tuple-element.58), channel_id=1, source_target_pairs={{0,2},{2,0},{4,6},{6,4},{1,3},{3,1},{5,7},{7,5},{8,10},{10,8},{12,... | collective-permute-start | bytes 98312 | tf_op jit(solution)/shard_map/cond/branch_1_fun/ppermute | solution.py:187
  22.8 1.5 %branch_1_fun.4.intra_ref = f32[256,1024]{1,0:T(8,128)S(1)} custom-call(bf16[256,1024]{1,0:T(8,128)(2,1)S(1)} %get-tuple-element.48.q_ref, bf16[256,1024]{1,0:T(8,128)(2,1)S(1)} %get-tuple-element.49.k_ref, bf16[256,1024]{1,0:T(8,128)(2,1)S(1)} %get-tuple-element.50.v_ref), custom_call_target="tpu_custom_call" | custom-call | flops 268435456 | bytes 1572864 | tf_op jit(solution)/shard_map/cond/branch_1_fun/pallas_call | solution.py:172
  24.3 0.0 collective-permute-done.refs_0_
  24.3 0.9 %collective-permute-done.1.refs_1_ = bf16[128,128]{1,0:T(8,128)(2,1)S(1)} collective-permute-done((bf16[128,128]{1,0:T(8,128)(2,1)S(1)}, bf16[128,128]{1,0:T(8,128)(2,1)S(1)}, u32[]{:S(2)}, u32[]{:S(2)}) %collective-permute-start.1) | collective-permute-done | bytes 32800 | tf_op jit(solution)/shard_map/cond/branch_1_fun/ppermute | solution.py:187
  25.2 0.2 collective-permute-done.2.refs_2_
  25.4 1.3 %branch_1_fun.7 = bf16[256,1024]{1,0:T(8,128)(2,1)} custom-call(bf16[256,1024]{1,0:T(8,128)(2,1)S(1)} %get-tuple-element.48.q_ref, f32[256,1024]{1,0:T(8,128)S(1)} %branch_1_fun.4.intra_ref, bf16[4,128,128]{2,1,0:T(8,128)(2,1)S(1)} %branch_1_fun.6.prefix_ref), custom_call_target="tpu_custom_call" | custom-call | flops 134217728 | bytes 1703936 | tf_op jit(solution)/shard_map/cond/branch_1_fun/pallas_call | solution.py:172
  26.7 0.0 collective-permute-done.12
  (4 shorter events, 0.1 us)
Async XLA Ops:
  0.0 19.1 %copy-start = (bf16[256,1024]{1,0:T(8,128)(2,1)S(1)}, bf16[256,1024]{1,0:T(8,128)(2,1)}, u32[]{:S(2)}) copy-start(bf16[256,1024]{1,0:T(8,128)(2,1)} %param.7) | copy-start | bytes 1572868
  2.1 5.9 %collective-permute-start.6 = (bf16[128,128]{1,0:T(8,128)(2,1)S(1)}, bf16[128,128]{1,0:T(8,128)(2,1)S(1)}, u32[]{:S(2)}, u32[]{:S(2)}) collective-permute-start(bf16[128,128]{1,0:T(8,128)(2,1)S(1)} %get-tuple-element.88), channel_id=1, source_target_pairs={{0,6},{2,4},{4,2},{6,0},{1,7},{3,5},{5,3},{7,1},{8,14},{10,12},{12... | collective-permute-start | bytes 98312 | tf_op jit(solution)/shard_map/ppermute | solution.py:187
  6.1 3.9 %collective-permute-start.7 = (bf16[128,128]{1,0:T(8,128)(2,1)S(1)}, bf16[128,128]{1,0:T(8,128)(2,1)S(1)}, u32[]{:S(2)}, u32[]{:S(2)}) collective-permute-start(bf16[128,128]{1,0:T(8,128)(2,1)S(1)} %get-tuple-element.89), channel_id=1, source_target_pairs={{0,4},{2,6},{4,0},{6,2},{1,5},{3,7},{5,1},{7,3},{8,12},{10,14},{12... | collective-permute-start | bytes 98312 | tf_op jit(solution)/shard_map/ppermute | solution.py:187
  6.6 3.9 %collective-permute-start.8 = (bf16[128,128]{1,0:T(8,128)(2,1)S(1)}, bf16[128,128]{1,0:T(8,128)(2,1)S(1)}, u32[]{:S(2)}, u32[]{:S(2)}) collective-permute-start(bf16[128,128]{1,0:T(8,128)(2,1)S(1)} %get-tuple-element.90), channel_id=1, source_target_pairs={{0,2},{2,0},{4,6},{6,4},{1,3},{3,1},{5,7},{7,5},{8,10},{10,8},{12,... | collective-permute-start | bytes 98312 | tf_op jit(solution)/shard_map/ppermute | solution.py:187
  10.5 5.8 %collective-permute-start.11 = (bf16[128,128]{1,0:T(8,128)(2,1)S(1)}, bf16[128,128]{1,0:T(8,128)(2,1)S(1)}, u32[]{:S(2)}, u32[]{:S(2)}) collective-permute-start(bf16[128,128]{1,0:T(8,128)(2,1)S(1)} %get-tuple-element.96), channel_id=1, source_target_pairs={{0,24},{8,16},{16,8},{24,0},{1,25},{9,17},{17,9},{25,1},{2,26},{10... | collective-permute-start | bytes 98312 | tf_op jit(solution)/shard_map/ppermute | solution.py:187
  14.2 4.8 %collective-permute-start.10 = (bf16[128,128]{1,0:T(8,128)(2,1)S(1)}, bf16[128,128]{1,0:T(8,128)(2,1)S(1)}, u32[]{:S(2)}, u32[]{:S(2)}) collective-permute-start(bf16[128,128]{1,0:T(8,128)(2,1)S(1)} %get-tuple-element.96), channel_id=1, source_target_pairs={{0,16},{8,24},{16,0},{24,8},{1,17},{9,25},{17,1},{25,9},{2,18},{10... | collective-permute-start | bytes 98312 | tf_op jit(solution)/shard_map/ppermute | solution.py:187
  14.2 4.8 %collective-permute-start.9 = (bf16[128,128]{1,0:T(8,128)(2,1)S(1)}, bf16[128,128]{1,0:T(8,128)(2,1)S(1)}, u32[]{:S(2)}, u32[]{:S(2)}) collective-permute-start(bf16[128,128]{1,0:T(8,128)(2,1)S(1)} %get-tuple-element.96), channel_id=1, source_target_pairs={{0,8},{8,0},{16,24},{24,16},{1,9},{9,1},{17,25},{25,17},{2,10},{10... | collective-permute-start | bytes 98312 | tf_op jit(solution)/shard_map/ppermute | solution.py:187
  19.0 7.6 %collective-permute-start.12 = (f32[128,128]{1,0:T(8,128)S(1)}, f32[128,128]{1,0:T(8,128)S(1)}, u32[]{:S(2)}, u32[]{:S(2)}) collective-permute-start(f32[128,128]{1,0:T(8,128)S(1)} %get-tuple-element.99), channel_id=1, source_target_pairs={{0,1},{1,0},{2,3},{3,2},{4,5},{5,4},{6,7},{7,6},{8,9},{9,8},{10,11... | collective-permute-start | bytes 196616 | tf_op jit(solution)/shard_map/ppermute | solution.py:204
  19.2 5.0 %collective-permute-start = (bf16[128,128]{1,0:T(8,128)(2,1)S(1)}, bf16[128,128]{1,0:T(8,128)(2,1)S(1)}, u32[]{:S(2)}, u32[]{:S(2)}) collective-permute-start(bf16[128,128]{1,0:T(8,128)(2,1)S(1)} %get-tuple-element.56), channel_id=1, source_target_pairs={{0,6},{2,4},{4,2},{6,0},{1,7},{3,5},{5,3},{7,1},{8,14},{10,12},{12... | collective-permute-start | bytes 98312 | tf_op jit(solution)/shard_map/cond/branch_1_fun/ppermute | solution.py:187
  20.8 4.4 %collective-permute-start.1 = (bf16[128,128]{1,0:T(8,128)(2,1)S(1)}, bf16[128,128]{1,0:T(8,128)(2,1)S(1)}, u32[]{:S(2)}, u32[]{:S(2)}) collective-permute-start(bf16[128,128]{1,0:T(8,128)(2,1)S(1)} %get-tuple-element.57), channel_id=1, source_target_pairs={{0,4},{2,6},{4,0},{6,2},{1,5},{3,7},{5,1},{7,3},{8,12},{10,14},{12... | collective-permute-start | bytes 98312 | tf_op jit(solution)/shard_map/cond/branch_1_fun/ppermute | solution.py:187
  21.3 4.1 %collective-permute-start.2 = (bf16[128,128]{1,0:T(8,128)(2,1)S(1)}, bf16[128,128]{1,0:T(8,128)(2,1)S(1)}, u32[]{:S(2)}, u32[]{:S(2)}) collective-permute-start(bf16[128,128]{1,0:T(8,128)(2,1)S(1)} %get-tuple-element.58), channel_id=1, source_target_pairs={{0,2},{2,0},{4,6},{6,4},{1,3},{3,1},{5,7},{7,5},{8,10},{10,8},{12,... | collective-permute-start | bytes 98312 | tf_op jit(solution)/shard_map/cond/branch_1_fun/ppermute | solution.py:187

commit v16 on v15

--- a/solution.py
+++ b/solution.py
@@ -119,41 +119,34 @@
         out_ref[:, lanes_of(p)] = jnp.where(first, intra[0], intra[1])
 
 
-def settle_kernel(inner, *refs):
-    *parts, out_ref = refs
-    me = lax.axis_index("inner")
-    for d, part in zip(reversed(range(inner)), parts):
-        out_ref[me ^ d] = part[...]
-
-
 def unused_kernel(*refs):
     del refs
 
 
-def attend_kernel(q_ref, intra_ref, prefix_ref, *refs):
-    *_, out_hbm, out_ref, sent = refs
-    share = prefix_ref.shape[1]
-    heads = SLAB // HEAD_DIM
+def attend_kernel(away, q_ref, intra_ref, *refs):
+    parts, (out_hbm, out_ref, sent) = refs[:len(away)], refs[-3:]
     blocks = ([lax.broadcasted_iota(jnp.int32, (SLAB, SLAB), d) // HEAD_DIM for d in range(2)])
     same = blocks[0] == blocks[1]
     ones = jnp.where(same, 1.0, 0.0).astype(BF16)
     zero = jnp.zeros((), BF16)
+    me = lax.axis_index("inner")
+    width = parts[0].shape[0] // HEAD_DIM * LANES
     copies = []
-    for s in range(HEADS // heads):
-        lanes = slice(s * SLAB, (s + 1) * SLAB)
-        rows = []
-        for p in range(s * heads // 2, (s + 1) * heads // 2):
-            row = p * HEAD_DIM
-            pair = prefix_ref[row // share, row % share:row % share + HEAD_DIM, :]
-            rows += [jnp.concatenate([pair] * (SLAB // LANES), axis=1)] * 2
-        prefix = jnp.where(same, jnp.concatenate(rows, axis=0), zero)
-        inter = jnp.dot(q_ref[:, lanes], prefix, preferred_element_type=F32)
-        total = intra_ref[:, lanes] + inter
-        square = total * total
-        sums = jnp.dot(square.astype(BF16), ones, preferred_element_type=F32)
-        out_ref[:, lanes] = (total * lax.rsqrt(sums * (1.0 / HEAD_DIM) + 1e-6)).astype(out_ref.dtype)
-        copies.append(pltpu.make_async_copy(out_ref.at[:, lanes], out_hbm.at[:, lanes], sent.at[s]))
-        copies[-1].start()
+    for j, (d, part) in enumerate(zip(away, parts)):
+        for t in range(width // SLAB):
+            lanes = pl.ds(pl.multiple_of((me ^ d) * width + t * SLAB, SLAB), SLAB)
+            rows = []
+            for p in range(t * SLAB // LANES, (t + 1) * SLAB // LANES):
+                rows += [jnp.concatenate([part[rows_of(p), :]] * (SLAB // LANES), axis=1)] * 2
+            prefix = jnp.where(same, jnp.concatenate(rows, axis=0), zero)
+            inter = jnp.dot(q_ref[:, lanes], prefix, preferred_element_type=F32)
+            total = intra_ref[:, lanes] + inter
+            square = total * total
+            sums = jnp.dot(square.astype(BF16), ones, preferred_element_type=F32)
+            n = len(copies)
+            out_ref[n] = (total * lax.rsqrt(sums * (1.0 / HEAD_DIM) + 1e-6)).astype(out_ref.dtype)
+            copies.append(pltpu.make_async_copy(out_ref.at[n], out_hbm.at[:, lanes], sent.at[n]))
+            copies[-1].start()
     for copy in copies:
         copy.wait()
 
@@ -211,10 +204,13 @@
         prefix = swapped(before, "inner", before[0])
         intra = call(intra_kernel, (queries.shape, F32), queries, keys, values,
                      flops=4 * rows * rows * HEADS * HEAD_DIM)
-        prefix = call(functools.partial(settle_kernel, inner), ((inner,) + share, BF16), *prefix)
-        return call(attend_kernel, output, queries, intra, prefix, result=pltpu.HBM, onto=onto,
-                    flops=2 * rows * SLAB * HEADS * HEAD_DIM,
-                    scratch=[pltpu.VMEM(*output), pltpu.SemaphoreType.DMA((HEADS * HEAD_DIM // SLAB,))])
+        for away in (0, inner - 1), tuple(range(1, inner - 1)):
+            slabs = len(away) * HEADS * HEAD_DIM // inner // SLAB
+            onto = call(functools.partial(attend_kernel, away), output, queries, intra,
+                        *[prefix[inner - 1 - d] for d in away], result=pltpu.HBM, onto=onto,
+                        flops=2 * rows * SLAB * slabs * SLAB,
+                        scratch=[pltpu.VMEM((slabs, rows, SLAB), BF16), pltpu.SemaphoreType.DMA((slabs,))])
+        return onto
 
     out = lax.cond(leads, lambda: way_back(None, below), lambda: call(unused_kernel, output, result=pltpu.HBM))
     out, groups = lax.optimization_barrier((out, groups))

time: 26.8 us -> 27.6 us (1.030)
  Pallas kernels: 4.96 us -> 5.88 us
    pallas_call x7, Pallas kernels: 4.96 us -> 5.88 us  [call(): pl.pallas_call(kernel, out_shape=[result(shape, dtype) for shape, dtype i...]
  transfers between devices with their start and end apart: 10 -> 10, of which waited for: 7 -> 6; matrix products, arithmetic and copies ran while one was open for 0% -> 0% of each run, Pallas kernels for 11% -> 14%
where the time goes in v16:
time: 27.6 us; the launch traced here: 27.5 us
  starting transfers between devices  12.7 us (46%)
  waiting for transfers between devices  8.79 us (32%)
  Pallas kernels  5.88 us (21%)
    ppermute x9, starting transfers between devices, swapped(): lax.ppermute(arrays[d], axis, [(i, i ^ d) for i in range(size)])  12.6 us
    ppermute x9, waiting for transfers between devices, swapped(): lax.ppermute(arrays[d], axis, [(i, i ^ d) for i in range(size)])  8.79 us
    pallas_call x7, Pallas kernels, call(): pl.pallas_call(kernel, out_shape=[result(shape, dtype) for shape, dtype i...  5.88 us
  transfers between devices with their start and end apart: 10, of which 6 were waited for; matrix products, arithmetic and copies ran while one was open for 0% of the time, Pallas kernels for 14%

profile of v16, /device:TPU:0, one launch (start us, length us, event | category | flops | bytes accessed | tf_op | source)
XLA Modules:
  0.0 27.5 jit_solution(4512052932025324152)
XLA Ops:
  0.0 0.0 copy-start
  0.0 2.1 %shard_map.39 = (f32[128,128]{1,0:T(8,128)S(1)}, bf16[128,128]{1,0:T(8,128)(2,1)S(1)}, bf16[128,128]{1,0:T(8,128)(2,1)S(1)}, bf16[128,128]{1,0:T(8,128)(2,1)S(1)...) custom-call(bf16[256,1024]{1,0:T(8,128)(2,1)} %k_hbm.1, bf16[256,1024]{1,0:T(8,128)(2,1)} %v_hbm.1), custom_call_target="tpu_custom_call" | custom-call | flops 67108864 | bytes 1048576 | tf_op jit(solution)/shard_map/pallas_call | solution.py:165
  2.1 4.0 %collective-permute-start.6 = (bf16[128,128]{1,0:T(8,128)(2,1)S(1)}, bf16[128,128]{1,0:T(8,128)(2,1)S(1)}, u32[]{:S(2)}, u32[]{:S(2)}) collective-permute-start(bf16[128,128]{1,0:T(8,128)(2,1)S(1)} %get-tuple-element.88), channel_id=1, source_target_pairs={{0,6},{2,4},{4,2},{6,0},{1,7},{3,5},{5,3},{7,1},{8,14},{10,12},{12... | collective-permute-start | bytes 98312 | tf_op jit(solution)/shard_map/ppermute | solution.py:180
  6.1 0.5 %collective-permute-start.7 = (bf16[128,128]{1,0:T(8,128)(2,1)S(1)}, bf16[128,128]{1,0:T(8,128)(2,1)S(1)}, u32[]{:S(2)}, u32[]{:S(2)}) collective-permute-start(bf16[128,128]{1,0:T(8,128)(2,1)S(1)} %get-tuple-element.89), channel_id=1, source_target_pairs={{0,4},{2,6},{4,0},{6,2},{1,5},{3,7},{5,1},{7,3},{8,12},{10,14},{12... | collective-permute-start | bytes 98312 | tf_op jit(solution)/shard_map/ppermute | solution.py:180
  6.6 0.1 collective-permute-start.8
  6.7 1.3 %collective-permute-done.6.refs_0_ = bf16[128,128]{1,0:T(8,128)(2,1)S(1)} collective-permute-done((bf16[128,128]{1,0:T(8,128)(2,1)S(1)}, bf16[128,128]{1,0:T(8,128)(2,1)S(1)}, u32[]{:S(2)}, u32[]{:S(2)}) %collective-permute-start.6) | collective-permute-done | bytes 32800 | tf_op jit(solution)/shard_map/ppermute | solution.py:180
  8.0 2.0 %collective-permute-done.7.refs_1_ = bf16[128,128]{1,0:T(8,128)(2,1)S(1)} collective-permute-done((bf16[128,128]{1,0:T(8,128)(2,1)S(1)}, bf16[128,128]{1,0:T(8,128)(2,1)S(1)}, u32[]{:S(2)}, u32[]{:S(2)}) %collective-permute-start.7) | collective-permute-done | bytes 32800 | tf_op jit(solution)/shard_map/ppermute | solution.py:180
  10.0 0.5 %collective-permute-done.8.refs_2_ = bf16[128,128]{1,0:T(8,128)(2,1)S(1)} collective-permute-done((bf16[128,128]{1,0:T(8,128)(2,1)S(1)}, bf16[128,128]{1,0:T(8,128)(2,1)S(1)}, u32[]{:S(2)}, u32[]{:S(2)}) %collective-permute-start.8) | collective-permute-done | bytes 32800 | tf_op jit(solution)/shard_map/ppermute | solution.py:180
  10.5 3.7 %collective-permute-start.11 = (bf16[128,128]{1,0:T(8,128)(2,1)S(1)}, bf16[128,128]{1,0:T(8,128)(2,1)S(1)}, u32[]{:S(2)}, u32[]{:S(2)}) collective-permute-start(bf16[128,128]{1,0:T(8,128)(2,1)S(1)} %get-tuple-element.96), channel_id=1, source_target_pairs={{0,24},{8,16},{16,8},{24,0},{1,25},{9,17},{17,9},{25,1},{2,26},{10... | collective-permute-start | bytes 98312 | tf_op jit(solution)/shard_map/ppermute | solution.py:180
  14.2 0.0 collective-permute-start.10
  14.2 0.8 %collective-permute-start.9 = (bf16[128,128]{1,0:T(8,128)(2,1)S(1)}, bf16[128,128]{1,0:T(8,128)(2,1)S(1)}, u32[]{:S(2)}, u32[]{:S(2)}) collective-permute-start(bf16[128,128]{1,0:T(8,128)(2,1)S(1)} %get-tuple-element.96), channel_id=1, source_target_pairs={{0,8},{8,0},{16,24},{24,16},{1,9},{9,1},{17,25},{25,17},{2,10},{10... | collective-permute-start | bytes 98312 | tf_op jit(solution)/shard_map/ppermute | solution.py:180
  15.0 1.3 %collective-permute-done.11.refs_2_ = bf16[128,128]{1,0:T(8,128)(2,1)S(1)} collective-permute-done((bf16[128,128]{1,0:T(8,128)(2,1)S(1)}, bf16[128,128]{1,0:T(8,128)(2,1)S(1)}, u32[]{:S(2)}, u32[]{:S(2)}) %collective-permute-start.11) | collective-permute-done | bytes 32800 | tf_op jit(solution)/shard_map/ppermute | solution.py:180
  16.3 2.7 %collective-permute-done.10.refs_1_ = bf16[128,128]{1,0:T(8,128)(2,1)S(1)} collective-permute-done((bf16[128,128]{1,0:T(8,128)(2,1)S(1)}, bf16[128,128]{1,0:T(8,128)(2,1)S(1)}, u32[]{:S(2)}, u32[]{:S(2)}) %collective-permute-start.10) | collective-permute-done | bytes 32800 | tf_op jit(solution)/shard_map/ppermute | solution.py:180
  19.0 0.0 collective-permute-done.9.refs_0_
  19.0 0.1 collective-permute-start.12
  19.1 0.0 copy-done
  19.1 8.3 %conditional.2 = (bf16[256,1024]{1,0:T(8,128)(2,1)}) conditional(s32[]{:T(128)} %convert_element_type.4, () %tuple.20, (bf16[256,1024]{1,0:T(8,128)(2,1)S(1)}, bf16[256,1024]{1,0:T(8,128)(2,1)S(1)}, bf16[256,1024]{1,0:T(8,128)(2,1)S(1)}, bf16[128,128]{1,0:T(8,128)(2,1)S(1)}, bf16[128,128]{1,0:T(8,128)(2,1)S(1)}, ...), branch_computations={%region_0.0_spmd, %region_1.0_spmd} | conditional | flops 402653184 | bytes 5472384 | solution.py:215
  19.2 0.1 branch_1_fun.5
  19.2 1.6 %collective-permute-start.2 = (bf16[128,128]{1,0:T(8,128)(2,1)S(1)}, bf16[128,128]{1,0:T(8,128)(2,1)S(1)}, u32[]{:S(2)}, u32[]{:S(2)}) collective-permute-start(bf16[128,128]{1,0:T(8,128)(2,1)S(1)} %get-tuple-element.59), channel_id=1, source_target_pairs={{0,6},{2,4},{4,2},{6,0},{1,7},{3,5},{5,3},{7,1},{8,14},{10,12},{12... | collective-permute-start | bytes 98312 | tf_op jit(solution)/shard_map/cond/branch_1_fun/ppermute | solution.py:180
  20.8 1.5 %collective-permute-start = (bf16[128,128]{1,0:T(8,128)(2,1)S(1)}, bf16[128,128]{1,0:T(8,128)(2,1)S(1)}, u32[]{:S(2)}, u32[]{:S(2)}) collective-permute-start(bf16[128,128]{1,0:T(8,128)(2,1)S(1)} %get-tuple-element.56), channel_id=1, source_target_pairs={{0,2},{2,0},{4,6},{6,4},{1,3},{3,1},{5,7},{7,5},{8,10},{10,8},{12,... | collective-permute-start | bytes 98312 | tf_op jit(solution)/shard_map/cond/branch_1_fun/ppermute | solution.py:180
  22.3 0.5 %collective-permute-start.1 = (bf16[128,128]{1,0:T(8,128)(2,1)S(1)}, bf16[128,128]{1,0:T(8,128)(2,1)S(1)}, u32[]{:S(2)}, u32[]{:S(2)}) collective-permute-start(bf16[128,128]{1,0:T(8,128)(2,1)S(1)} %get-tuple-element.57), channel_id=1, source_target_pairs={{0,4},{2,6},{4,0},{6,2},{1,5},{3,7},{5,1},{7,3},{8,12},{10,14},{12... | collective-permute-start | bytes 98312 | tf_op jit(solution)/shard_map/cond/branch_1_fun/ppermute | solution.py:180
  22.8 1.5 %branch_1_fun.4.intra_ref = f32[256,1024]{1,0:T(8,128)S(1)} custom-call(bf16[256,1024]{1,0:T(8,128)(2,1)S(1)} %get-tuple-element.48.q_ref, bf16[256,1024]{1,0:T(8,128)(2,1)S(1)} %get-tuple-element.49.k_ref, bf16[256,1024]{1,0:T(8,128)(2,1)S(1)} %get-tuple-element.50.v_ref), custom_call_target="tpu_custom_call" | custom-call | flops 268435456 | bytes 1572864 | tf_op jit(solution)/shard_map/cond/branch_1_fun/pallas_call | solution.py:165
  24.3 0.0 collective-permute-done.2.refs_1_
  24.3 1.1 %branch_1_fun.6.refs_2_ = bf16[256,1024]{1,0:T(8,128)(2,1)} custom-call(bf16[256,1024]{1,0:T(8,128)(2,1)S(1)} %get-tuple-element.48.q_ref, f32[256,1024]{1,0:T(8,128)S(1)} %branch_1_fun.4.intra_ref, bf16[128,128]{1,0:T(8,128)(2,1)S(1)} %get-tuple-element.58.refs_0_, bf16[128,128]{1,0:T(8,128)(2,1)S(1)} %collective-permute-done.2.refs_1_), custom_call_target="tpu_custom_call" | custom-call | flops 67108864 | bytes 1638400 | tf_op jit(solution)/shard_map/cond/branch_1_fun/pallas_call | solution.py:165
  25.4 0.0 collective-permute-done.refs_0_
  25.4 1.0 %collective-permute-done.1.refs_1_ = bf16[128,128]{1,0:T(8,128)(2,1)S(1)} collective-permute-done((bf16[128,128]{1,0:T(8,128)(2,1)S(1)}, bf16[128,128]{1,0:T(8,128)(2,1)S(1)}, u32[]{:S(2)}, u32[]{:S(2)}) %collective-permute-start.1) | collective-permute-done | bytes 32800 | tf_op jit(solution)/shard_map/cond/branch_1_fun/ppermute | solution.py:180
  26.4 1.1 %branch_1_fun.7 = bf16[256,1024]{1,0:T(8,128)(2,1)} custom-call(bf16[256,1024]{1,0:T(8,128)(2,1)S(1)} %get-tuple-element.48.q_ref, f32[256,1024]{1,0:T(8,128)S(1)} %branch_1_fun.4.intra_ref, bf16[128,128]{1,0:T(8,128)(2,1)S(1)} %collective-permute-done.refs_0_, bf16[128,128]{1,0:T(8,128)(2,1)S(1)} %collective-permute-done.1.refs_1_, ...), custom_call_target="tpu_custom_call", output_to_operand_aliasing={{}: (4, {})} | custom-call | flops 67108864 | bytes 1638400 | tf_op jit(solution)/shard_map/cond/branch_1_fun/pallas_call | solution.py:165
  27.5 0.0 collective-permute-done.12
  (3 shorter events, 0.1 us)
Async XLA Ops:
  0.0 19.1 %copy-start = (bf16[256,1024]{1,0:T(8,128)(2,1)S(1)}, bf16[256,1024]{1,0:T(8,128)(2,1)}, u32[]{:S(2)}) copy-start(bf16[256,1024]{1,0:T(8,128)(2,1)} %param.7) | copy-start | bytes 1572868
  2.1 5.9 %collective-permute-start.6 = (bf16[128,128]{1,0:T(8,128)(2,1)S(1)}, bf16[128,128]{1,0:T(8,128)(2,1)S(1)}, u32[]{:S(2)}, u32[]{:S(2)}) collective-permute-start(bf16[128,128]{1,0:T(8,128)(2,1)S(1)} %get-tuple-element.88), channel_id=1, source_target_pairs={{0,6},{2,4},{4,2},{6,0},{1,7},{3,5},{5,3},{7,1},{8,14},{10,12},{12... | collective-permute-start | bytes 98312 | tf_op jit(solution)/shard_map/ppermute | solution.py:180
  6.1 3.9 %collective-permute-start.7 = (bf16[128,128]{1,0:T(8,128)(2,1)S(1)}, bf16[128,128]{1,0:T(8,128)(2,1)S(1)}, u32[]{:S(2)}, u32[]{:S(2)}) collective-permute-start(bf16[128,128]{1,0:T(8,128)(2,1)S(1)} %get-tuple-element.89), channel_id=1, source_target_pairs={{0,4},{2,6},{4,0},{6,2},{1,5},{3,7},{5,1},{7,3},{8,12},{10,14},{12... | collective-permute-start | bytes 98312 | tf_op jit(solution)/shard_map/ppermute | solution.py:180
  6.6 3.9 %collective-permute-start.8 = (bf16[128,128]{1,0:T(8,128)(2,1)S(1)}, bf16[128,128]{1,0:T(8,128)(2,1)S(1)}, u32[]{:S(2)}, u32[]{:S(2)}) collective-permute-start(bf16[128,128]{1,0:T(8,128)(2,1)S(1)} %get-tuple-element.90), channel_id=1, source_target_pairs={{0,2},{2,0},{4,6},{6,4},{1,3},{3,1},{5,7},{7,5},{8,10},{10,8},{12,... | collective-permute-start | bytes 98312 | tf_op jit(solution)/shard_map/ppermute | solution.py:180
  10.5 5.8 %collective-permute-start.11 = (bf16[128,128]{1,0:T(8,128)(2,1)S(1)}, bf16[128,128]{1,0:T(8,128)(2,1)S(1)}, u32[]{:S(2)}, u32[]{:S(2)}) collective-permute-start(bf16[128,128]{1,0:T(8,128)(2,1)S(1)} %get-tuple-element.96), channel_id=1, source_target_pairs={{0,24},{8,16},{16,8},{24,0},{1,25},{9,17},{17,9},{25,1},{2,26},{10... | collective-permute-start | bytes 98312 | tf_op jit(solution)/shard_map/ppermute | solution.py:180
  14.2 4.8 %collective-permute-start.10 = (bf16[128,128]{1,0:T(8,128)(2,1)S(1)}, bf16[128,128]{1,0:T(8,128)(2,1)S(1)}, u32[]{:S(2)}, u32[]{:S(2)}) collective-permute-start(bf16[128,128]{1,0:T(8,128)(2,1)S(1)} %get-tuple-element.96), channel_id=1, source_target_pairs={{0,16},{8,24},{16,0},{24,8},{1,17},{9,25},{17,1},{25,9},{2,18},{10... | collective-permute-start | bytes 98312 | tf_op jit(solution)/shard_map/ppermute | solution.py:180
  14.2 4.8 %collective-permute-start.9 = (bf16[128,128]{1,0:T(8,128)(2,1)S(1)}, bf16[128,128]{1,0:T(8,128)(2,1)S(1)}, u32[]{:S(2)}, u32[]{:S(2)}) collective-permute-start(bf16[128,128]{1,0:T(8,128)(2,1)S(1)} %get-tuple-element.96), channel_id=1, source_target_pairs={{0,8},{8,0},{16,24},{24,16},{1,9},{9,1},{17,25},{25,17},{2,10},{10... | collective-permute-start | bytes 98312 | tf_op jit(solution)/shard_map/ppermute | solution.py:180
  19.0 8.4 %collective-permute-start.12 = (f32[128,128]{1,0:T(8,128)S(1)}, f32[128,128]{1,0:T(8,128)S(1)}, u32[]{:S(2)}, u32[]{:S(2)}) collective-permute-start(f32[128,128]{1,0:T(8,128)S(1)} %get-tuple-element.99), channel_id=1, source_target_pairs={{0,1},{1,0},{2,3},{3,2},{4,5},{5,4},{6,7},{7,6},{8,9},{9,8},{10,11... | collective-permute-start | bytes 196616 | tf_op jit(solution)/shard_map/ppermute | solution.py:197
  19.2 5.0 %collective-permute-start.2 = (bf16[128,128]{1,0:T(8,128)(2,1)S(1)}, bf16[128,128]{1,0:T(8,128)(2,1)S(1)}, u32[]{:S(2)}, u32[]{:S(2)}) collective-permute-start(bf16[128,128]{1,0:T(8,128)(2,1)S(1)} %get-tuple-element.59), channel_id=1, source_target_pairs={{0,6},{2,4},{4,2},{6,0},{1,7},{3,5},{5,3},{7,1},{8,14},{10,12},{12... | collective-permute-start | bytes 98312 | tf_op jit(solution)/shard_map/cond/branch_1_fun/ppermute | solution.py:180
  20.8 4.6 %collective-permute-start = (bf16[128,128]{1,0:T(8,128)(2,1)S(1)}, bf16[128,128]{1,0:T(8,128)(2,1)S(1)}, u32[]{:S(2)}, u32[]{:S(2)}) collective-permute-start(bf16[128,128]{1,0:T(8,128)(2,1)S(1)} %get-tuple-element.56), channel_id=1, source_target_pairs={{0,2},{2,0},{4,6},{6,4},{1,3},{3,1},{5,7},{7,5},{8,10},{10,8},{12,... | collective-permute-start | bytes 98312 | tf_op jit(solution)/shard_map/cond/branch_1_fun/ppermute | solution.py:180
  22.3 4.1 %collective-permute-start.1 = (bf16[128,128]{1,0:T(8,128)(2,1)S(1)}, bf16[128,128]{1,0:T(8,128)(2,1)S(1)}, u32[]{:S(2)}, u32[]{:S(2)}) collective-permute-start(bf16[128,128]{1,0:T(8,128)(2,1)S(1)} %get-tuple-element.57), channel_id=1, source_target_pairs={{0,4},{2,6},{4,0},{6,2},{1,5},{3,7},{5,1},{7,3},{8,12},{10,14},{12... | collective-permute-start | bytes 98312 | tf_op jit(solution)/shard_map/cond/branch_1_fun/ppermute | solution.py:180

commit v17 on v15

--- a/solution.py
+++ b/solution.py
@@ -76,9 +76,9 @@
     plane = lax.axis_index("outer")
     whole = own[...]
     below = jnp.zeros_like(whole)
-    for e, there in enumerate(totals, 1):
+    for s, there in zip(reversed(range(1, len(totals) + 1)), totals):
         there = there[...].astype(F32)
-        below = below + jnp.where((plane ^ e) < plane, there, 0.0)
+        below = below + jnp.where(plane >= s, there, 0.0)
         whole = whole + there
     below_ref[...] = below
     whole_ref[...] = whole
@@ -198,8 +198,8 @@
     mine = swapped([own] + states, "inner", own)
     total, sent = call(totals_kernel, [(share, F32), (share, BF16)], *mine)
     total, queries = lax.optimization_barrier((total, queries))
-    *totals, _ = swapped([sent] * planes, "outer", total)
-    totals = totals[::-1] + [total]
+    totals = [lax.ppermute(sent, "outer", [(z, (z + s) % planes) for z in range(planes)])
+              for s in reversed(range(1, planes))] + [total]
     below, whole = call(planes_kernel, [(share, F32)] * 2, *totals)
     groups = [lax.ppermute(whole, "chain", [(c, c ^ d) for c in range(chains)]) for d in range(1, chains)]
     leads = lax.axis_index("chain") == 0

time: 26.8 us -> 26.5 us (0.989)
  waiting for transfers between devices: 8.91 us -> 7.44 us
  starting transfers between devices: 12.7 us -> 13.8 us
    ppermute x0 -> x3, starting transfers between devices: none -> 5.57 us  [per_device(): lax.ppermute(sent, 'outer', [(z, (z + s) % planes) for z in range(planes)])]
    ppermute x9 -> x6, starting transfers between devices: 12.6 us -> 8.16 us  [swapped(): lax.ppermute(arrays[d], axis, [(i, i ^ d) for i in range(size)])]
    ppermute x9 -> x6, waiting for transfers between devices: 8.9 us -> 4.87 us  [swapped(): lax.ppermute(arrays[d], axis, [(i, i ^ d) for i in range(size)])]
    ppermute x0 -> x3, waiting for transfers between devices: none -> 2.57 us  [per_device(): lax.ppermute(sent, 'outer', [(z, (z + s) % planes) for z in range(planes)])]
  transfers between devices with their start and end apart: 10 -> 10, of which waited for: 7 -> 8; matrix products, arithmetic and copies ran while one was open for 0% -> 0% of each run, Pallas kernels for 11% -> 11%
where the time goes in v17:
time: 26.5 us; the launch traced here: 26.3 us
  starting transfers between devices  13.8 us (52%)
  waiting for transfers between devices  7.44 us (28%)
  Pallas kernels  4.96 us (19%)
    ppermute x6, starting transfers between devices, swapped(): lax.ppermute(arrays[d], axis, [(i, i ^ d) for i in range(size)])  8.16 us
    ppermute x3, starting transfers between devices, per_device(): lax.ppermute(sent, 'outer', [(z, (z + s) % planes) for z in range(planes)])  5.57 us
    pallas_call x7, Pallas kernels, call(): pl.pallas_call(kernel, out_shape=[result(shape, dtype) for shape, dtype i...  4.96 us
    ppermute x6, waiting for transfers between devices, swapped(): lax.ppermute(arrays[d], axis, [(i, i ^ d) for i in range(size)])  4.87 us
    ppermute x3, waiting for transfers between devices, per_device(): lax.ppermute(sent, 'outer', [(z, (z + s) % planes) for z in range(planes)])  2.57 us
  transfers between devices with their start and end apart: 10, of which 8 were waited for; matrix products, arithmetic and copies ran while one was open for 0% of the time, Pallas kernels for 11%

profile of v17, /device:TPU:0, one launch (start us, length us, event | category | flops | bytes accessed | tf_op | source)
XLA Modules:
  0.0 26.3 jit_solution(14472724276016421526)
XLA Ops:
  0.0 0.0 copy-start
  0.0 2.1 %shard_map.39 = (f32[128,128]{1,0:T(8,128)S(1)}, bf16[128,128]{1,0:T(8,128)(2,1)S(1)}, bf16[128,128]{1,0:T(8,128)(2,1)S(1)}, bf16[128,128]{1,0:T(8,128)(2,1)S(1)...) custom-call(bf16[256,1024]{1,0:T(8,128)(2,1)} %k_hbm.1, bf16[256,1024]{1,0:T(8,128)(2,1)} %v_hbm.1), custom_call_target="tpu_custom_call" | custom-call | flops 67108864 | bytes 1048576 | tf_op jit(solution)/shard_map/pallas_call | solution.py:172
  2.1 4.0 %collective-permute-start.6 = (bf16[128,128]{1,0:T(8,128)(2,1)S(1)}, bf16[128,128]{1,0:T(8,128)(2,1)S(1)}, u32[]{:S(2)}, u32[]{:S(2)}) collective-permute-start(bf16[128,128]{1,0:T(8,128)(2,1)S(1)} %get-tuple-element.88), channel_id=1, source_target_pairs={{0,6},{2,4},{4,2},{6,0},{1,7},{3,5},{5,3},{7,1},{8,14},{10,12},{12... | collective-permute-start | bytes 98312 | tf_op jit(solution)/shard_map/ppermute | solution.py:187
  6.1 0.5 %collective-permute-start.7 = (bf16[128,128]{1,0:T(8,128)(2,1)S(1)}, bf16[128,128]{1,0:T(8,128)(2,1)S(1)}, u32[]{:S(2)}, u32[]{:S(2)}) collective-permute-start(bf16[128,128]{1,0:T(8,128)(2,1)S(1)} %get-tuple-element.89), channel_id=1, source_target_pairs={{0,4},{2,6},{4,0},{6,2},{1,5},{3,7},{5,1},{7,3},{8,12},{10,14},{12... | collective-permute-start | bytes 98312 | tf_op jit(solution)/shard_map/ppermute | solution.py:187
  6.6 0.1 collective-permute-start.8
  6.7 1.3 %collective-permute-done.6.refs_0_ = bf16[128,128]{1,0:T(8,128)(2,1)S(1)} collective-permute-done((bf16[128,128]{1,0:T(8,128)(2,1)S(1)}, bf16[128,128]{1,0:T(8,128)(2,1)S(1)}, u32[]{:S(2)}, u32[]{:S(2)}) %collective-permute-start.6) | collective-permute-done | bytes 32800 | tf_op jit(solution)/shard_map/ppermute | solution.py:187
  8.0 2.0 %collective-permute-done.7.refs_1_ = bf16[128,128]{1,0:T(8,128)(2,1)S(1)} collective-permute-done((bf16[128,128]{1,0:T(8,128)(2,1)S(1)}, bf16[128,128]{1,0:T(8,128)(2,1)S(1)}, u32[]{:S(2)}, u32[]{:S(2)}) %collective-permute-start.7) | collective-permute-done | bytes 32800 | tf_op jit(solution)/shard_map/ppermute | solution.py:187
  10.0 0.5 %collective-permute-done.8.refs_2_ = bf16[128,128]{1,0:T(8,128)(2,1)S(1)} collective-permute-done((bf16[128,128]{1,0:T(8,128)(2,1)S(1)}, bf16[128,128]{1,0:T(8,128)(2,1)S(1)}, u32[]{:S(2)}, u32[]{:S(2)}) %collective-permute-start.8) | collective-permute-done | bytes 32800 | tf_op jit(solution)/shard_map/ppermute | solution.py:187
  10.5 1.6 %collective-permute-start.11 = (bf16[128,128]{1,0:T(8,128)(2,1)S(1)}, bf16[128,128]{1,0:T(8,128)(2,1)S(1)}, u32[]{:S(2)}, u32[]{:S(2)}) collective-permute-start(bf16[128,128]{1,0:T(8,128)(2,1)S(1)} %get-tuple-element.96), channel_id=1, source_target_pairs={{0,8},{8,16},{16,24},{24,0},{1,9},{9,17},{17,25},{25,1},{2,10},{10... | collective-permute-start | bytes 98312 | tf_op jit(solution)/shard_map/ppermute | solution.py:201
  12.1 2.6 %collective-permute-start.10 = (bf16[128,128]{1,0:T(8,128)(2,1)S(1)}, bf16[128,128]{1,0:T(8,128)(2,1)S(1)}, u32[]{:S(2)}, u32[]{:S(2)}) collective-permute-start(bf16[128,128]{1,0:T(8,128)(2,1)S(1)} %get-tuple-element.96), channel_id=1, source_target_pairs={{0,16},{8,24},{16,0},{24,8},{1,17},{9,25},{17,1},{25,9},{2,18},{10... | collective-permute-start | bytes 98312 | tf_op jit(solution)/shard_map/ppermute | solution.py:201
  14.7 1.3 %collective-permute-start.9 = (bf16[128,128]{1,0:T(8,128)(2,1)S(1)}, bf16[128,128]{1,0:T(8,128)(2,1)S(1)}, u32[]{:S(2)}, u32[]{:S(2)}) collective-permute-start(bf16[128,128]{1,0:T(8,128)(2,1)S(1)} %get-tuple-element.96), channel_id=1, source_target_pairs={{0,24},{8,0},{16,8},{24,16},{1,25},{9,1},{17,9},{25,17},{2,26},{10... | collective-permute-start | bytes 98312 | tf_op jit(solution)/shard_map/ppermute | solution.py:201
  16.1 0.2 collective-permute-done.11.refs_2_
  16.3 0.7 %collective-permute-done.10.refs_1_ = bf16[128,128]{1,0:T(8,128)(2,1)S(1)} collective-permute-done((bf16[128,128]{1,0:T(8,128)(2,1)S(1)}, bf16[128,128]{1,0:T(8,128)(2,1)S(1)}, u32[]{:S(2)}, u32[]{:S(2)}) %collective-permute-start.10) | collective-permute-done | bytes 32800 | tf_op jit(solution)/shard_map/ppermute | solution.py:201
  17.0 1.7 %collective-permute-done.9.refs_0_ = bf16[128,128]{1,0:T(8,128)(2,1)S(1)} collective-permute-done((bf16[128,128]{1,0:T(8,128)(2,1)S(1)}, bf16[128,128]{1,0:T(8,128)(2,1)S(1)}, u32[]{:S(2)}, u32[]{:S(2)}) %collective-permute-start.9) | collective-permute-done | bytes 32800 | tf_op jit(solution)/shard_map/ppermute | solution.py:201
  18.7 0.1 collective-permute-start.12
  18.8 0.0 copy-done
  18.8 7.5 %conditional.2 = (bf16[256,1024]{1,0:T(8,128)(2,1)}) conditional(s32[]{:T(128)} %convert_element_type.4, () %tuple.20, (bf16[256,1024]{1,0:T(8,128)(2,1)S(1)}, bf16[256,1024]{1,0:T(8,128)(2,1)S(1)}, bf16[256,1024]{1,0:T(8,128)(2,1)S(1)}, bf16[128,128]{1,0:T(8,128)(2,1)S(1)}, bf16[128,128]{1,0:T(8,128)(2,1)S(1)}, ...), branch_computations={%region_0.0_spmd, %region_1.0_spmd} | conditional | flops 402653184 | bytes 4030592 | solution.py:219
  18.8 0.1 branch_1_fun.5
  18.9 1.6 %collective-permute-start = (bf16[128,128]{1,0:T(8,128)(2,1)S(1)}, bf16[128,128]{1,0:T(8,128)(2,1)S(1)}, u32[]{:S(2)}, u32[]{:S(2)}) collective-permute-start(bf16[128,128]{1,0:T(8,128)(2,1)S(1)} %get-tuple-element.56), channel_id=1, source_target_pairs={{0,6},{2,4},{4,2},{6,0},{1,7},{3,5},{5,3},{7,1},{8,14},{10,12},{12... | collective-permute-start | bytes 98312 | tf_op jit(solution)/shard_map/cond/branch_1_fun/ppermute | solution.py:187
  20.4 0.5 %collective-permute-start.1 = (bf16[128,128]{1,0:T(8,128)(2,1)S(1)}, bf16[128,128]{1,0:T(8,128)(2,1)S(1)}, u32[]{:S(2)}, u32[]{:S(2)}) collective-permute-start(bf16[128,128]{1,0:T(8,128)(2,1)S(1)} %get-tuple-element.57), channel_id=1, source_target_pairs={{0,4},{2,6},{4,0},{6,2},{1,5},{3,7},{5,1},{7,3},{8,12},{10,14},{12... | collective-permute-start | bytes 98312 | tf_op jit(solution)/shard_map/cond/branch_1_fun/ppermute | solution.py:187
  20.9 1.5 %collective-permute-start.2 = (bf16[128,128]{1,0:T(8,128)(2,1)S(1)}, bf16[128,128]{1,0:T(8,128)(2,1)S(1)}, u32[]{:S(2)}, u32[]{:S(2)}) collective-permute-start(bf16[128,128]{1,0:T(8,128)(2,1)S(1)} %get-tuple-element.58), channel_id=1, source_target_pairs={{0,2},{2,0},{4,6},{6,4},{1,3},{3,1},{5,7},{7,5},{8,10},{10,8},{12,... | collective-permute-start | bytes 98312 | tf_op jit(solution)/shard_map/cond/branch_1_fun/ppermute | solution.py:187
  22.4 1.5 %branch_1_fun.4.intra_ref = f32[256,1024]{1,0:T(8,128)S(1)} custom-call(bf16[256,1024]{1,0:T(8,128)(2,1)S(1)} %get-tuple-element.48.q_ref, bf16[256,1024]{1,0:T(8,128)(2,1)S(1)} %get-tuple-element.49.k_ref, bf16[256,1024]{1,0:T(8,128)(2,1)S(1)} %get-tuple-element.50.v_ref), custom_call_target="tpu_custom_call" | custom-call | flops 268435456 | bytes 1572864 | tf_op jit(solution)/shard_map/cond/branch_1_fun/pallas_call | solution.py:172
  23.9 0.0 collective-permute-done.refs_0_
  23.9 0.9 %collective-permute-done.1.refs_1_ = bf16[128,128]{1,0:T(8,128)(2,1)S(1)} collective-permute-done((bf16[128,128]{1,0:T(8,128)(2,1)S(1)}, bf16[128,128]{1,0:T(8,128)(2,1)S(1)}, u32[]{:S(2)}, u32[]{:S(2)}) %collective-permute-start.1) | collective-permute-done | bytes 32800 | tf_op jit(solution)/shard_map/cond/branch_1_fun/ppermute | solution.py:187
  24.8 0.2 collective-permute-done.2.refs_2_
  25.0 1.3 %branch_1_fun.7 = bf16[256,1024]{1,0:T(8,128)(2,1)} custom-call(bf16[256,1024]{1,0:T(8,128)(2,1)S(1)} %get-tuple-element.48.q_ref, f32[256,1024]{1,0:T(8,128)S(1)} %branch_1_fun.4.intra_ref, bf16[4,128,128]{2,1,0:T(8,128)(2,1)S(1)} %branch_1_fun.6.prefix_ref), custom_call_target="tpu_custom_call" | custom-call | flops 134217728 | bytes 1703936 | tf_op jit(solution)/shard_map/cond/branch_1_fun/pallas_call | solution.py:172
  26.3 0.0 collective-permute-done.12
  (4 shorter events, 0.1 us)
Async XLA Ops:
  0.0 18.8 %copy-start = (bf16[256,1024]{1,0:T(8,128)(2,1)S(1)}, bf16[256,1024]{1,0:T(8,128)(2,1)}, u32[]{:S(2)}) copy-start(bf16[256,1024]{1,0:T(8,128)(2,1)} %param.7) | copy-start | bytes 1572868
  2.1 5.9 %collective-permute-start.6 = (bf16[128,128]{1,0:T(8,128)(2,1)S(1)}, bf16[128,128]{1,0:T(8,128)(2,1)S(1)}, u32[]{:S(2)}, u32[]{:S(2)}) collective-permute-start(bf16[128,128]{1,0:T(8,128)(2,1)S(1)} %get-tuple-element.88), channel_id=1, source_target_pairs={{0,6},{2,4},{4,2},{6,0},{1,7},{3,5},{5,3},{7,1},{8,14},{10,12},{12... | collective-permute-start | bytes 98312 | tf_op jit(solution)/shard_map/ppermute | solution.py:187
  6.1 3.9 %collective-permute-start.7 = (bf16[128,128]{1,0:T(8,128)(2,1)S(1)}, bf16[128,128]{1,0:T(8,128)(2,1)S(1)}, u32[]{:S(2)}, u32[]{:S(2)}) collective-permute-start(bf16[128,128]{1,0:T(8,128)(2,1)S(1)} %get-tuple-element.89), channel_id=1, source_target_pairs={{0,4},{2,6},{4,0},{6,2},{1,5},{3,7},{5,1},{7,3},{8,12},{10,14},{12... | collective-permute-start | bytes 98312 | tf_op jit(solution)/shard_map/ppermute | solution.py:187
  6.6 3.9 %collective-permute-start.8 = (bf16[128,128]{1,0:T(8,128)(2,1)S(1)}, bf16[128,128]{1,0:T(8,128)(2,1)S(1)}, u32[]{:S(2)}, u32[]{:S(2)}) collective-permute-start(bf16[128,128]{1,0:T(8,128)(2,1)S(1)} %get-tuple-element.90), channel_id=1, source_target_pairs={{0,2},{2,0},{4,6},{6,4},{1,3},{3,1},{5,7},{7,5},{8,10},{10,8},{12,... | collective-permute-start | bytes 98312 | tf_op jit(solution)/shard_map/ppermute | solution.py:187
  10.5 5.8 %collective-permute-start.11 = (bf16[128,128]{1,0:T(8,128)(2,1)S(1)}, bf16[128,128]{1,0:T(8,128)(2,1)S(1)}, u32[]{:S(2)}, u32[]{:S(2)}) collective-permute-start(bf16[128,128]{1,0:T(8,128)(2,1)S(1)} %get-tuple-element.96), channel_id=1, source_target_pairs={{0,8},{8,16},{16,24},{24,0},{1,9},{9,17},{17,25},{25,1},{2,10},{10... | collective-permute-start | bytes 98312 | tf_op jit(solution)/shard_map/ppermute | solution.py:201
  12.1 4.8 %collective-permute-start.10 = (bf16[128,128]{1,0:T(8,128)(2,1)S(1)}, bf16[128,128]{1,0:T(8,128)(2,1)S(1)}, u32[]{:S(2)}, u32[]{:S(2)}) collective-permute-start(bf16[128,128]{1,0:T(8,128)(2,1)S(1)} %get-tuple-element.96), channel_id=1, source_target_pairs={{0,16},{8,24},{16,0},{24,8},{1,17},{9,25},{17,1},{25,9},{2,18},{10... | collective-permute-start | bytes 98312 | tf_op jit(solution)/shard_map/ppermute | solution.py:201
  14.7 3.9 %collective-permute-start.9 = (bf16[128,128]{1,0:T(8,128)(2,1)S(1)}, bf16[128,128]{1,0:T(8,128)(2,1)S(1)}, u32[]{:S(2)}, u32[]{:S(2)}) collective-permute-start(bf16[128,128]{1,0:T(8,128)(2,1)S(1)} %get-tuple-element.96), channel_id=1, source_target_pairs={{0,24},{8,0},{16,8},{24,16},{1,25},{9,1},{17,9},{25,17},{2,26},{10... | collective-permute-start | bytes 98312 | tf_op jit(solution)/shard_map/ppermute | solution.py:201
  18.7 7.6 %collective-permute-start.12 = (f32[128,128]{1,0:T(8,128)S(1)}, f32[128,128]{1,0:T(8,128)S(1)}, u32[]{:S(2)}, u32[]{:S(2)}) collective-permute-start(f32[128,128]{1,0:T(8,128)S(1)} %get-tuple-element.99), channel_id=1, source_target_pairs={{0,1},{1,0},{2,3},{3,2},{4,5},{5,4},{6,7},{7,6},{8,9},{9,8},{10,11... | collective-permute-start | bytes 196616 | tf_op jit(solution)/shard_map/ppermute | solution.py:204
  18.9 5.0 %collective-permute-start = (bf16[128,128]{1,0:T(8,128)(2,1)S(1)}, bf16[128,128]{1,0:T(8,128)(2,1)S(1)}, u32[]{:S(2)}, u32[]{:S(2)}) collective-permute-start(bf16[128,128]{1,0:T(8,128)(2,1)S(1)} %get-tuple-element.56), channel_id=1, source_target_pairs={{0,6},{2,4},{4,2},{6,0},{1,7},{3,5},{5,3},{7,1},{8,14},{10,12},{12... | collective-permute-start | bytes 98312 | tf_op jit(solution)/shard_map/cond/branch_1_fun/ppermute | solution.py:187
  20.4 4.4 %collective-permute-start.1 = (bf16[128,128]{1,0:T(8,128)(2,1)S(1)}, bf16[128,128]{1,0:T(8,128)(2,1)S(1)}, u32[]{:S(2)}, u32[]{:S(2)}) collective-permute-start(bf16[128,128]{1,0:T(8,128)(2,1)S(1)} %get-tuple-element.57), channel_id=1, source_target_pairs={{0,4},{2,6},{4,0},{6,2},{1,5},{3,7},{5,1},{7,3},{8,12},{10,14},{12... | collective-permute-start | bytes 98312 | tf_op jit(solution)/shard_map/cond/branch_1_fun/ppermute | solution.py:187
  20.9 4.1 %collective-permute-start.2 = (bf16[128,128]{1,0:T(8,128)(2,1)S(1)}, bf16[128,128]{1,0:T(8,128)(2,1)S(1)}, u32[]{:S(2)}, u32[]{:S(2)}) collective-permute-start(bf16[128,128]{1,0:T(8,128)(2,1)S(1)} %get-tuple-element.58), channel_id=1, source_target_pairs={{0,2},{2,0},{4,6},{6,4},{1,3},{3,1},{5,7},{7,5},{8,10},{10,8},{12,... | collective-permute-start | bytes 98312 | tf_op jit(solution)/shard_map/cond/branch_1_fun/ppermute | solution.py:187

commit v18 on v17

--- a/solution.py
+++ b/solution.py
@@ -12,7 +12,6 @@
 PAIRS = HEADS // 2
 LANES = 2 * HEAD_DIM
 SLABS = 4
-HALVES = 2
 SLAB = 256
 VMEM = pl.BlockSpec(memory_space=pltpu.VMEM)
 BF16 = jnp.bfloat16
@@ -31,35 +30,40 @@
     return slice(p * HEAD_DIM, (p + 1) * HEAD_DIM)
 
 
-def states_kernel(k_hbm, v_hbm, *refs):
-    *outs, k_ref, v_ref, states, arrived = refs
-    rows = k_ref.shape[0] // HALVES
+def share_states(k_ref, v_ref, out_ref, away):
+    first = first_head((HEAD_DIM, LANES))
+    width = out_ref.shape[0] // HEAD_DIM * LANES
+    start = (lax.axis_index("inner") ^ away) * width
+    for p in range(width // LANES):
+        lanes = pl.ds(pl.multiple_of(start + p * LANES, LANES), LANES)
+        both = lax.dot_general(
+            k_ref[:, lanes], v_ref[:, lanes], (((0,), (0,)), ((), ())), preferred_element_type=F32)
+        out_ref[rows_of(p), :] = jnp.where(first, both[:HEAD_DIM], both[HEAD_DIM:]).astype(out_ref.dtype)
+
+
+def first_kernel(away, k_hbm, v_hbm, out_ref, k_ref, v_ref, arrived):
     copies = []
     for s in range(SLABS):
         lanes = slice(s * SLAB, (s + 1) * SLAB)
-        copies.append([])
-        for r in range(HALVES):
-            part = (pl.ds(r * rows, rows), lanes)
-            copies[-1] += [
-                pltpu.make_async_copy(k_hbm.at[part], k_ref.at[part], arrived.at[0, s, r]),
-                pltpu.make_async_copy(v_hbm.at[part], v_ref.at[part], arrived.at[1, s, r])]
-        for copy in copies[-1]:
-            copy.start()
-    first = first_head((HEAD_DIM, LANES))
-    share = states.shape[1]
-    for p in range(PAIRS):
-        if p * LANES % SLAB == 0:
-            for copy in copies[p * LANES // SLAB]:
-                copy.wait()
-        both = lax.dot_general(
-            k_ref[:, lanes_of(p)], v_ref[:, lanes_of(p)], (((0,), (0,)), ((), ())),
-            preferred_element_type=jnp.float32)
-        packed = jnp.where(first, both[:HEAD_DIM], both[HEAD_DIM:])
-        row = p * HEAD_DIM
-        states[row // share, row % share:row % share + HEAD_DIM, :] = packed
-    me = lax.axis_index("inner")
-    for d, out in enumerate(outs):
-        out[...] = states[me ^ d].astype(out.dtype)
+        copies += [
+            pltpu.make_async_copy(k_hbm.at[:, lanes], k_ref.at[:, lanes], arrived.at[0, s]),
+            pltpu.make_async_copy(v_hbm.at[:, lanes], v_ref.at[:, lanes], arrived.at[1, s])]
+    for copy in copies:
+        copy.start()
+    for copy in copies:
+        copy.wait()
+    share_states(k_ref, v_ref, out_ref, away)
+
+
+def near_kernel(away, k_ref, v_ref, out_ref):
+    share_states(k_ref, v_ref, out_ref, away)
+
+
+def own_kernel(k_ref, v_ref, q_hbm, out_ref, q_ref, arrived):
+    copy = pltpu.make_async_copy(q_hbm, q_ref, arrived)
+    copy.start()
+    share_states(k_ref, v_ref, out_ref, 0)
+    copy.wait()
 
 
 def totals_kernel(*refs):
@@ -162,8 +166,9 @@
     moved = sum(a.size * a.dtype.itemsize for a in args)
     single = not isinstance(outs, list)
     outs = [outs] if single else outs
-    specs = [pl.BlockSpec(memory_space=source)] * len(args)
-    args = [pltpu.with_memory_space_constraint(a, source) for a in args]
+    sources = source if isinstance(source, list) else [source] * len(args)
+    specs = [pl.BlockSpec(memory_space=s) for s in sources]
+    args = [pltpu.with_memory_space_constraint(a, s) for a, s in zip(args, sources)]
     aliases = {}
     if onto is not None:
         aliases = {len(args): 0}
@@ -190,14 +195,17 @@
 def per_device(chains, planes, inner, queries, keys, values):
     rows = queries.shape[0]
     share = (PAIRS * HEAD_DIM // inner, LANES)
-    own, *states, keys, values = call(
-        states_kernel,
-        [(share, F32)] + [(share, BF16)] * (inner - 1) + [(keys.shape, keys.dtype), (values.shape, values.dtype)],
-        keys, values, flops=2 * rows * LANES * LANES * PAIRS, source=pltpu.HBM,
-        scratch=[pltpu.VMEM((inner,) + share, F32), pltpu.SemaphoreType.DMA((2, SLABS, HALVES))])
-    mine = swapped([own] + states, "inner", own)
+    flops = 2 * rows * LANES * share[0] // HEAD_DIM * LANES
+    sent, keys, values = call(
+        functools.partial(first_kernel, 1),
+        [(share, BF16), (keys.shape, keys.dtype), (values.shape, values.dtype)], keys, values,
+        flops=flops, source=pltpu.HBM, scratch=[pltpu.SemaphoreType.DMA((2, SLABS))])
+    near = [call(functools.partial(near_kernel, d), (share, BF16), keys, values, flops=flops) for d in range(2, inner)]
+    own, queries = call(
+        own_kernel, [(share, F32), (queries.shape, queries.dtype)], keys, values, queries, flops=flops,
+        source=[pltpu.VMEM, pltpu.VMEM, pltpu.HBM], scratch=[pltpu.SemaphoreType.DMA(())])
+    mine = swapped([own, sent] + near, "inner", own)
     total, sent = call(totals_kernel, [(share, F32), (share, BF16)], *mine)
-    total, queries = lax.optimization_barrier((total, queries))
     totals = [lax.ppermute(sent, "outer", [(z, (z + s) % planes) for z in range(planes)])
               for s in reversed(range(1, planes))] + [total]
     below, whole = call(planes_kernel, [(share, F32)] * 2, *totals)

time: 26.5 us -> 26.7 us (level)
  Pallas kernels: 4.96 us -> 6.08 us
  waiting for transfers between devices: 7.44 us -> 6.43 us
    pallas_call x7 -> x10, Pallas kernels: 4.96 us -> 6.08 us  [call(): pl.pallas_call(kernel, out_shape=[result(shape, dtype) for shape, dtype i...]
    ppermute x6, waiting for transfers between devices: 4.87 us -> 3.86 us  [swapped(): lax.ppermute(arrays[d], axis, [(i, i ^ d) for i in range(size)])]
  transfers between devices with their start and end apart: 10 -> 10, of which waited for: 8 -> 7; matrix products, arithmetic and copies ran while one was open for 0% -> 0% of each run, Pallas kernels for 11% -> 16%
where the time goes in v18:
time: 26.7 us; the launch traced here: 26.5 us
  starting transfers between devices  13.8 us (52%)
  waiting for transfers between devices  6.43 us (24%)
  Pallas kernels  6.08 us (23%)
    ppermute x6, starting transfers between devices, swapped(): lax.ppermute(arrays[d], axis, [(i, i ^ d) for i in range(size)])  8.19 us
    pallas_call x10, Pallas kernels, call(): pl.pallas_call(kernel, out_shape=[result(shape, dtype) for shape, dtype i...  6.08 us
    ppermute x3, starting transfers between devices, per_device(): lax.ppermute(sent, 'outer', [(z, (z + s) % planes) for z in range(planes)])  5.57 us
    ppermute x6, waiting for transfers between devices, swapped(): lax.ppermute(arrays[d], axis, [(i, i ^ d) for i in range(size)])  3.86 us
    ppermute x3, waiting for transfers between devices, per_device(): lax.ppermute(sent, 'outer', [(z, (z + s) % planes) for z in range(planes)])  2.56 us
  transfers between devices with their start and end apart: 10, of which 7 were waited for; matrix products, arithmetic and copies ran while one was open for 0% of the time, Pallas kernels for 16%

profile of v18, /device:TPU:0, one launch (start us, length us, event | category | flops | bytes accessed | tf_op | source)
XLA Modules:
  0.0 26.5 jit_solution(694277013564307475)
XLA Ops:
  0.0 1.6 %shard_map.39 = (bf16[128,128]{1,0:T(8,128)(2,1)S(1)}, bf16[256,1024]{1,0:T(8,128)(2,1)S(1)}, bf16[256,1024]{1,0:T(8,128)(2,1)S(1)}) custom-call(bf16[256,1024]{1,0:T(8,128)(2,1)} %k_hbm.1, bf16[256,1024]{1,0:T(8,128)(2,1)} %v_hbm.1), custom_call_target="tpu_custom_call" | custom-call | flops 16777216 | bytes 1048576 | tf_op jit(solution)/shard_map/pallas_call | solution.py:177
  1.6 0.3 %shard_map.41 = bf16[128,128]{1,0:T(8,128)(2,1)S(1)} custom-call(bf16[256,1024]{1,0:T(8,128)(2,1)S(1)} %get-tuple-element.85.k_ref, bf16[256,1024]{1,0:T(8,128)(2,1)S(1)} %get-tuple-element.86.v_ref), custom_call_target="tpu_custom_call" | custom-call | flops 16777216 | bytes 1048576 | tf_op jit(solution)/shard_map/pallas_call | solution.py:177
  1.9 4.0 %collective-permute-start.6 = (bf16[128,128]{1,0:T(8,128)(2,1)S(1)}, bf16[128,128]{1,0:T(8,128)(2,1)S(1)}, u32[]{:S(2)}, u32[]{:S(2)}) collective-permute-start(bf16[128,128]{1,0:T(8,128)(2,1)S(1)} %shard_map.41), channel_id=1, source_target_pairs={{0,6},{2,4},{4,2},{6,0},{1,7},{3,5},{5,3},{7,1},{8,14},{10,12},{12... | collective-permute-start | bytes 98312 | tf_op jit(solution)/shard_map/ppermute | solution.py:192
  5.9 0.3 shard_map.42
  6.2 0.6 %collective-permute-start.7 = (bf16[128,128]{1,0:T(8,128)(2,1)S(1)}, bf16[128,128]{1,0:T(8,128)(2,1)S(1)}, u32[]{:S(2)}, u32[]{:S(2)}) collective-permute-start(bf16[128,128]{1,0:T(8,128)(2,1)S(1)} %shard_map.42), channel_id=1, source_target_pairs={{0,4},{2,6},{4,0},{6,2},{1,5},{3,7},{5,1},{7,3},{8,12},{10,14},{12... | collective-permute-start | bytes 98312 | tf_op jit(solution)/shard_map/ppermute | solution.py:192
  6.7 0.1 collective-permute-start.8
  6.8 1.1 %shard_map.40 = (f32[128,128]{1,0:T(8,128)S(1)}, bf16[256,1024]{1,0:T(8,128)(2,1)S(1)}) custom-call(bf16[256,1024]{1,0:T(8,128)(2,1)S(1)} %get-tuple-element.85.k_ref, bf16[256,1024]{1,0:T(8,128)(2,1)S(1)} %get-tuple-element.86.v_ref, bf16[256,1024]{1,0:T(8,128)(2,1)} %q_hbm.1), custom_call_target="tpu_custom_call" | custom-call | flops 16777216 | bytes 1572864 | tf_op jit(solution)/shard_map/pallas_call | solution.py:177
  7.9 0.0 collective-permute-done.6.refs_0_
  7.9 2.2 %collective-permute-done.7.refs_1_ = bf16[128,128]{1,0:T(8,128)(2,1)S(1)} collective-permute-done((bf16[128,128]{1,0:T(8,128)(2,1)S(1)}, bf16[128,128]{1,0:T(8,128)(2,1)S(1)}, u32[]{:S(2)}, u32[]{:S(2)}) %collective-permute-start.7) | collective-permute-done | bytes 32800 | tf_op jit(solution)/shard_map/ppermute | solution.py:192
  10.1 0.5 %collective-permute-done.8.refs_2_ = bf16[128,128]{1,0:T(8,128)(2,1)S(1)} collective-permute-done((bf16[128,128]{1,0:T(8,128)(2,1)S(1)}, bf16[128,128]{1,0:T(8,128)(2,1)S(1)}, u32[]{:S(2)}, u32[]{:S(2)}) %collective-permute-start.8) | collective-permute-done | bytes 32800 | tf_op jit(solution)/shard_map/ppermute | solution.py:192
  10.7 1.6 %collective-permute-start.11 = (bf16[128,128]{1,0:T(8,128)(2,1)S(1)}, bf16[128,128]{1,0:T(8,128)(2,1)S(1)}, u32[]{:S(2)}, u32[]{:S(2)}) collective-permute-start(bf16[128,128]{1,0:T(8,128)(2,1)S(1)} %get-tuple-element.90), channel_id=1, source_target_pairs={{0,8},{8,16},{16,24},{24,0},{1,9},{9,17},{17,25},{25,1},{2,10},{10... | collective-permute-start | bytes 98312 | tf_op jit(solution)/shard_map/ppermute | solution.py:209
  12.3 2.6 %collective-permute-start.10 = (bf16[128,128]{1,0:T(8,128)(2,1)S(1)}, bf16[128,128]{1,0:T(8,128)(2,1)S(1)}, u32[]{:S(2)}, u32[]{:S(2)}) collective-permute-start(bf16[128,128]{1,0:T(8,128)(2,1)S(1)} %get-tuple-element.90), channel_id=1, source_target_pairs={{0,16},{8,24},{16,0},{24,8},{1,17},{9,25},{17,1},{25,9},{2,18},{10... | collective-permute-start | bytes 98312 | tf_op jit(solution)/shard_map/ppermute | solution.py:209
  14.9 1.3 %collective-permute-start.9 = (bf16[128,128]{1,0:T(8,128)(2,1)S(1)}, bf16[128,128]{1,0:T(8,128)(2,1)S(1)}, u32[]{:S(2)}, u32[]{:S(2)}) collective-permute-start(bf16[128,128]{1,0:T(8,128)(2,1)S(1)} %get-tuple-element.90), channel_id=1, source_target_pairs={{0,24},{8,0},{16,8},{24,16},{1,25},{9,1},{17,9},{25,17},{2,26},{10... | collective-permute-start | bytes 98312 | tf_op jit(solution)/shard_map/ppermute | solution.py:209
  16.2 0.2 collective-permute-done.11.refs_2_
  16.4 0.7 %collective-permute-done.10.refs_1_ = bf16[128,128]{1,0:T(8,128)(2,1)S(1)} collective-permute-done((bf16[128,128]{1,0:T(8,128)(2,1)S(1)}, bf16[128,128]{1,0:T(8,128)(2,1)S(1)}, u32[]{:S(2)}, u32[]{:S(2)}) %collective-permute-start.10) | collective-permute-done | bytes 32800 | tf_op jit(solution)/shard_map/ppermute | solution.py:209
  17.1 1.7 %collective-permute-done.9.refs_0_ = bf16[128,128]{1,0:T(8,128)(2,1)S(1)} collective-permute-done((bf16[128,128]{1,0:T(8,128)(2,1)S(1)}, bf16[128,128]{1,0:T(8,128)(2,1)S(1)}, u32[]{:S(2)}, u32[]{:S(2)}) %collective-permute-start.9) | collective-permute-done | bytes 32800 | tf_op jit(solution)/shard_map/ppermute | solution.py:209
  18.8 0.1 collective-permute-start.12
  18.9 7.5 %conditional.2 = (bf16[256,1024]{1,0:T(8,128)(2,1)}) conditional(s32[]{:T(128)} %convert_element_type.4, () %tuple.18, (bf16[256,1024]{1,0:T(8,128)(2,1)S(1)}, bf16[256,1024]{1,0:T(8,128)(2,1)S(1)}, bf16[256,1024]{1,0:T(8,128)(2,1)S(1)}, bf16[128,128]{1,0:T(8,128)(2,1)S(1)}, bf16[128,128]{1,0:T(8,128)(2,1)S(1)}, ...), branch_computations={%region_0.0_spmd, %region_1.0_spmd} | conditional | flops 402653184 | bytes 4030592 | solution.py:227
  18.9 0.1 branch_1_fun.5
  19.0 1.6 %collective-permute-start = (bf16[128,128]{1,0:T(8,128)(2,1)S(1)}, bf16[128,128]{1,0:T(8,128)(2,1)S(1)}, u32[]{:S(2)}, u32[]{:S(2)}) collective-permute-start(bf16[128,128]{1,0:T(8,128)(2,1)S(1)} %get-tuple-element.56), channel_id=1, source_target_pairs={{0,6},{2,4},{4,2},{6,0},{1,7},{3,5},{5,3},{7,1},{8,14},{10,12},{12... | collective-permute-start | bytes 98312 | tf_op jit(solution)/shard_map/cond/branch_1_fun/ppermute | solution.py:192
  20.6 0.5 %collective-permute-start.1 = (bf16[128,128]{1,0:T(8,128)(2,1)S(1)}, bf16[128,128]{1,0:T(8,128)(2,1)S(1)}, u32[]{:S(2)}, u32[]{:S(2)}) collective-permute-start(bf16[128,128]{1,0:T(8,128)(2,1)S(1)} %get-tuple-element.57), channel_id=1, source_target_pairs={{0,4},{2,6},{4,0},{6,2},{1,5},{3,7},{5,1},{7,3},{8,12},{10,14},{12... | collective-permute-start | bytes 98312 | tf_op jit(solution)/shard_map/cond/branch_1_fun/ppermute | solution.py:192
  21.1 1.5 %collective-permute-start.2 = (bf16[128,128]{1,0:T(8,128)(2,1)S(1)}, bf16[128,128]{1,0:T(8,128)(2,1)S(1)}, u32[]{:S(2)}, u32[]{:S(2)}) collective-permute-start(bf16[128,128]{1,0:T(8,128)(2,1)S(1)} %get-tuple-element.58), channel_id=1, source_target_pairs={{0,2},{2,0},{4,6},{6,4},{1,3},{3,1},{5,7},{7,5},{8,10},{10,8},{12,... | collective-permute-start | bytes 98312 | tf_op jit(solution)/shard_map/cond/branch_1_fun/ppermute | solution.py:192
  22.6 1.5 %branch_1_fun.4.intra_ref = f32[256,1024]{1,0:T(8,128)S(1)} custom-call(bf16[256,1024]{1,0:T(8,128)(2,1)S(1)} %get-tuple-element.48.q_ref, bf16[256,1024]{1,0:T(8,128)(2,1)S(1)} %get-tuple-element.49.k_ref, bf16[256,1024]{1,0:T(8,128)(2,1)S(1)} %get-tuple-element.50.v_ref), custom_call_target="tpu_custom_call" | custom-call | flops 268435456 | bytes 1572864 | tf_op jit(solution)/shard_map/cond/branch_1_fun/pallas_call | solution.py:177
  24.0 0.0 collective-permute-done.refs_0_
  24.1 0.9 %collective-permute-done.1.refs_1_ = bf16[128,128]{1,0:T(8,128)(2,1)S(1)} collective-permute-done((bf16[128,128]{1,0:T(8,128)(2,1)S(1)}, bf16[128,128]{1,0:T(8,128)(2,1)S(1)}, u32[]{:S(2)}, u32[]{:S(2)}) %collective-permute-start.1) | collective-permute-done | bytes 32800 | tf_op jit(solution)/shard_map/cond/branch_1_fun/ppermute | solution.py:192
  25.0 0.2 collective-permute-done.2.refs_2_
  25.2 1.3 %branch_1_fun.7 = bf16[256,1024]{1,0:T(8,128)(2,1)} custom-call(bf16[256,1024]{1,0:T(8,128)(2,1)S(1)} %get-tuple-element.48.q_ref, f32[256,1024]{1,0:T(8,128)S(1)} %branch_1_fun.4.intra_ref, bf16[4,128,128]{2,1,0:T(8,128)(2,1)S(1)} %branch_1_fun.6.prefix_ref), custom_call_target="tpu_custom_call" | custom-call | flops 134217728 | bytes 1703936 | tf_op jit(solution)/shard_map/cond/branch_1_fun/pallas_call | solution.py:177
  26.5 0.0 collective-permute-done.12
  (4 shorter events, 0.1 us)
Async XLA Ops:
  1.9 6.0 %collective-permute-start.6 = (bf16[128,128]{1,0:T(8,128)(2,1)S(1)}, bf16[128,128]{1,0:T(8,128)(2,1)S(1)}, u32[]{:S(2)}, u32[]{:S(2)}) collective-permute-start(bf16[128,128]{1,0:T(8,128)(2,1)S(1)} %shard_map.41), channel_id=1, source_target_pairs={{0,6},{2,4},{4,2},{6,0},{1,7},{3,5},{5,3},{7,1},{8,14},{10,12},{12... | collective-permute-start | bytes 98312 | tf_op jit(solution)/shard_map/ppermute | solution.py:192
  6.2 4.0 %collective-permute-start.7 = (bf16[128,128]{1,0:T(8,128)(2,1)S(1)}, bf16[128,128]{1,0:T(8,128)(2,1)S(1)}, u32[]{:S(2)}, u32[]{:S(2)}) collective-permute-start(bf16[128,128]{1,0:T(8,128)(2,1)S(1)} %shard_map.42), channel_id=1, source_target_pairs={{0,4},{2,6},{4,0},{6,2},{1,5},{3,7},{5,1},{7,3},{8,12},{10,14},{12... | collective-permute-start | bytes 98312 | tf_op jit(solution)/shard_map/ppermute | solution.py:192
  6.7 3.9 %collective-permute-start.8 = (bf16[128,128]{1,0:T(8,128)(2,1)S(1)}, bf16[128,128]{1,0:T(8,128)(2,1)S(1)}, u32[]{:S(2)}, u32[]{:S(2)}) collective-permute-start(bf16[128,128]{1,0:T(8,128)(2,1)S(1)} %get-tuple-element.88), channel_id=1, source_target_pairs={{0,2},{2,0},{4,6},{6,4},{1,3},{3,1},{5,7},{7,5},{8,10},{10,8},{12,... | collective-permute-start | bytes 98312 | tf_op jit(solution)/shard_map/ppermute | solution.py:192
  10.7 5.8 %collective-permute-start.11 = (bf16[128,128]{1,0:T(8,128)(2,1)S(1)}, bf16[128,128]{1,0:T(8,128)(2,1)S(1)}, u32[]{:S(2)}, u32[]{:S(2)}) collective-permute-start(bf16[128,128]{1,0:T(8,128)(2,1)S(1)} %get-tuple-element.90), channel_id=1, source_target_pairs={{0,8},{8,16},{16,24},{24,0},{1,9},{9,17},{17,25},{25,1},{2,10},{10... | collective-permute-start | bytes 98312 | tf_op jit(solution)/shard_map/ppermute | solution.py:209
  12.3 4.8 %collective-permute-start.10 = (bf16[128,128]{1,0:T(8,128)(2,1)S(1)}, bf16[128,128]{1,0:T(8,128)(2,1)S(1)}, u32[]{:S(2)}, u32[]{:S(2)}) collective-permute-start(bf16[128,128]{1,0:T(8,128)(2,1)S(1)} %get-tuple-element.90), channel_id=1, source_target_pairs={{0,16},{8,24},{16,0},{24,8},{1,17},{9,25},{17,1},{25,9},{2,18},{10... | collective-permute-start | bytes 98312 | tf_op jit(solution)/shard_map/ppermute | solution.py:209
  14.9 3.9 %collective-permute-start.9 = (bf16[128,128]{1,0:T(8,128)(2,1)S(1)}, bf16[128,128]{1,0:T(8,128)(2,1)S(1)}, u32[]{:S(2)}, u32[]{:S(2)}) collective-permute-start(bf16[128,128]{1,0:T(8,128)(2,1)S(1)} %get-tuple-element.90), channel_id=1, source_target_pairs={{0,24},{8,0},{16,8},{24,16},{1,25},{9,1},{17,9},{25,17},{2,26},{10... | collective-permute-start | bytes 98312 | tf_op jit(solution)/shard_map/ppermute | solution.py:209
  18.8 7.6 %collective-permute-start.12 = (f32[128,128]{1,0:T(8,128)S(1)}, f32[128,128]{1,0:T(8,128)S(1)}, u32[]{:S(2)}, u32[]{:S(2)}) collective-permute-start(f32[128,128]{1,0:T(8,128)S(1)} %get-tuple-element.93), channel_id=1, source_target_pairs={{0,1},{1,0},{2,3},{3,2},{4,5},{5,4},{6,7},{7,6},{8,9},{9,8},{10,11... | collective-permute-start | bytes 196616 | tf_op jit(solution)/shard_map/ppermute | solution.py:212
  19.0 5.0 %collective-permute-start = (bf16[128,128]{1,0:T(8,128)(2,1)S(1)}, bf16[128,128]{1,0:T(8,128)(2,1)S(1)}, u32[]{:S(2)}, u32[]{:S(2)}) collective-permute-start(bf16[128,128]{1,0:T(8,128)(2,1)S(1)} %get-tuple-element.56), channel_id=1, source_target_pairs={{0,6},{2,4},{4,2},{6,0},{1,7},{3,5},{5,3},{7,1},{8,14},{10,12},{12... | collective-permute-start | bytes 98312 | tf_op jit(solution)/shard_map/cond/branch_1_fun/ppermute | solution.py:192
  20.6 4.4 %collective-permute-start.1 = (bf16[128,128]{1,0:T(8,128)(2,1)S(1)}, bf16[128,128]{1,0:T(8,128)(2,1)S(1)}, u32[]{:S(2)}, u32[]{:S(2)}) collective-permute-start(bf16[128,128]{1,0:T(8,128)(2,1)S(1)} %get-tuple-element.57), channel_id=1, source_target_pairs={{0,4},{2,6},{4,0},{6,2},{1,5},{3,7},{5,1},{7,3},{8,12},{10,14},{12... | collective-permute-start | bytes 98312 | tf_op jit(solution)/shard_map/cond/branch_1_fun/ppermute | solution.py:192
  21.1 4.1 %collective-permute-start.2 = (bf16[128,128]{1,0:T(8,128)(2,1)S(1)}, bf16[128,128]{1,0:T(8,128)(2,1)S(1)}, u32[]{:S(2)}, u32[]{:S(2)}) collective-permute-start(bf16[128,128]{1,0:T(8,128)(2,1)S(1)} %get-tuple-element.58), channel_id=1, source_target_pairs={{0,2},{2,0},{4,6},{6,4},{1,3},{3,1},{5,7},{7,5},{8,10},{10,8},{12,... | collective-permute-start | bytes 98312 | tf_op jit(solution)/shard_map/cond/branch_1_fun/ppermute | solution.py:192

commit v19 on v17

--- a/solution.py
+++ b/solution.py
@@ -47,10 +47,10 @@
             copy.start()
     first = first_head((HEAD_DIM, LANES))
     share = states.shape[1]
+    for slab in copies:
+        for copy in slab:
+            copy.wait()
     for p in range(PAIRS):
-        if p * LANES % SLAB == 0:
-            for copy in copies[p * LANES // SLAB]:
-                copy.wait()
         both = lax.dot_general(
             k_ref[:, lanes_of(p)], v_ref[:, lanes_of(p)], (((0,), (0,)), ((), ())),
             preferred_element_type=jnp.float32)
@@ -62,8 +62,15 @@
         out[...] = states[me ^ d].astype(out.dtype)
 
 
+def load_kernel(q_hbm, after_ref, q_ref, arrived):
+    del after_ref
+    copy = pltpu.make_async_copy(q_hbm, q_ref, arrived)
+    copy.start()
+    copy.wait()
+
+
 def totals_kernel(*refs):
-    *parts, own, out_ref, sent_ref = refs
+    _, *parts, own, out_ref, sent_ref = refs
     total = own[...]
     for part in parts:
         total = total + part[...].astype(F32)
@@ -162,8 +169,9 @@
     moved = sum(a.size * a.dtype.itemsize for a in args)
     single = not isinstance(outs, list)
     outs = [outs] if single else outs
-    specs = [pl.BlockSpec(memory_space=source)] * len(args)
-    args = [pltpu.with_memory_space_constraint(a, source) for a in args]
+    sources = source if isinstance(source, list) else [source] * len(args)
+    specs = [pl.BlockSpec(memory_space=s) for s in sources]
+    args = [pltpu.with_memory_space_constraint(a, s) for a, s in zip(args, sources)]
     aliases = {}
     if onto is not None:
         aliases = {len(args): 0}
@@ -195,9 +203,10 @@
         [(share, F32)] + [(share, BF16)] * (inner - 1) + [(keys.shape, keys.dtype), (values.shape, values.dtype)],
         keys, values, flops=2 * rows * LANES * LANES * PAIRS, source=pltpu.HBM,
         scratch=[pltpu.VMEM((inner,) + share, F32), pltpu.SemaphoreType.DMA((2, SLABS, HALVES))])
+    queries = call(load_kernel, (queries.shape, queries.dtype), queries, own,
+                   source=[pltpu.HBM, pltpu.VMEM], scratch=[pltpu.SemaphoreType.DMA(())])
     mine = swapped([own] + states, "inner", own)
-    total, sent = call(totals_kernel, [(share, F32), (share, BF16)], *mine)
-    total, queries = lax.optimization_barrier((total, queries))
+    total, sent = call(totals_kernel, [(share, F32), (share, BF16)], queries, *mine)
     totals = [lax.ppermute(sent, "outer", [(z, (z + s) % planes) for z in range(planes)])
               for s in reversed(range(1, planes))] + [total]
     below, whole = call(planes_kernel, [(share, F32)] * 2, *totals)

time: 26.5 us -> 26.2 us (0.989)
  waiting for transfers between devices: 7.44 us -> 6.4 us
  Pallas kernels: 4.96 us -> 5.67 us
    ppermute x6, waiting for transfers between devices: 4.87 us -> 3.83 us  [swapped(): lax.ppermute(arrays[d], axis, [(i, i ^ d) for i in range(size)])]
    pallas_call x7 -> x8, Pallas kernels: 4.96 us -> 5.67 us  [call(): pl.pallas_call(kernel, out_shape=[result(shape, dtype) for shape, dtype i...]
  transfers between devices with their start and end apart: 10 -> 10, of which waited for: 8 -> 8; matrix products, arithmetic and copies ran while one was open for 0% -> 0% of each run, Pallas kernels for 11% -> 15%
where the time goes in v19:
time: 26.2 us; the launch traced here: 26 us
  starting transfers between devices  13.8 us (53%)
  waiting for transfers between devices  6.4 us (24%)
  Pallas kernels  5.67 us (22%)
    ppermute x6, starting transfers between devices, swapped(): lax.ppermute(arrays[d], axis, [(i, i ^ d) for i in range(size)])  8.16 us
    pallas_call x8, Pallas kernels, call(): pl.pallas_call(kernel, out_shape=[result(shape, dtype) for shape, dtype i...  5.67 us
    ppermute x3, starting transfers between devices, per_device(): lax.ppermute(sent, 'outer', [(z, (z + s) % planes) for z in range(planes)])  5.56 us
    ppermute x6, waiting for transfers between devices, swapped(): lax.ppermute(arrays[d], axis, [(i, i ^ d) for i in range(size)])  3.83 us
    ppermute x3, waiting for transfers between devices, per_device(): lax.ppermute(sent, 'outer', [(z, (z + s) % planes) for z in range(planes)])  2.57 us
  transfers between devices with their start and end apart: 10, of which 8 were waited for; matrix products, arithmetic and copies ran while one was open for 0% of the time, Pallas kernels for 15%

profile of v19, /device:TPU:0, one launch (start us, length us, event | category | flops | bytes accessed | tf_op | source)
XLA Modules:
  0.0 26.0 jit_solution(9633827232926125828)
XLA Ops:
  0.0 1.8 %shard_map.39 = (f32[128,128]{1,0:T(8,128)S(1)}, bf16[128,128]{1,0:T(8,128)(2,1)S(1)}, bf16[128,128]{1,0:T(8,128)(2,1)S(1)}, bf16[128,128]{1,0:T(8,128)(2,1)S(1)...) custom-call(bf16[256,1024]{1,0:T(8,128)(2,1)} %k_hbm.1, bf16[256,1024]{1,0:T(8,128)(2,1)} %v_hbm.1), custom_call_target="tpu_custom_call" | custom-call | flops 67108864 | bytes 1048576 | tf_op jit(solution)/shard_map/pallas_call | solution.py:180
  1.8 4.0 %collective-permute-start.6 = (bf16[128,128]{1,0:T(8,128)(2,1)S(1)}, bf16[128,128]{1,0:T(8,128)(2,1)S(1)}, u32[]{:S(2)}, u32[]{:S(2)}) collective-permute-start(bf16[128,128]{1,0:T(8,128)(2,1)S(1)} %get-tuple-element.89), channel_id=1, source_target_pairs={{0,6},{2,4},{4,2},{6,0},{1,7},{3,5},{5,3},{7,1},{8,14},{10,12},{12... | collective-permute-start | bytes 98312 | tf_op jit(solution)/shard_map/ppermute | solution.py:195
  5.7 0.5 %collective-permute-start.7 = (bf16[128,128]{1,0:T(8,128)(2,1)S(1)}, bf16[128,128]{1,0:T(8,128)(2,1)S(1)}, u32[]{:S(2)}, u32[]{:S(2)}) collective-permute-start(bf16[128,128]{1,0:T(8,128)(2,1)S(1)} %get-tuple-element.90), channel_id=1, source_target_pairs={{0,4},{2,6},{4,0},{6,2},{1,5},{3,7},{5,1},{7,3},{8,12},{10,14},{12... | collective-permute-start | bytes 98312 | tf_op jit(solution)/shard_map/ppermute | solution.py:195
  6.2 0.1 collective-permute-start.8
  6.4 1.0 %shard_map.40.refs_0_ = bf16[256,1024]{1,0:T(8,128)(2,1)S(1)} custom-call(bf16[256,1024]{1,0:T(8,128)(2,1)} %q_hbm.1, f32[128,128]{1,0:T(8,128)S(1)} %get-tuple-element.86.after_ref.refs_4_), custom_call_target="tpu_custom_call" | custom-call | bytes 589824 | tf_op jit(solution)/shard_map/pallas_call | solution.py:180
  7.4 0.2 collective-permute-done.6.refs_1_
  7.6 2.0 %collective-permute-done.7.refs_2_ = bf16[128,128]{1,0:T(8,128)(2,1)S(1)} collective-permute-done((bf16[128,128]{1,0:T(8,128)(2,1)S(1)}, bf16[128,128]{1,0:T(8,128)(2,1)S(1)}, u32[]{:S(2)}, u32[]{:S(2)}) %collective-permute-start.7) | collective-permute-done | bytes 32800 | tf_op jit(solution)/shard_map/ppermute | solution.py:195
  9.7 0.5 %collective-permute-done.8.refs_3_ = bf16[128,128]{1,0:T(8,128)(2,1)S(1)} collective-permute-done((bf16[128,128]{1,0:T(8,128)(2,1)S(1)}, bf16[128,128]{1,0:T(8,128)(2,1)S(1)}, u32[]{:S(2)}, u32[]{:S(2)}) %collective-permute-start.8) | collective-permute-done | bytes 32800 | tf_op jit(solution)/shard_map/ppermute | solution.py:195
  10.2 1.6 %collective-permute-start.11 = (bf16[128,128]{1,0:T(8,128)(2,1)S(1)}, bf16[128,128]{1,0:T(8,128)(2,1)S(1)}, u32[]{:S(2)}, u32[]{:S(2)}) collective-permute-start(bf16[128,128]{1,0:T(8,128)(2,1)S(1)} %get-tuple-element.92), channel_id=1, source_target_pairs={{0,8},{8,16},{16,24},{24,0},{1,9},{9,17},{17,25},{25,1},{2,10},{10... | collective-permute-start | bytes 98312 | tf_op jit(solution)/shard_map/ppermute | solution.py:210
  11.8 2.6 %collective-permute-start.10 = (bf16[128,128]{1,0:T(8,128)(2,1)S(1)}, bf16[128,128]{1,0:T(8,128)(2,1)S(1)}, u32[]{:S(2)}, u32[]{:S(2)}) collective-permute-start(bf16[128,128]{1,0:T(8,128)(2,1)S(1)} %get-tuple-element.92), channel_id=1, source_target_pairs={{0,16},{8,24},{16,0},{24,8},{1,17},{9,25},{17,1},{25,9},{2,18},{10... | collective-permute-start | bytes 98312 | tf_op jit(solution)/shard_map/ppermute | solution.py:210
  14.4 1.3 %collective-permute-start.9 = (bf16[128,128]{1,0:T(8,128)(2,1)S(1)}, bf16[128,128]{1,0:T(8,128)(2,1)S(1)}, u32[]{:S(2)}, u32[]{:S(2)}) collective-permute-start(bf16[128,128]{1,0:T(8,128)(2,1)S(1)} %get-tuple-element.92), channel_id=1, source_target_pairs={{0,24},{8,0},{16,8},{24,16},{1,25},{9,1},{17,9},{25,17},{2,26},{10... | collective-permute-start | bytes 98312 | tf_op jit(solution)/shard_map/ppermute | solution.py:210
  15.7 0.2 collective-permute-done.11.refs_2_
  15.9 0.7 %collective-permute-done.10.refs_1_ = bf16[128,128]{1,0:T(8,128)(2,1)S(1)} collective-permute-done((bf16[128,128]{1,0:T(8,128)(2,1)S(1)}, bf16[128,128]{1,0:T(8,128)(2,1)S(1)}, u32[]{:S(2)}, u32[]{:S(2)}) %collective-permute-start.10) | collective-permute-done | bytes 32800 | tf_op jit(solution)/shard_map/ppermute | solution.py:210
  16.6 1.7 %collective-permute-done.9.refs_0_ = bf16[128,128]{1,0:T(8,128)(2,1)S(1)} collective-permute-done((bf16[128,128]{1,0:T(8,128)(2,1)S(1)}, bf16[128,128]{1,0:T(8,128)(2,1)S(1)}, u32[]{:S(2)}, u32[]{:S(2)}) %collective-permute-start.9) | collective-permute-done | bytes 32800 | tf_op jit(solution)/shard_map/ppermute | solution.py:210
  18.3 0.1 collective-permute-start.12
  18.4 7.5 %conditional.2 = (bf16[256,1024]{1,0:T(8,128)(2,1)}) conditional(s32[]{:T(128)} %convert_element_type.4, () %tuple.18, (bf16[256,1024]{1,0:T(8,128)(2,1)S(1)}, bf16[256,1024]{1,0:T(8,128)(2,1)S(1)}, bf16[256,1024]{1,0:T(8,128)(2,1)S(1)}, bf16[128,128]{1,0:T(8,128)(2,1)S(1)}, bf16[128,128]{1,0:T(8,128)(2,1)S(1)}, ...), branch_computations={%region_0.0_spmd, %region_1.0_spmd} | conditional | flops 402653184 | bytes 4030592 | solution.py:228
  18.4 0.1 branch_1_fun.5
  18.5 1.6 %collective-permute-start = (bf16[128,128]{1,0:T(8,128)(2,1)S(1)}, bf16[128,128]{1,0:T(8,128)(2,1)S(1)}, u32[]{:S(2)}, u32[]{:S(2)}) collective-permute-start(bf16[128,128]{1,0:T(8,128)(2,1)S(1)} %get-tuple-element.56), channel_id=1, source_target_pairs={{0,6},{2,4},{4,2},{6,0},{1,7},{3,5},{5,3},{7,1},{8,14},{10,12},{12... | collective-permute-start | bytes 98312 | tf_op jit(solution)/shard_map/cond/branch_1_fun/ppermute | solution.py:195
  20.1 0.5 %collective-permute-start.1 = (bf16[128,128]{1,0:T(8,128)(2,1)S(1)}, bf16[128,128]{1,0:T(8,128)(2,1)S(1)}, u32[]{:S(2)}, u32[]{:S(2)}) collective-permute-start(bf16[128,128]{1,0:T(8,128)(2,1)S(1)} %get-tuple-element.57), channel_id=1, source_target_pairs={{0,4},{2,6},{4,0},{6,2},{1,5},{3,7},{5,1},{7,3},{8,12},{10,14},{12... | collective-permute-start | bytes 98312 | tf_op jit(solution)/shard_map/cond/branch_1_fun/ppermute | solution.py:195
  20.6 1.5 %collective-permute-start.2 = (bf16[128,128]{1,0:T(8,128)(2,1)S(1)}, bf16[128,128]{1,0:T(8,128)(2,1)S(1)}, u32[]{:S(2)}, u32[]{:S(2)}) collective-permute-start(bf16[128,128]{1,0:T(8,128)(2,1)S(1)} %get-tuple-element.58), channel_id=1, source_target_pairs={{0,2},{2,0},{4,6},{6,4},{1,3},{3,1},{5,7},{7,5},{8,10},{10,8},{12,... | collective-permute-start | bytes 98312 | tf_op jit(solution)/shard_map/cond/branch_1_fun/ppermute | solution.py:195
  22.1 1.5 %branch_1_fun.4.intra_ref = f32[256,1024]{1,0:T(8,128)S(1)} custom-call(bf16[256,1024]{1,0:T(8,128)(2,1)S(1)} %get-tuple-element.48.q_ref, bf16[256,1024]{1,0:T(8,128)(2,1)S(1)} %get-tuple-element.49.k_ref, bf16[256,1024]{1,0:T(8,128)(2,1)S(1)} %get-tuple-element.50.v_ref), custom_call_target="tpu_custom_call" | custom-call | flops 268435456 | bytes 1572864 | tf_op jit(solution)/shard_map/cond/branch_1_fun/pallas_call | solution.py:180
  23.6 0.0 collective-permute-done.refs_0_
  23.6 0.9 %collective-permute-done.1.refs_1_ = bf16[128,128]{1,0:T(8,128)(2,1)S(1)} collective-permute-done((bf16[128,128]{1,0:T(8,128)(2,1)S(1)}, bf16[128,128]{1,0:T(8,128)(2,1)S(1)}, u32[]{:S(2)}, u32[]{:S(2)}) %collective-permute-start.1) | collective-permute-done | bytes 32800 | tf_op jit(solution)/shard_map/cond/branch_1_fun/ppermute | solution.py:195
  24.5 0.2 collective-permute-done.2.refs_2_
  24.7 1.3 %branch_1_fun.7 = bf16[256,1024]{1,0:T(8,128)(2,1)} custom-call(bf16[256,1024]{1,0:T(8,128)(2,1)S(1)} %get-tuple-element.48.q_ref, f32[256,1024]{1,0:T(8,128)S(1)} %branch_1_fun.4.intra_ref, bf16[4,128,128]{2,1,0:T(8,128)(2,1)S(1)} %branch_1_fun.6.prefix_ref), custom_call_target="tpu_custom_call" | custom-call | flops 134217728 | bytes 1703936 | tf_op jit(solution)/shard_map/cond/branch_1_fun/pallas_call | solution.py:180
  26.0 0.0 collective-permute-done.12
  (4 shorter events, 0.1 us)
Async XLA Ops:
  1.8 5.9 %collective-permute-start.6 = (bf16[128,128]{1,0:T(8,128)(2,1)S(1)}, bf16[128,128]{1,0:T(8,128)(2,1)S(1)}, u32[]{:S(2)}, u32[]{:S(2)}) collective-permute-start(bf16[128,128]{1,0:T(8,128)(2,1)S(1)} %get-tuple-element.89), channel_id=1, source_target_pairs={{0,6},{2,4},{4,2},{6,0},{1,7},{3,5},{5,3},{7,1},{8,14},{10,12},{12... | collective-permute-start | bytes 98312 | tf_op jit(solution)/shard_map/ppermute | solution.py:195
  5.7 3.9 %collective-permute-start.7 = (bf16[128,128]{1,0:T(8,128)(2,1)S(1)}, bf16[128,128]{1,0:T(8,128)(2,1)S(1)}, u32[]{:S(2)}, u32[]{:S(2)}) collective-permute-start(bf16[128,128]{1,0:T(8,128)(2,1)S(1)} %get-tuple-element.90), channel_id=1, source_target_pairs={{0,4},{2,6},{4,0},{6,2},{1,5},{3,7},{5,1},{7,3},{8,12},{10,14},{12... | collective-permute-start | bytes 98312 | tf_op jit(solution)/shard_map/ppermute | solution.py:195
  6.2 3.9 %collective-permute-start.8 = (bf16[128,128]{1,0:T(8,128)(2,1)S(1)}, bf16[128,128]{1,0:T(8,128)(2,1)S(1)}, u32[]{:S(2)}, u32[]{:S(2)}) collective-permute-start(bf16[128,128]{1,0:T(8,128)(2,1)S(1)} %get-tuple-element.91), channel_id=1, source_target_pairs={{0,2},{2,0},{4,6},{6,4},{1,3},{3,1},{5,7},{7,5},{8,10},{10,8},{12,... | collective-permute-start | bytes 98312 | tf_op jit(solution)/shard_map/ppermute | solution.py:195
  10.2 5.8 %collective-permute-start.11 = (bf16[128,128]{1,0:T(8,128)(2,1)S(1)}, bf16[128,128]{1,0:T(8,128)(2,1)S(1)}, u32[]{:S(2)}, u32[]{:S(2)}) collective-permute-start(bf16[128,128]{1,0:T(8,128)(2,1)S(1)} %get-tuple-element.92), channel_id=1, source_target_pairs={{0,8},{8,16},{16,24},{24,0},{1,9},{9,17},{17,25},{25,1},{2,10},{10... | collective-permute-start | bytes 98312 | tf_op jit(solution)/shard_map/ppermute | solution.py:210
  11.8 4.8 %collective-permute-start.10 = (bf16[128,128]{1,0:T(8,128)(2,1)S(1)}, bf16[128,128]{1,0:T(8,128)(2,1)S(1)}, u32[]{:S(2)}, u32[]{:S(2)}) collective-permute-start(bf16[128,128]{1,0:T(8,128)(2,1)S(1)} %get-tuple-element.92), channel_id=1, source_target_pairs={{0,16},{8,24},{16,0},{24,8},{1,17},{9,25},{17,1},{25,9},{2,18},{10... | collective-permute-start | bytes 98312 | tf_op jit(solution)/shard_map/ppermute | solution.py:210
  14.4 3.9 %collective-permute-start.9 = (bf16[128,128]{1,0:T(8,128)(2,1)S(1)}, bf16[128,128]{1,0:T(8,128)(2,1)S(1)}, u32[]{:S(2)}, u32[]{:S(2)}) collective-permute-start(bf16[128,128]{1,0:T(8,128)(2,1)S(1)} %get-tuple-element.92), channel_id=1, source_target_pairs={{0,24},{8,0},{16,8},{24,16},{1,25},{9,1},{17,9},{25,17},{2,26},{10... | collective-permute-start | bytes 98312 | tf_op jit(solution)/shard_map/ppermute | solution.py:210
  18.3 7.6 %collective-permute-start.12 = (f32[128,128]{1,0:T(8,128)S(1)}, f32[128,128]{1,0:T(8,128)S(1)}, u32[]{:S(2)}, u32[]{:S(2)}) collective-permute-start(f32[128,128]{1,0:T(8,128)S(1)} %get-tuple-element.95), channel_id=1, source_target_pairs={{0,1},{1,0},{2,3},{3,2},{4,5},{5,4},{6,7},{7,6},{8,9},{9,8},{10,11... | collective-permute-start | bytes 196616 | tf_op jit(solution)/shard_map/ppermute | solution.py:213
  18.5 5.0 %collective-permute-start = (bf16[128,128]{1,0:T(8,128)(2,1)S(1)}, bf16[128,128]{1,0:T(8,128)(2,1)S(1)}, u32[]{:S(2)}, u32[]{:S(2)}) collective-permute-start(bf16[128,128]{1,0:T(8,128)(2,1)S(1)} %get-tuple-element.56), channel_id=1, source_target_pairs={{0,6},{2,4},{4,2},{6,0},{1,7},{3,5},{5,3},{7,1},{8,14},{10,12},{12... | collective-permute-start | bytes 98312 | tf_op jit(solution)/shard_map/cond/branch_1_fun/ppermute | solution.py:195
  20.1 4.4 %collective-permute-start.1 = (bf16[128,128]{1,0:T(8,128)(2,1)S(1)}, bf16[128,128]{1,0:T(8,128)(2,1)S(1)}, u32[]{:S(2)}, u32[]{:S(2)}) collective-permute-start(bf16[128,128]{1,0:T(8,128)(2,1)S(1)} %get-tuple-element.57), channel_id=1, source_target_pairs={{0,4},{2,6},{4,0},{6,2},{1,5},{3,7},{5,1},{7,3},{8,12},{10,14},{12... | collective-permute-start | bytes 98312 | tf_op jit(solution)/shard_map/cond/branch_1_fun/ppermute | solution.py:195
  20.6 4.1 %collective-permute-start.2 = (bf16[128,128]{1,0:T(8,128)(2,1)S(1)}, bf16[128,128]{1,0:T(8,128)(2,1)S(1)}, u32[]{:S(2)}, u32[]{:S(2)}) collective-permute-start(bf16[128,128]{1,0:T(8,128)(2,1)S(1)} %get-tuple-element.58), channel_id=1, source_target_pairs={{0,2},{2,0},{4,6},{6,4},{1,3},{3,1},{5,7},{7,5},{8,10},{10,8},{12,... | collective-permute-start | bytes 98312 | tf_op jit(solution)/shard_map/cond/branch_1_fun/ppermute | solution.py:195

commit v20 on v19

--- a/solution.py
+++ b/solution.py
@@ -11,7 +11,6 @@
 HEAD_DIM = 64
 PAIRS = HEADS // 2
 LANES = 2 * HEAD_DIM
-SLABS = 4
 HALVES = 2
 SLAB = 256
 VMEM = pl.BlockSpec(memory_space=pltpu.VMEM)
@@ -35,20 +34,17 @@
     *outs, k_ref, v_ref, states, arrived = refs
     rows = k_ref.shape[0] // HALVES
     copies = []
-    for s in range(SLABS):
-        lanes = slice(s * SLAB, (s + 1) * SLAB)
-        copies.append([])
-        for r in range(HALVES):
-            part = (pl.ds(r * rows, rows), lanes)
-            copies[-1] += [
-                pltpu.make_async_copy(k_hbm.at[part], k_ref.at[part], arrived.at[0, s, r]),
-                pltpu.make_async_copy(v_hbm.at[part], v_ref.at[part], arrived.at[1, s, r])]
+    for r in range(HALVES):
+        part = pl.ds(r * rows, rows)
+        copies.append([
+            pltpu.make_async_copy(k_hbm.at[part], k_ref.at[part], arrived.at[0, r]),
+            pltpu.make_async_copy(v_hbm.at[part], v_ref.at[part], arrived.at[1, r])])
         for copy in copies[-1]:
             copy.start()
     first = first_head((HEAD_DIM, LANES))
     share = states.shape[1]
-    for slab in copies:
-        for copy in slab:
+    for half in copies:
+        for copy in half:
             copy.wait()
     for p in range(PAIRS):
         both = lax.dot_general(
@@ -202,7 +198,7 @@
         states_kernel,
         [(share, F32)] + [(share, BF16)] * (inner - 1) + [(keys.shape, keys.dtype), (values.shape, values.dtype)],
         keys, values, flops=2 * rows * LANES * LANES * PAIRS, source=pltpu.HBM,
-        scratch=[pltpu.VMEM((inner,) + share, F32), pltpu.SemaphoreType.DMA((2, SLABS, HALVES))])
+        scratch=[pltpu.VMEM((inner,) + share, F32), pltpu.SemaphoreType.DMA((2, HALVES))])
     queries = call(load_kernel, (queries.shape, queries.dtype), queries, own,
                    source=[pltpu.HBM, pltpu.VMEM], scratch=[pltpu.SemaphoreType.DMA(())])
     mine = swapped([own] + states, "inner", own)

time: 26.2 us -> 26 us (level)
  no operation moved by 1% of the time
where the time goes in v20:
time: 26 us; the launch traced here: 25.8 us
  starting transfers between devices  13.8 us (53%)
  waiting for transfers between devices  6.4 us (25%)
  Pallas kernels  5.51 us (21%)
    ppermute x6, starting transfers between devices, swapped(): lax.ppermute(arrays[d], axis, [(i, i ^ d) for i in range(size)])  8.16 us
    ppermute x3, starting transfers between devices, per_device(): lax.ppermute(sent, 'outer', [(z, (z + s) % planes) for z in range(planes)])  5.57 us
    pallas_call x8, Pallas kernels, call(): pl.pallas_call(kernel, out_shape=[result(shape, dtype) for shape, dtype i...  5.51 us
    ppermute x6, waiting for transfers between devices, swapped(): lax.ppermute(arrays[d], axis, [(i, i ^ d) for i in range(size)])  3.83 us
    ppermute x3, waiting for transfers between devices, per_device(): lax.ppermute(sent, 'outer', [(z, (z + s) % planes) for z in range(planes)])  2.56 us
  transfers between devices with their start and end apart: 10, of which 8 were waited for; matrix products, arithmetic and copies ran while one was open for 0% of the time, Pallas kernels for 15%

profile of v20, /device:TPU:0, one launch (start us, length us, event | category | flops | bytes accessed | tf_op | source)
XLA Modules:
  0.0 25.8 jit_solution(5357042983363371106)
XLA Ops:
  0.0 1.6 %shard_map.39 = (f32[128,128]{1,0:T(8,128)S(1)}, bf16[128,128]{1,0:T(8,128)(2,1)S(1)}, bf16[128,128]{1,0:T(8,128)(2,1)S(1)}, bf16[128,128]{1,0:T(8,128)(2,1)S(1)...) custom-call(bf16[256,1024]{1,0:T(8,128)(2,1)} %k_hbm.1, bf16[256,1024]{1,0:T(8,128)(2,1)} %v_hbm.1), custom_call_target="tpu_custom_call" | custom-call | flops 67108864 | bytes 1048576 | tf_op jit(solution)/shard_map/pallas_call | solution.py:176
  1.6 4.0 %collective-permute-start.6 = (bf16[128,128]{1,0:T(8,128)(2,1)S(1)}, bf16[128,128]{1,0:T(8,128)(2,1)S(1)}, u32[]{:S(2)}, u32[]{:S(2)}) collective-permute-start(bf16[128,128]{1,0:T(8,128)(2,1)S(1)} %get-tuple-element.89), channel_id=1, source_target_pairs={{0,6},{2,4},{4,2},{6,0},{1,7},{3,5},{5,3},{7,1},{8,14},{10,12},{12... | collective-permute-start | bytes 98312 | tf_op jit(solution)/shard_map/ppermute | solution.py:191
  5.6 0.5 %collective-permute-start.7 = (bf16[128,128]{1,0:T(8,128)(2,1)S(1)}, bf16[128,128]{1,0:T(8,128)(2,1)S(1)}, u32[]{:S(2)}, u32[]{:S(2)}) collective-permute-start(bf16[128,128]{1,0:T(8,128)(2,1)S(1)} %get-tuple-element.90), channel_id=1, source_target_pairs={{0,4},{2,6},{4,0},{6,2},{1,5},{3,7},{5,1},{7,3},{8,12},{10,14},{12... | collective-permute-start | bytes 98312 | tf_op jit(solution)/shard_map/ppermute | solution.py:191
  6.1 0.1 collective-permute-start.8
  6.2 1.0 %shard_map.40.refs_0_ = bf16[256,1024]{1,0:T(8,128)(2,1)S(1)} custom-call(bf16[256,1024]{1,0:T(8,128)(2,1)} %q_hbm.1, f32[128,128]{1,0:T(8,128)S(1)} %get-tuple-element.86.after_ref.refs_4_), custom_call_target="tpu_custom_call" | custom-call | bytes 589824 | tf_op jit(solution)/shard_map/pallas_call | solution.py:176
  7.3 0.2 collective-permute-done.6.refs_1_
  7.5 2.0 %collective-permute-done.7.refs_2_ = bf16[128,128]{1,0:T(8,128)(2,1)S(1)} collective-permute-done((bf16[128,128]{1,0:T(8,128)(2,1)S(1)}, bf16[128,128]{1,0:T(8,128)(2,1)S(1)}, u32[]{:S(2)}, u32[]{:S(2)}) %collective-permute-start.7) | collective-permute-done | bytes 32800 | tf_op jit(solution)/shard_map/ppermute | solution.py:191
  9.5 0.5 %collective-permute-done.8.refs_3_ = bf16[128,128]{1,0:T(8,128)(2,1)S(1)} collective-permute-done((bf16[128,128]{1,0:T(8,128)(2,1)S(1)}, bf16[128,128]{1,0:T(8,128)(2,1)S(1)}, u32[]{:S(2)}, u32[]{:S(2)}) %collective-permute-start.8) | collective-permute-done | bytes 32800 | tf_op jit(solution)/shard_map/ppermute | solution.py:191
  10.0 1.6 %collective-permute-start.11 = (bf16[128,128]{1,0:T(8,128)(2,1)S(1)}, bf16[128,128]{1,0:T(8,128)(2,1)S(1)}, u32[]{:S(2)}, u32[]{:S(2)}) collective-permute-start(bf16[128,128]{1,0:T(8,128)(2,1)S(1)} %get-tuple-element.92), channel_id=1, source_target_pairs={{0,8},{8,16},{16,24},{24,0},{1,9},{9,17},{17,25},{25,1},{2,10},{10... | collective-permute-start | bytes 98312 | tf_op jit(solution)/shard_map/ppermute | solution.py:206
  11.6 2.6 %collective-permute-start.10 = (bf16[128,128]{1,0:T(8,128)(2,1)S(1)}, bf16[128,128]{1,0:T(8,128)(2,1)S(1)}, u32[]{:S(2)}, u32[]{:S(2)}) collective-permute-start(bf16[128,128]{1,0:T(8,128)(2,1)S(1)} %get-tuple-element.92), channel_id=1, source_target_pairs={{0,16},{8,24},{16,0},{24,8},{1,17},{9,25},{17,1},{25,9},{2,18},{10... | collective-permute-start | bytes 98312 | tf_op jit(solution)/shard_map/ppermute | solution.py:206
  14.2 1.4 %collective-permute-start.9 = (bf16[128,128]{1,0:T(8,128)(2,1)S(1)}, bf16[128,128]{1,0:T(8,128)(2,1)S(1)}, u32[]{:S(2)}, u32[]{:S(2)}) collective-permute-start(bf16[128,128]{1,0:T(8,128)(2,1)S(1)} %get-tuple-element.92), channel_id=1, source_target_pairs={{0,24},{8,0},{16,8},{24,16},{1,25},{9,1},{17,9},{25,17},{2,26},{10... | collective-permute-start | bytes 98312 | tf_op jit(solution)/shard_map/ppermute | solution.py:206
  15.6 0.2 collective-permute-done.11.refs_2_
  15.8 0.7 %collective-permute-done.10.refs_1_ = bf16[128,128]{1,0:T(8,128)(2,1)S(1)} collective-permute-done((bf16[128,128]{1,0:T(8,128)(2,1)S(1)}, bf16[128,128]{1,0:T(8,128)(2,1)S(1)}, u32[]{:S(2)}, u32[]{:S(2)}) %collective-permute-start.10) | collective-permute-done | bytes 32800 | tf_op jit(solution)/shard_map/ppermute | solution.py:206
  16.5 1.7 %collective-permute-done.9.refs_0_ = bf16[128,128]{1,0:T(8,128)(2,1)S(1)} collective-permute-done((bf16[128,128]{1,0:T(8,128)(2,1)S(1)}, bf16[128,128]{1,0:T(8,128)(2,1)S(1)}, u32[]{:S(2)}, u32[]{:S(2)}) %collective-permute-start.9) | collective-permute-done | bytes 32800 | tf_op jit(solution)/shard_map/ppermute | solution.py:206
  18.2 0.1 collective-permute-start.12
  18.3 7.5 %conditional.2 = (bf16[256,1024]{1,0:T(8,128)(2,1)}) conditional(s32[]{:T(128)} %convert_element_type.4, () %tuple.18, (bf16[256,1024]{1,0:T(8,128)(2,1)S(1)}, bf16[256,1024]{1,0:T(8,128)(2,1)S(1)}, bf16[256,1024]{1,0:T(8,128)(2,1)S(1)}, bf16[128,128]{1,0:T(8,128)(2,1)S(1)}, bf16[128,128]{1,0:T(8,128)(2,1)S(1)}, ...), branch_computations={%region_0.0_spmd, %region_1.0_spmd} | conditional | flops 402653184 | bytes 4030592 | solution.py:224
  18.3 0.1 branch_1_fun.5
  18.4 1.6 %collective-permute-start = (bf16[128,128]{1,0:T(8,128)(2,1)S(1)}, bf16[128,128]{1,0:T(8,128)(2,1)S(1)}, u32[]{:S(2)}, u32[]{:S(2)}) collective-permute-start(bf16[128,128]{1,0:T(8,128)(2,1)S(1)} %get-tuple-element.56), channel_id=1, source_target_pairs={{0,6},{2,4},{4,2},{6,0},{1,7},{3,5},{5,3},{7,1},{8,14},{10,12},{12... | collective-permute-start | bytes 98312 | tf_op jit(solution)/shard_map/cond/branch_1_fun/ppermute | solution.py:191
  19.9 0.5 %collective-permute-start.1 = (bf16[128,128]{1,0:T(8,128)(2,1)S(1)}, bf16[128,128]{1,0:T(8,128)(2,1)S(1)}, u32[]{:S(2)}, u32[]{:S(2)}) collective-permute-start(bf16[128,128]{1,0:T(8,128)(2,1)S(1)} %get-tuple-element.57), channel_id=1, source_target_pairs={{0,4},{2,6},{4,0},{6,2},{1,5},{3,7},{5,1},{7,3},{8,12},{10,14},{12... | collective-permute-start | bytes 98312 | tf_op jit(solution)/shard_map/cond/branch_1_fun/ppermute | solution.py:191
  20.4 1.5 %collective-permute-start.2 = (bf16[128,128]{1,0:T(8,128)(2,1)S(1)}, bf16[128,128]{1,0:T(8,128)(2,1)S(1)}, u32[]{:S(2)}, u32[]{:S(2)}) collective-permute-start(bf16[128,128]{1,0:T(8,128)(2,1)S(1)} %get-tuple-element.58), channel_id=1, source_target_pairs={{0,2},{2,0},{4,6},{6,4},{1,3},{3,1},{5,7},{7,5},{8,10},{10,8},{12,... | collective-permute-start | bytes 98312 | tf_op jit(solution)/shard_map/cond/branch_1_fun/ppermute | solution.py:191
  21.9 1.5 %branch_1_fun.4.intra_ref = f32[256,1024]{1,0:T(8,128)S(1)} custom-call(bf16[256,1024]{1,0:T(8,128)(2,1)S(1)} %get-tuple-element.48.q_ref, bf16[256,1024]{1,0:T(8,128)(2,1)S(1)} %get-tuple-element.49.k_ref, bf16[256,1024]{1,0:T(8,128)(2,1)S(1)} %get-tuple-element.50.v_ref), custom_call_target="tpu_custom_call" | custom-call | flops 268435456 | bytes 1572864 | tf_op jit(solution)/shard_map/cond/branch_1_fun/pallas_call | solution.py:176
  23.4 0.0 collective-permute-done.refs_0_
  23.4 0.9 %collective-permute-done.1.refs_1_ = bf16[128,128]{1,0:T(8,128)(2,1)S(1)} collective-permute-done((bf16[128,128]{1,0:T(8,128)(2,1)S(1)}, bf16[128,128]{1,0:T(8,128)(2,1)S(1)}, u32[]{:S(2)}, u32[]{:S(2)}) %collective-permute-start.1) | collective-permute-done | bytes 32800 | tf_op jit(solution)/shard_map/cond/branch_1_fun/ppermute | solution.py:191
  24.3 0.2 collective-permute-done.2.refs_2_
  24.5 1.3 %branch_1_fun.7 = bf16[256,1024]{1,0:T(8,128)(2,1)} custom-call(bf16[256,1024]{1,0:T(8,128)(2,1)S(1)} %get-tuple-element.48.q_ref, f32[256,1024]{1,0:T(8,128)S(1)} %branch_1_fun.4.intra_ref, bf16[4,128,128]{2,1,0:T(8,128)(2,1)S(1)} %branch_1_fun.6.prefix_ref), custom_call_target="tpu_custom_call" | custom-call | flops 134217728 | bytes 1703936 | tf_op jit(solution)/shard_map/cond/branch_1_fun/pallas_call | solution.py:176
  25.8 0.0 collective-permute-done.12
  (4 shorter events, 0.1 us)
Async XLA Ops:
  1.6 5.9 %collective-permute-start.6 = (bf16[128,128]{1,0:T(8,128)(2,1)S(1)}, bf16[128,128]{1,0:T(8,128)(2,1)S(1)}, u32[]{:S(2)}, u32[]{:S(2)}) collective-permute-start(bf16[128,128]{1,0:T(8,128)(2,1)S(1)} %get-tuple-element.89), channel_id=1, source_target_pairs={{0,6},{2,4},{4,2},{6,0},{1,7},{3,5},{5,3},{7,1},{8,14},{10,12},{12... | collective-permute-start | bytes 98312 | tf_op jit(solution)/shard_map/ppermute | solution.py:191
  5.6 3.9 %collective-permute-start.7 = (bf16[128,128]{1,0:T(8,128)(2,1)S(1)}, bf16[128,128]{1,0:T(8,128)(2,1)S(1)}, u32[]{:S(2)}, u32[]{:S(2)}) collective-permute-start(bf16[128,128]{1,0:T(8,128)(2,1)S(1)} %get-tuple-element.90), channel_id=1, source_target_pairs={{0,4},{2,6},{4,0},{6,2},{1,5},{3,7},{5,1},{7,3},{8,12},{10,14},{12... | collective-permute-start | bytes 98312 | tf_op jit(solution)/shard_map/ppermute | solution.py:191
  6.1 3.9 %collective-permute-start.8 = (bf16[128,128]{1,0:T(8,128)(2,1)S(1)}, bf16[128,128]{1,0:T(8,128)(2,1)S(1)}, u32[]{:S(2)}, u32[]{:S(2)}) collective-permute-start(bf16[128,128]{1,0:T(8,128)(2,1)S(1)} %get-tuple-element.91), channel_id=1, source_target_pairs={{0,2},{2,0},{4,6},{6,4},{1,3},{3,1},{5,7},{7,5},{8,10},{10,8},{12,... | collective-permute-start | bytes 98312 | tf_op jit(solution)/shard_map/ppermute | solution.py:191
  10.0 5.8 %collective-permute-start.11 = (bf16[128,128]{1,0:T(8,128)(2,1)S(1)}, bf16[128,128]{1,0:T(8,128)(2,1)S(1)}, u32[]{:S(2)}, u32[]{:S(2)}) collective-permute-start(bf16[128,128]{1,0:T(8,128)(2,1)S(1)} %get-tuple-element.92), channel_id=1, source_target_pairs={{0,8},{8,16},{16,24},{24,0},{1,9},{9,17},{17,25},{25,1},{2,10},{10... | collective-permute-start | bytes 98312 | tf_op jit(solution)/shard_map/ppermute | solution.py:206
  11.6 4.8 %collective-permute-start.10 = (bf16[128,128]{1,0:T(8,128)(2,1)S(1)}, bf16[128,128]{1,0:T(8,128)(2,1)S(1)}, u32[]{:S(2)}, u32[]{:S(2)}) collective-permute-start(bf16[128,128]{1,0:T(8,128)(2,1)S(1)} %get-tuple-element.92), channel_id=1, source_target_pairs={{0,16},{8,24},{16,0},{24,8},{1,17},{9,25},{17,1},{25,9},{2,18},{10... | collective-permute-start | bytes 98312 | tf_op jit(solution)/shard_map/ppermute | solution.py:206
  14.2 3.9 %collective-permute-start.9 = (bf16[128,128]{1,0:T(8,128)(2,1)S(1)}, bf16[128,128]{1,0:T(8,128)(2,1)S(1)}, u32[]{:S(2)}, u32[]{:S(2)}) collective-permute-start(bf16[128,128]{1,0:T(8,128)(2,1)S(1)} %get-tuple-element.92), channel_id=1, source_target_pairs={{0,24},{8,0},{16,8},{24,16},{1,25},{9,1},{17,9},{25,17},{2,26},{10... | collective-permute-start | bytes 98312 | tf_op jit(solution)/shard_map/ppermute | solution.py:206
  18.2 7.6 %collective-permute-start.12 = (f32[128,128]{1,0:T(8,128)S(1)}, f32[128,128]{1,0:T(8,128)S(1)}, u32[]{:S(2)}, u32[]{:S(2)}) collective-permute-start(f32[128,128]{1,0:T(8,128)S(1)} %get-tuple-element.95), channel_id=1, source_target_pairs={{0,1},{1,0},{2,3},{3,2},{4,5},{5,4},{6,7},{7,6},{8,9},{9,8},{10,11... | collective-permute-start | bytes 196616 | tf_op jit(solution)/shard_map/ppermute | solution.py:209
  18.4 5.0 %collective-permute-start = (bf16[128,128]{1,0:T(8,128)(2,1)S(1)}, bf16[128,128]{1,0:T(8,128)(2,1)S(1)}, u32[]{:S(2)}, u32[]{:S(2)}) collective-permute-start(bf16[128,128]{1,0:T(8,128)(2,1)S(1)} %get-tuple-element.56), channel_id=1, source_target_pairs={{0,6},{2,4},{4,2},{6,0},{1,7},{3,5},{5,3},{7,1},{8,14},{10,12},{12... | collective-permute-start | bytes 98312 | tf_op jit(solution)/shard_map/cond/branch_1_fun/ppermute | solution.py:191
  19.9 4.4 %collective-permute-start.1 = (bf16[128,128]{1,0:T(8,128)(2,1)S(1)}, bf16[128,128]{1,0:T(8,128)(2,1)S(1)}, u32[]{:S(2)}, u32[]{:S(2)}) collective-permute-start(bf16[128,128]{1,0:T(8,128)(2,1)S(1)} %get-tuple-element.57), channel_id=1, source_target_pairs={{0,4},{2,6},{4,0},{6,2},{1,5},{3,7},{5,1},{7,3},{8,12},{10,14},{12... | collective-permute-start | bytes 98312 | tf_op jit(solution)/shard_map/cond/branch_1_fun/ppermute | solution.py:191
  20.4 4.1 %collective-permute-start.2 = (bf16[128,128]{1,0:T(8,128)(2,1)S(1)}, bf16[128,128]{1,0:T(8,128)(2,1)S(1)}, u32[]{:S(2)}, u32[]{:S(2)}) collective-permute-start(bf16[128,128]{1,0:T(8,128)(2,1)S(1)} %get-tuple-element.58), channel_id=1, source_target_pairs={{0,2},{2,0},{4,6},{6,4},{1,3},{3,1},{5,7},{7,5},{8,10},{10,8},{12,... | collective-permute-start | bytes 98312 | tf_op jit(solution)/shard_map/cond/branch_1_fun/ppermute | solution.py:191
